TPU v7x, 32 devices: a whole 2x2x4 slice. The times are simulated.
32 devices in a mesh: dp: 8 (over z, core), tensor: 4 (over y, x).
Axes of the slice: x: 2, y: 2, z: 4, core: 2. Of those that a mesh axis runs over, the one named last changes fastest.
Arguments:
- tokens: bfloat16 [16384, 2048], P(('dp', 'tensor')), may hold values from -6 to 6
- norm_gain: float32 [2048], replicated, may hold values from 0.1 to 1.9
- norm_shift: float32 [2048], replicated, may hold values from -1.75 to 1.75
- weight_qkv: bfloat16 [2048, 3, 2048], P('dp', None, 'tensor'), may hold values from -0.125 to 0.125
- bias_qkv: float32 [3, 2048], P(None, 'tensor'), may hold values from -1.5 to 1.5
- weight_dense: bfloat16 [2048, 2048], P('tensor', 'dp'), may hold values from -0.5 to 0.5
- weight_up: bfloat16 [2048, 8192], P('dp', 'tensor'), may hold values from -0.125 to 0.125
- bias_up: float32 [8192], P('tensor'), may hold values from -3 to 3
- weight_down: bfloat16 [8192, 2048], P('tensor', 'dp'), may hold values from -0.0625 to 0.0625
- bias_out: float32 [2048], replicated, may hold values from -1.75 to 1.75
- cotangent: bfloat16 [16384, 2048], P(('dp', 'tensor')), may hold values from -6 to 6
Outputs:
- block_out: bfloat16 [16384, 2048], P(('dp', 'tensor'))
- grad_tokens: bfloat16 [16384, 2048], P(('dp', 'tensor'))
- grad_norm_gain: float32 [2048], replicated
- grad_norm_shift: float32 [2048], replicated
- grad_weight_qkv: float32 [2048, 3, 2048], P('dp', None, 'tensor')
- grad_bias_qkv: float32 [3, 2048], P(None, 'tensor')
- grad_weight_dense: float32 [2048, 2048], P('tensor', 'dp')
- grad_weight_up: float32 [2048, 8192], P('dp', 'tensor')
- grad_bias_up: float32 [8192], P('tensor')
- grad_weight_down: float32 [8192, 2048], P('tensor', 'dp')
- grad_bias_out: float32 [2048], replicated
All inputs are finite; a program needn't handle non-finite values.
Results may differ from a plain program's by a relative error of at most 0.009.
Values may be sent and summed in bfloat16 or wider, within the bound.
No kernel may reach another device: no remote copies, remote signals or barrier semaphores. Data moves between devices by JAX's collectives and lax.ppermute only.
A program may use at most 320 MiB of HBM per device.

v0:
```python
from functools import partial

import jax
import jax.numpy as jnp
from jax import lax
from jax.sharding import PartitionSpec as P

HEAD_DIM = 64
ROT = 32
LENGTH = 2048


epsilon = 1e-05
masked_score = -1e30


def layer_norm(token_rows, norm_gain, norm_shift):
    mean_row = jnp.mean(token_rows, axis=-1, keepdims=True)
    centred = token_rows - mean_row
    variance = jnp.mean(centred * centred, axis=-1, keepdims=True)
    return centred * lax.rsqrt(variance + epsilon) * norm_gain + norm_shift


def tables(row_total):
    half_rot = ROT // 2
    positions = (jnp.arange(row_total, dtype=jnp.int32) % LENGTH).astype(jnp.float32)
    inverse = 10000.0 ** (-(2.0 * jnp.arange(half_rot, dtype=jnp.float32)) / ROT)
    angles = positions[:, None] * inverse[None, :]
    return (jnp.cos(angles)[:, None, :], jnp.sin(angles)[:, None, :])


def rotate(field_in, cosine, sine_table):
    half_rot = ROT // 2
    first_half = field_in[..., :half_rot]
    second_half = field_in[..., half_rot:ROT]
    return jnp.concatenate(
        [
            first_half * cosine - second_half * sine_table,
            second_half * cosine + first_half * sine_table,
            field_in[..., ROT:],
        ],
        axis=-1,
    )


def block_scores(query_block, key_seq, row_start):
    scores = jnp.einsum(
        "qhe,khe->hqk", query_block, key_seq, preferred_element_type=jnp.float32
    ) * HEAD_DIM ** (-0.5)
    query_pos = row_start + jnp.arange(query_block.shape[0], dtype=jnp.int32)
    key_pos = jnp.arange(key_seq.shape[0], dtype=jnp.int32)
    causal = query_pos[:, None] >= key_pos[None, :]
    return jnp.where(causal[None], scores, masked_score)


def attend(query_block, key_seq, value_seq, row_start):
    scores = block_scores(query_block, key_seq, row_start)
    row_top = jnp.max(scores, axis=-1, keepdims=True)
    weights = jnp.exp(scores - row_top)
    row_total = jnp.sum(weights, axis=-1, keepdims=True)
    probabilities = (weights / row_total).astype(jnp.bfloat16)
    mixed_heads = jnp.einsum(
        "hqk,khe->qhe", probabilities, value_seq, preferred_element_type=jnp.float32
    )
    return (mixed_heads, row_top, row_total)


def attend_back(query_block, key_seq, value_seq, grad_block, row_top, row_total, row_start):
    scores = block_scores(query_block, key_seq, row_start)
    exact_probs = jnp.exp(scores - row_top) / row_total
    rounded_probs = exact_probs.astype(jnp.bfloat16)
    grad_probs = jnp.einsum(
        "qhe,khe->hqk", grad_block, value_seq, preferred_element_type=jnp.float32
    )
    grad_value_seq = jnp.einsum(
        "hqk,qhe->khe", rounded_probs, grad_block, preferred_element_type=jnp.float32
    )
    inner_sum = jnp.sum(exact_probs * grad_probs, axis=-1, keepdims=True)
    grad_scores = (exact_probs * (grad_probs - inner_sum)).astype(jnp.bfloat16)
    scale_factor = HEAD_DIM ** (-0.5)
    grad_query_block = (
        jnp.einsum("hqk,khe->qhe", grad_scores, key_seq, preferred_element_type=jnp.float32)
        * scale_factor
    )
    grad_key_seq = (
        jnp.einsum("hqk,qhe->khe", grad_scores, query_block, preferred_element_type=jnp.float32)
        * scale_factor
    )
    return (grad_query_block, grad_key_seq, grad_value_seq)


def on_device(
    tokens,
    norm_gain,
    norm_shift,
    weight_qkv,
    bias_qkv,
    weight_dense,
    weight_up,
    bias_up,
    weight_down,
    bias_out,
    cotangent,
):
    local_rows = tokens.shape[0]
    token_rows = tokens.astype(jnp.float32)
    normed, norm_pullback = jax.vjp(layer_norm, token_rows, norm_gain, norm_shift)
    normed_low = normed.astype(jnp.bfloat16)
    full_qkv, full_dense, full_up, full_down = (
        lax.all_gather(weight_qkv, "dp", axis=0, tiled=True),
        lax.all_gather(weight_dense, "dp", axis=1, tiled=True),
        lax.all_gather(weight_up, "dp", axis=0, tiled=True),
        lax.all_gather(weight_down, "dp", axis=1, tiled=True),
    )
    gathered = lax.all_gather(normed_low, "tensor", axis=0, tiled=True)
    group_rows = gathered.shape[0]
    width_in = full_qkv.shape[0]
    local_width = full_qkv.shape[2]
    local_heads = local_width // HEAD_DIM
    joined = jnp.dot(
        gathered, full_qkv.reshape(width_in, 3 * local_width), preferred_element_type=jnp.float32
    ) + bias_qkv.reshape(3 * local_width)
    joined = joined.reshape(group_rows, 3, local_heads, HEAD_DIM)
    cosine, sine_table = tables(group_rows)
    query_low = rotate(joined[:, 0], cosine, sine_table).astype(jnp.bfloat16)
    key_low = rotate(joined[:, 1], cosine, sine_table).astype(jnp.bfloat16)
    value_low = joined[:, 2].astype(jnp.bfloat16)
    block_rows = min(512, LENGTH)
    per_sequence = LENGTH // block_rows
    block_count = group_rows // LENGTH * per_sequence
    block_ids = jnp.arange(block_count, dtype=jnp.int32)

    def block_place(block_index):
        seq_start = block_index // per_sequence * LENGTH
        row_start = block_index % per_sequence * block_rows
        return (seq_start, row_start)

    def forward_block(block_index):
        seq_start, row_start = block_place(block_index)
        query_block = lax.dynamic_slice_in_dim(query_low, seq_start + row_start, block_rows, 0)
        return attend(query_block, key_low, value_low, row_start)

    mixed_blocks, row_tops, row_totals = lax.map(forward_block, block_ids)
    mixed_low = mixed_blocks.reshape(group_rows, local_width).astype(jnp.bfloat16)
    hidden = jnp.dot(gathered, full_up, preferred_element_type=jnp.float32) + bias_up
    activated, gelu_pullback = jax.vjp(partial(jax.nn.gelu, approximate=True), hidden)
    activated_low = activated.astype(jnp.bfloat16)
    active_rows = lax.slice_in_dim(activated_low, 0, local_rows * lax.axis_size("tensor"), axis=0)
    branch_sum = lax.psum_scatter(
        jnp.dot(mixed_low, full_dense, preferred_element_type=jnp.float32)
        + jnp.dot(active_rows, full_down, preferred_element_type=jnp.float32),
        "tensor",
        scatter_dimension=0,
        tiled=True,
    )
    block_out = (token_rows + branch_sum + bias_out).astype(jnp.bfloat16)
    back_qkv, back_dense, back_up, back_down = (
        lax.all_gather(weight_qkv, "dp", axis=0, tiled=True),
        lax.all_gather(weight_dense, "dp", axis=1, tiled=True),
        lax.all_gather(weight_up, "dp", axis=0, tiled=True),
        lax.all_gather(weight_down, "dp", axis=1, tiled=True),
    )
    grad_rows = lax.all_gather(cotangent, "tensor", axis=0, tiled=True)
    grad_mixed = jnp.einsum(
        "td,kd->tk", grad_rows, back_dense, preferred_element_type=jnp.float32
    ).astype(jnp.bfloat16)
    grad_active = jnp.einsum("td,fd->tf", grad_rows, back_down, preferred_element_type=jnp.float32)
    grad_hidden = gelu_pullback(grad_active)[0].astype(jnp.bfloat16)
    grad_mixed_heads = grad_mixed.reshape(group_rows, local_heads, HEAD_DIM)

    def backward_block(carried, block_inputs):
        grad_keys_all, grad_values_all = carried
        block_index, row_top, row_total = block_inputs
        seq_start, row_start = block_place(block_index)
        query_block = lax.dynamic_slice_in_dim(query_low, seq_start + row_start, block_rows, 0)
        grad_block = lax.dynamic_slice_in_dim(
            grad_mixed_heads, seq_start + row_start, block_rows, 0
        )
        grad_query_block, grad_key_seq, grad_value_seq = attend_back(
            query_block, key_low, value_low, grad_block, row_top, row_total, row_start
        )
        grad_keys_all = grad_keys_all + grad_key_seq
        grad_values_all = grad_values_all + grad_value_seq
        return ((grad_keys_all, grad_values_all), grad_query_block)

    empty_heads = jnp.zeros((group_rows, local_heads, HEAD_DIM), jnp.float32)
    (grad_keys_all, grad_values_all), grad_query_blocks = lax.scan(
        backward_block, (empty_heads, empty_heads), (block_ids, row_tops, row_totals)
    )
    grad_query_all = grad_query_blocks.reshape(group_rows, local_heads, HEAD_DIM)
    minus_sine = -sine_table
    grad_joined = jnp.stack(
        [
            rotate(grad_query_all, cosine, minus_sine),
            rotate(grad_keys_all, cosine, minus_sine),
            grad_values_all,
        ],
        axis=1,
    )
    grad_joined_low = grad_joined.reshape(group_rows, 3 * local_width).astype(jnp.bfloat16)
    bias_qkv_part = jnp.sum(grad_joined_low, axis=0, dtype=jnp.float32).reshape(3, local_width)
    bias_up_part = jnp.sum(grad_hidden, axis=0, dtype=jnp.float32)
    flat_qkv = back_qkv.reshape(width_in, 3 * local_width)
    grad_normed = lax.psum_scatter(
        jnp.einsum("tj,dj->td", grad_joined_low, flat_qkv, preferred_element_type=jnp.float32)
        + jnp.einsum("tf,df->td", grad_hidden, back_up, preferred_element_type=jnp.float32),
        "tensor",
        scatter_dimension=0,
        tiled=True,
    )
    grad_input, gain_part, shift_part = norm_pullback(grad_normed)
    grad_tokens = (cotangent.astype(jnp.float32) + grad_input).astype(jnp.bfloat16)
    grad_qkv = jnp.einsum(
        "td,tj->dj", gathered, grad_joined_low, preferred_element_type=jnp.float32
    ).reshape(width_in, 3, local_width)
    grad_up = jnp.einsum("td,tf->df", gathered, grad_hidden, preferred_element_type=jnp.float32)
    grad_dense = jnp.einsum("tk,td->kd", mixed_low, grad_rows, preferred_element_type=jnp.float32)
    grad_down = jnp.einsum(
        "tf,td->fd", activated_low, grad_rows, preferred_element_type=jnp.float32
    )
    grad_qkv, grad_dense, grad_up, grad_down = (
        lax.psum_scatter(grad_qkv, "dp", scatter_dimension=0, tiled=True),
        lax.psum_scatter(grad_dense, "dp", scatter_dimension=1, tiled=True),
        lax.psum_scatter(grad_up, "dp", scatter_dimension=0, tiled=True),
        lax.psum_scatter(grad_down, "dp", scatter_dimension=1, tiled=True),
    )
    grad_bias_qkv, grad_bias_up = lax.psum((bias_qkv_part, bias_up_part), "dp")
    out_part = jnp.sum(cotangent, axis=0, dtype=jnp.float32)
    grad_gain, grad_shift, grad_bias_out = lax.psum(
        (gain_part, shift_part, out_part), ("dp", "tensor")
    )
    return (
        block_out,
        grad_tokens,
        grad_gain,
        grad_shift,
        grad_qkv,
        grad_bias_qkv,
        grad_dense,
        grad_up,
        grad_bias_up,
        grad_down,
        grad_bias_out,
    )


def solution(mesh):
    in_specs = (
        P(("dp", "tensor"), None),
        P(),
        P(),
        P("dp", None, "tensor"),
        P(None, "tensor"),
        P("tensor", "dp"),
        P("dp", "tensor"),
        P("tensor"),
        P("tensor", "dp"),
        P(),
        P(("dp", "tensor"), None),
    )
    out_specs = (
        P(("dp", "tensor"), None),
        P(("dp", "tensor"), None),
        P(),
        P(),
        P("dp", None, "tensor"),
        P(None, "tensor"),
        P("tensor", "dp"),
        P("dp", "tensor"),
        P("tensor"),
        P("tensor", "dp"),
        P(),
    )
    return jax.shard_map(
        on_device, mesh=mesh, in_specs=in_specs, out_specs=out_specs, check_vma=False
    )
```

profile of v0, /device:TPU:0, one launch (start us, length us, event | category | flops | bytes accessed | tf_op | source)
XLA Modules:
  0.0 1908.8 jit_solution(15833524200114558816)
XLA Ops:
  21.2 56.9 %all-gather.9.cloned.1.call-done = bf16[2048,3,512]{0,2,1:T(8,128)(2,1)} async-done(((bf16[256,3,512]{0,2,1:T(8,128)(2,1)}), bf16[2048,3,512]{0,2,1:T(8,128)(2,1)}) %all-gather.9.cloned.1.call-update) | async-done | bytes 6291472 | tf_op jit(solution)/shard_map/all_gather | solution.py:110
  78.1 88.2 %all-gather.7.cloned.1.call-done = bf16[2048,2048]{1,0:T(8,128)(2,1)} async-done(((bf16[512,2048]{1,0:T(8,128)(2,1)}), bf16[2048,2048]{1,0:T(8,128)(2,1)}) %all-gather.7.cloned.1.call-update) | async-done | bytes 8388624 | tf_op jit(solution)/shard_map/all_gather | solution.py:115
  166.4 17.8 convolution_add_fusion
  195.4 204.2 %while.33 = (s32[]{:T(128)}, bf16[4,512,8,64]{1,3,2,0:T(8,128)(2,1)}, f32[4,8,512,1]{2,1,3,0:T(8,128)S(1)}, f32[4,8,512,1]{2,1,3,0:T(8,128)S(1)}, s32[4]{0:T(128...) while((s32[]{:T(128)}, ...), condition=%wide.region_5.6_spmd, body=%wide.region_2.5_spmd.sunk | while | flops 2249187840 | bytes 110777256 | solution.py:143
  199.6 17.1 fusion.109
  231.7 17.1 fusion.111
  409.5 537.0 %while.34 = (s32[]{:T(128)}, f32[2048,8,64]{0,2,1:T(8,128)}, f32[2048,8,64]{0,2,1:T(8,128)}, f32[4,512,8,64]{1,0,3,2:T(4,128)}, s32[4]{0:T(128)S(1)}, /*index=5*...) while((s32[]{:T(128)}, f32[2048,8,64]{0,2,1:T(8,128)}, ...), condition=%wide.region_9.10_spmd.clone, body=%wide.region_7.9_spmd.clone.sunk | while | flops 5459145216 | bytes 292688384 | solution.py:187
  438.2 25.8 %multiply_reduce_fusion.2 = (f32[8,512]{1,0:T(8,128)S(1)}, f32[8,512,2048]{2,1,0:T(8,128)}) fusion(f32[8,512,2048]{2,1,0:T(8,128)} %fusion.121, f32[8,512]{1,0:T(8,128)S(1)} %get-tuple-element.510, f32[8,512]{1,0:T(8,128)S(1)} %get-tuple-element.511, bf16[2048,8,64]{0,2,1:T(8,128)(2,1)S(1)} %copy-done, bf16[2048,8,64]{0,2,1:T(8,128)(2,1)} %get-tuple-element.605, ...), kind=kOutput, calls=%fused_computation.18.clone.1 | convolution fusion | flops 1124069376 | bytes 70828032 | tf_op jit(solution)/shard_map/while/body/eval_jaxpr/qhe,khe->hqk/dot_general | solution.py:47
  464.0 27.4 %multiply_convert_fusion.5 = bf16[8,512,2048]{2,1,0:T(8,128)(2,1)} fusion(f32[8,512,2048]{2,1,0:T(8,128)} %get-tuple-element.512, f32[8,512,2048]{2,1,0:T(8,128)} %fusion.121, f32[8,512]{1,0:T(8,128)S(1)} %get-tuple-element.513), kind=kLoop, calls=%fused_computation.17.clone.1 | loop fusion | flops 25165824 | bytes 83902464 | tf_op jit(solution)/shard_map/while/body/eval_jaxpr/convert_element_type | solution.py:79
  501.9 21.0 %dynamic_update_slice.35 = f32[4,512,8,64]{1,0,3,2:T(4,128)} dynamic-update-slice(f32[4,512,8,64]{1,0,3,2:T(4,128)} %get-tuple-element.584, f32[1,512,8,64]{1,0,3,2:T(1,128)S(1)} %copy.42, s32[]{:T(128)} %get-tuple-element.581, s32[]{:T(128)} %constant.199.clone.1..sunk.1, s32[]{:T(128)} %constant.199.clone.1..sunk.1, s32[]{:T(128)} %constant.199.clone.1..sunk.1) | dynamic-update-slice | bytes 2097156 | tf_op jit(solution)/shard_map/while/body/jit(dynamic_update_index_in_dim)/dynamic_update_slice | solution.py:143
  568.0 25.8 %multiply_reduce_fusion.2 = (f32[8,512]{1,0:T(8,128)S(1)}, f32[8,512,2048]{2,1,0:T(8,128)}) fusion(f32[8,512,2048]{2,1,0:T(8,128)} %fusion.121, f32[8,512]{1,0:T(8,128)S(1)} %get-tuple-element.510, f32[8,512]{1,0:T(8,128)S(1)} %get-tuple-element.511, bf16[2048,8,64]{0,2,1:T(8,128)(2,1)S(1)} %copy-done, bf16[2048,8,64]{0,2,1:T(8,128)(2,1)} %get-tuple-element.605, ...), kind=kOutput, calls=%fused_computation.18.clone.1 | convolution fusion | flops 1124069376 | bytes 70828032 | tf_op jit(solution)/shard_map/while/body/eval_jaxpr/qhe,khe->hqk/dot_general | solution.py:47
  593.8 27.4 %multiply_convert_fusion.5 = bf16[8,512,2048]{2,1,0:T(8,128)(2,1)} fusion(f32[8,512,2048]{2,1,0:T(8,128)} %get-tuple-element.512, f32[8,512,2048]{2,1,0:T(8,128)} %fusion.121, f32[8,512]{1,0:T(8,128)S(1)} %get-tuple-element.513), kind=kLoop, calls=%fused_computation.17.clone.1 | loop fusion | flops 25165824 | bytes 83902464 | tf_op jit(solution)/shard_map/while/body/eval_jaxpr/convert_element_type | solution.py:79
  631.7 21.0 %dynamic_update_slice.35 = f32[4,512,8,64]{1,0,3,2:T(4,128)} dynamic-update-slice(f32[4,512,8,64]{1,0,3,2:T(4,128)} %get-tuple-element.584, f32[1,512,8,64]{1,0,3,2:T(1,128)S(1)} %copy.42, s32[]{:T(128)} %get-tuple-element.581, s32[]{:T(128)} %constant.199.clone.1..sunk.1, s32[]{:T(128)} %constant.199.clone.1..sunk.1, s32[]{:T(128)} %constant.199.clone.1..sunk.1) | dynamic-update-slice | bytes 2097156 | tf_op jit(solution)/shard_map/while/body/jit(dynamic_update_index_in_dim)/dynamic_update_slice | solution.py:143
  700.2 25.8 %multiply_reduce_fusion.2 = (f32[8,512]{1,0:T(8,128)S(1)}, f32[8,512,2048]{2,1,0:T(8,128)}) fusion(f32[8,512,2048]{2,1,0:T(8,128)} %fusion.121, f32[8,512]{1,0:T(8,128)S(1)} %get-tuple-element.510, f32[8,512]{1,0:T(8,128)S(1)} %get-tuple-element.511, bf16[2048,8,64]{0,2,1:T(8,128)(2,1)S(1)} %copy-done, bf16[2048,8,64]{0,2,1:T(8,128)(2,1)} %get-tuple-element.605, ...), kind=kOutput, calls=%fused_computation.18.clone.1 | convolution fusion | flops 1124069376 | bytes 70828032 | tf_op jit(solution)/shard_map/while/body/eval_jaxpr/qhe,khe->hqk/dot_general | solution.py:47
  726.0 27.4 %multiply_convert_fusion.5 = bf16[8,512,2048]{2,1,0:T(8,128)(2,1)} fusion(f32[8,512,2048]{2,1,0:T(8,128)} %get-tuple-element.512, f32[8,512,2048]{2,1,0:T(8,128)} %fusion.121, f32[8,512]{1,0:T(8,128)S(1)} %get-tuple-element.513), kind=kLoop, calls=%fused_computation.17.clone.1 | loop fusion | flops 25165824 | bytes 83902464 | tf_op jit(solution)/shard_map/while/body/eval_jaxpr/convert_element_type | solution.py:79
  763.9 21.0 %dynamic_update_slice.35 = f32[4,512,8,64]{1,0,3,2:T(4,128)} dynamic-update-slice(f32[4,512,8,64]{1,0,3,2:T(4,128)} %get-tuple-element.584, f32[1,512,8,64]{1,0,3,2:T(1,128)S(1)} %copy.42, s32[]{:T(128)} %get-tuple-element.581, s32[]{:T(128)} %constant.199.clone.1..sunk.1, s32[]{:T(128)} %constant.199.clone.1..sunk.1, s32[]{:T(128)} %constant.199.clone.1..sunk.1) | dynamic-update-slice | bytes 2097156 | tf_op jit(solution)/shard_map/while/body/jit(dynamic_update_index_in_dim)/dynamic_update_slice | solution.py:143
  832.4 25.8 %multiply_reduce_fusion.2 = (f32[8,512]{1,0:T(8,128)S(1)}, f32[8,512,2048]{2,1,0:T(8,128)}) fusion(f32[8,512,2048]{2,1,0:T(8,128)} %fusion.121, f32[8,512]{1,0:T(8,128)S(1)} %get-tuple-element.510, f32[8,512]{1,0:T(8,128)S(1)} %get-tuple-element.511, bf16[2048,8,64]{0,2,1:T(8,128)(2,1)S(1)} %copy-done, bf16[2048,8,64]{0,2,1:T(8,128)(2,1)} %get-tuple-element.605, ...), kind=kOutput, calls=%fused_computation.18.clone.1 | convolution fusion | flops 1124069376 | bytes 70828032 | tf_op jit(solution)/shard_map/while/body/eval_jaxpr/qhe,khe->hqk/dot_general | solution.py:47
  858.2 27.4 %multiply_convert_fusion.5 = bf16[8,512,2048]{2,1,0:T(8,128)(2,1)} fusion(f32[8,512,2048]{2,1,0:T(8,128)} %get-tuple-element.512, f32[8,512,2048]{2,1,0:T(8,128)} %fusion.121, f32[8,512]{1,0:T(8,128)S(1)} %get-tuple-element.513), kind=kLoop, calls=%fused_computation.17.clone.1 | loop fusion | flops 25165824 | bytes 83902464 | tf_op jit(solution)/shard_map/while/body/eval_jaxpr/convert_element_type | solution.py:79
  896.1 21.0 %dynamic_update_slice.35 = f32[4,512,8,64]{1,0,3,2:T(4,128)} dynamic-update-slice(f32[4,512,8,64]{1,0,3,2:T(4,128)} %get-tuple-element.584, f32[1,512,8,64]{1,0,3,2:T(1,128)S(1)} %copy.42, s32[]{:T(128)} %get-tuple-element.581, s32[]{:T(128)} %constant.199.clone.1..sunk.1, s32[]{:T(128)} %constant.199.clone.1..sunk.1, s32[]{:T(128)} %constant.199.clone.1..sunk.1) | dynamic-update-slice | bytes 2097156 | tf_op jit(solution)/shard_map/while/body/jit(dynamic_update_index_in_dim)/dynamic_update_slice | solution.py:143
  980.2 24.2 %fusion.59 = f32[2048,2048]{1,0:T(8,128)} fusion(bf16[2048,2048]{1,0:T(8,128)(2,1)} %all-gather.7.cloned.1.call-done, bf16[2048,2048]{1,0:T(8,128)(2,1)} %all-gather.13.cloned.1.call-done), kind=kOutput, calls=%fused_computation.115 | convolution fusion | flops 17179869184 | bytes 33554432 | tf_op jit(solution)/shard_map/dot_general | solution.py:145
  1004.4 36.4 %convert_reduce_fusion = (f32[2048]{0:T(1024)}, bf16[2048,2048]{1,0:T(8,128)(2,1)}) fusion(f32[2048,2048]{1,0:T(8,128)} %fusion.59, f32[2048]{0:T(1024)S(1)} %copy-done.25, bf16[2048,2048]{1,0:T(8,128)(2,1)} %all-gather.17.cloned.1.call-done, bf16[2048,2048]{1,0:T(8,128)(2,1)} %all-gather.15.cloned.1.call-done), kind=kOutput, calls=%fused_computation.48 | convolution fusion | flops 17276336128 | bytes 41959424 | tf_op jit(solution)/shard_map/td,fd->tf/dot_general | solution.py:167
  1040.8 26.5 %convolution_add_fusion.1 = f32[2048,2048]{1,0:T(8,128)} fusion(f32[2048,2048]{1,0:T(8,128)} %fusion.60, bf16[2048,2048]{1,0:T(8,128)(2,1)} %get-tuple-element.349, bf16[2048,2048]{1,0:T(8,128)(2,1)} %all-gather.13.cloned.1.call-done), kind=kOutput, calls=%fused_computation.53 | convolution fusion | flops 17184063488 | bytes 50331648 | tf_op jit(solution)/shard_map/tf,df->td/dot_general | solution.py:206
  1079.5 29.8 %convolution_add_fusion.2 = f32[2048,2048]{1,0:T(8,128)} fusion(f32[2048,2048]{1,0:T(8,128)} %fusion.58, bf16[2048,2048]{1,0:T(8,128)(2,1)} %all-gather.15.cloned.1.call-done, f32[2048,2048]{1,0:T(8,128)} %fusion.59, f32[2048]{0:T(1024)S(1)} %copy-done.25), kind=kOutput, calls=%fused_computation.54 | convolution fusion | flops 17226006528 | bytes 58728448 | tf_op jit(solution)/shard_map/dot_general | solution.py:151
  1119.2 19.5 %fusion.31 = f32[2048,3,512]{2,0,1:T(8,128)} fusion(bf16[3,512,2048]{2,1,0:T(8,128)(2,1)} %bitcast.117, bf16[2048,2048]{1,0:T(8,128)(2,1)} %all-gather.7.cloned.1.call-done), kind=kOutput, calls=%fused_computation.55 | convolution fusion | flops 12884901888 | bytes 27262976 | tf_op jit(solution)/shard_map/td,tj->dj/dot_general | solution.py:213
  1138.7 24.8 %fusion.62 = f32[2048,2048]{1,0:T(8,128)} fusion(bf16[2048,2048]{1,0:T(8,128)(2,1)} %all-gather.7.cloned.1.call-done, bf16[2048,2048]{1,0:T(8,128)(2,1)} %get-tuple-element.349), kind=kOutput, calls=%fused_computation.118 | convolution fusion | flops 17179869184 | bytes 33554432 | tf_op jit(solution)/shard_map/td,tf->df/dot_general | solution.py:216
  1163.6 27.4 %fusion.55 = f32[2048,2048]{1,0:T(8,128)} fusion(bf16[2048,2048]{1,0:T(8,128)(2,1)} %all-gather.17.cloned.1.call-done, f32[2048,2048]{1,0:T(8,128)} %fusion.59, f32[2048]{0:T(1024)S(1)} %copy-done.25), kind=kOutput, calls=%fused_computation.112 | convolution fusion | flops 17221812224 | bytes 41951232 | tf_op jit(solution)/shard_map/tf,td->fd/dot_general | solution.py:218
  1191.8 29.5 %all-reduce.1 = (f32[3,512]{1,0:T(4,128)}, f32[2048]{0:T(1024)}) all-reduce(f32[3,512]{1,0:T(4,128)S(1)} %reshape.236, f32[2048]{0:T(1024)S(1)} %copy-done.23), channel_id=1, replica_groups=mesh['dp'=8,'tensor'=4] {'dp'}, use_global_device_ids=true, to_apply=%region_19.20 | all-reduce | flops 3584 | bytes 28672 | tf_op jit(solution)/shard_map/psum | solution.py:227
  1226.8 151.5 %reduce-scatter.7.cloned.1.call-done = f32[512,2048]{1,0:T(8,128)} async-done(((f32[2048,2048]{1,0:T(8,128)}), f32[512,2048]{1,0:T(8,128)}) %reduce-scatter.7.cloned.1.call-update) | async-done | bytes 4194320 | tf_op jit(solution)/shard_map/reduce_scatter | solution.py:149
  1385.4 41.6 %all-reduce = (f32[2048]{0:T(1024)}, f32[2048]{0:T(1024)}, f32[2048]{0:T(1024)}) all-reduce(f32[2048]{0:T(1024)S(1)} %get-tuple-element.301, f32[2048]{0:T(1024)S(1)} %get-tuple-element.303, f32[2048]{0:T(1024)S(1)} %get-tuple-element.370), channel_id=1, replica_groups=mesh['dp'=8,'tensor'=4] {'dp','tensor'}, use_global_device_ids=true, to_apply=%region_14.15 | all-reduce | flops 6144 | bytes 49152 | tf_op jit(solution)/shard_map/psum | solution.py:229
  1432.3 130.1 %reduce-scatter.11.cloned.1.call-done = f32[256,3,512]{2,0,1:T(8,128)} async-done(((f32[2048,3,512]{2,0,1:T(8,128)}), f32[256,3,512]{2,0,1:T(8,128)}) %reduce-scatter.11.cloned.1.call-update) | async-done | bytes 1572880 | tf_op jit(solution)/shard_map/reduce_scatter | solution.py:222
  1562.4 169.6 %reduce-scatter.15.cloned.1.call-done = f32[256,2048]{1,0:T(8,128)} async-done(((f32[2048,2048]{1,0:T(8,128)}), f32[256,2048]{1,0:T(8,128)}) %reduce-scatter.15.cloned.1.call-update) | async-done | bytes 2097168 | tf_op jit(solution)/shard_map/reduce_scatter | solution.py:224
  1732.0 169.4 %reduce-scatter.17.cloned.1.call-done = f32[2048,256]{1,0:T(8,128)} async-done(((f32[2048,2048]{1,0:T(8,128)}), f32[2048,256]{1,0:T(8,128)}) %reduce-scatter.17.cloned.1.call-update) | async-done | bytes 2097168 | tf_op jit(solution)/shard_map/reduce_scatter | solution.py:225
  (198 shorter events, 487.2 us)
Async XLA Ops:
  7.2 8.0 copy-start.2
  7.2 8.0 copy-start.11
  7.2 8.0 copy-start.20
  7.2 70.9 %all-gather.9.cloned.1.call-start = ((), (), s32[]{:S(2)}) async-start(), calls=%async_computation.7 | async-start | bytes 7077888 | tf_op jit(solution)/shard_map/all_gather | solution.py:110
  9.7 156.7 %all-gather.7.cloned.1.call-start = ((), (), s32[]{:S(2)}) async-start(), calls=%async_computation.6 | async-start | bytes 10485760 | tf_op jit(solution)/shard_map/all_gather | solution.py:115
  11.7 8.3 copy-start.22
  17.4 382.3 %all-gather.11.cloned.1.call-start = ((), (), s32[]{:S(2)}) async-start(), calls=%async_computation.8 | async-start | bytes 2359296 | tf_op jit(solution)/shard_map/all_gather | solution.py:111
  18.1 381.5 %all-gather.17.cloned.1.call-start = ((), (), s32[]{:S(2)}) async-start(), calls=%async_computation.12 | async-start | bytes 10485760 | tf_op jit(solution)/shard_map/all_gather | solution.py:163
  18.7 961.5 %all-gather.13.cloned.1.call-start = ((), (), s32[]{:S(2)}) async-start(), calls=%async_computation.9 | async-start | bytes 9437184 | tf_op jit(solution)/shard_map/all_gather | solution.py:112
  19.3 985.1 %all-gather.15.cloned.1.call-start = ((), (), s32[]{:S(2)}) async-start(), calls=%async_computation.10 | async-start | bytes 9437184 | tf_op jit(solution)/shard_map/all_gather | solution.py:113
  19.8 1201.6 %reduce-scatter.9.cloned.1.call-start = ((), (), s32[]{:S(2)}) async-start(), calls=%async_computation.13 | async-start | bytes 20971520 | tf_op jit(solution)/shard_map/reduce_scatter | solution.py:204
  21.2 171.4 %copy-start.8 = (f32[2048,16]{0,1:T(8,128)}, f32[2048,16]{0,1:T(8,128)S(1)}, u32[]{:S(2)}) copy-start(f32[2048,16]{0,1:T(8,128)S(1)} %get-tuple-element.379) | copy-start | bytes 393220
  422.7 15.4 copy-start
  552.9 15.1 copy-start
  685.1 15.1 copy-start
  817.3 15.1 copy-start
  946.5 9.6 copy-start.9
  946.5 9.6 copy-start.10
  959.3 4.8 slice-start
  959.6 4.6 slice-start.1
  980.2 24.2 %copy-start.25 = (f32[2048]{0:T(1024)S(1)}, f32[2048]{0:T(1024)}, u32[]{:S(2)}) copy-start(f32[2048]{0:T(1024)} %param.22) | copy-start | bytes 24580
  1067.2 311.1 %reduce-scatter.7.cloned.1.call-start = ((), (), s32[]{:S(2)}) async-start(), calls=%async_computation.11 | async-start | bytes 20971520 | tf_op jit(solution)/shard_map/reduce_scatter | solution.py:149
  1109.3 323.0 %reduce-scatter.13.cloned.1.call-start = ((), (), s32[]{:S(2)}) async-start(), calls=%async_computation.15 | async-start | bytes 4718592 | tf_op jit(solution)/shard_map/reduce_scatter | solution.py:223
  1119.1 443.3 %reduce-scatter.11.cloned.1.call-start = ((), (), s32[]{:S(2)}) async-start(), calls=%async_computation.14 | async-start | bytes 14155776 | tf_op jit(solution)/shard_map/reduce_scatter | solution.py:222
  1138.7 593.3 %reduce-scatter.15.cloned.1.call-start = ((), (), s32[]{:S(2)}) async-start(), calls=%async_computation.16 | async-start | bytes 18874368 | tf_op jit(solution)/shard_map/reduce_scatter | solution.py:224
  1163.6 737.8 %reduce-scatter.17.cloned.1.call-start = ((), (), s32[]{:S(2)}) async-start(), calls=%async_computation.17 | async-start | bytes 18874368 | tf_op jit(solution)/shard_map/reduce_scatter | solution.py:225
  1191.0 30.4 %copy-start.3 = (bf16[512,2048]{1,0:T(8,128)(2,1)S(1)}, bf16[512,2048]{1,0:T(8,128)(2,1)}, u32[]{:S(2)}) copy-start(bf16[512,2048]{1,0:T(8,128)(2,1)} %param.15) | copy-start | bytes 6291460
  1191.0 30.4 %copy-start.12 = (f32[2048]{0:T(1024)S(1)}, f32[2048]{0:T(1024)}, u32[]{:S(2)}) copy-start(f32[2048]{0:T(1024)} %param.16) | copy-start | bytes 24580
  1191.0 30.4 %copy-start.14 = (f32[512]{0:T(512)S(1)}, f32[512]{0:T(512)}, u32[]{:S(2)}) copy-start(f32[512]{0:T(512)} %copy-done.13) | copy-start | bytes 6148
  1191.1 33.6 %copy-start.19 = (f32[512]{0:T(512)S(1)}, f32[512]{0:T(512)}, u32[]{:S(2)}) copy-start(f32[512]{0:T(512)} %copy-done.18) | copy-start | bytes 6148
  1191.1 33.6 %copy-start.17 = (f32[512]{0:T(512)S(1)}, f32[512]{0:T(512)}, u32[]{:S(2)}) copy-start(f32[512]{0:T(512)} %copy-done.16) | copy-start | bytes 6148
  1221.3 157.0 %copy-start.21 = (f32[2048]{0:T(1024)S(1)}, f32[2048]{0:T(1024)}, u32[]{:S(2)}) copy-start(f32[2048]{0:T(1024)} %param.24) | copy-start | bytes 24580
  (11 other events, 25.0 us)
Sparse Core Ops, SparseCore 0:
  10.2 67.8 all-gather.8
  80.5 85.7 all-gather.6
  168.0 30.8 all-gather.10
  200.5 86.6 all-gather.16
  288.7 82.0 all-gather.12
  372.2 81.0 all-gather.14
  1067.4 153.9 reduce-scatter.8
  1224.5 153.8 reduce-scatter.6
  1381.2 51.0 reduce-scatter.12
  1435.0 127.3 reduce-scatter.10
  1565.3 166.6 reduce-scatter.14
  1734.8 166.5 reduce-scatter.16
where the time goes:
time: 1920 us; the launch traced here: 1910 us
  waiting for transfers between devices  774 us (40%)
  matrix products  691 us (36%)
  other arithmetic  204 us (11%)
  local copies, waits for them, and re-layouts  122 us (6%)
  blocking collectives  71.1 us (4%)
  loops' own time  31.8 us (2%)
    reduce_scatter x1, waiting for transfers between devices, on_device(): lax.psum_scatter(grad_up, 'dp', scatter_dimension=0, tiled=True)  170 us
    reduce_scatter x1, waiting for transfers between devices, on_device(): lax.psum_scatter(grad_down, 'dp', scatter_dimension=1, tiled=True)  169 us
    dot_general x8, matrix products, block_scores(): jnp.einsum('qhe,khe->hqk', query_block, key_seq, preferred_element_type=j...  166 us
    reduce_scatter x1, waiting for transfers between devices, on_device(): lax.psum_scatter(jnp.dot(mixed_low, full_dense, preferred_element_type=jn...  151 us
    reduce_scatter x1, waiting for transfers between devices, on_device(): lax.psum_scatter(grad_qkv, 'dp', scatter_dimension=0, tiled=True)  130 us
    convert_element_type x4, other arithmetic, attend_back(): grad_scores = (exact_probs * (grad_probs - inner_sum)).astype(jnp.bfloat16)  110 us
    dynamic_update_slice x12, local copies, waits for them, and re-layouts, on_device(): mixed_blocks, row_tops, row_totals = lax.map(forward_block, block_ids)  88.5 us
    all_gather x1, waiting for transfers between devices, on_device(): gathered = lax.all_gather(normed_low, 'tensor', axis=0, tiled=True)  88.2 us
  transfers between devices with their start and end apart: 12, of which 8 were waited for; matrix products, arithmetic and copies ran while one was open for 49% of the time, Pallas kernels for 0%

commit v1 on v0

v1 whole, which is shorter than its diff:
```python
import functools

import jax
import jax.numpy as jnp
from jax import lax
from jax.experimental import pallas as pl
from jax.experimental.pallas import tpu as pltpu
from jax.sharding import PartitionSpec as P

HEAD_DIM = 64
ROT = 32
LENGTH = 2048
PAIR = 2 * HEAD_DIM

epsilon = 1e-05
masked_score = -1e30
MIB = 1024 * 1024
ROWS_BY_ROWS = (((1,), (1,)), ((), ()))


def after(value, *earlier):
    return lax.optimization_barrier((value,) + earlier)[0]


def swap(value, bit):
    count = lax.axis_size("tensor")
    return lax.ppermute(value, "tensor", [(i, i ^ bit) for i in range(count)])


def group_gather(block):
    half = block.shape[0] // 2
    one = swap(block, 1)
    two = swap(block, 2)
    low = swap(one[:half], 2)
    high = swap(two[half:], 1)
    return block, one, two, low, high


def place_group(parts):
    block, one, two, low, high = parts
    rows = block.shape[0]
    me = lax.axis_index("tensor")
    full = jnp.zeros((4 * rows,) + block.shape[1:], block.dtype)

    def put(full, piece, owner, shift=0):
        start = (owner * rows + shift,) + (0,) * (block.ndim - 1)
        return lax.dynamic_update_slice(full, piece, start)

    full = put(full, block, me)
    full = put(full, one, me ^ 1)
    full = put(full, two, me ^ 2)
    full = put(full, low, me ^ 3)
    return put(full, high, me ^ 3, rows // 2)


def group_scatter(partial):
    rows = partial.shape[0] // 4
    half = rows // 2
    me = lax.axis_index("tensor")

    def take(bit, shift):
        return lax.dynamic_slice_in_dim(partial, (me ^ bit) * rows + shift, half, 0)

    def wide(piece):
        return piece.astype(jnp.float32)

    first = swap(jnp.concatenate([take(1, 0), take(3, 0)]), 1)
    second = swap(jnp.concatenate([take(2, half), take(3, half)]), 2)
    forward_first = (wide(take(2, 0)) + wide(first[half:])).astype(partial.dtype)
    forward_second = (wide(take(1, half)) + wide(second[half:])).astype(partial.dtype)
    last_first = swap(forward_first, 2)
    last_second = swap(forward_second, 1)
    low = wide(take(0, 0)) + wide(first[:half]) + wide(last_first)
    high = wide(take(0, half)) + wide(second[:half]) + wide(last_second)
    return jnp.concatenate([low, high])


def lane_tables(row_total):
    half_rot = ROT // 2
    positions = (jnp.arange(row_total, dtype=jnp.int32) % LENGTH).astype(jnp.float32)
    inverse = 10000.0 ** (-(2.0 * jnp.arange(half_rot, dtype=jnp.float32)) / ROT)
    angles = positions[:, None] * inverse[None, :]
    cosine, sine = jnp.cos(angles), jnp.sin(angles)
    ones = jnp.ones((row_total, HEAD_DIM - ROT), jnp.float32)
    zeros = jnp.zeros((row_total, half_rot), jnp.float32)
    rest = jnp.zeros((row_total, HEAD_DIM - ROT), jnp.float32)
    cos_lanes = jnp.concatenate([cosine, cosine, ones] * 2, axis=1)
    from_above = jnp.concatenate([-sine, zeros, rest] * 2, axis=1)
    from_below = jnp.concatenate([zeros, sine, rest] * 2, axis=1)
    return cos_lanes, from_above, from_below


def turn(field, cos_lanes, from_above, from_below):
    half_rot = ROT // 2
    above = pltpu.roll(field, PAIR - half_rot, 1)
    below = pltpu.roll(field, half_rot, 1)
    return field * cos_lanes + above * from_above + below * from_below


def turn_back(field, cos_lanes, from_above, from_below):
    half_rot = ROT // 2
    above = pltpu.roll(field, PAIR - half_rot, 1)
    below = pltpu.roll(field, half_rot, 1)
    return field * cos_lanes - above * from_above - below * from_below


def joined_kernel(x_ref, w_ref, bias_ref, cos_ref, above_ref, below_ref, out_ref):
    product = jnp.dot(x_ref[...], w_ref[0], preferred_element_type=jnp.float32) + bias_ref[0]
    slot = pl.program_id(1)

    @pl.when(slot < 2)
    def _():
        for start in range(0, product.shape[1], PAIR):
            lanes = product[:, start : start + PAIR]
            turned = turn(lanes, cos_ref[...], above_ref[...], below_ref[...])
            out_ref[:, start : start + PAIR] = turned.astype(out_ref.dtype)

    @pl.when(slot == 2)
    def _():
        out_ref[...] = product.astype(out_ref.dtype)


def joined_rows(x, w, bias, lanes):
    rows, depth = x.shape
    width = w.shape[2]
    block = min(512, rows)
    return pl.pallas_call(
        joined_kernel,
        grid=(rows // block, 3),
        in_specs=[
            pl.BlockSpec((block, depth), lambda i, j: (i, 0)),
            pl.BlockSpec((1, depth, width), lambda i, j: (j, 0, 0)),
            pl.BlockSpec((1, 1, width), lambda i, j: (j, 0, 0)),
        ]
        + [pl.BlockSpec((block, PAIR), lambda i, j: (i, 0))] * 3,
        out_specs=pl.BlockSpec((block, width), lambda i, j: (i, j)),
        out_shape=jax.ShapeDtypeStruct((rows, 3 * width), jnp.bfloat16),
        compiler_params=pltpu.CompilerParams(vmem_limit_bytes=48 * MIB),
        cost_estimate=pl.CostEstimate(
            flops=6 * rows * depth * width, bytes_accessed=24 * MIB, transcendentals=0
        ),
    )(x, w, bias.reshape(3, 1, width), *lanes)


def hidden_kernel(x_ref, w_ref, bias_ref, active_ref, slope_ref):
    hidden = jnp.dot(x_ref[...], w_ref[...], preferred_element_type=jnp.float32) + bias_ref[...]
    scale = (2.0 / jnp.pi) ** 0.5
    square = hidden * hidden
    inner = scale * hidden * (1.0 + 0.044715 * square)
    bent = jnp.tanh(inner)
    half = 0.5 * (1.0 + bent)
    active_ref[...] = (hidden * half).astype(active_ref.dtype)
    growth = scale * (1.0 + (3.0 * 0.044715) * square)
    slope = half + 0.5 * hidden * (1.0 - bent * bent) * growth
    slope_ref[...] = slope.astype(slope_ref.dtype)


def hidden_rows(x, w, bias):
    rows, depth = x.shape
    width = w.shape[1]
    block, columns = min(512, rows), min(512, width)
    return pl.pallas_call(
        hidden_kernel,
        grid=(width // columns, rows // block),
        in_specs=[
            pl.BlockSpec((block, depth), lambda j, i: (i, 0)),
            pl.BlockSpec((depth, columns), lambda j, i: (0, j)),
            pl.BlockSpec((1, columns), lambda j, i: (0, j)),
        ],
        out_specs=[pl.BlockSpec((block, columns), lambda j, i: (i, j))] * 2,
        out_shape=[jax.ShapeDtypeStruct((rows, width), jnp.bfloat16)] * 2,
        compiler_params=pltpu.CompilerParams(vmem_limit_bytes=48 * MIB),
        cost_estimate=pl.CostEstimate(
            flops=2 * rows * depth * width, bytes_accessed=40 * MIB, transcendentals=rows * width
        ),
    )(x, w, bias.reshape(1, width))


def grad_hidden_kernel(g_ref, w_ref, slope_ref, out_ref, sum_ref):
    product = lax.dot_general(
        g_ref[...], w_ref[...], ROWS_BY_ROWS, preferred_element_type=jnp.float32
    )
    low = (product * slope_ref[...].astype(jnp.float32)).astype(out_ref.dtype)
    out_ref[...] = low

    @pl.when(pl.program_id(1) == 0)
    def _():
        sum_ref[...] = jnp.zeros_like(sum_ref)

    sum_ref[...] += jnp.sum(low.astype(jnp.float32), axis=0, keepdims=True)


def grad_hidden_rows(g, w, slope):
    rows, depth = g.shape
    width = w.shape[0]
    block, columns = min(512, rows), min(512, width)
    return pl.pallas_call(
        grad_hidden_kernel,
        grid=(width // columns, rows // block),
        in_specs=[
            pl.BlockSpec((block, depth), lambda j, i: (i, 0)),
            pl.BlockSpec((columns, depth), lambda j, i: (j, 0)),
            pl.BlockSpec((block, columns), lambda j, i: (i, j)),
        ],
        out_specs=[
            pl.BlockSpec((block, columns), lambda j, i: (i, j)),
            pl.BlockSpec((1, columns), lambda j, i: (0, j)),
        ],
        out_shape=[
            jax.ShapeDtypeStruct((rows, width), jnp.bfloat16),
            jax.ShapeDtypeStruct((1, width), jnp.float32),
        ],
        compiler_params=pltpu.CompilerParams(vmem_limit_bytes=48 * MIB),
        cost_estimate=pl.CostEstimate(
            flops=2 * rows * depth * width, bytes_accessed=40 * MIB, transcendentals=0
        ),
    )(g, w, slope)


def attention_kernel(
    q_ref,
    k_ref,
    v_ref,
    g_ref,
    cos_ref,
    above_ref,
    below_ref,
    mixed_ref,
    grads_ref,
    sums_ref,
    keys_across,
    values_across,
    query_total,
    key_total,
    value_total,
    *,
    block,
    block_count,
):
    step = pl.program_id(1)
    scale = HEAD_DIM**-0.5
    log2_e = 1.4426950408889634

    @pl.when(step == 0)
    def _():
        keys_across[...] = k_ref[...].T
        values_across[...] = v_ref[...].T
        key_total[...] = jnp.zeros_like(key_total)
        value_total[...] = jnp.zeros_like(value_total)

    def rows_from(index):
        reach = (index + 1) * block
        queries, grads = q_ref[...], g_ref[...]
        keys, values = k_ref[0:reach, :], v_ref[0:reach, :]
        grads_across = grads.T.astype(jnp.float32)
        lane = lax.broadcasted_iota(jnp.int32, (block, PAIR), 1)
        key_pos = lax.broadcasted_iota(jnp.int32, (block, block), 0)
        query_pos = lax.broadcasted_iota(jnp.int32, (block, block), 1)
        mixed, grad_queries = [], []
        grad_keys = grad_values = None
        for head in range(2):
            own = lane // HEAD_DIM == head
            part = slice(head * HEAD_DIM, (head + 1) * HEAD_DIM)
            query_own = jnp.where(own, queries, jnp.zeros_like(queries))
            grad_own = jnp.where(own, grads, jnp.zeros_like(grads))
            scores = lax.dot_general(
                keys, query_own, ROWS_BY_ROWS, preferred_element_type=jnp.float32
            )
            corner = jnp.where(key_pos <= query_pos, scores[reach - block :], masked_score)
            if index:
                scores = jnp.concatenate([scores[: reach - block], corner], axis=0)
            else:
                scores = corner
            top = jnp.max(scores, axis=0, keepdims=True)
            weights = jnp.exp2(scores * (scale * log2_e) - top * (scale * log2_e))
            total = jnp.sum(weights, axis=0, keepdims=True)
            exact = weights * (1.0 / total)
            rounded = exact.astype(jnp.bfloat16)
            out = jnp.dot(
                values_across[part, 0:reach], rounded, preferred_element_type=jnp.float32
            )
            inner = jnp.sum(out * grads_across[part], axis=0, keepdims=True)
            grad_probs = lax.dot_general(
                values, grad_own, ROWS_BY_ROWS, preferred_element_type=jnp.float32
            )
            grad_scores = (exact * (grad_probs - inner)).astype(jnp.bfloat16)
            mixed.append(out)
            grad_queries.append(
                jnp.dot(
                    keys_across[part, 0:reach], grad_scores, preferred_element_type=jnp.float32
                )
            )
            value_part = jnp.dot(rounded, grad_own, preferred_element_type=jnp.float32)
            key_part = jnp.dot(grad_scores, query_own, preferred_element_type=jnp.float32)
            grad_values = value_part if head == 0 else grad_values + value_part
            grad_keys = key_part if head == 0 else grad_keys + key_part
        value_total[0:reach, :] += grad_values
        key_total[0:reach, :] += grad_keys
        mixed_ref[...] = jnp.concatenate(mixed, axis=0).T.astype(mixed_ref.dtype)
        query_total[reach - block : reach, :] = jnp.concatenate(grad_queries, axis=0).T

    for index in range(block_count):
        pl.when(step == index)(functools.partial(rows_from, index))

    @pl.when(step == block_count - 1)
    def _():
        lanes = cos_ref[...], above_ref[...], below_ref[...]
        for slot, field in enumerate(
            (
                turn_back(query_total[...] * scale, *lanes),
                turn_back(key_total[...] * scale, *lanes),
                value_total[...],
            )
        ):
            low = field.astype(grads_ref.dtype)
            grads_ref[slot] = low
            sums_ref[slot] = jnp.sum(low.astype(jnp.float32), axis=0, keepdims=True)


def attention(joined, grad_mixed, lanes):
    rows, width = grad_mixed.shape
    block = 256
    pairs, block_count = width // PAIR, LENGTH // block
    row_block = pl.BlockSpec((block, PAIR), lambda p, i: (i, p))
    table = pl.BlockSpec((LENGTH, PAIR), lambda p, i: (0, 0))
    return pl.pallas_call(
        functools.partial(attention_kernel, block=block, block_count=block_count),
        grid=(pairs, block_count),
        in_specs=[
            row_block,
            pl.BlockSpec((LENGTH, PAIR), lambda p, i: (0, pairs + p)),
            pl.BlockSpec((LENGTH, PAIR), lambda p, i: (0, 2 * pairs + p)),
            row_block,
            table,
            table,
            table,
        ],
        out_specs=[
            row_block,
            pl.BlockSpec((3, LENGTH, PAIR), lambda p, i: (0, 0, p)),
            pl.BlockSpec((3, 1, PAIR), lambda p, i: (0, 0, p)),
        ],
        out_shape=[
            jax.ShapeDtypeStruct((rows, width), jnp.bfloat16),
            jax.ShapeDtypeStruct((3, rows, width), jnp.bfloat16),
            jax.ShapeDtypeStruct((3, 1, width), jnp.float32),
        ],
        scratch_shapes=[
            pltpu.VMEM((PAIR, LENGTH), jnp.bfloat16),
            pltpu.VMEM((PAIR, LENGTH), jnp.bfloat16),
            pltpu.VMEM((LENGTH, PAIR), jnp.float32),
            pltpu.VMEM((LENGTH, PAIR), jnp.float32),
            pltpu.VMEM((LENGTH, PAIR), jnp.float32),
        ],
        compiler_params=pltpu.CompilerParams(vmem_limit_bytes=56 * MIB),
        cost_estimate=pl.CostEstimate(
            flops=100 * rows * rows * width, bytes_accessed=16 * MIB, transcendentals=0
        ),
    )(joined, joined, joined, grad_mixed, *lanes)


def on_device(
    tokens,
    norm_gain,
    norm_shift,
    weight_qkv,
    bias_qkv,
    weight_dense,
    weight_up,
    bias_up,
    weight_down,
    bias_out,
    cotangent,
):
    f32 = jnp.float32
    token_rows = tokens.astype(f32)
    mean_row = jnp.mean(token_rows, axis=-1, keepdims=True)
    centred = token_rows - mean_row
    variance = jnp.mean(centred * centred, axis=-1, keepdims=True)
    root = lax.rsqrt(variance + epsilon)
    normed_low = (centred * root * norm_gain + norm_shift).astype(jnp.bfloat16)

    full_qkv = lax.all_gather(jnp.transpose(weight_qkv, (1, 0, 2)), "dp", axis=1, tiled=True)
    full_up = lax.all_gather(weight_up, "dp", axis=0, tiled=True)
    full_dense = lax.all_gather(weight_dense, "dp", axis=1, tiled=True)
    full_down = lax.all_gather(weight_down, "dp", axis=1, tiled=True)
    normed_parts = group_gather(normed_low)
    grad_parts = group_gather(after(cotangent, normed_parts[-1]))
    gathered = place_group(normed_parts)
    grad_rows = place_group(grad_parts)
    group_rows = gathered.shape[0]
    lanes = lane_tables(LENGTH)

    joined = joined_rows(gathered, full_qkv, bias_qkv, lanes)
    active, slope = hidden_rows(gathered, full_up, bias_up)
    grad_mixed = jnp.einsum(
        "td,kd->tk", grad_rows, full_dense, preferred_element_type=f32
    ).astype(jnp.bfloat16)
    grad_down = jnp.einsum("tf,td->fd", active, grad_rows, preferred_element_type=f32)
    grad_down = lax.psum_scatter(
        grad_down.astype(jnp.bfloat16), "dp", scatter_dimension=1, tiled=True
    )
    mixed, grad_joined, bias_qkv_part = attention(joined, grad_mixed, lanes)
    branch = (
        jnp.dot(mixed, full_dense, preferred_element_type=f32)
        + jnp.dot(active, full_down, preferred_element_type=f32)
    ).astype(jnp.bfloat16)
    branch_sum = group_scatter(branch)
    block_out = (token_rows + branch_sum + bias_out).astype(jnp.bfloat16)

    grad_hidden, bias_up_part = grad_hidden_rows(grad_rows, full_down, slope)
    grad_up = jnp.einsum("td,tf->df", gathered, grad_hidden, preferred_element_type=f32)
    grad_up = lax.psum_scatter(
        grad_up.astype(jnp.bfloat16), "dp", scatter_dimension=0, tiled=True
    )
    grad_qkv = jnp.einsum("td,jtc->jdc", gathered, grad_joined, preferred_element_type=f32)
    grad_qkv = lax.psum_scatter(
        grad_qkv.astype(jnp.bfloat16), "dp", scatter_dimension=1, tiled=True
    )
    grad_dense = jnp.einsum("tk,td->kd", mixed, grad_rows, preferred_element_type=f32)
    grad_dense = lax.psum_scatter(
        grad_dense.astype(jnp.bfloat16), "dp", scatter_dimension=1, tiled=True
    )
    grad_normed = (
        jnp.einsum("jtc,jdc->td", grad_joined, full_qkv, preferred_element_type=f32)
        + jnp.einsum("tf,df->td", grad_hidden, full_up, preferred_element_type=f32)
    ).astype(jnp.bfloat16)
    grad_normed = group_scatter(grad_normed)

    hat = centred * root
    scaled = grad_normed * norm_gain
    grad_input = root * (
        scaled
        - jnp.mean(scaled, axis=-1, keepdims=True)
        - hat * jnp.mean(scaled * hat, axis=-1, keepdims=True)
    )
    grad_tokens = (cotangent.astype(f32) + grad_input).astype(jnp.bfloat16)
    grad_bias_qkv, grad_bias_up = lax.psum(
        (bias_qkv_part.reshape(bias_qkv.shape), bias_up_part.reshape(bias_up.shape)), "dp"
    )
    gain_part = jnp.sum(grad_normed * hat, axis=0)
    shift_part = jnp.sum(grad_normed, axis=0)
    out_part = jnp.sum(cotangent, axis=0, dtype=f32)
    grad_gain, grad_shift, grad_bias_out = lax.psum(
        (gain_part, shift_part, out_part), ("dp", "tensor")
    )
    return (
        block_out,
        grad_tokens,
        grad_gain,
        grad_shift,
        jnp.transpose(grad_qkv, (1, 0, 2)).astype(f32),
        grad_bias_qkv,
        grad_dense.astype(f32),
        grad_up.astype(f32),
        grad_bias_up,
        grad_down.astype(f32),
        grad_bias_out,
    )


def solution(mesh):
    in_specs = (
        P(("dp", "tensor"), None),
        P(),
        P(),
        P("dp", None, "tensor"),
        P(None, "tensor"),
        P("tensor", "dp"),
        P("dp", "tensor"),
        P("tensor"),
        P("tensor", "dp"),
        P(),
        P(("dp", "tensor"), None),
    )
    out_specs = (
        P(("dp", "tensor"), None),
        P(("dp", "tensor"), None),
        P(),
        P(),
        P("dp", None, "tensor"),
        P(None, "tensor"),
        P("tensor", "dp"),
        P("dp", "tensor"),
        P("tensor"),
        P("tensor", "dp"),
        P(),
    )
    return jax.shard_map(
        on_device, mesh=mesh, in_specs=in_specs, out_specs=out_specs, check_vma=False
    )
```

time: 1920 us -> 844 us (0.44)
  waiting for transfers between devices: 774 us -> 224 us
  matrix products: 691 us -> 167 us
  Pallas kernels: 0 us -> 235 us
  other arithmetic: 204 us -> 52.4 us
  local copies, waits for them, and re-layouts: 122 us -> 58.8 us
  loops' own time: 31.8 us -> 0 us
  starting transfers between devices: 0.48 us -> 22.2 us
    reduce_scatter x6 -> x4, waiting for transfers between devices: 626 us -> 0.01 us  [the longest x1 0.01 us: on_device(): lax.psum_scatter(grad_dense.astype(jnp.bfloat16), 'dp', scatter_dimension...]
    dot_general x40 -> x9, matrix products: 691 us -> 167 us  [the longest x1 25.9 us: on_device(): jnp.einsum('tf,df->td', grad_hidden, full_up, preferred_element_type=f32)]
    pallas_call x0 -> x4, Pallas kernels: none -> 235 us  [the longest x1 139 us: attention(): pl.pallas_call(functools.partial(attention_kernel, block=block, block_cou...]
    ppermute x0 -> x16, waiting for transfers between devices: none -> 222 us  [swap(): return lax.ppermute(value, 'tensor', [(i, i ^ bit) for i in range(count)])]
    all_gather x6 -> x4, waiting for transfers between devices: 145 us -> 0.02 us  [the longest x1 0.02 us: on_device(): full_up = lax.all_gather(weight_up, 'dp', axis=0, tiled=True)]
    convert_element_type x6 -> x7, other arithmetic: 112 us -> 13.9 us  [the longest x2 5.21 us: group_scatter(): (wide(take(2, 0)) + wide(first[half:])).astype(partial.dtype)]
    dynamic_update_slice x12 -> x9, local copies, waits for them, and re-layouts: 88.5 us -> 21.3 us  [put(): return lax.dynamic_update_slice(full, piece, start)]
    reduce_sum x10 -> x7, other arithmetic: 79.1 us -> 18.1 us  [the longest x3 6.88 us: on_device(): shift_part = jnp.sum(grad_normed, axis=0)]
  transfers between devices with their start and end apart: 12 -> 24, of which waited for: 8 -> 10; matrix products, arithmetic and copies ran while one was open for 49% -> 32% of each run, Pallas kernels for 0% -> 28%
where the time goes in v1:
time: 844 us; the launch traced here: 838 us
  Pallas kernels  235 us (28%)
  waiting for transfers between devices  224 us (27%)
  matrix products  167 us (20%)
  blocking collectives  64.7 us (8%)
  local copies, waits for them, and re-layouts  58.8 us (7%)
  other arithmetic  52.4 us (6%)
  starting transfers between devices  22.2 us (3%)
  between operations  15.1 us (2%)
    ppermute x16, waiting for transfers between devices, swap(): return lax.ppermute(value, 'tensor', [(i, i ^ bit) for i in range(count)])  222 us
    pallas_call x1, Pallas kernels, attention(): pl.pallas_call(functools.partial(attention_kernel, block=block, block_cou...  139 us
    psum x1, blocking collectives, on_device(): lax.psum((gain_part, shift_part, out_part), ('dp', 'tensor'))  37.9 us
    pallas_call x1, Pallas kernels, hidden_rows(): pl.pallas_call(hidden_kernel, grid=(width // columns, rows // block), in_...  35.7 us
    pallas_call x1, Pallas kernels, grad_hidden_rows(): pl.pallas_call(grad_hidden_kernel, grid=(width // columns, rows // block)...  30.9 us
    pallas_call x1, Pallas kernels, joined_rows(): pl.pallas_call(joined_kernel, grid=(rows // block, 3), in_specs=[pl.Block...  28.5 us
    psum x1, blocking collectives, on_device(): lax.psum((bias_qkv_part.reshape(bias_qkv.shape), bias_up_part.reshape(bia...  26.8 us
    dot_general x1, matrix products, on_device(): jnp.einsum('tf,df->td', grad_hidden, full_up, preferred_element_type=f32)  25.9 us
  transfers between devices with their start and end apart: 24, of which 10 were waited for; matrix products, arithmetic and copies ran while one was open for 32% of the time, Pallas kernels for 28%

profile of v1, /device:TPU:0, one launch (start us, length us, event | category | flops | bytes accessed | tf_op | source)
XLA Modules:
  0.0 838.5 jit_solution(9720050037000330644)
XLA Ops:
  12.2 4.3 broadcast.81.clone
  23.8 44.3 %collective-permute-done.1 = bf16[512,2048]{1,0:T(8,128)(2,1)S(1)} collective-permute-done((bf16[512,2048]{1,0:T(8,128)(2,1)}, bf16[512,2048]{1,0:T(8,128)(2,1)S(1)}, u32[]{:S(2)}, u32[]{:S(2)}) %collective-permute-start.1) | collective-permute-done | bytes 2097184 | tf_op jit(solution)/shard_map/ppermute | solution.py:27
  71.4 22.8 %collective-permute-done.3 = bf16[256,2048]{1,0:T(8,128)(2,1)} collective-permute-done((bf16[256,2048]{1,0:T(8,128)(2,1)S(1)}, bf16[256,2048]{1,0:T(8,128)(2,1)}, u32[]{:S(2)}, u32[]{:S(2)}) %collective-permute-start.3) | collective-permute-done | bytes 1048608 | tf_op jit(solution)/shard_map/ppermute | solution.py:27
  99.2 5.7 multiply_sine_fusion
  105.0 3.9 concatenate.29.below_ref
  109.0 4.2 concatenate.28.above_ref
  114.4 5.2 concatenate.27.cos_ref
  124.6 4.3 broadcast.81
  132.2 8.4 collective-permute-done.4
  143.0 24.0 %collective-permute-done.2 = bf16[256,2048]{1,0:T(8,128)(2,1)} collective-permute-done((bf16[256,2048]{1,0:T(8,128)(2,1)}, bf16[256,2048]{1,0:T(8,128)(2,1)}, u32[]{:S(2)}, u32[]{:S(2)}) %collective-permute-start.2) | collective-permute-done | bytes 1048608 | tf_op jit(solution)/shard_map/ppermute | solution.py:27
  179.9 6.3 collective-permute-done.6
  190.7 9.9 %convolution_convert_fusion.3.g_ref = bf16[2048,512]{1,0:T(8,128)(2,1)} fusion(bf16[2048,2048]{1,0:T(8,128)(2,1)} %constant_dynamic-update-slice_fusion.g_ref, bf16[512,2048]{1,0:T(8,128)(2,1)} %all-gather.7.cloned.1.call-done), kind=kOutput, calls=%fused_computation.32 | convolution fusion | flops 4296015872 | bytes 12582912 | tf_op jit(solution)/shard_map/td,kd->tk/dot_general | solution.py:396
  200.5 28.5 %shard_map.194.q_ref.k_ref.v_ref = bf16[2048,1536]{1,0:T(8,128)(2,1)} custom-call(bf16[2048,2048]{1,0:T(8,128)(2,1)} %constant_dynamic-update-slice_fusion.5.x_ref, bf16[3,2048,512]{2,1,0:T(8,128)(2,1)} %all-gather.5.cloned.1.call-done.w_ref, f32[3,1,512]{2,1,0:T(1,128)S(1)} %reshape.74.bias_ref, f32[2048,128]{1,0:T(8,128)S(1)} %concatenate.27.cos_ref, ...), custom_call_target="tpu_custom_call" | custom-call | flops 12884901888 | bytes 25165824 | tf_op jit(solution)/shard_map/pallas_call | solution.py:127
  229.0 139.5 %shard_map.195 = (bf16[2048,512]{1,0:T(8,128)(2,1)}, bf16[3,2048,512]{2,1,0:T(8,128)(2,1)}, f32[3,1,512]{2,1,0:T(1,128)}) custom-call(bf16[2048,1536]{1,0:T(8,128)(2,1)} %shard_map.194.q_ref.k_ref.v_ref, bf16[2048,1536]{1,0:T(8,128)(2,1)} %shard_map.194.q_ref.k_ref.v_ref, bf16[2048,1536]{1,0:T(8,128)(2,1)} %shard_map.194.q_ref.k_ref.v_ref, ...), custom_call_target="tpu_custom_call" | custom-call | flops 214748364800 | bytes 16777216 | tf_op jit(solution)/shard_map/pallas_call | solution.py:326
  368.5 9.9 %convolution_convert_fusion.2 = bf16[512,2048]{1,0:T(8,128)(2,1)} fusion(bf16[2048,512]{1,0:T(8,128)(2,1)} %get-tuple-element.20, bf16[2048,2048]{1,0:T(8,128)(2,1)} %constant_dynamic-update-slice_fusion.g_ref), kind=kOutput, calls=%fused_computation.31 | convolution fusion | flops 4296015872 | bytes 12582912 | tf_op jit(solution)/shard_map/tk,td->kd/dot_general | solution.py:420
  378.5 19.1 %convert_bitcast_fusion = bf16[3,2048,512]{1,2,0:T(8,128)(2,1)} fusion(bf16[3,2048,512]{2,1,0:T(8,128)(2,1)} %get-tuple-element.22, bf16[2048,2048]{1,0:T(8,128)(2,1)} %constant_dynamic-update-slice_fusion.5.x_ref), kind=kOutput, calls=%fused_computation.7 | convolution fusion | flops 12888047616 | bytes 20971520 | tf_op jit(solution)/shard_map/td,jtc->jdc/dot_general | solution.py:416
  398.3 35.7 %shard_map.196 = (bf16[2048,2048]{1,0:T(8,128)(2,1)}, bf16[2048,2048]{1,0:T(8,128)(2,1)}) custom-call(bf16[2048,2048]{1,0:T(8,128)(2,1)} %constant_dynamic-update-slice_fusion.5.x_ref, bf16[2048,2048]{1,0:T(8,128)(2,1)} %all-gather.9.cloned.1.call-done.w_ref, f32[1,2048]{1,0:T(1,128)S(1)} %bitcast.37), custom_call_target="tpu_custom_call" | custom-call | flops 17179869184 | bytes 41943040 | tf_op jit(solution)/shard_map/pallas_call | solution.py:162
  434.0 30.9 %shard_map.197 = (bf16[2048,2048]{1,0:T(8,128)(2,1)}, f32[1,2048]{1,0:T(1,128)S(1)}) custom-call(bf16[2048,2048]{1,0:T(8,128)(2,1)} %constant_dynamic-update-slice_fusion.g_ref, bf16[2048,2048]{1,0:T(8,128)(2,1)} %all-gather.11.cloned.1.call-done.w_ref, bf16[2048,2048]{1,0:T(8,128)(2,1)} %get-tuple-element.23.slope_ref), custom_call_target="tpu_custom_call" | custom-call | flops 17179869184 | bytes 41943040 | tf_op jit(solution)/shard_map/pallas_call | solution.py:197
  464.9 23.8 %convolution_convert_fusion.1 = bf16[2048,2048]{1,0:T(8,128)(2,1)} fusion(bf16[2048,2048]{1,0:T(8,128)(2,1)} %constant_dynamic-update-slice_fusion.5.x_ref, bf16[2048,2048]{1,0:T(8,128)(2,1)} %get-tuple-element.24), kind=kOutput, calls=%fused_computation.6 | convolution fusion | flops 17184063488 | bytes 25165824 | tf_op jit(solution)/shard_map/td,tf->df/dot_general | solution.py:412
  488.8 19.7 %fusion.30 = f32[2048,2048,1]{1,0,2:T(8,128)} fusion(bf16[3,2048,512]{2,1,0:T(8,128)(2,1)} %get-tuple-element.22, bf16[3,2048,512]{2,1,0:T(8,128)(2,1)} %all-gather.5.cloned.1.call-done.w_ref), kind=kOutput, calls=%fused_computation.82 | convolution fusion | flops 12884901888 | bytes 29360128 | tf_op jit(solution)/shard_map/jtc,jdc->td/dot_general | solution.py:425
  508.6 23.8 %convolution_convert_fusion = bf16[2048,2048]{1,0:T(8,128)(2,1)} fusion(bf16[2048,2048]{1,0:T(8,128)(2,1)} %get-tuple-element.21, bf16[2048,2048]{1,0:T(8,128)(2,1)} %constant_dynamic-update-slice_fusion.g_ref), kind=kOutput, calls=%fused_computation.5 | convolution fusion | flops 17184063488 | bytes 25165824 | tf_op jit(solution)/shard_map/tf,td->fd/dot_general | solution.py:399
  532.4 25.9 %fusion = bf16[2048,2048]{1,0:T(8,128)(2,1)} fusion(f32[2048,2048,1]{1,0,2:T(8,128)} %fusion.30, bf16[2048,2048]{1,0:T(8,128)(2,1)} %get-tuple-element.24, bf16[2048,2048]{1,0:T(8,128)(2,1)} %all-gather.9.cloned.1.call-done.w_ref), kind=kOutput, calls=%fused_computation.1 | convolution fusion | flops 17188257792 | bytes 41943040 | tf_op jit(solution)/shard_map/tf,df->td/dot_general | solution.py:426
  564.1 24.3 %fusion.29 = f32[2048,2048]{1,0:T(8,128)} fusion(bf16[2048,2048]{1,0:T(8,128)(2,1)} %get-tuple-element.21, bf16[2048,2048]{1,0:T(8,128)(2,1)} %all-gather.11.cloned.1.call-done.w_ref), kind=kOutput, calls=%fused_computation.81 | convolution fusion | flops 17179869184 | bytes 33554432 | tf_op jit(solution)/shard_map/dot_general | solution.py:406
  588.4 10.4 %add_convert_fusion = bf16[2048,2048]{1,0:T(8,128)(2,1)} fusion(f32[2048,2048]{1,0:T(8,128)} %fusion.29, bf16[2048,512]{1,0:T(8,128)(2,1)S(1)} %copy-done.25, bf16[512,2048]{1,0:T(8,128)(2,1)S(1)} %copy-done.24), kind=kOutput, calls=%fused_computation.2 | convolution fusion | flops 4303355904 | bytes 29360128 | tf_op jit(solution)/shard_map/dot_general | solution.py:405
  614.8 35.2 %collective-permute-done.8 = bf16[512,2048]{1,0:T(8,128)(2,1)S(1)} collective-permute-done((bf16[512,2048]{1,0:T(8,128)(2,1)S(1)}, bf16[512,2048]{1,0:T(8,128)(2,1)S(1)}, u32[]{:S(2)}, u32[]{:S(2)}) %collective-permute-start.8) | collective-permute-done | bytes 2097184 | tf_op jit(solution)/shard_map/ppermute | solution.py:27
  655.4 65.0 %collective-permute-done.13 = bf16[256,2048]{1,0:T(8,128)(2,1)S(1)} collective-permute-done((bf16[256,2048]{1,0:T(8,128)(2,1)}, bf16[256,2048]{1,0:T(8,128)(2,1)S(1)}, u32[]{:S(2)}, u32[]{:S(2)}) %collective-permute-start.13) | collective-permute-done | bytes 1048608 | tf_op jit(solution)/shard_map/ppermute | solution.py:27
  720.4 4.5 fusion.27
  726.0 10.7 %collective-permute-done.9 = bf16[256,2048]{1,0:T(8,128)(2,1)} collective-permute-done((bf16[256,2048]{1,0:T(8,128)(2,1)}, bf16[256,2048]{1,0:T(8,128)(2,1)}, u32[]{:S(2)}, u32[]{:S(2)}) %collective-permute-start.9) | collective-permute-done | bytes 1048608 | tf_op jit(solution)/shard_map/ppermute | solution.py:27
  736.7 4.4 convert_add_fusion.5
  742.4 26.8 %all-reduce.1 = (f32[3,512]{1,0:T(4,128)}, f32[2048]{0:T(1024)}) all-reduce(f32[3,512]{1,0:T(4,128)S(1)} %bitcast.39, f32[2048]{0:T(1024)S(1)} %bitcast.36), channel_id=1, replica_groups=mesh['dp'=8,'tensor'=4] {'dp'}, use_global_device_ids=true, to_apply=%region_10.11 | all-reduce | flops 3584 | bytes 28672 | tf_op jit(solution)/shard_map/psum | solution.py:438
  778.5 6.4 convert_reduce_fusion.1
  784.8 37.9 %all-reduce = (f32[2048]{0:T(1024)}, f32[2048]{0:T(1024)}, f32[2048]{0:T(1024)}) all-reduce(f32[2048]{0:T(1024)S(1)} %get-tuple-element.49, f32[2048]{0:T(1024)S(1)} %reduce_sum.78, f32[2048]{0:T(1024)S(1)} %get-tuple-element.74), channel_id=1, replica_groups=mesh['dp'=8,'tensor'=4] {'dp','tensor'}, use_global_device_ids=true, to_apply=%region_5.6 | all-reduce | flops 6144 | bytes 49152 | tf_op jit(solution)/shard_map/psum | solution.py:444
  (143 shorter events, 97.7 us)
Async XLA Ops:
  7.2 183.5 %all-gather.7.cloned.1.call-start = ((), (), s32[]{:S(2)}) async-start(), calls=%async_computation.5 | async-start | bytes 2359296 | tf_op jit(solution)/shard_map/all_gather | solution.py:385
  7.9 192.6 %all-gather.5.cloned.1.call-start = ((), (), s32[]{:S(2)}) async-start(), calls=%async_computation.4 | async-start | bytes 7077888 | tf_op jit(solution)/shard_map/all_gather | solution.py:383
  8.7 389.1 %all-gather.9.cloned.1.call-start = ((), (), s32[]{:S(2)}) async-start(), calls=%async_computation.6 | async-start | bytes 9437184 | tf_op jit(solution)/shard_map/all_gather | solution.py:384
  9.4 424.6 %all-gather.11.cloned.1.call-start = ((), (), s32[]{:S(2)}) async-start(), calls=%async_computation.7 | async-start | bytes 9437184 | tf_op jit(solution)/shard_map/all_gather | solution.py:386
  19.4 85.4 %copy-start.22 = (f32[3,512]{1,0:T(4,128)S(1)}, f32[3,512]{1,0:T(4,128)}, u32[]{:S(2)}) copy-start(f32[3,512]{1,0:T(4,128)} %param.15) | copy-start | bytes 18436
  19.4 48.7 %collective-permute-start.1 = (bf16[512,2048]{1,0:T(8,128)(2,1)}, bf16[512,2048]{1,0:T(8,128)(2,1)S(1)}, u32[]{:S(2)}, u32[]{:S(2)}) collective-permute-start(bf16[512,2048]{1,0:T(8,128)(2,1)} %get-tuple-element.62), channel_id=1, source_target_pairs={{0,2},{1,3},{2,0},{3,1},{4,6},{5,7},{6,4},{7,5},{8,10},{9,11},{10,... | collective-permute-start | bytes 6291464 | tf_op jit(solution)/shard_map/ppermute | solution.py:27
  22.3 75.2 %collective-permute-start = (bf16[512,2048]{1,0:T(8,128)(2,1)}, bf16[512,2048]{1,0:T(8,128)(2,1)S(1)}, u32[]{:S(2)}, u32[]{:S(2)}) collective-permute-start(bf16[512,2048]{1,0:T(8,128)(2,1)} %get-tuple-element.62), channel_id=1, source_target_pairs={{0,1},{1,0},{2,3},{3,2},{4,5},{5,4},{6,7},{7,6},{8,9},{9,8},{10,11... | collective-permute-start | bytes 6291464 | tf_op jit(solution)/shard_map/ppermute | solution.py:27
  69.6 24.6 %collective-permute-start.3 = (bf16[256,2048]{1,0:T(8,128)(2,1)S(1)}, bf16[256,2048]{1,0:T(8,128)(2,1)}, u32[]{:S(2)}, u32[]{:S(2)}) collective-permute-start(bf16[256,2048]{1,0:T(8,128)(2,1)S(1)} %slice.49), channel_id=1, source_target_pairs={{0,1},{1,0},{2,3},{3,2},{4,5},{5,4},{6,7},{7,6},{8,9},{9,8},{10,11... | collective-permute-start | bytes 3145736 | tf_op jit(solution)/shard_map/ppermute | solution.py:27
  94.2 46.3 %collective-permute-start.4 = (bf16[512,2048]{1,0:T(8,128)(2,1)}, bf16[512,2048]{1,0:T(8,128)(2,1)}, u32[]{:S(2)}, u32[]{:S(2)}) collective-permute-start(bf16[512,2048]{1,0:T(8,128)(2,1)} %param.21), channel_id=1, source_target_pairs={{0,1},{1,0},{2,3},{3,2},{4,5},{5,4},{6,7},{7,6},{8,9},{9,8},{10,11... | collective-permute-start | bytes 6291464 | tf_op jit(solution)/shard_map/ppermute | solution.py:27
  95.7 73.7 %collective-permute-start.5 = (bf16[512,2048]{1,0:T(8,128)(2,1)}, bf16[512,2048]{1,0:T(8,128)(2,1)}, u32[]{:S(2)}, u32[]{:S(2)}) collective-permute-start(bf16[512,2048]{1,0:T(8,128)(2,1)} %param.21), channel_id=1, source_target_pairs={{0,2},{1,3},{2,0},{3,1},{4,6},{5,7},{6,4},{7,5},{8,10},{9,11},{10,... | collective-permute-start | bytes 6291464 | tf_op jit(solution)/shard_map/ppermute | solution.py:27
  97.2 672.0 %reduce-scatter.7.cloned.1.call-start = ((), (), s32[]{:S(2)}) async-start(), calls=%async_computation.9 | async-start | bytes 2359296 | tf_op jit(solution)/shard_map/reduce_scatter | solution.py:421
  98.6 68.4 %collective-permute-start.2 = (bf16[256,2048]{1,0:T(8,128)(2,1)}, bf16[256,2048]{1,0:T(8,128)(2,1)}, u32[]{:S(2)}, u32[]{:S(2)}) collective-permute-start(bf16[256,2048]{1,0:T(8,128)(2,1)} %slice.48), channel_id=1, source_target_pairs={{0,2},{1,3},{2,0},{3,1},{4,6},{5,7},{6,4},{7,5},{8,10},{9,11},{10,... | collective-permute-start | bytes 3145736 | tf_op jit(solution)/shard_map/ppermute | solution.py:27
  109.0 91.6 %copy-start = (f32[2048,128]{1,0:T(8,128)}, f32[2048,128]{1,0:T(8,128)S(1)}, u32[]{:S(2)}) copy-start(f32[2048,128]{1,0:T(8,128)S(1)} %concatenate.29.below_ref) | copy-start | bytes 3145732
  113.2 87.3 %copy-start.1 = (f32[2048,128]{1,0:T(8,128)}, f32[2048,128]{1,0:T(8,128)S(1)}, u32[]{:S(2)}) copy-start(f32[2048,128]{1,0:T(8,128)S(1)} %concatenate.28.above_ref) | copy-start | bytes 3145732
  119.5 81.0 %copy-start.2 = (f32[2048,128]{1,0:T(8,128)}, f32[2048,128]{1,0:T(8,128)S(1)}, u32[]{:S(2)}) copy-start(f32[2048,128]{1,0:T(8,128)S(1)} %concatenate.27.cos_ref) | copy-start | bytes 3145732
  141.9 44.3 %collective-permute-start.6 = (bf16[256,2048]{1,0:T(8,128)(2,1)S(1)}, bf16[256,2048]{1,0:T(8,128)(2,1)S(1)}, u32[]{:S(2)}, u32[]{:S(2)}) collective-permute-start(bf16[256,2048]{1,0:T(8,128)(2,1)S(1)} %slice.50), channel_id=1, source_target_pairs={{0,2},{1,3},{2,0},{3,1},{4,6},{5,7},{6,4},{7,5},{8,10},{9,11},{10,... | collective-permute-start | bytes 3145736 | tf_op jit(solution)/shard_map/ppermute | solution.py:27
  170.6 18.9 %collective-permute-start.7 = (bf16[256,2048]{1,0:T(8,128)(2,1)S(1)}, bf16[256,2048]{1,0:T(8,128)(2,1)S(1)}, u32[]{:S(2)}, u32[]{:S(2)}) collective-permute-start(bf16[256,2048]{1,0:T(8,128)(2,1)S(1)} %slice.51), channel_id=1, source_target_pairs={{0,1},{1,0},{2,3},{3,2},{4,5},{5,4},{6,7},{7,6},{8,9},{9,8},{10,11... | collective-permute-start | bytes 3145736 | tf_op jit(solution)/shard_map/ppermute | solution.py:27
  378.5 444.3 %reduce-scatter.5.cloned.1.call-start = ((), (), s32[]{:S(2)}) async-start(), calls=%async_computation.8 | async-start | bytes 7077888 | tf_op jit(solution)/shard_map/reduce_scatter | solution.py:417
  397.7 428.0 %reduce-scatter.9.cloned.1.call-start = ((), (), s32[]{:S(2)}) async-start(), calls=%async_computation.10 | async-start | bytes 9437184 | tf_op jit(solution)/shard_map/reduce_scatter | solution.py:413
  488.8 339.6 %reduce-scatter.11.cloned.1.call-start = ((), (), s32[]{:S(2)}) async-start(), calls=%async_computation.11 | async-start | bytes 9437184 | tf_op jit(solution)/shard_map/reduce_scatter | solution.py:400
  562.7 47.8 %collective-permute-start.12 = (bf16[512,2048]{1,0:T(8,128)(2,1)}, bf16[512,2048]{1,0:T(8,128)(2,1)S(1)}, u32[]{:S(2)}, u32[]{:S(2)}) collective-permute-start(bf16[512,2048]{1,0:T(8,128)(2,1)} %pad_maximum_fusion.3), channel_id=1, source_target_pairs={{0,1},{1,0},{2,3},{3,2},{4,5},{5,4},{6,7},{7,6},{8,9},{9,8},{10,11... | collective-permute-start | bytes 6291464 | tf_op jit(solution)/shard_map/ppermute | solution.py:27
  601.6 48.3 %collective-permute-start.8 = (bf16[512,2048]{1,0:T(8,128)(2,1)S(1)}, bf16[512,2048]{1,0:T(8,128)(2,1)S(1)}, u32[]{:S(2)}, u32[]{:S(2)}) collective-permute-start(bf16[512,2048]{1,0:T(8,128)(2,1)S(1)} %pad_maximum_fusion.1), channel_id=1, source_target_pairs={{0,1},{1,0},{2,3},{3,2},{4,5},{5,4},{6,7},{7,6},{8,9},{9,8},{10,11... | collective-permute-start | bytes 6291464 | tf_op jit(solution)/shard_map/ppermute | solution.py:27
  604.2 51.2 %collective-permute-start.14 = (bf16[512,2048]{1,0:T(8,128)(2,1)}, bf16[512,2048]{1,0:T(8,128)(2,1)}, u32[]{:S(2)}, u32[]{:S(2)}) collective-permute-start(bf16[512,2048]{1,0:T(8,128)(2,1)} %pad_maximum_fusion.4), channel_id=1, source_target_pairs={{0,2},{1,3},{2,0},{3,1},{4,6},{5,7},{6,4},{7,5},{8,10},{9,11},{10,... | collective-permute-start | bytes 6291464 | tf_op jit(solution)/shard_map/ppermute | solution.py:27
  607.0 118.9 %collective-permute-start.10 = (bf16[512,2048]{1,0:T(8,128)(2,1)}, bf16[512,2048]{1,0:T(8,128)(2,1)}, u32[]{:S(2)}, u32[]{:S(2)}) collective-permute-start(bf16[512,2048]{1,0:T(8,128)(2,1)} %pad_maximum_fusion.2), channel_id=1, source_target_pairs={{0,2},{1,3},{2,0},{3,1},{4,6},{5,7},{6,4},{7,5},{8,10},{9,11},{10,... | collective-permute-start | bytes 6291464 | tf_op jit(solution)/shard_map/ppermute | solution.py:27
  613.1 107.3 %collective-permute-start.13 = (bf16[256,2048]{1,0:T(8,128)(2,1)}, bf16[256,2048]{1,0:T(8,128)(2,1)S(1)}, u32[]{:S(2)}, u32[]{:S(2)}) collective-permute-start(bf16[256,2048]{1,0:T(8,128)(2,1)} %add_convert_fusion.2), channel_id=1, source_target_pairs={{0,2},{1,3},{2,0},{3,1},{4,6},{5,7},{6,4},{7,5},{8,10},{9,11},{10,... | collective-permute-start | bytes 3145736 | tf_op jit(solution)/shard_map/ppermute | solution.py:27
  653.9 82.8 %collective-permute-start.9 = (bf16[256,2048]{1,0:T(8,128)(2,1)}, bf16[256,2048]{1,0:T(8,128)(2,1)}, u32[]{:S(2)}, u32[]{:S(2)}) collective-permute-start(bf16[256,2048]{1,0:T(8,128)(2,1)} %add_convert_fusion.4), channel_id=1, source_target_pairs={{0,2},{1,3},{2,0},{3,1},{4,6},{5,7},{6,4},{7,5},{8,10},{9,11},{10,... | collective-permute-start | bytes 3145736 | tf_op jit(solution)/shard_map/ppermute | solution.py:27
  655.4 81.3 %copy-start.13 = (bf16[512,2048]{1,0:T(8,128)(2,1)S(1)}, bf16[512,2048]{1,0:T(8,128)(2,1)}, u32[]{:S(2)}) copy-start(bf16[512,2048]{1,0:T(8,128)(2,1)} %copy-done.12) | copy-start | bytes 6291460
  724.9 46.2 %collective-permute-start.15 = (bf16[256,2048]{1,0:T(8,128)(2,1)}, bf16[256,2048]{1,0:T(8,128)(2,1)}, u32[]{:S(2)}, u32[]{:S(2)}) collective-permute-start(bf16[256,2048]{1,0:T(8,128)(2,1)} %get-tuple-element.63), channel_id=1, source_target_pairs={{0,1},{1,0},{2,3},{3,2},{4,5},{5,4},{6,7},{7,6},{8,9},{9,8},{10,11... | collective-permute-start | bytes 3145736 | tf_op jit(solution)/shard_map/ppermute | solution.py:27
  741.0 32.5 %copy-start.15 = (f32[2048]{0:T(1024)S(1)}, f32[2048]{0:T(1024)}, u32[]{:S(2)}) copy-start(f32[2048]{0:T(1024)} %param.12) | copy-start | bytes 24580
  741.1 32.5 %copy-start.17 = (f32[512]{0:T(512)S(1)}, f32[512]{0:T(512)}, u32[]{:S(2)}) copy-start(f32[512]{0:T(512)} %copy-done.16) | copy-start | bytes 6148
  741.1 32.6 %copy-start.19 = (f32[512]{0:T(512)S(1)}, f32[512]{0:T(512)}, u32[]{:S(2)}) copy-start(f32[512]{0:T(512)} %copy-done.18) | copy-start | bytes 6148
  741.1 34.8 %collective-permute-start.11 = (bf16[256,2048]{1,0:T(8,128)(2,1)S(1)}, bf16[256,2048]{1,0:T(8,128)(2,1)}, u32[]{:S(2)}, u32[]{:S(2)}) collective-permute-start(bf16[256,2048]{1,0:T(8,128)(2,1)S(1)} %get-tuple-element.69), channel_id=1, source_target_pairs={{0,1},{1,0},{2,3},{3,2},{4,5},{5,4},{6,7},{7,6},{8,9},{9,8},{10,11... | collective-permute-start | bytes 3145736 | tf_op jit(solution)/shard_map/ppermute | solution.py:27
  (18 other events, 151.6 us)
Sparse Core Ops, SparseCore 0:
  9.6 33.5 all-gather.6
  44.8 63.7 all-gather.4
  110.2 80.7 all-gather.8
  192.4 81.0 all-gather.10
  378.6 36.4 reduce-scatter.6
  417.2 68.5 reduce-scatter.4
  488.9 90.2 reduce-scatter.8
  581.5 87.9 reduce-scatter.10

commit v2 on v1

--- a/solution.py
+++ b/solution.py
@@ -1,4 +1,5 @@
 import functools
+import math
 
 import jax
 import jax.numpy as jnp
@@ -22,38 +23,92 @@
     return lax.optimization_barrier((value,) + earlier)[0]
 
 
-def swap(value, bit):
-    count = lax.axis_size("tensor")
-    return lax.ppermute(value, "tensor", [(i, i ^ bit) for i in range(count)])
-
-
-def group_gather(block):
+def swap(value, axis, bit):
+    count = lax.axis_size(axis)
+    return lax.ppermute(value, axis, [(i, i ^ bit) for i in range(count)])
+
+
+def place_kernel(starts_ref, *refs, dim):
+    count = (len(refs) - 2) // 2
+    pieces, out, buffers, sems = refs[:count], refs[count], refs[count + 1 : -1], refs[-1]
+    for slot in range(count):
+        pltpu.make_async_copy(pieces[slot], buffers[slot], sems.at[0, slot]).start()
+    writes = []
+    for slot in range(count):
+        buffer = buffers[slot]
+        size = buffer.shape[dim]
+        where = [slice(None)] * len(buffer.shape)
+        where[dim] = pl.ds(pl.multiple_of(starts_ref[slot], size), size)
+        pltpu.make_async_copy(pieces[slot], buffer, sems.at[0, slot]).wait()
+        write = pltpu.make_async_copy(buffer, out.at[tuple(where)], sems.at[1, slot])
+        write.start()
+        writes.append(write)
+    for write in writes:
+        write.wait()
+
+
+def place(pieces, dim, total):
+    starts = jnp.stack([jnp.asarray(start, jnp.int32) for start, _ in pieces])
+    sources = [piece for _, piece in pieces]
+    shape = list(sources[0].shape)
+    shape[dim] = total
+    any_space = pl.BlockSpec(memory_space=pl.ANY)
+    return pl.pallas_call(
+        functools.partial(place_kernel, dim=dim),
+        in_specs=[pl.BlockSpec(memory_space=pltpu.SMEM)] + [any_space] * len(sources),
+        out_specs=any_space,
+        out_shape=jax.ShapeDtypeStruct(tuple(shape), sources[0].dtype),
+        scratch_shapes=[pltpu.VMEM(source.shape, source.dtype) for source in sources]
+        + [pltpu.SemaphoreType.DMA((2, len(pieces)))],
+        compiler_params=pltpu.CompilerParams(vmem_limit_bytes=60 * MIB),
+        cost_estimate=pl.CostEstimate(
+            flops=0, bytes_accessed=4 * math.prod(shape), transcendentals=0
+        ),
+    )(starts, *sources)
+
+
+def gather_start(block):
+    if lax.axis_size("tensor") != 4:
+        return (lax.all_gather(block, "tensor", axis=0, tiled=True),)
+    return block, swap(block, "tensor", 1), swap(block, "tensor", 2)
+
+
+def gather_pass(parts):
+    if len(parts) == 1:
+        return parts
+    block, one, two = parts
     half = block.shape[0] // 2
-    one = swap(block, 1)
-    two = swap(block, 2)
-    low = swap(one[:half], 2)
-    high = swap(two[half:], 1)
-    return block, one, two, low, high
-
-
-def place_group(parts):
+    return block, one, two, swap(one[:half], "tensor", 2), swap(two[half:], "tensor", 1)
+
+
+def gathered_pieces(parts):
+    if len(parts) == 1:
+        return [(0, parts[0])]
     block, one, two, low, high = parts
     rows = block.shape[0]
     me = lax.axis_index("tensor")
-    full = jnp.zeros((4 * rows,) + block.shape[1:], block.dtype)
-
-    def put(full, piece, owner, shift=0):
-        start = (owner * rows + shift,) + (0,) * (block.ndim - 1)
-        return lax.dynamic_update_slice(full, piece, start)
-
-    full = put(full, block, me)
-    full = put(full, one, me ^ 1)
-    full = put(full, two, me ^ 2)
-    full = put(full, low, me ^ 3)
-    return put(full, high, me ^ 3, rows // 2)
-
-
-def group_scatter(partial):
+    return [
+        (me * rows, block),
+        ((me ^ 1) * rows, one),
+        ((me ^ 2) * rows, two),
+        ((me ^ 3) * rows, low),
+        ((me ^ 3) * rows + rows // 2, high),
+    ]
+
+
+def gather_end(parts):
+    if len(parts) == 1:
+        return parts[0]
+    return place(gathered_pieces(parts), 0, 4 * parts[0].shape[0])
+
+
+def wide(piece):
+    return piece.astype(jnp.float32)
+
+
+def scatter_cut(partial):
+    if lax.axis_size("tensor") != 4:
+        return (partial,)
     rows = partial.shape[0] // 4
     half = rows // 2
     me = lax.axis_index("tensor")
@@ -61,18 +116,91 @@
     def take(bit, shift):
         return lax.dynamic_slice_in_dim(partial, (me ^ bit) * rows + shift, half, 0)
 
-    def wide(piece):
-        return piece.astype(jnp.float32)
-
-    first = swap(jnp.concatenate([take(1, 0), take(3, 0)]), 1)
-    second = swap(jnp.concatenate([take(2, half), take(3, half)]), 2)
-    forward_first = (wide(take(2, 0)) + wide(first[half:])).astype(partial.dtype)
-    forward_second = (wide(take(1, half)) + wide(second[half:])).astype(partial.dtype)
-    last_first = swap(forward_first, 2)
-    last_second = swap(forward_second, 1)
-    low = wide(take(0, 0)) + wide(first[:half]) + wide(last_first)
-    high = wide(take(0, half)) + wide(second[:half]) + wide(last_second)
-    return jnp.concatenate([low, high])
+    return tuple(take(bit, shift) for bit in (3, 1, 2, 0) for shift in (0, half))
+
+
+def scatter_send(cuts):
+    if len(cuts) == 1:
+        return (lax.psum_scatter(wide(cuts[0]), "tensor", scatter_dimension=0, tiled=True),)
+    far_low, far_high, one_low, one_high, two_low, two_high, low, high = cuts
+    return (
+        swap(far_low, "tensor", 1),
+        swap(far_high, "tensor", 2),
+        swap(one_low, "tensor", 1),
+        swap(two_high, "tensor", 2),
+        two_low,
+        one_high,
+        low,
+        high,
+    )
+
+
+def scatter_fold(parts):
+    if len(parts) == 1:
+        return parts
+    first_far, second_far, first_near, second_near, two_low, one_high, low, high = parts
+    return (
+        (wide(two_low) + wide(first_far)).astype(low.dtype),
+        (wide(one_high) + wide(second_far)).astype(low.dtype),
+        first_near,
+        second_near,
+        low,
+        high,
+    )
+
+
+def scatter_pass(parts):
+    if len(parts) == 1:
+        return parts
+    two_low, one_high, first_near, second_near, low, high = parts
+    return (
+        swap(two_low, "tensor", 2),
+        swap(one_high, "tensor", 1),
+        first_near,
+        second_near,
+        low,
+        high,
+    )
+
+
+def scatter_end(parts):
+    if len(parts) == 1:
+        return parts[0]
+    last_first, last_second, first_near, second_near, low, high = parts
+    return jnp.concatenate(
+        [
+            wide(low) + wide(first_near) + wide(last_first),
+            wide(high) + wide(second_near) + wide(last_second),
+        ]
+    )
+
+
+def exchange_start(columns):
+    if lax.axis_size("tensor") != 4:
+        return (lax.all_to_all(columns, "tensor", 0, 1, tiled=True),)
+    rows = columns.shape[0] // 4
+    me = lax.axis_index("tensor")
+    pieces = []
+    for bit in range(4):
+        piece = lax.dynamic_slice_in_dim(columns, (me ^ bit) * rows, rows, 0)
+        pieces.append(swap(piece, "tensor", bit) if bit else piece)
+    return tuple(pieces)
+
+
+def exchange_end(pieces):
+    if len(pieces) == 1:
+        return pieces[0]
+    width = pieces[0].shape[1]
+    me = lax.axis_index("tensor")
+    return place([((me ^ bit) * width, piece) for bit, piece in enumerate(pieces)], 1, 4 * width)
+
+
+def exchange_sum(value, axis):
+    count = lax.axis_size(axis)
+    parts = [value]
+    for bit in range(1, count):
+        parts.append(swap(value, axis, bit))
+    return functools.reduce(lambda a, b: a + b, parts)
 
 
 def lane_tables(row_total):
@@ -106,7 +234,7 @@
 
 def joined_kernel(x_ref, w_ref, bias_ref, cos_ref, above_ref, below_ref, out_ref):
     product = jnp.dot(x_ref[...], w_ref[0], preferred_element_type=jnp.float32) + bias_ref[0]
-    slot = pl.program_id(1)
+    slot = pl.program_id(0)
 
     @pl.when(slot < 2)
     def _():
@@ -123,19 +251,19 @@
 def joined_rows(x, w, bias, lanes):
     rows, depth = x.shape
     width = w.shape[2]
-    block = min(512, rows)
+    block = min(1024, rows)
     return pl.pallas_call(
         joined_kernel,
-        grid=(rows // block, 3),
+        grid=(3, rows // block),
         in_specs=[
-            pl.BlockSpec((block, depth), lambda i, j: (i, 0)),
-            pl.BlockSpec((1, depth, width), lambda i, j: (j, 0, 0)),
-            pl.BlockSpec((1, 1, width), lambda i, j: (j, 0, 0)),
+            pl.BlockSpec((block, depth), lambda j, i: (i, 0)),
+            pl.BlockSpec((1, depth, width), lambda j, i: (j, 0, 0)),
+            pl.BlockSpec((1, 1, width), lambda j, i: (j, 0, 0)),
         ]
-        + [pl.BlockSpec((block, PAIR), lambda i, j: (i, 0))] * 3,
-        out_specs=pl.BlockSpec((block, width), lambda i, j: (i, j)),
+        + [pl.BlockSpec((block, PAIR), lambda j, i: (i, 0))] * 3,
+        out_specs=pl.BlockSpec((block, width), lambda j, i: (i, j)),
         out_shape=jax.ShapeDtypeStruct((rows, 3 * width), jnp.bfloat16),
-        compiler_params=pltpu.CompilerParams(vmem_limit_bytes=48 * MIB),
+        compiler_params=pltpu.CompilerParams(vmem_limit_bytes=60 * MIB),
         cost_estimate=pl.CostEstimate(
             flops=6 * rows * depth * width, bytes_accessed=24 * MIB, transcendentals=0
         ),
@@ -158,7 +286,7 @@
 def hidden_rows(x, w, bias):
     rows, depth = x.shape
     width = w.shape[1]
-    block, columns = min(512, rows), min(512, width)
+    block, columns = min(1024, rows), min(1024, width)
     return pl.pallas_call(
         hidden_kernel,
         grid=(width // columns, rows // block),
@@ -169,7 +297,7 @@
         ],
         out_specs=[pl.BlockSpec((block, columns), lambda j, i: (i, j))] * 2,
         out_shape=[jax.ShapeDtypeStruct((rows, width), jnp.bfloat16)] * 2,
-        compiler_params=pltpu.CompilerParams(vmem_limit_bytes=48 * MIB),
+        compiler_params=pltpu.CompilerParams(vmem_limit_bytes=60 * MIB),
         cost_estimate=pl.CostEstimate(
             flops=2 * rows * depth * width, bytes_accessed=40 * MIB, transcendentals=rows * width
         ),
@@ -193,7 +321,7 @@
 def grad_hidden_rows(g, w, slope):
     rows, depth = g.shape
     width = w.shape[0]
-    block, columns = min(512, rows), min(512, width)
+    block, columns = min(1024, rows), min(1024, width)
     return pl.pallas_call(
         grad_hidden_kernel,
         grid=(width // columns, rows // block),
@@ -210,7 +338,7 @@
             jax.ShapeDtypeStruct((rows, width), jnp.bfloat16),
             jax.ShapeDtypeStruct((1, width), jnp.float32),
         ],
-        compiler_params=pltpu.CompilerParams(vmem_limit_bytes=48 * MIB),
+        compiler_params=pltpu.CompilerParams(vmem_limit_bytes=60 * MIB),
         cost_estimate=pl.CostEstimate(
             flops=2 * rows * depth * width, bytes_accessed=40 * MIB, transcendentals=0
         ),
@@ -317,28 +445,35 @@
             sums_ref[slot] = jnp.sum(low.astype(jnp.float32), axis=0, keepdims=True)
 
 
-def attention(joined, grad_mixed, lanes):
+def attention(joined, grad_mixed, lanes, first, last, earlier=None):
     rows, width = grad_mixed.shape
-    block = 256
+    block = min(256, LENGTH)
     pairs, block_count = width // PAIR, LENGTH // block
-    row_block = pl.BlockSpec((block, PAIR), lambda p, i: (i, p))
+    row_block = pl.BlockSpec((block, PAIR), lambda p, i: (i, first + p))
     table = pl.BlockSpec((LENGTH, PAIR), lambda p, i: (0, 0))
+    kept = () if earlier is None else tuple(earlier)
+    kernel = functools.partial(attention_kernel, block=block, block_count=block_count)
+
+    def body(*refs):
+        kernel(*refs[:7], *refs[7 + len(kept) :])
+
     return pl.pallas_call(
-        functools.partial(attention_kernel, block=block, block_count=block_count),
-        grid=(pairs, block_count),
+        body,
+        grid=(last - first, block_count),
         in_specs=[
             row_block,
-            pl.BlockSpec((LENGTH, PAIR), lambda p, i: (0, pairs + p)),
-            pl.BlockSpec((LENGTH, PAIR), lambda p, i: (0, 2 * pairs + p)),
+            pl.BlockSpec((LENGTH, PAIR), lambda p, i: (0, pairs + first + p)),
+            pl.BlockSpec((LENGTH, PAIR), lambda p, i: (0, 2 * pairs + first + p)),
             row_block,
             table,
             table,
             table,
-        ],
+        ]
+        + [pl.BlockSpec(memory_space=pl.ANY)] * len(kept),
         out_specs=[
             row_block,
-            pl.BlockSpec((3, LENGTH, PAIR), lambda p, i: (0, 0, p)),
-            pl.BlockSpec((3, 1, PAIR), lambda p, i: (0, 0, p)),
+            pl.BlockSpec((3, LENGTH, PAIR), lambda p, i: (0, 0, first + p)),
+            pl.BlockSpec((3, 1, PAIR), lambda p, i: (0, 0, first + p)),
         ],
         out_shape=[
             jax.ShapeDtypeStruct((rows, width), jnp.bfloat16),
@@ -352,11 +487,134 @@
             pltpu.VMEM((LENGTH, PAIR), jnp.float32),
             pltpu.VMEM((LENGTH, PAIR), jnp.float32),
         ],
-        compiler_params=pltpu.CompilerParams(vmem_limit_bytes=56 * MIB),
+        input_output_aliases={7 + i: i for i in range(len(kept))},
+        compiler_params=pltpu.CompilerParams(vmem_limit_bytes=60 * MIB),
         cost_estimate=pl.CostEstimate(
-            flops=100 * rows * rows * width, bytes_accessed=16 * MIB, transcendentals=0
+            flops=60000 * MIB * (last - first) // 4 * 2, bytes_accessed=16 * MIB, transcendentals=0
         ),
-    )(joined, joined, joined, grad_mixed, *lanes)
+    )(joined, joined, joined, grad_mixed, *lanes, *kept)
+
+
+def norm_kernel(starts_ref, gain_ref, shift_ref, *refs):
+    count = (len(refs) - 5) // 3
+    pieces = refs[:count]
+    raw, normed, mean_ref, root_ref = refs[count : count + 4]
+    buffers = refs[count + 4 : 2 * count + 4]
+    results = refs[2 * count + 4 : 3 * count + 4]
+    sems = refs[-1]
+    for slot in range(count):
+        pltpu.make_async_copy(pieces[slot], buffers[slot], sems.at[0, slot]).start()
+    writes = []
+    for slot in range(count):
+        buffer, result = buffers[slot], results[slot]
+        size = buffer.shape[0]
+        where = pl.ds(pl.multiple_of(starts_ref[slot], size), size)
+        pltpu.make_async_copy(pieces[slot], buffer, sems.at[0, slot]).wait()
+        write = pltpu.make_async_copy(buffer, raw.at[where, :], sems.at[1, slot])
+        write.start()
+        writes.append(write)
+        chunk = min(128, size)
+
+        @pl.loop(0, size // chunk)
+        def _(step, buffer=buffer, result=result, slot=slot):
+            here = pl.ds(pl.multiple_of(step * chunk, chunk), chunk)
+            rows = buffer[here, :].astype(jnp.float32)
+            mean = jnp.mean(rows, axis=-1, keepdims=True)
+            centred = rows - mean
+            variance = jnp.mean(centred * centred, axis=-1, keepdims=True)
+            root = lax.rsqrt(variance + epsilon)
+            out = centred * root * gain_ref[...] + shift_ref[...]
+            result[here, :] = out.astype(result.dtype)
+            there = pl.ds(pl.multiple_of(starts_ref[slot] + step * chunk, chunk), chunk)
+            mean_ref[there, :] = mean
+            root_ref[there, :] = root
+
+        write = pltpu.make_async_copy(result, normed.at[where, :], sems.at[2, slot])
+        write.start()
+        writes.append(write)
+    for write in writes:
+        write.wait()
+
+
+def norm_rows(pieces, gain, shift):
+    depth = gain.shape[0]
+    total = sum(piece.shape[0] for _, piece in pieces)
+    count = len(pieces)
+    low = jnp.bfloat16
+    starts = jnp.stack([jnp.asarray(start, jnp.int32) for start, _ in pieces])
+    any_space = pl.BlockSpec(memory_space=pl.ANY)
+    vmem = pl.BlockSpec(memory_space=pltpu.VMEM)
+    stage = [pltpu.VMEM(piece.shape, low) for _, piece in pieces]
+    return pl.pallas_call(
+        norm_kernel,
+        in_specs=[pl.BlockSpec(memory_space=pltpu.SMEM), vmem, vmem] + [any_space] * count,
+        out_specs=[any_space, any_space, vmem, vmem],
+        out_shape=[
+            jax.ShapeDtypeStruct((total, depth), low),
+            jax.ShapeDtypeStruct((total, depth), low),
+            jax.ShapeDtypeStruct((total, 1), jnp.float32),
+            jax.ShapeDtypeStruct((total, 1), jnp.float32),
+        ],
+        scratch_shapes=stage + stage + [pltpu.SemaphoreType.DMA((3, count))],
+        compiler_params=pltpu.CompilerParams(vmem_limit_bytes=60 * MIB),
+        cost_estimate=pl.CostEstimate(flops=0, bytes_accessed=24 * MIB, transcendentals=0),
+    )(starts, gain.reshape(1, depth), shift.reshape(1, depth), *[piece for _, piece in pieces])
+
+
+def grad_normed_kernel(
+    joined_ref, qkv_ref, hidden_ref, up_ref, x_ref, mean_ref, root_ref, out_ref, gain_ref, shift_ref
+):
+    total = lax.dot_general(
+        hidden_ref[...], up_ref[...], ROWS_BY_ROWS, preferred_element_type=jnp.float32
+    )
+    for slot in range(3):
+        total += lax.dot_general(
+            joined_ref[slot], qkv_ref[slot], ROWS_BY_ROWS, preferred_element_type=jnp.float32
+        )
+    out_ref[...] = total.astype(out_ref.dtype)
+
+    @pl.when(pl.program_id(1) == 0)
+    def _():
+        gain_ref[...] = jnp.zeros_like(gain_ref)
+        shift_ref[...] = jnp.zeros_like(shift_ref)
+
+    hat = (x_ref[...].astype(jnp.float32) - mean_ref[...]) * root_ref[...]
+    gain_ref[...] += jnp.sum(total * hat, axis=0, keepdims=True)
+    shift_ref[...] += jnp.sum(total, axis=0, keepdims=True)
+
+
+def grad_normed_rows(grad_joined, full_qkv, grad_hidden, full_up, x, mean, root, first, last):
+    rows, hidden = grad_hidden.shape
+    width = grad_joined.shape[2]
+    block, columns = min(1024, rows), min(512, last - first)
+    skip = first // columns
+    thin = pl.BlockSpec((block, 1), lambda j, i: (i, 0))
+    line = pl.BlockSpec((1, columns), lambda j, i: (0, j))
+    return pl.pallas_call(
+        grad_normed_kernel,
+        grid=((last - first) // columns, rows // block),
+        in_specs=[
+            pl.BlockSpec((3, block, width), lambda j, i: (0, i, 0)),
+            pl.BlockSpec((3, columns, width), lambda j, i: (0, skip + j, 0)),
+            pl.BlockSpec((block, hidden), lambda j, i: (i, 0)),
+            pl.BlockSpec((columns, hidden), lambda j, i: (skip + j, 0)),
+            pl.BlockSpec((block, columns), lambda j, i: (i, skip + j)),
+            thin,
+            thin,
+        ],
+        out_specs=[pl.BlockSpec((block, columns), lambda j, i: (i, j)), line, line],
+        out_shape=[
+            jax.ShapeDtypeStruct((rows, last - first), jnp.bfloat16),
+            jax.ShapeDtypeStruct((1, last - first), jnp.float32),
+            jax.ShapeDtypeStruct((1, last - first), jnp.float32),
+        ],
+        compiler_params=pltpu.CompilerParams(vmem_limit_bytes=60 * MIB),
+        cost_estimate=pl.CostEstimate(
+            flops=2 * rows * (hidden + 3 * width) * (last - first),
+            bytes_accessed=50 * MIB,
+            transcendentals=0,
+        ),
+    )(grad_joined, full_qkv, grad_hidden, full_up, x, mean, root)
 
 
 def on_device(
@@ -372,89 +630,135 @@
     bias_out,
     cotangent,
 ):
-    f32 = jnp.float32
+    f32, low = jnp.float32, jnp.bfloat16
+    depth = tokens.shape[1]
+    local_rows = tokens.shape[0]
+    tensor_index = lax.axis_index("tensor")
+
+    full_up = lax.all_gather(weight_up, "dp", axis=0, tiled=True)
+    token_parts = gather_start(tokens)
+    lanes = lane_tables(LENGTH)
+    out_part = jnp.sum(cotangent, axis=0, dtype=f32)
+    lanes, out_part, token_parts = after((lanes, out_part, token_parts))
+    full_qkv = lax.all_gather(
+        after(jnp.transpose(weight_qkv, (1, 0, 2)), token_parts), "dp", axis=1, tiled=True
+    )
+    token_parts = gather_pass(token_parts)
+    grad_parts = gather_start(after(cotangent, token_parts[:3]))
+    all_tokens, gathered, mean, root = norm_rows(
+        gathered_pieces(token_parts), norm_gain, norm_shift
+    )
+    full_dense = lax.all_gather(after(weight_dense, gathered), "dp", axis=1, tiled=True)
+
+    active, slope = hidden_rows(gathered, full_up, bias_up)
+    grad_parts, active = after((grad_parts, active))
+    full_down = lax.all_gather(after(weight_down, grad_parts), "dp", axis=1, tiled=True)
+    grad_parts = gather_pass(grad_parts)
+    joined = joined_rows(after(gathered, active, grad_parts[:3]), full_qkv, bias_qkv, lanes)
+    grad_parts, joined = after((grad_parts, joined))
+    grad_rows = gather_end(grad_parts)
+    dense_parts = gather_start(after(full_dense, joined))
+    grad_down = jnp.einsum("tf,td->fd", active, grad_rows, preferred_element_type=f32).astype(low)
+    grad_mixed = jnp.einsum(
+        "td,kd->tk", after(grad_rows, grad_down), full_dense, preferred_element_type=f32
+    ).astype(low)
+    grad_down_sum = lax.psum_scatter(grad_down, "dp", scatter_dimension=1, tiled=True)
+
+    pairs = grad_mixed.shape[1] // PAIR
+    middle = pairs // 2
+    part = attention(joined, grad_mixed, lanes, 0, middle)
+    dense_parts, part = after((dense_parts, part))
+    dense_parts = gather_pass(dense_parts)
+
+    feed = jnp.dot(after(active, part), full_down, preferred_element_type=f32).astype(low)
+    feed, dense_parts = after((feed, dense_parts))
+    feed_parts = scatter_send(scatter_cut(feed))
+    grad_hidden, bias_up_part = grad_hidden_rows(after(grad_rows, feed), full_down, slope)
+    dense_rows = gather_end(dense_parts)
+    grad_up = jnp.einsum(
+        "td,tf->df", after(gathered, dense_rows), grad_hidden, preferred_element_type=f32
+    ).astype(low)
+    grad_up, feed_parts = after((grad_up, feed_parts))
+    grad_up_sum = lax.psum_scatter(
+        after(grad_up, grad_down_sum), "dp", scatter_dimension=0, tiled=True
+    )
+    feed_parts = scatter_pass(scatter_fold(feed_parts))
+    mixed, grad_joined, bias_qkv_part = attention(
+        after(joined, grad_up), grad_mixed, lanes, middle, pairs, part
+    )
+    mixed, grad_joined, feed_parts = after((mixed, grad_joined, feed_parts))
+
+    mixed_parts = exchange_start(mixed)
+    grad_qkv = jnp.einsum("td,jtc->jdc", gathered, grad_joined, preferred_element_type=f32)
+    grad_qkv, mixed_parts = after((grad_qkv.astype(low), mixed_parts))
+    grad_qkv_sum = lax.psum_scatter(
+        after(grad_qkv, grad_up_sum), "dp", scatter_dimension=1, tiled=True
+    )
+    half = depth // 2
+    sources = full_qkv, grad_hidden, full_up, all_tokens, mean, root
+    left = grad_normed_rows(after(grad_joined, grad_qkv), *sources, 0, half)
+    left_cuts = after(scatter_cut(left[0]), left)
+    left_parts = scatter_send(left_cuts)
+    right = grad_normed_rows(after(grad_joined, left_cuts), *sources, half, depth)
+    sums = jnp.stack(
+        [
+            jnp.concatenate([left[1][0], right[1][0]]),
+            jnp.concatenate([left[2][0], right[2][0]]),
+            out_part,
+        ]
+    )
+    left_parts, sums, right = after((left_parts, sums, right))
+    left_parts = scatter_fold(left_parts)
+    right_cuts = scatter_cut(right[0])
+    left_parts, right_cuts, sums, mixed = after((left_parts, right_cuts, sums, mixed))
+    over_group = exchange_sum(sums, "tensor")
+    left_parts = scatter_pass(left_parts)
+    right_parts = scatter_send(right_cuts)
+    grad_dense = jnp.einsum("tk,td->kd", mixed, grad_rows, preferred_element_type=f32).astype(low)
+    grad_dense_sum = lax.psum_scatter(
+        after(grad_dense, grad_qkv_sum), "dp", scatter_dimension=1, tiled=True
+    )
+    over_group, mixed_parts = after((over_group, mixed_parts), grad_dense)
+    bias_size = bias_qkv.size
+    over_dp = exchange_sum(
+        jnp.concatenate(
+            [over_group.reshape(-1), bias_qkv_part.reshape(-1), bias_up_part.reshape(-1)]
+        ).reshape(-1, 128),
+        "dp",
+    ).reshape(-1)
+    attended = jnp.dot(exchange_end(mixed_parts), dense_rows, preferred_element_type=f32)
     token_rows = tokens.astype(f32)
-    mean_row = jnp.mean(token_rows, axis=-1, keepdims=True)
-    centred = token_rows - mean_row
-    variance = jnp.mean(centred * centred, axis=-1, keepdims=True)
-    root = lax.rsqrt(variance + epsilon)
-    normed_low = (centred * root * norm_gain + norm_shift).astype(jnp.bfloat16)
-
-    full_qkv = lax.all_gather(jnp.transpose(weight_qkv, (1, 0, 2)), "dp", axis=1, tiled=True)
-    full_up = lax.all_gather(weight_up, "dp", axis=0, tiled=True)
-    full_dense = lax.all_gather(weight_dense, "dp", axis=1, tiled=True)
-    full_down = lax.all_gather(weight_down, "dp", axis=1, tiled=True)
-    normed_parts = group_gather(normed_low)
-    grad_parts = group_gather(after(cotangent, normed_parts[-1]))
-    gathered = place_group(normed_parts)
-    grad_rows = place_group(grad_parts)
-    group_rows = gathered.shape[0]
-    lanes = lane_tables(LENGTH)
-
-    joined = joined_rows(gathered, full_qkv, bias_qkv, lanes)
-    active, slope = hidden_rows(gathered, full_up, bias_up)
-    grad_mixed = jnp.einsum(
-        "td,kd->tk", grad_rows, full_dense, preferred_element_type=f32
-    ).astype(jnp.bfloat16)
-    grad_down = jnp.einsum("tf,td->fd", active, grad_rows, preferred_element_type=f32)
-    grad_down = lax.psum_scatter(
-        grad_down.astype(jnp.bfloat16), "dp", scatter_dimension=1, tiled=True
-    )
-    mixed, grad_joined, bias_qkv_part = attention(joined, grad_mixed, lanes)
-    branch = (
-        jnp.dot(mixed, full_dense, preferred_element_type=f32)
-        + jnp.dot(active, full_down, preferred_element_type=f32)
-    ).astype(jnp.bfloat16)
-    branch_sum = group_scatter(branch)
-    block_out = (token_rows + branch_sum + bias_out).astype(jnp.bfloat16)
-
-    grad_hidden, bias_up_part = grad_hidden_rows(grad_rows, full_down, slope)
-    grad_up = jnp.einsum("td,tf->df", gathered, grad_hidden, preferred_element_type=f32)
-    grad_up = lax.psum_scatter(
-        grad_up.astype(jnp.bfloat16), "dp", scatter_dimension=0, tiled=True
-    )
-    grad_qkv = jnp.einsum("td,jtc->jdc", gathered, grad_joined, preferred_element_type=f32)
-    grad_qkv = lax.psum_scatter(
-        grad_qkv.astype(jnp.bfloat16), "dp", scatter_dimension=1, tiled=True
-    )
-    grad_dense = jnp.einsum("tk,td->kd", mixed, grad_rows, preferred_element_type=f32)
-    grad_dense = lax.psum_scatter(
-        grad_dense.astype(jnp.bfloat16), "dp", scatter_dimension=1, tiled=True
-    )
-    grad_normed = (
-        jnp.einsum("jtc,jdc->td", grad_joined, full_qkv, preferred_element_type=f32)
-        + jnp.einsum("tf,df->td", grad_hidden, full_up, preferred_element_type=f32)
-    ).astype(jnp.bfloat16)
-    grad_normed = group_scatter(grad_normed)
-
-    hat = centred * root
+    block_out = (token_rows + attended + scatter_end(feed_parts) + bias_out).astype(low)
+    done = block_out, grad_up_sum.astype(f32), grad_down_sum.astype(f32), over_dp
+    right_parts, left_parts, done = after((right_parts, left_parts, done))
+    block_out, grad_up_sum, grad_down_sum, over_dp = done
+    right_parts = scatter_pass(scatter_fold(right_parts))
+    grad_gain, grad_shift, grad_bias_out = over_dp[: 3 * depth].reshape(3, depth)
+    grad_bias_qkv = over_dp[3 * depth : 3 * depth + bias_size].reshape(bias_qkv.shape)
+    grad_bias_up = over_dp[3 * depth + bias_size :]
+
+    grad_normed = jnp.concatenate([scatter_end(left_parts), scatter_end(right_parts)], axis=1)
+    own_mean = lax.dynamic_slice_in_dim(mean, tensor_index * local_rows, local_rows, 0)
+    own_root = lax.dynamic_slice_in_dim(root, tensor_index * local_rows, local_rows, 0)
+    hat = (token_rows - own_mean) * own_root
     scaled = grad_normed * norm_gain
-    grad_input = root * (
+    grad_input = own_root * (
         scaled
         - jnp.mean(scaled, axis=-1, keepdims=True)
         - hat * jnp.mean(scaled * hat, axis=-1, keepdims=True)
     )
-    grad_tokens = (cotangent.astype(f32) + grad_input).astype(jnp.bfloat16)
-    grad_bias_qkv, grad_bias_up = lax.psum(
-        (bias_qkv_part.reshape(bias_qkv.shape), bias_up_part.reshape(bias_up.shape)), "dp"
-    )
-    gain_part = jnp.sum(grad_normed * hat, axis=0)
-    shift_part = jnp.sum(grad_normed, axis=0)
-    out_part = jnp.sum(cotangent, axis=0, dtype=f32)
-    grad_gain, grad_shift, grad_bias_out = lax.psum(
-        (gain_part, shift_part, out_part), ("dp", "tensor")
-    )
+    grad_tokens = (cotangent.astype(f32) + grad_input).astype(low)
     return (
         block_out,
         grad_tokens,
         grad_gain,
         grad_shift,
-        jnp.transpose(grad_qkv, (1, 0, 2)).astype(f32),
+        jnp.transpose(grad_qkv_sum, (1, 0, 2)).astype(f32),
         grad_bias_qkv,
-        grad_dense.astype(f32),
-        grad_up.astype(f32),
+        grad_dense_sum.astype(f32),
+        grad_up_sum,
         grad_bias_up,
-        grad_down.astype(f32),
+        grad_down_sum,
         grad_bias_out,
     )
 

time: 844 us -> 688 us (0.82)
  waiting for transfers between devices: 224 us -> 92 us
  Pallas kernels: 235 us -> 303 us
  blocking collectives: 64.7 us -> 0 us
  matrix products: 167 us -> 121 us
  starting transfers between devices: 22.2 us -> 48.6 us
    ppermute x16 -> x43, waiting for transfers between devices: 222 us -> 84 us  [swap(): return lax.ppermute(value, axis, [(i, i ^ bit) for i in range(count)])]
    pallas_call x2 -> x9, Pallas kernels: 168 us -> 246 us  [the longest x2 143 us: attention(): pl.pallas_call(body, grid=(last - first, block_count), in_specs=[row_bloc...]
    psum x2 -> x0, blocking collectives: 64.7 us -> none  [the longest x1 37.9 us: on_device(): lax.psum((gain_part, shift_part, out_part), ('dp', 'tensor'))]
    dot_general x6 -> x4, matrix products: 114 us -> 68.9 us  [the longest x1 23.9 us: on_device(): jnp.einsum('td,tf->df', after(gathered, dense_rows), grad_hidden, preferr...]
    ppermute x16 -> x43, starting transfers between devices: 21.6 us -> 48.1 us  [swap(): return lax.ppermute(value, axis, [(i, i ^ bit) for i in range(count)])]
    dynamic_update_slice x9 -> x0, local copies, waits for them, and re-layouts: 21.3 us -> none  [put(): return lax.dynamic_update_slice(full, piece, start)]
    dynamic_slice x2 -> x3, local copies, waits for them, and re-layouts: 5.5 us -> 15 us  [take(): return lax.dynamic_slice_in_dim(partial, (me ^ bit) * rows + shift, half, 0)]
    slice x4 -> x8, local copies, waits for them, and re-layouts: 3.84 us -> 13 us  [the longest x3 6.7 us: gather_pass(): one[:half]]
  transfers between devices with their start and end apart: 24 -> 51, of which waited for: 10 -> 14; matrix products, arithmetic and copies ran while one was open for 32% -> 32% of each run, Pallas kernels for 28% -> 45%
where the time goes in v2:
time: 688 us; the launch traced here: 679 us
  Pallas kernels  303 us (44%)
  matrix products  121 us (18%)
  waiting for transfers between devices  92 us (13%)
  local copies, waits for them, and re-layouts  54.6 us (8%)
  starting transfers between devices  48.6 us (7%)
  other arithmetic  44.9 us (7%)
  between operations  15 us (2%)
    pallas_call x2, Pallas kernels, attention(): pl.pallas_call(body, grid=(last - first, block_count), in_specs=[row_bloc...  143 us
    ppermute x43, waiting for transfers between devices, swap(): return lax.ppermute(value, axis, [(i, i ^ bit) for i in range(count)])  84 us
    pallas_call x2, Pallas kernels, grad_normed_rows(): pl.pallas_call(grad_normed_kernel, grid=((last - first) // columns, rows...  49.2 us
    ppermute x43, starting transfers between devices, swap(): return lax.ppermute(value, axis, [(i, i ^ bit) for i in range(count)])  48.1 us
    pallas_call x1, Pallas kernels, hidden_rows(): pl.pallas_call(hidden_kernel, grid=(width // columns, rows // block), in_...  32.8 us
    pallas_call x1, Pallas kernels, grad_hidden_rows(): pl.pallas_call(grad_hidden_kernel, grid=(width // columns, rows // block)...  24.6 us
    pallas_call x1, Pallas kernels, joined_rows(): pl.pallas_call(joined_kernel, grid=(3, rows // block), in_specs=[pl.Block...  24.2 us
    dot_general x1, matrix products, on_device(): jnp.einsum('td,tf->df', after(gathered, dense_rows), grad_hidden, preferr...  23.9 us
  transfers between devices with their start and end apart: 51, of which 14 were waited for; matrix products, arithmetic and copies ran while one was open for 32% of the time, Pallas kernels for 45%

profile of v2, /device:TPU:0, one launch (start us, length us, event | category | flops | bytes accessed | tf_op | source)
XLA Modules:
  0.0 679.2 jit_solution(16999809225434495010)
XLA Ops:
  12.5 5.5 multiply_sine_fusion
  18.2 4.4 concatenate.32.below_ref.refs_6_
  22.6 4.4 concatenate.31.above_ref.refs_5_
  28.1 4.4 concatenate.30.cos_ref.refs_4_
  33.5 23.4 %collective-permute-done.1.refs_2_ = bf16[512,2048]{1,0:T(8,128)(2,1)} collective-permute-done((bf16[512,2048]{1,0:T(8,128)(2,1)}, bf16[512,2048]{1,0:T(8,128)(2,1)}, u32[]{:S(2)}, u32[]{:S(2)}) %collective-permute-start.1) | collective-permute-done | bytes 2097184 | tf_op jit(solution)/shard_map/ppermute | solution.py:28
  65.7 21.3 %collective-permute-done.5.refs_4_ = bf16[256,2048]{1,0:T(8,128)(2,1)S(1)} collective-permute-done((bf16[256,2048]{1,0:T(8,128)(2,1)}, bf16[256,2048]{1,0:T(8,128)(2,1)S(1)}, u32[]{:S(2)}, u32[]{:S(2)}) %collective-permute-start.5) | collective-permute-done | bytes 1048608 | tf_op jit(solution)/shard_map/ppermute | solution.py:28
  88.3 10.9 %shard_map.194 = (bf16[2048,2048]{1,0:T(8,128)(2,1)}, bf16[2048,2048]{1,0:T(8,128)(2,1)}, f32[2048,1]{1,0:T(8,128)}, f32[2048,1]{1,0:T(8,128)}) custom-call(s32[5]{0:T(128)} %stack.54.starts_ref, f32[1,2048]{1,0:T(1,128)} %bitcast.46, f32[1,2048]{1,0:T(1,128)} %bitcast.52, bf16[512,2048]{1,0:T(8,128)(2,1)} %refs_0_, ...), custom_call_target="tpu_custom_call" | custom-call | bytes 25165824 | tf_op jit(solution)/shard_map/pallas_call | solution.py:548
  101.1 32.8 %shard_map.195 = (bf16[2048,2048]{1,0:T(8,128)(2,1)}, bf16[2048,2048]{1,0:T(8,128)(2,1)}) custom-call(bf16[2048,2048]{1,0:T(8,128)(2,1)} %get-tuple-element.195.x_ref, bf16[2048,2048]{1,0:T(8,128)(2,1)} %all-gather.5.cloned.1.call-done.w_ref.up_ref, f32[1,2048]{1,0:T(1,128)} %bitcast.57), custom_call_target="tpu_custom_call" | custom-call | flops 17179869184 | bytes 41943040 | tf_op jit(solution)/shard_map/pallas_call | solution.py:290
  133.9 10.5 %collective-permute-done.3.refs_2_ = bf16[512,2048]{1,0:T(8,128)(2,1)} collective-permute-done((bf16[512,2048]{1,0:T(8,128)(2,1)S(1)}, bf16[512,2048]{1,0:T(8,128)(2,1)}, u32[]{:S(2)}, u32[]{:S(2)}) %collective-permute-start.3) | collective-permute-done | bytes 2097184 | tf_op jit(solution)/shard_map/ppermute | solution.py:28
  152.1 7.1 %all-gather.7.cloned.1.call-done.w_ref.qkv_ref = bf16[3,2048,512]{2,1,0:T(8,128)(2,1)} async-done(((bf16[3,256,512]{2,1,0:T(8,128)(2,1)}), bf16[3,2048,512]{2,1,0:T(8,128)(2,1)}) %all-gather.7.cloned.1.call-update) | async-done | bytes 6291472 | tf_op jit(solution)/shard_map/all_gather | solution.py:643
  159.3 24.2 %shard_map.196.refs_0_.refs_1_.refs_2_ = bf16[2048,1536]{1,0:T(8,128)(2,1)} custom-call(bf16[2048,2048]{1,0:T(8,128)(2,1)} %get-tuple-element.195.x_ref, bf16[3,2048,512]{2,1,0:T(8,128)(2,1)} %all-gather.7.cloned.1.call-done.w_ref.qkv_ref, f32[3,1,512]{2,1,0:T(1,128)} %reshape.95.bias_ref, f32[2048,128]{1,0:T(8,128)} %concatenate.30.cos_ref.refs_4_, ...), custom_call_target="tpu_custom_call" | custom-call | flops 12884901888 | bytes 25165824 | tf_op jit(solution)/shard_map/pallas_call | solution.py:255
  185.4 7.3 %shard_map.197.g_ref = bf16[2048,2048]{1,0:T(8,128)(2,1)} custom-call(s32[5]{0:T(128)} %stack.54.starts_ref, bf16[512,2048]{1,0:T(8,128)(2,1)} %refs_0_.1, bf16[512,2048]{1,0:T(8,128)(2,1)} %collective-permute-done.2.refs_1_, bf16[512,2048]{1,0:T(8,128)(2,1)} %collective-permute-done.3.refs_2_, bf16[256,2048]{1,0:T(8,128)(2,1)} %copy-done.15, ...), custom_call_target="tpu_custom_call" | custom-call | bytes 16777216 | tf_op jit(solution)/shard_map/pallas_call | solution.py:56
  192.7 23.7 %convolution_convert_fusion.2 = bf16[2048,2048]{1,0:T(8,128)(2,1)} fusion(bf16[2048,2048]{1,0:T(8,128)(2,1)} %get-tuple-element.185, bf16[2048,2048]{1,0:T(8,128)(2,1)} %shard_map.197.g_ref), kind=kOutput, calls=%fused_computation.4 | convolution fusion | flops 17184063488 | bytes 25165824 | tf_op jit(solution)/shard_map/tf,td->fd/dot_general | solution.py:661
  219.6 10.1 %convolution_convert_fusion.4.refs_3_ = bf16[2048,512]{1,0:T(8,128)(2,1)} fusion(bf16[2048,2048]{1,0:T(8,128)(2,1)} %shard_map.197.g_ref, bf16[512,2048]{1,0:T(8,128)(2,1)} %all-gather.9.cloned.1.call-done.refs_0_), kind=kOutput, calls=%fused_computation.22 | convolution fusion | flops 4296015872 | bytes 12582912 | tf_op jit(solution)/shard_map/td,kd->tk/dot_general | solution.py:662
  229.8 80.0 %shard_map.198 = (bf16[2048,512]{1,0:T(8,128)(2,1)}, bf16[3,2048,512]{2,1,0:T(8,128)(2,1)}, f32[3,1,512]{2,1,0:T(1,128)}) custom-call(bf16[2048,1536]{1,0:T(8,128)(2,1)} %shard_map.196.refs_0_.refs_1_.refs_2_, bf16[2048,1536]{1,0:T(8,128)(2,1)} %shard_map.196.refs_0_.refs_1_.refs_2_, bf16[2048,1536]{1,0:T(8,128)(2,1)} %shard_map.196.refs_0_.refs_1_.refs_2_, ...), custom_call_target="tpu_custom_call" | custom-call | flops 62914560000 | bytes 16777216 | tf_op jit(solution)/shard_map/pallas_call | solution.py:460
  315.1 23.7 %convolution_convert_fusion.1 = bf16[2048,2048]{1,0:T(8,128)(2,1)} fusion(bf16[2048,2048]{1,0:T(8,128)(2,1)} %get-tuple-element.185, bf16[2048,2048]{1,0:T(8,128)(2,1)} %all-gather.11.cloned.1.call-done.w_ref), kind=kOutput, calls=%fused_computation.3 | convolution fusion | flops 17184063488 | bytes 25165824 | tf_op jit(solution)/shard_map/dot_general | solution.py:673
  339.9 7.4 %shard_map.199 = bf16[2048,2048]{1,0:T(8,128)(2,1)} custom-call(s32[5]{0:T(128)} %stack.54.starts_ref, bf16[512,2048]{1,0:T(8,128)(2,1)} %all-gather.9.cloned.1.call-done.refs_0_, bf16[512,2048]{1,0:T(8,128)(2,1)} %collective-permute-done.8.refs_1_, bf16[512,2048]{1,0:T(8,128)(2,1)} %copy-done.4, bf16[256,2048]{1,0:T(8,128)(2,1)} %collective-permute-done.10.refs_3_, ...), custom_call_target="tpu_custom_call" | custom-call | bytes 16777216 | tf_op jit(solution)/shard_map/pallas_call | solution.py:56
  347.3 6.7 constant_dynamic-slice_fusion.20
  358.1 24.6 %shard_map.200 = (bf16[2048,2048]{1,0:T(8,128)(2,1)}, f32[1,2048]{1,0:T(1,128)}) custom-call(bf16[2048,2048]{1,0:T(8,128)(2,1)} %shard_map.197.g_ref, bf16[2048,2048]{1,0:T(8,128)(2,1)} %all-gather.11.cloned.1.call-done.w_ref, bf16[2048,2048]{1,0:T(8,128)(2,1)} %get-tuple-element.198.slope_ref), custom_call_target="tpu_custom_call" | custom-call | flops 17179869184 | bytes 41943040 | tf_op jit(solution)/shard_map/pallas_call | solution.py:325
  382.7 23.9 %convolution_convert_fusion = bf16[2048,2048]{1,0:T(8,128)(2,1)} fusion(bf16[2048,2048]{1,0:T(8,128)(2,1)} %get-tuple-element.195.x_ref, bf16[2048,2048]{1,0:T(8,128)(2,1)} %get-tuple-element.199.hidden_ref), kind=kOutput, calls=%fused_computation.2 | convolution fusion | flops 17184063488 | bytes 25165824 | tf_op jit(solution)/shard_map/td,tf->df/dot_general | solution.py:678
  414.8 63.4 %shard_map.201 = (bf16[2048,512]{1,0:T(8,128)(2,1)}, bf16[3,2048,512]{2,1,0:T(8,128)(2,1)}, f32[3,1,512]{2,1,0:T(1,128)}) custom-call(bf16[2048,1536]{1,0:T(8,128)(2,1)} %shard_map.196.refs_0_.refs_1_.refs_2_, bf16[2048,1536]{1,0:T(8,128)(2,1)} %shard_map.196.refs_0_.refs_1_.refs_2_, ...), custom_call_target="tpu_custom_call", output_to_operand_aliasing={{0}: (7, {}), {1}: (8, {}), {2}: (9, {})} | custom-call | flops 62914560000 | bytes 16777216 | tf_op jit(solution)/shard_map/pallas_call | solution.py:460
  484.8 19.1 %convert_bitcast_fusion = bf16[3,2048,512]{1,2,0:T(8,128)(2,1)} fusion(bf16[3,2048,512]{2,1,0:T(8,128)(2,1)} %get-tuple-element.230.joined_ref, bf16[2048,2048]{1,0:T(8,128)(2,1)} %get-tuple-element.195.x_ref), kind=kOutput, calls=%fused_computation.5 | convolution fusion | flops 12888047616 | bytes 20971520 | tf_op jit(solution)/shard_map/td,jtc->jdc/dot_general | solution.py:692
  505.0 24.8 %shard_map.202 = (bf16[2048,1024]{1,0:T(8,128)(2,1)}, f32[1,1024]{1,0:T(1,128)}, f32[1,1024]{1,0:T(1,128)}) custom-call(bf16[3,2048,512]{2,1,0:T(8,128)(2,1)} %get-tuple-element.230.joined_ref, bf16[3,2048,512]{2,1,0:T(8,128)(2,1)} %all-gather.7.cloned.1.call-done.w_ref.qkv_ref, bf16[2048,2048]{1,0:T(8,128)(2,1)} %get-tuple-element.199.hidden_ref, ...), custom_call_target="tpu_custom_call" | custom-call | flops 15032385536 | bytes 52428800 | tf_op jit(solution)/shard_map/pallas_call | solution.py:593
  538.0 24.3 %shard_map.203 = (bf16[2048,1024]{1,0:T(8,128)(2,1)}, f32[1,1024]{1,0:T(1,128)}, f32[1,1024]{1,0:T(1,128)}) custom-call(bf16[3,2048,512]{2,1,0:T(8,128)(2,1)} %get-tuple-element.230.joined_ref, bf16[3,2048,512]{2,1,0:T(8,128)(2,1)} %all-gather.7.cloned.1.call-done.w_ref.qkv_ref, bf16[2048,2048]{1,0:T(8,128)(2,1)} %get-tuple-element.199.hidden_ref, ...), custom_call_target="tpu_custom_call" | custom-call | flops 15032385536 | bytes 52428800 | tf_op jit(solution)/shard_map/pallas_call | solution.py:593
  564.6 4.3 constant_dynamic-slice_fusion
  573.8 9.3 %convolution_convert_fusion.3 = bf16[512,2048]{1,0:T(8,128)(2,1)} fusion(bf16[2048,512]{1,0:T(8,128)(2,1)S(1)} %copy-done.7, bf16[2048,2048]{1,0:T(8,128)(2,1)} %shard_map.197.g_ref), kind=kOutput, calls=%fused_computation.21 | convolution fusion | flops 4296015872 | bytes 12582912 | tf_op jit(solution)/shard_map/tk,td->kd/dot_general | solution.py:717
  593.8 5.3 convert_add_fusion.2
  608.6 11.1 %fusion.7 = bf16[512,2048]{1,0:T(8,128)(2,1)} fusion(bf16[512,2048]{1,0:T(8,128)(2,1)S(1)} %copy-done.2, f32[256,2048]{1,0:T(8,128)} %get-tuple-element.371, f32[256,2048]{1,0:T(8,128)} %get-tuple-element.372, bf16[512,2048]{1,0:T(8,128)(2,1)} %shard_map.204, bf16[2048,2048]{1,0:T(8,128)(2,1)} %shard_map.199, f32[2048]{0:T(1024)S(1)} %copy-done.33), kind=kOutput, calls=%fused_computation.13 | convolution fusion | flops 4301258752 | bytes 18882560 | tf_op jit(solution)/shard_map/dot_general | solution.py:729
  622.8 7.5 %collective-permute-done.28 = bf16[256,1024]{1,0:T(8,128)(2,1)} collective-permute-done((bf16[256,1024]{1,0:T(8,128)(2,1)}, bf16[256,1024]{1,0:T(8,128)(2,1)}, u32[]{:S(2)}, u32[]{:S(2)}) %collective-permute-start.28) | collective-permute-done | bytes 524320 | tf_op jit(solution)/shard_map/ppermute | solution.py:28
  630.3 10.3 %collective-permute-done.29 = bf16[256,1024]{1,0:T(8,128)(2,1)} collective-permute-done((bf16[256,1024]{1,0:T(8,128)(2,1)}, bf16[256,1024]{1,0:T(8,128)(2,1)}, u32[]{:S(2)}, u32[]{:S(2)}) %collective-permute-start.29) | collective-permute-done | bytes 524320 | tf_op jit(solution)/shard_map/ppermute | solution.py:28
  651.6 4.3 collective-permute-done.42
  664.2 4.4 fusion.4
  (219 shorter events, 119.2 us)
Async XLA Ops:
  7.2 94.0 %all-gather.5.cloned.1.call-start = ((), (), s32[]{:S(2)}) async-start(), calls=%async_computation.4 | async-start | bytes 9437184 | tf_op jit(solution)/shard_map/all_gather | solution.py:638
  7.9 151.4 %all-gather.7.cloned.1.call-start = ((), (), s32[]{:S(2)}) async-start(), calls=%async_computation.5 | async-start | bytes 7077888 | tf_op jit(solution)/shard_map/all_gather | solution.py:643
  8.0 49.0 %collective-permute-start.1 = (bf16[512,2048]{1,0:T(8,128)(2,1)}, bf16[512,2048]{1,0:T(8,128)(2,1)}, u32[]{:S(2)}, u32[]{:S(2)}) collective-permute-start(bf16[512,2048]{1,0:T(8,128)(2,1)} %refs_0_), channel_id=1, source_target_pairs={{0,2},{1,3},{2,0},{3,1},{4,6},{5,7},{6,4},{7,5},{8,10},{9,11},{10,... | collective-permute-start | bytes 6291464 | tf_op jit(solution)/shard_map/ppermute | solution.py:28
  11.0 47.4 %collective-permute-start = (bf16[512,2048]{1,0:T(8,128)(2,1)}, bf16[512,2048]{1,0:T(8,128)(2,1)}, u32[]{:S(2)}, u32[]{:S(2)}) collective-permute-start(bf16[512,2048]{1,0:T(8,128)(2,1)} %refs_0_), channel_id=1, source_target_pairs={{0,1},{1,0},{2,3},{3,2},{4,5},{5,4},{6,7},{7,6},{8,9},{9,8},{10,11... | collective-permute-start | bytes 6291464 | tf_op jit(solution)/shard_map/ppermute | solution.py:28
  58.4 158.2 %all-gather.9.cloned.1.call-start = ((), (), s32[]{:S(2)}) async-start(), calls=%async_computation.6 | async-start | bytes 2359296 | tf_op jit(solution)/shard_map/all_gather | solution.py:651
  63.1 23.9 %collective-permute-start.5 = (bf16[256,2048]{1,0:T(8,128)(2,1)}, bf16[256,2048]{1,0:T(8,128)(2,1)S(1)}, u32[]{:S(2)}, u32[]{:S(2)}) collective-permute-start(bf16[256,2048]{1,0:T(8,128)(2,1)} %slice.42), channel_id=1, source_target_pairs={{0,1},{1,0},{2,3},{3,2},{4,5},{5,4},{6,7},{7,6},{8,9},{9,8},{10,11... | collective-permute-start | bytes 3145736 | tf_op jit(solution)/shard_map/ppermute | solution.py:28
  99.3 215.8 %all-gather.11.cloned.1.call-start = ((), (), s32[]{:S(2)}) async-start(), calls=%async_computation.7 | async-start | bytes 9437184 | tf_op jit(solution)/shard_map/all_gather | solution.py:655
  99.3 45.1 %collective-permute-start.3 = (bf16[512,2048]{1,0:T(8,128)(2,1)S(1)}, bf16[512,2048]{1,0:T(8,128)(2,1)}, u32[]{:S(2)}, u32[]{:S(2)}) collective-permute-start(bf16[512,2048]{1,0:T(8,128)(2,1)S(1)} %copy-done), channel_id=1, source_target_pairs={{0,2},{1,3},{2,0},{3,1},{4,6},{5,7},{6,4},{7,5},{8,10},{9,11},{10,... | collective-permute-start | bytes 6291464 | tf_op jit(solution)/shard_map/ppermute | solution.py:28
  100.0 45.2 %collective-permute-start.2 = (bf16[512,2048]{1,0:T(8,128)(2,1)S(1)}, bf16[512,2048]{1,0:T(8,128)(2,1)}, u32[]{:S(2)}, u32[]{:S(2)}) collective-permute-start(bf16[512,2048]{1,0:T(8,128)(2,1)S(1)} %copy-done), channel_id=1, source_target_pairs={{0,1},{1,0},{2,3},{3,2},{4,5},{5,4},{6,7},{7,6},{8,9},{9,8},{10,11... | collective-permute-start | bytes 6291464 | tf_op jit(solution)/shard_map/ppermute | solution.py:28
  145.2 261.5 %reduce-scatter.5.cloned.1.call-start = ((), (), s32[]{:S(2)}) async-start(), calls=%async_computation.8 | async-start | bytes 9437184 | tf_op jit(solution)/shard_map/reduce_scatter | solution.py:665
  149.6 33.9 %collective-permute-start.7 = (bf16[256,2048]{1,0:T(8,128)(2,1)}, bf16[256,2048]{1,0:T(8,128)(2,1)S(1)}, u32[]{:S(2)}, u32[]{:S(2)}) collective-permute-start(bf16[256,2048]{1,0:T(8,128)(2,1)} %slice.44), channel_id=1, source_target_pairs={{0,1},{1,0},{2,3},{3,2},{4,5},{5,4},{6,7},{7,6},{8,9},{9,8},{10,11... | collective-permute-start | bytes 3145736 | tf_op jit(solution)/shard_map/ppermute | solution.py:28
  150.9 32.6 %collective-permute-start.6 = (bf16[256,2048]{1,0:T(8,128)(2,1)S(1)}, bf16[256,2048]{1,0:T(8,128)(2,1)S(1)}, u32[]{:S(2)}, u32[]{:S(2)}) collective-permute-start(bf16[256,2048]{1,0:T(8,128)(2,1)S(1)} %slice.43), channel_id=1, source_target_pairs={{0,2},{1,3},{2,0},{3,1},{4,6},{5,7},{6,4},{7,5},{8,10},{9,11},{10,... | collective-permute-start | bytes 3145736 | tf_op jit(solution)/shard_map/ppermute | solution.py:28
  216.5 288.3 %reduce-scatter.7.cloned.1.call-start = ((), (), s32[]{:S(2)}) async-start(), calls=%async_computation.9 | async-start | bytes 9437184 | tf_op jit(solution)/shard_map/reduce_scatter | solution.py:682
  216.6 93.2 %collective-permute-start.9 = (bf16[512,2048]{1,0:T(8,128)(2,1)}, bf16[512,2048]{1,0:T(8,128)(2,1)S(1)}, u32[]{:S(2)}, u32[]{:S(2)}) collective-permute-start(bf16[512,2048]{1,0:T(8,128)(2,1)} %all-gather.9.cloned.1.call-done.refs_0_), channel_id=1, source_target_pairs={{0,2},{1,3},{2,0},{3,1},{4,6},{5,7},{6,4},{7,5},{8,10},{9,11},{10,... | collective-permute-start | bytes 6291464 | tf_op jit(solution)/shard_map/ppermute | solution.py:28
  218.2 91.7 %collective-permute-start.8 = (bf16[512,2048]{1,0:T(8,128)(2,1)}, bf16[512,2048]{1,0:T(8,128)(2,1)}, u32[]{:S(2)}, u32[]{:S(2)}) collective-permute-start(bf16[512,2048]{1,0:T(8,128)(2,1)} %all-gather.9.cloned.1.call-done.refs_0_), channel_id=1, source_target_pairs={{0,1},{1,0},{2,3},{3,2},{4,5},{5,4},{6,7},{7,6},{8,9},{9,8},{10,11... | collective-permute-start | bytes 6291464 | tf_op jit(solution)/shard_map/ppermute | solution.py:28
  314.0 25.0 %collective-permute-start.11 = (bf16[256,2048]{1,0:T(8,128)(2,1)}, bf16[256,2048]{1,0:T(8,128)(2,1)S(1)}, u32[]{:S(2)}, u32[]{:S(2)}) collective-permute-start(bf16[256,2048]{1,0:T(8,128)(2,1)} %slice.46), channel_id=1, source_target_pairs={{0,1},{1,0},{2,3},{3,2},{4,5},{5,4},{6,7},{7,6},{8,9},{9,8},{10,11... | collective-permute-start | bytes 3145736 | tf_op jit(solution)/shard_map/ppermute | solution.py:28
  314.5 24.8 %collective-permute-start.10 = (bf16[256,2048]{1,0:T(8,128)(2,1)}, bf16[256,2048]{1,0:T(8,128)(2,1)}, u32[]{:S(2)}, u32[]{:S(2)}) collective-permute-start(bf16[256,2048]{1,0:T(8,128)(2,1)} %slice.45), channel_id=1, source_target_pairs={{0,2},{1,3},{2,0},{3,1},{4,6},{5,7},{6,4},{7,5},{8,10},{9,11},{10,... | collective-permute-start | bytes 3145736 | tf_op jit(solution)/shard_map/ppermute | solution.py:28
  354.0 52.6 %collective-permute-start.15 = (bf16[256,2048]{1,0:T(8,128)(2,1)}, bf16[256,2048]{1,0:T(8,128)(2,1)S(1)}, u32[]{:S(2)}, u32[]{:S(2)}) collective-permute-start(bf16[256,2048]{1,0:T(8,128)(2,1)} %get-tuple-element.338), channel_id=1, source_target_pairs={{0,2},{1,3},{2,0},{3,1},{4,6},{5,7},{6,4},{7,5},{8,10},{9,11},{10,... | collective-permute-start | bytes 3145736 | tf_op jit(solution)/shard_map/ppermute | solution.py:28
  355.3 51.3 %collective-permute-start.14 = (bf16[256,2048]{1,0:T(8,128)(2,1)}, bf16[256,2048]{1,0:T(8,128)(2,1)}, u32[]{:S(2)}, u32[]{:S(2)}) collective-permute-start(bf16[256,2048]{1,0:T(8,128)(2,1)} %get-tuple-element.339), channel_id=1, source_target_pairs={{0,1},{1,0},{2,3},{3,2},{4,5},{5,4},{6,7},{7,6},{8,9},{9,8},{10,11... | collective-permute-start | bytes 3145736 | tf_op jit(solution)/shard_map/ppermute | solution.py:28
  356.7 49.9 %collective-permute-start.13 = (bf16[256,2048]{1,0:T(8,128)(2,1)}, bf16[256,2048]{1,0:T(8,128)(2,1)}, u32[]{:S(2)}, u32[]{:S(2)}) collective-permute-start(bf16[256,2048]{1,0:T(8,128)(2,1)} %get-tuple-element.340), channel_id=1, source_target_pairs={{0,2},{1,3},{2,0},{3,1},{4,6},{5,7},{6,4},{7,5},{8,10},{9,11},{10,... | collective-permute-start | bytes 3145736 | tf_op jit(solution)/shard_map/ppermute | solution.py:28
  357.2 49.4 %collective-permute-start.12 = (bf16[256,2048]{1,0:T(8,128)(2,1)}, bf16[256,2048]{1,0:T(8,128)(2,1)}, u32[]{:S(2)}, u32[]{:S(2)}) collective-permute-start(bf16[256,2048]{1,0:T(8,128)(2,1)} %get-tuple-element.341), channel_id=1, source_target_pairs={{0,1},{1,0},{2,3},{3,2},{4,5},{5,4},{6,7},{7,6},{8,9},{9,8},{10,11... | collective-permute-start | bytes 3145736 | tf_op jit(solution)/shard_map/ppermute | solution.py:28
  407.6 212.2 %reduce-scatter.9.cloned.1.call-start = ((), (), s32[]{:S(2)}) async-start(), calls=%async_computation.10 | async-start | bytes 7077888 | tf_op jit(solution)/shard_map/reduce_scatter | solution.py:694
  409.2 69.0 %collective-permute-start.17 = (bf16[256,2048]{1,0:T(8,128)(2,1)S(1)}, bf16[256,2048]{1,0:T(8,128)(2,1)S(1)}, u32[]{:S(2)}, u32[]{:S(2)}) collective-permute-start(bf16[256,2048]{1,0:T(8,128)(2,1)S(1)} %add_convert_fusion), channel_id=1, source_target_pairs={{0,1},{1,0},{2,3},{3,2},{4,5},{5,4},{6,7},{7,6},{8,9},{9,8},{10,11... | collective-permute-start | bytes 3145736 | tf_op jit(solution)/shard_map/ppermute | solution.py:28
  413.4 64.8 %collective-permute-start.16 = (bf16[256,2048]{1,0:T(8,128)(2,1)}, bf16[256,2048]{1,0:T(8,128)(2,1)}, u32[]{:S(2)}, u32[]{:S(2)}) collective-permute-start(bf16[256,2048]{1,0:T(8,128)(2,1)} %add_convert_fusion.1), channel_id=1, source_target_pairs={{0,2},{1,3},{2,0},{3,1},{4,6},{5,7},{6,4},{7,5},{8,10},{9,11},{10,... | collective-permute-start | bytes 3145736 | tf_op jit(solution)/shard_map/ppermute | solution.py:28
  504.9 165.5 %reduce-scatter.11.cloned.1.call-start = ((), (), s32[]{:S(2)}) async-start(), calls=%async_computation.11 | async-start | bytes 2359296 | tf_op jit(solution)/shard_map/reduce_scatter | solution.py:718
  533.9 29.9 %collective-permute-start.21 = (bf16[256,1024]{1,0:T(8,128)(2,1)}, bf16[256,1024]{1,0:T(8,128)(2,1)S(1)}, u32[]{:S(2)}, u32[]{:S(2)}) collective-permute-start(bf16[256,1024]{1,0:T(8,128)(2,1)} %get-tuple-element.222), channel_id=1, source_target_pairs={{0,1},{1,0},{2,3},{3,2},{4,5},{5,4},{6,7},{7,6},{8,9},{9,8},{10,11... | collective-permute-start | bytes 1572872 | tf_op jit(solution)/shard_map/ppermute | solution.py:28
  534.5 29.2 %collective-permute-start.22 = (bf16[256,1024]{1,0:T(8,128)(2,1)}, bf16[256,1024]{1,0:T(8,128)(2,1)S(1)}, u32[]{:S(2)}, u32[]{:S(2)}) collective-permute-start(bf16[256,1024]{1,0:T(8,128)(2,1)} %get-tuple-element.223), channel_id=1, source_target_pairs={{0,2},{1,3},{2,0},{3,1},{4,6},{5,7},{6,4},{7,5},{8,10},{9,11},{10,... | collective-permute-start | bytes 1572872 | tf_op jit(solution)/shard_map/ppermute | solution.py:28
  535.2 28.6 %collective-permute-start.23 = (bf16[256,1024]{1,0:T(8,128)(2,1)}, bf16[256,1024]{1,0:T(8,128)(2,1)S(1)}, u32[]{:S(2)}, u32[]{:S(2)}) collective-permute-start(bf16[256,1024]{1,0:T(8,128)(2,1)} %get-tuple-element.224), channel_id=1, source_target_pairs={{0,1},{1,0},{2,3},{3,2},{4,5},{5,4},{6,7},{7,6},{8,9},{9,8},{10,11... | collective-permute-start | bytes 1572872 | tf_op jit(solution)/shard_map/ppermute | solution.py:28
  536.5 27.4 %collective-permute-start.24 = (bf16[256,1024]{1,0:T(8,128)(2,1)S(1)}, bf16[256,1024]{1,0:T(8,128)(2,1)S(1)}, u32[]{:S(2)}, u32[]{:S(2)}) collective-permute-start(bf16[256,1024]{1,0:T(8,128)(2,1)S(1)} %get-tuple-element.225), channel_id=1, source_target_pairs={{0,2},{1,3},{2,0},{3,1},{4,6},{5,7},{6,4},{7,5},{8,10},{9,11},{10,... | collective-permute-start | bytes 1572872 | tf_op jit(solution)/shard_map/ppermute | solution.py:28
  605.8 24.4 %collective-permute-start.28 = (bf16[256,1024]{1,0:T(8,128)(2,1)}, bf16[256,1024]{1,0:T(8,128)(2,1)}, u32[]{:S(2)}, u32[]{:S(2)}) collective-permute-start(bf16[256,1024]{1,0:T(8,128)(2,1)} %get-tuple-element.248), channel_id=1, source_target_pairs={{0,2},{1,3},{2,0},{3,1},{4,6},{5,7},{6,4},{7,5},{8,10},{9,11},{10,... | collective-permute-start | bytes 1572872 | tf_op jit(solution)/shard_map/ppermute | solution.py:28
  607.5 33.1 %collective-permute-start.29 = (bf16[256,1024]{1,0:T(8,128)(2,1)}, bf16[256,1024]{1,0:T(8,128)(2,1)}, u32[]{:S(2)}, u32[]{:S(2)}) collective-permute-start(bf16[256,1024]{1,0:T(8,128)(2,1)} %get-tuple-element.253), channel_id=1, source_target_pairs={{0,2},{1,3},{2,0},{3,1},{4,6},{5,7},{6,4},{7,5},{8,10},{9,11},{10,... | collective-permute-start | bytes 1572872 | tf_op jit(solution)/shard_map/ppermute | solution.py:28
  607.9 32.7 %collective-permute-start.30 = (bf16[256,1024]{1,0:T(8,128)(2,1)}, bf16[256,1024]{1,0:T(8,128)(2,1)}, u32[]{:S(2)}, u32[]{:S(2)}) collective-permute-start(bf16[256,1024]{1,0:T(8,128)(2,1)} %get-tuple-element.254), channel_id=1, source_target_pairs={{0,1},{1,0},{2,3},{3,2},{4,5},{5,4},{6,7},{7,6},{8,9},{9,8},{10,11... | collective-permute-start | bytes 1572872 | tf_op jit(solution)/shard_map/ppermute | solution.py:28
  (53 other events, 802.9 us)
Sparse Core Ops, SparseCore 0:
  9.6 84.7 all-gather.4
  96.0 63.2 all-gather.6
  160.9 29.5 all-gather.8
  191.9 81.5 all-gather.10
  275.6 87.7 reduce-scatter.4
  406.8 88.0 reduce-scatter.6
  505.0 67.5 reduce-scatter.8
  619.9 33.6 reduce-scatter.10

commit v3 on v2

v3 whole, which is shorter than its diff:
```python
import functools

import jax
import jax.numpy as jnp
from jax import lax
from jax.experimental import pallas as pl
from jax.experimental.pallas import tpu as pltpu
from jax.sharding import PartitionSpec as P

HEAD_DIM = 64
ROT = 32
LENGTH = 2048
PAIR = 2 * HEAD_DIM

epsilon = 1e-05
masked_score = -1e30
MIB = 1024 * 1024
VMEM_BYTES = 64 * MIB - 256 * 1024
ROWS_BY_ROWS = (((1,), (1,)), ((), ()))
COLUMNS_BY_COLUMNS = (((0,), (0,)), ((), ()))


SHORT = pl.CostEstimate(flops=1, bytes_accessed=1, transcendentals=0)


def after(value, *earlier):
    return lax.optimization_barrier((value,) + earlier)[0]


def swap(value, axis, bit):
    count = lax.axis_size(axis)
    return lax.ppermute(value, axis, [(i, i ^ bit) for i in range(count)])


def gather_start(block):
    if lax.axis_size("tensor") != 4:
        return (lax.all_gather(block, "tensor", axis=0, tiled=True),)
    return block, swap(block, "tensor", 1), swap(block, "tensor", 2)


def halves_kernel(one_ref, two_ref, low_ref, high_ref):
    half = one_ref.shape[0] // 2
    low_ref[...] = one_ref[:half, :]
    high_ref[...] = two_ref[half:, :]


def gather_pass(parts):
    if len(parts) == 1:
        return parts
    block, one, two = parts
    rows, depth = block.shape
    half = jax.ShapeDtypeStruct((rows // 2, depth), block.dtype)
    low, high = pl.pallas_call(
        halves_kernel,
        out_shape=[half, half],
        compiler_params=pltpu.CompilerParams(vmem_limit_bytes=VMEM_BYTES),
        cost_estimate=SHORT,
    )(one, two)
    return block, one, two, swap(low, "tensor", 2), swap(high, "tensor", 1)


def gathered_pieces(parts):
    if len(parts) == 1:
        return [(0, parts[0])]
    block, one, two, low, high = parts
    rows = block.shape[0]
    me = lax.axis_index("tensor")
    return [
        (me * rows, block),
        ((me ^ 1) * rows, one),
        ((me ^ 2) * rows, two),
        ((me ^ 3) * rows, low),
        ((me ^ 3) * rows + rows // 2, high),
    ]


def wide(piece):
    return piece.astype(jnp.float32)


def owner_cuts(total):
    count = lax.axis_size("tensor")
    rows = total // count
    me = lax.axis_index("tensor")
    order = [me ^ bit for bit in (3, 1, 2, 0)] if count == 4 else list(range(count))
    starts = jnp.stack([jnp.asarray(owner * rows, jnp.int32) for owner in order])
    return starts, count, 2 if count == 4 else 1


def scatter_send(cuts):
    if lax.axis_size("tensor") != 4:
        whole = wide(jnp.concatenate(cuts))
        return (lax.psum_scatter(whole, "tensor", scatter_dimension=0, tiled=True),)
    far_low, far_high, one_low, one_high, two_low, two_high, low, high = cuts
    return (
        swap(far_low, "tensor", 1),
        swap(far_high, "tensor", 2),
        swap(one_low, "tensor", 1),
        swap(two_high, "tensor", 2),
        two_low,
        one_high,
        low,
        high,
    )


def fold_kernel(a_ref, b_ref, c_ref, d_ref, ab_ref, cd_ref):
    ab_ref[...] = (wide(a_ref[...]) + wide(b_ref[...])).astype(ab_ref.dtype)
    cd_ref[...] = (wide(c_ref[...]) + wide(d_ref[...])).astype(cd_ref.dtype)


def scatter_fold(parts):
    if len(parts) == 1:
        return parts
    first_far, second_far, first_near, second_near, two_low, one_high, low, high = parts
    shape = jax.ShapeDtypeStruct(low.shape, low.dtype)
    forward = pl.pallas_call(
        fold_kernel,
        out_shape=[shape, shape],
        compiler_params=pltpu.CompilerParams(vmem_limit_bytes=VMEM_BYTES),
    )(two_low, first_far, one_high, second_far)
    return (*forward, first_near, second_near, low, high)


def scatter_pass(parts):
    if len(parts) == 1:
        return parts
    two_low, one_high, first_near, second_near, low, high = parts
    return (
        swap(two_low, "tensor", 2),
        swap(one_high, "tensor", 1),
        first_near,
        second_near,
        low,
        high,
    )


def exchange_start(columns):
    if lax.axis_size("tensor") != 4:
        return (lax.all_to_all(columns, "tensor", 0, 1, tiled=True),)
    rows = columns.shape[0] // 4
    me = lax.axis_index("tensor")
    pieces = []
    for bit in range(4):
        piece = lax.dynamic_slice_in_dim(columns, (me ^ bit) * rows, rows, 0)
        pieces.append(swap(piece, "tensor", bit) if bit else piece)
    return tuple(pieces)


def exchange_sum(value, axis, step=1):
    parts = [value]
    for bit in range(step, lax.axis_size(axis), step):
        parts.append(swap(value, axis, bit))
    return functools.reduce(lambda a, b: a + b, parts)


def lane_tables(row_total):
    half_rot = ROT // 2
    positions = (jnp.arange(row_total, dtype=jnp.int32) % LENGTH).astype(jnp.float32)
    inverse = 10000.0 ** (-(2.0 * jnp.arange(half_rot, dtype=jnp.float32)) / ROT)
    angles = positions[:, None] * inverse[None, :]
    cosine, sine = jnp.cos(angles), jnp.sin(angles)
    ones = jnp.ones((row_total, HEAD_DIM - ROT), jnp.float32)
    zeros = jnp.zeros((row_total, half_rot), jnp.float32)
    rest = jnp.zeros((row_total, HEAD_DIM - ROT), jnp.float32)
    cos_lanes = jnp.concatenate([cosine, cosine, ones] * 2, axis=1)
    from_above = jnp.concatenate([-sine, zeros, rest] * 2, axis=1)
    from_below = jnp.concatenate([zeros, sine, rest] * 2, axis=1)
    return cos_lanes, from_above, from_below


def turn(field, cos_lanes, from_above, from_below):
    half_rot = ROT // 2
    above = pltpu.roll(field, PAIR - half_rot, 1)
    below = pltpu.roll(field, half_rot, 1)
    return field * cos_lanes + above * from_above + below * from_below


def turn_back(field, cos_lanes, from_above, from_below):
    half_rot = ROT // 2
    above = pltpu.roll(field, PAIR - half_rot, 1)
    below = pltpu.roll(field, half_rot, 1)
    return field * cos_lanes - above * from_above - below * from_below


def joined_kernel(x_ref, w_ref, bias_ref, cos_ref, above_ref, below_ref, out_ref):
    width = out_ref.shape[1]
    chunk = min(256, width)
    slot = pl.program_id(0)

    def product(start):
        columns = slice(start, start + chunk)
        part = jnp.dot(x_ref[...], w_ref[0, :, columns], preferred_element_type=jnp.float32)
        return part + bias_ref[0, :, columns]

    @pl.when(slot < 2)
    def _():
        for start in range(0, width, chunk):
            part = product(start)
            for shift in range(0, chunk, PAIR):
                lanes = part[:, shift : shift + PAIR]
                turned = turn(lanes, cos_ref[...], above_ref[...], below_ref[...])
                columns = slice(start + shift, start + shift + PAIR)
                out_ref[:, columns] = turned.astype(out_ref.dtype)

    @pl.when(slot == 2)
    def _():
        for start in range(0, width, chunk):
            out_ref[:, start : start + chunk] = product(start).astype(out_ref.dtype)


def joined_rows(x, w, bias, lanes):
    rows, depth = x.shape
    width = w.shape[2]
    block = min(1024, rows)
    return pl.pallas_call(
        joined_kernel,
        grid=(3, rows // block),
        in_specs=[
            pl.BlockSpec((block, depth), lambda j, i: (i, 0)),
            pl.BlockSpec((1, depth, width), lambda j, i: (j, 0, 0)),
            pl.BlockSpec((1, 1, width), lambda j, i: (j, 0, 0)),
        ]
        + [pl.BlockSpec((block, PAIR), lambda j, i: (i, 0))] * 3,
        out_specs=pl.BlockSpec((block, width), lambda j, i: (i, j)),
        out_shape=jax.ShapeDtypeStruct((rows, 3 * width), jnp.bfloat16),
        compiler_params=pltpu.CompilerParams(vmem_limit_bytes=VMEM_BYTES),
        cost_estimate=SHORT,
    )(x, w, bias.reshape(3, 1, width), *lanes)


def hidden_kernel(x_ref, w_ref, bias_ref, active_ref, slope_ref):
    hidden = jnp.dot(x_ref[...], w_ref[...], preferred_element_type=jnp.float32) + bias_ref[...]
    scale = (2.0 / jnp.pi) ** 0.5
    square = hidden * hidden
    inner = scale * hidden * (1.0 + 0.044715 * square)
    bent = jnp.tanh(inner)
    half = 0.5 * (1.0 + bent)
    active_ref[...] = (hidden * half).astype(active_ref.dtype)
    growth = scale * (1.0 + (3.0 * 0.044715) * square)
    slope = half + 0.5 * hidden * (1.0 - bent * bent) * growth
    slope_ref[...] = slope.astype(slope_ref.dtype)


def hidden_rows(x, w, bias):
    rows, depth = x.shape
    width = w.shape[1]
    block, columns = min(1024, rows), min(1024, width)
    return pl.pallas_call(
        hidden_kernel,
        grid=(width // columns, rows // block),
        in_specs=[
            pl.BlockSpec((block, depth), lambda j, i: (i, 0)),
            pl.BlockSpec((depth, columns), lambda j, i: (0, j)),
            pl.BlockSpec((1, columns), lambda j, i: (0, j)),
        ],
        out_specs=[pl.BlockSpec((block, columns), lambda j, i: (i, j))] * 2,
        out_shape=[jax.ShapeDtypeStruct((rows, width), jnp.bfloat16)] * 2,
        compiler_params=pltpu.CompilerParams(vmem_limit_bytes=VMEM_BYTES),
        cost_estimate=SHORT,
    )(x, w, bias.reshape(1, width))


def whole_call(kernel, in_specs, out_specs, out_shape, scratch):
    return pl.pallas_call(
        kernel,
        in_specs=in_specs,
        out_specs=out_specs,
        out_shape=out_shape,
        scratch_shapes=scratch,
        compiler_params=pltpu.CompilerParams(vmem_limit_bytes=VMEM_BYTES),
        cost_estimate=SHORT,
    )


def columns_of(ref, index, size):
    return ref.at[:, pl.ds(pl.multiple_of(index * size, size), size)]


def rows_of(ref, index, size):
    return ref.at[pl.ds(pl.multiple_of(index * size, size), size), :]


def nt_dot(a, b):
    return lax.dot_general(a, b, ROWS_BY_ROWS, preferred_element_type=jnp.float32)


def tn_dot(a, b):
    return lax.dot_general(a, b, COLUMNS_BY_COLUMNS, preferred_element_type=jnp.float32)


ANY = pl.BlockSpec(memory_space=pl.ANY)
SMEM = pl.BlockSpec(memory_space=pltpu.SMEM)
VMEM = pl.BlockSpec(memory_space=pltpu.VMEM)


def tile_loop(count, tiles, tile_sems, where, compute):
    def write(step, slot):
        return pltpu.make_async_copy(tiles.at[slot], where(step), tile_sems.at[slot])

    @pl.loop(0, count)
    def _(step):
        slot = lax.rem(step, 2)

        @pl.when(step >= 2)
        def _():
            write(step, slot).wait()

        tiles[slot] = compute(step).astype(tiles.dtype)
        write(step, slot).start()

    for step in range(max(count - 2, 0), count):
        write(step, step % 2).wait()


def first_grads_kernel(starts_ref, active, dense, *refs):
    count = len(refs) - 11
    pieces = refs[:count]
    rows_out, mixed_out, down_out, grad_buf, active_buf, dense_buf, tiles = refs[count:-4]
    piece_sems, load_sems, row_sems, tile_sems = refs[-4:]
    _, rows, half = grad_buf.shape
    blocks, _, block = active_buf.shape

    def piece_copy(slot, side):
        size = pieces[slot].shape[0]
        there = pl.ds(pl.multiple_of(starts_ref[slot], size), size)
        return pltpu.make_async_copy(
            pieces[slot].at[:, pl.ds(side * half, half)],
            grad_buf.at[side, there, :],
            piece_sems.at[slot, side],
        )

    def active_copy(index):
        return pltpu.make_async_copy(
            columns_of(active, index, block), active_buf.at[index], load_sems.at[index]
        )

    def row_copy(side):
        return pltpu.make_async_copy(
            grad_buf.at[side], rows_out.at[:, pl.ds(side * half, half)], row_sems.at[side]
        )

    dense_copy = pltpu.make_async_copy(dense, dense_buf, load_sems.at[blocks])
    dense_copy.start()
    for slot in range(count):
        for side in range(2):
            piece_copy(slot, side).start()
    for index in range(blocks):
        active_copy(index).start()
    dense_copy.wait()
    for slot in range(count):
        for side in range(2):
            piece_copy(slot, side).wait()
        size = pieces[slot].shape[0]
        chunk = min(512, size)

        @pl.loop(0, size // chunk)
        def _(step, slot=slot, chunk=chunk):
            here = pl.ds(pl.multiple_of(starts_ref[slot] + step * chunk, chunk), chunk)
            mixed_out[here, :] = (
                nt_dot(grad_buf[0, here, :], dense_buf[:, :half])
                + nt_dot(grad_buf[1, here, :], dense_buf[:, half:])
            ).astype(mixed_out.dtype)

    for side in range(2):
        row_copy(side).start()
    for index in range(blocks):
        active_copy(index).wait()
    tile_loop(
        2 * blocks,
        tiles,
        tile_sems,
        lambda step: down_out.at[
            pl.ds(pl.multiple_of(lax.div(step, 2) * block, block), block),
            pl.ds(pl.multiple_of(lax.rem(step, 2) * half, half), half),
        ],
        lambda step: tn_dot(active_buf[lax.div(step, 2)], grad_buf[lax.rem(step, 2)]),
    )
    for side in range(2):
        row_copy(side).wait()


def first_grads(pieces, active, dense):
    low = jnp.bfloat16
    rows, hidden = active.shape
    width, depth = dense.shape
    half, block = depth // 2, min(512, hidden)
    count = len(pieces)
    starts = jnp.stack([jnp.asarray(start, jnp.int32) for start, _ in pieces])
    return whole_call(
        first_grads_kernel,
        [SMEM] + [ANY] * (2 + count),
        [ANY, VMEM, ANY],
        [
            jax.ShapeDtypeStruct((rows, depth), low),
            jax.ShapeDtypeStruct((rows, width), low),
            jax.ShapeDtypeStruct((hidden, depth), low),
        ],
        [
            pltpu.VMEM((2, rows, half), low),
            pltpu.VMEM((hidden // block, rows, block), low),
            pltpu.VMEM((width, depth), low),
            pltpu.VMEM((2, block, half), low),
            pltpu.SemaphoreType.DMA((count, 2)),
            pltpu.SemaphoreType.DMA((hidden // block + 1,)),
            pltpu.SemaphoreType.DMA((2,)),
            pltpu.SemaphoreType.DMA((2,)),
        ],
    )(starts, active, dense, *[piece for _, piece in pieces])


def feed_kernel(starts_ref, active, weight, *refs, halves):
    cuts = refs[:-5]
    active_buf, weight_buf, out_buf, load_sems, cut_sems = refs[-5:]
    owners = len(cuts) // halves
    rows = active_buf.shape[0]
    half = weight_buf.shape[2]
    owner_rows = rows // owners
    piece = owner_rows // halves

    def weight_load(side):
        return pltpu.make_async_copy(
            weight.at[:, pl.ds(side * half, half)], weight_buf.at[side], load_sems.at[side]
        )

    def row_load(owner):
        here = pl.ds(pl.multiple_of(starts_ref[owner], owner_rows), owner_rows)
        return pltpu.make_async_copy(
            active.at[here, :], active_buf.at[here, :], load_sems.at[2 + owner]
        )

    weight_load(0).start()
    row_load(0).start()
    weight_load(1).start()
    for owner in range(1, owners):
        row_load(owner).start()

    def cut_copy(owner, part_of, side):
        return pltpu.make_async_copy(
            out_buf.at[side, pl.ds(owner * owner_rows + part_of * piece, piece), :],
            cuts[owner * halves + part_of].at[:, pl.ds(pl.multiple_of(side * half, half), half)],
            cut_sems.at[side, owner * halves + part_of],
        )

    @pl.loop(0, 2 * owners)
    def _(step):
        owner, side = lax.div(step, 2), lax.rem(step, 2)
        for own in range(owners):
            pl.when(step == 2 * own)(row_load(own).wait)
        for own in range(2):
            pl.when(step == own)(weight_load(own).wait)
        here = pl.ds(pl.multiple_of(starts_ref[owner], owner_rows), owner_rows)
        there = pl.ds(pl.multiple_of(owner * owner_rows, owner_rows), owner_rows)
        out_buf[side, there, :] = jnp.dot(
            active_buf[here, :], weight_buf[side], preferred_element_type=jnp.float32
        ).astype(out_buf.dtype)
        for own in range(owners):

            @pl.when(owner == own)
            def _(own=own):
                for part_of in range(halves):
                    cut_copy(own, part_of, side).start()

    for side in range(2):
        for own in range(owners):
            for part_of in range(halves):
                cut_copy(own, part_of, side).wait()


def feed_rows(active, weight):
    low = jnp.bfloat16
    rows, hidden = active.shape
    depth = weight.shape[1]
    half = depth // 2
    starts, owners, halves = owner_cuts(rows)
    cut = jax.ShapeDtypeStruct((rows // owners // halves, depth), low)
    return tuple(
        whole_call(
            functools.partial(feed_kernel, halves=halves),
            [SMEM] + [ANY] * 2,
            [ANY] * (owners * halves),
            [cut] * (owners * halves),
            [
                pltpu.VMEM((rows, hidden), low),
                pltpu.VMEM((2, hidden, half), low),
                pltpu.VMEM((2, rows, half), low),
                pltpu.SemaphoreType.DMA((2 + owners,)),
                pltpu.SemaphoreType.DMA((2, owners * halves)),
            ],
        )(starts, active, weight)
    )


def hidden_grads_kernel(grad_rows, weight, slope, x, hidden_out, up_out, sum_out, *refs):
    grad_buf, weight_buf, slope_buf, x_buf, hidden_buf, tiles = refs[:6]
    load_sems, slope_sems, hidden_sems, tile_sems = refs[6:]
    rows = grad_buf.shape[0]
    parts, _, part = hidden_buf.shape
    x_blocks, _, x_block = x_buf.shape
    chunk = slope_buf.shape[1]
    chunks = rows // chunk

    def load(source, target, index):
        return pltpu.make_async_copy(source, target, load_sems.at[index])

    def grad_load(index):
        here = pl.ds(pl.multiple_of(index * chunk, chunk), chunk)
        return load(grad_rows.at[here, :], grad_buf.at[here, :], index)

    def weight_load(index):
        here = pl.ds(pl.multiple_of(index * part, part), part)
        return load(weight.at[here, :], weight_buf.at[here, :], chunks + index)

    x_loads = [
        load(columns_of(x, i, x_block), x_buf.at[i], chunks + parts + i) for i in range(x_blocks)
    ]

    def slope_copy(step, slot):
        place = (
            pl.ds(pl.multiple_of(lax.rem(step, chunks) * chunk, chunk), chunk),
            pl.ds(pl.multiple_of(lax.div(step, chunks) * part, part), part),
        )
        return pltpu.make_async_copy(slope.at[place], slope_buf.at[slot], slope_sems.at[slot])

    def hidden_copy(index):
        return pltpu.make_async_copy(
            hidden_buf.at[index],
            hidden_out.at[:, pl.ds(index * part, part)],
            hidden_sems.at[index],
        )

    weight_load(0).start()
    grad_load(0).start()
    slope_copy(0, 0).start()
    for index in range(1, chunks):
        grad_load(index).start()
    for index in range(1, parts):
        weight_load(index).start()
    for copy in x_loads:
        copy.start()
    sum_out[...] = jnp.zeros_like(sum_out)

    @pl.loop(0, parts * chunks)
    def _(step):
        slot = lax.rem(step, 2)
        index = lax.div(step, chunks)

        @pl.when(step + 1 < parts * chunks)
        def _():
            slope_copy(step + 1, 1 - slot).start()

        @pl.when(lax.rem(step, chunks) == 0)
        def _():
            weight_load(index).wait()

        @pl.when(index == 0)
        def _():
            grad_load(step).wait()

        slope_copy(step, slot).wait()
        here = pl.ds(pl.multiple_of(lax.rem(step, chunks) * chunk, chunk), chunk)
        units = pl.ds(pl.multiple_of(index * part, part), part)
        product = nt_dot(grad_buf[here, :], weight_buf[units, :])
        low = (product * wide(slope_buf[slot])).astype(hidden_buf.dtype)
        hidden_buf[index, here, :] = low
        sum_out[index] += jnp.sum(wide(low), axis=0, keepdims=True)

    for index in range(parts):
        hidden_copy(index).start()
    for copy in x_loads:
        copy.wait()
    tile_loop(
        x_blocks * parts,
        tiles,
        tile_sems,
        lambda step: up_out.at[
            pl.ds(pl.multiple_of(lax.div(step, parts) * x_block, x_block), x_block),
            pl.ds(pl.multiple_of(lax.rem(step, parts) * part, part), part),
        ],
        lambda step: tn_dot(x_buf[lax.div(step, parts)], hidden_buf[lax.rem(step, parts)]),
    )
    for index in range(parts):
        hidden_copy(index).wait()


def hidden_grads(grad_rows, weight, slope, x):
    low = jnp.bfloat16
    rows, depth = grad_rows.shape
    hidden = weight.shape[0]
    part, x_block, chunk = min(1024, hidden), min(512, depth), min(512, rows)
    return whole_call(
        hidden_grads_kernel,
        [ANY] * 4,
        [ANY, ANY, VMEM],
        [
            jax.ShapeDtypeStruct((rows, hidden), low),
            jax.ShapeDtypeStruct((depth, hidden), low),
            jax.ShapeDtypeStruct((hidden // part, 1, part), jnp.float32),
        ],
        [
            pltpu.VMEM((rows, depth), low),
            pltpu.VMEM((hidden, depth), low),
            pltpu.VMEM((2, chunk, part), low),
            pltpu.VMEM((depth // x_block, rows, x_block), low),
            pltpu.VMEM((hidden // part, rows, part), low),
            pltpu.VMEM((2, x_block, part), low),
            pltpu.SemaphoreType.DMA((rows // chunk + hidden // part + depth // x_block,)),
            pltpu.SemaphoreType.DMA((2,)),
            pltpu.SemaphoreType.DMA((hidden // part,)),
            pltpu.SemaphoreType.DMA((2,)),
        ],
    )(grad_rows, weight, slope, x)


def qkv_grads_kernel(x, joined, out, x_buf, joined_buf, tiles, x_sems, joined_sems, tile_sems):
    blocks, _, block = x_buf.shape
    x_loads = [
        pltpu.make_async_copy(columns_of(x, i, block), x_buf.at[i], x_sems.at[i])
        for i in range(blocks)
    ]
    joined_loads = [
        pltpu.make_async_copy(joined.at[i], joined_buf.at[i], joined_sems.at[i]) for i in range(3)
    ]
    joined_loads[0].start()
    for copy in x_loads + joined_loads[1:]:
        copy.start()

    def compute(step):
        for index in range(3):
            pl.when(step == index * blocks)(joined_loads[index].wait)
        for index in range(blocks):
            pl.when(step == index)(x_loads[index].wait)
        return tn_dot(x_buf[lax.rem(step, blocks)], joined_buf[lax.div(step, blocks)])

    tile_loop(
        3 * blocks,
        tiles,
        tile_sems,
        lambda step: rows_of(out.at[lax.div(step, blocks)], lax.rem(step, blocks), block),
        compute,
    )


def qkv_grads(x, joined):
    low = jnp.bfloat16
    rows, depth = x.shape
    width = joined.shape[2]
    block = min(1024, depth)
    return whole_call(
        qkv_grads_kernel,
        [ANY] * 2,
        ANY,
        jax.ShapeDtypeStruct((3, depth, width), low),
        [
            pltpu.VMEM((depth // block, rows, block), low),
            pltpu.VMEM((3, rows, width), low),
            pltpu.VMEM((2, block, width), low),
            pltpu.SemaphoreType.DMA((depth // block,)),
            pltpu.SemaphoreType.DMA((3,)),
            pltpu.SemaphoreType.DMA((2,)),
        ],
    )(x, joined)


def normed_grads_kernel(
    starts_ref, joined, qkv, hidden, up, x, mean_ref, root_ref, gain_ref, shift_ref, *refs, halves
):
    cuts = refs[:-8]
    joined_buf, qkv_buf, hidden_buf, up_buf, x_buf, out_buf, load_sems, cut_sems = refs[-8:]
    owners = len(cuts) // halves
    rows = hidden_buf.shape[0]
    owner_rows = rows // owners
    piece = owner_rows // halves

    def load(source, target, index):
        return pltpu.make_async_copy(source, target, load_sems.at[index])

    def row_loads(owner):
        here = pl.ds(pl.multiple_of(starts_ref[owner], owner_rows), owner_rows)
        at = 4 + owner * 3
        return (
            load(hidden.at[here, :], hidden_buf.at[here, :], at),
            load(joined.at[:, here, :], joined_buf.at[:, here, :], at + 1),
            load(x.at[here, :], x_buf.at[here, :], at + 2),
        )

    weights = [load(up, up_buf, 0), load(qkv, qkv_buf, 1)]
    weights[0].start()
    for copy in row_loads(0):
        copy.start()
    weights[1].start()
    for owner in range(1, owners):
        for copy in row_loads(owner):
            copy.start()
    gain_ref[...] = jnp.zeros_like(gain_ref)
    shift_ref[...] = jnp.zeros_like(shift_ref)
    for copy in weights:
        copy.wait()

    def cut_copy(owner, part_of):
        return pltpu.make_async_copy(
            out_buf.at[pl.ds(owner * owner_rows + part_of * piece, piece), :],
            cuts[owner * halves + part_of],
            cut_sems.at[owner * halves + part_of],
        )

    @pl.loop(0, owners)
    def _(owner):
        for copy in row_loads(owner):
            copy.wait()
        here = pl.ds(pl.multiple_of(starts_ref[owner], owner_rows), owner_rows)
        there = pl.ds(pl.multiple_of(owner * owner_rows, owner_rows), owner_rows)
        columns = up_buf.shape[0]
        chunk = min(512, columns)
        for start in range(0, columns, chunk):
            mine = slice(start, start + chunk)
            total = nt_dot(hidden_buf[here, :], up_buf[mine, :])
            for slot in range(3):
                total += nt_dot(joined_buf[slot, here, :], qkv_buf[slot, mine, :])
            out_buf[there, mine] = total.astype(out_buf.dtype)
            hat = (wide(x_buf[here, mine]) - mean_ref[here, :]) * root_ref[here, :]
            gain_ref[:, mine] += jnp.sum(total * hat, axis=0, keepdims=True)
            shift_ref[:, mine] += jnp.sum(total, axis=0, keepdims=True)
        for own in range(owners):

            @pl.when(owner == own)
            def _(own=own):
                for part_of in range(halves):
                    cut_copy(own, part_of).start()

    for own in range(owners):
        for part_of in range(halves):
            cut_copy(own, part_of).wait()


def normed_grads(joined, qkv, hidden, up, x, mean, root, first, last):
    low = jnp.bfloat16
    rows, units = hidden.shape
    width = joined.shape[2]
    columns = last - first
    starts, owners, halves = owner_cuts(rows)
    cut = jax.ShapeDtypeStruct((rows // owners // halves, columns), low)
    line = jax.ShapeDtypeStruct((1, columns), jnp.float32)

    def kernel(starts_ref, joined, qkv, hidden, up, x, *refs):
        mine = pl.ds(first, columns)
        normed_grads_kernel(
            starts_ref,
            joined,
            qkv.at[:, mine, :],
            hidden,
            up.at[mine, :],
            x.at[:, mine],
            *refs,
            halves=halves,
        )

    result = whole_call(
        kernel,
        [SMEM] + [ANY] * 5 + [VMEM] * 2,
        [VMEM, VMEM] + [ANY] * (owners * halves),
        [line, line] + [cut] * (owners * halves),
        [
            pltpu.VMEM((3, rows, width), low),
            pltpu.VMEM((3, columns, width), low),
            pltpu.VMEM((rows, units), low),
            pltpu.VMEM((columns, units), low),
            pltpu.VMEM((rows, columns), low),
            pltpu.VMEM((rows, columns), low),
            pltpu.SemaphoreType.DMA((4 + 3 * owners,)),
            pltpu.SemaphoreType.DMA((owners * halves,)),
        ],
    )(starts, joined, qkv, hidden, up, x, mean, root)
    return result[0], result[1], tuple(result[2:])


def finish_kernel(*refs):
    mixed, dense = refs[:4], refs[4:9]
    token_ref, bias_ref = refs[9:11]
    last_first, last_second, first_near, second_near, low, high = refs[11:17]
    out_ref = refs[17]
    half = low.shape[0]
    far = dense[3].shape[0]
    total = jnp.dot(mixed[0][...], dense[0][...], preferred_element_type=jnp.float32)
    total += jnp.dot(mixed[1][...], dense[1][...], preferred_element_type=jnp.float32)
    total += jnp.dot(mixed[2][...], dense[2][...], preferred_element_type=jnp.float32)
    total += jnp.dot(mixed[3][:, :far], dense[3][...], preferred_element_type=jnp.float32)
    total += jnp.dot(mixed[3][:, far:], dense[4][...], preferred_element_type=jnp.float32)
    total += wide(token_ref[...]) + bias_ref[...]
    for here, parts in (
        (slice(0, half), (low, first_near, last_first)),
        (slice(half, 2 * half), (high, second_near, last_second)),
    ):
        feed = wide(parts[0][...]) + wide(parts[1][...]) + wide(parts[2][...])
        out_ref[here, :] = (total[here] + feed).astype(out_ref.dtype)


def finish_output(mixed_parts, dense_parts, tokens, bias, feed_parts):
    rows, depth = tokens.shape
    if len(feed_parts) == 1:
        attended = jnp.dot(mixed_parts[0], dense_parts[0], preferred_element_type=jnp.float32)
        return (wide(tokens) + attended + feed_parts[0] + bias).astype(tokens.dtype)
    columns = min(512, depth)

    def column_block(piece):
        return pl.BlockSpec((piece.shape[0], columns), lambda j: (0, j))

    return pl.pallas_call(
        finish_kernel,
        grid=(depth // columns,),
        in_specs=[pl.BlockSpec(piece.shape, lambda j: (0, 0)) for piece in mixed_parts]
        + [column_block(piece) for piece in dense_parts]
        + [column_block(tokens), pl.BlockSpec((1, columns), lambda j: (0, j))]
        + [column_block(piece) for piece in feed_parts],
        out_specs=column_block(tokens),
        out_shape=jax.ShapeDtypeStruct(tokens.shape, tokens.dtype),
        compiler_params=pltpu.CompilerParams(vmem_limit_bytes=VMEM_BYTES),
        cost_estimate=SHORT,
    )(*mixed_parts, *dense_parts, tokens, bias.reshape(1, depth), *feed_parts)


def token_grads_kernel(*refs):
    left, right = refs[:6], refs[6:12]
    token_ref, grad_ref, mean_ref, root_ref, gain_ref, out_ref = refs[12:]
    half = left[4].shape[0]
    split = left[4].shape[1]
    chunk = min(32, half)
    for upper in range(2):
        chosen = [(side[4 + upper], side[2 + upper], side[upper]) for side in (left, right)]

        @pl.loop(0, half // chunk)
        def _(step, chosen=chosen, upper=upper):
            there = pl.ds(pl.multiple_of(step * chunk, chunk), chunk)
            here = pl.ds(pl.multiple_of(upper * half + step * chunk, chunk), chunk)
            scaled = []
            hats = []
            for side, parts in enumerate(chosen):
                columns = slice(side * split, (side + 1) * split)
                total = sum(wide(part[there, :]) for part in parts)
                scaled.append(total * gain_ref[:, columns])
                hats.append(
                    (wide(token_ref[here, columns]) - mean_ref[here, :]) * root_ref[here, :]
                )
            count = 2 * split
            mean = sum(jnp.sum(v, axis=-1, keepdims=True) for v in scaled) / count
            slant = (
                sum(jnp.sum(v * h, axis=-1, keepdims=True) for v, h in zip(scaled, hats)) / count
            )
            for side in range(2):
                columns = slice(side * split, (side + 1) * split)
                grad = root_ref[here, :] * (scaled[side] - mean - hats[side] * slant)
                out_ref[here, columns] = (wide(grad_ref[here, columns]) + grad).astype(
                    out_ref.dtype
                )


def token_grads(left_parts, right_parts, tokens, cotangent, mean, root, gain):
    if len(left_parts) == 1:
        grad = jnp.concatenate([left_parts[0], right_parts[0]], axis=1)
        hat = (wide(tokens) - mean) * root
        scaled = grad * gain
        grad_input = root * (
            scaled
            - jnp.mean(scaled, axis=-1, keepdims=True)
            - hat * jnp.mean(scaled * hat, axis=-1, keepdims=True)
        )
        return (wide(cotangent) + grad_input).astype(tokens.dtype)
    return pl.pallas_call(
        token_grads_kernel,
        out_shape=jax.ShapeDtypeStruct(tokens.shape, tokens.dtype),
        compiler_params=pltpu.CompilerParams(vmem_limit_bytes=VMEM_BYTES),
        cost_estimate=SHORT,
    )(*left_parts, *right_parts, tokens, cotangent, mean, root, gain.reshape(1, -1))


def attention_kernel(
    q_ref,
    k_ref,
    v_ref,
    g_ref,
    cos_ref,
    above_ref,
    below_ref,
    mixed_ref,
    grads_ref,
    sums_ref,
    keys_across,
    values_across,
    query_total,
    key_total,
    value_total,
    weight_buf,
    top_buf,
    out_buf,
    across_buf,
    *,
    block,
    block_count,
):
    step = pl.program_id(1)
    scale = HEAD_DIM**-0.5
    rate = scale * 1.4426950408889634

    @pl.when(step == 0)
    def _():
        keys_across[...] = k_ref[...].T
        values_across[...] = v_ref[...].T
        key_total[...] = jnp.zeros_like(key_total)
        value_total[...] = jnp.zeros_like(value_total)

    rows = pl.ds(pl.multiple_of(step * block, block), block)
    queries, grads = q_ref[rows, :], g_ref[rows, :]
    lane = lax.broadcasted_iota(jnp.int32, (block, PAIR), 1)
    own_lanes = [lane // HEAD_DIM == head for head in range(2)]
    query_heads = [jnp.where(own, queries, jnp.zeros_like(queries)) for own in own_lanes]
    grad_heads = [jnp.where(own, grads, jnp.zeros_like(grads)) for own in own_lanes]
    parts = [slice(head * HEAD_DIM, (head + 1) * HEAD_DIM) for head in range(2)]

    def weigh(there, index, first):
        keys = k_ref[there, :]
        score_heads = [
            lax.dot_general(keys, own, ROWS_BY_ROWS, preferred_element_type=jnp.float32)
            for own in query_heads
        ]
        for head in range(2):
            scores = score_heads[head]
            if first:
                key_pos = lax.broadcasted_iota(jnp.int32, (block, block), 0)
                query_pos = lax.broadcasted_iota(jnp.int32, (block, block), 1)
                scores = jnp.where(key_pos <= query_pos, scores, masked_score)
            top = jnp.max(scores, axis=0, keepdims=True) * rate
            if not first:
                before = top_buf[head, 0]
                top = jnp.maximum(top, before)
            weights = jnp.exp2(scores * rate - top)
            weight_buf[head, there, :] = weights
            top_buf[head, 2 + index] = top
            total = jnp.sum(weights, axis=0, keepdims=True)
            out = jnp.dot(
                values_across[parts[head], there],
                weights.astype(jnp.bfloat16),
                preferred_element_type=jnp.float32,
            )
            if not first:
                shrink = jnp.exp2(before - top)
                total += top_buf[head, 1] * shrink
                out += out_buf[parts[head], :] * shrink
            top_buf[head, 0] = top
            top_buf[head, 1] = total
            out_buf[parts[head], :] = out

    weigh(rows, step, True)

    @pl.loop(0, step)
    def _(index):
        weigh(pl.ds(pl.multiple_of(index * block, block), block), index, False)

    grads_across = grads.T.astype(jnp.float32)
    inner, share = [], []
    for head in range(2):
        share.append(1.0 / top_buf[head, 1])
        out = out_buf[parts[head], :] * share[head]
        out_buf[parts[head], :] = out
        inner.append(jnp.sum(out * grads_across[parts[head]], axis=0, keepdims=True))
    mixed_ref[rows, :] = out_buf[...].T.astype(mixed_ref.dtype)

    def differentiate(there, index, first):
        values = v_ref[there, :]
        prob_heads = [
            lax.dot_general(values, own, ROWS_BY_ROWS, preferred_element_type=jnp.float32)
            for own in grad_heads
        ]
        value_parts, key_parts = [], []
        for head in range(2):
            factor = jnp.exp2(top_buf[head, 2 + index] - top_buf[head, 0]) * share[head]
            exact = weight_buf[head, there, :] * factor
            rounded = exact.astype(jnp.bfloat16)
            grad_scores = (exact * (prob_heads[head] - inner[head])).astype(jnp.bfloat16)
            value_parts.append(
                jnp.dot(rounded, grad_heads[head], preferred_element_type=jnp.float32)
            )
            key_parts.append(
                jnp.dot(grad_scores, query_heads[head], preferred_element_type=jnp.float32)
            )
            across = jnp.dot(
                keys_across[parts[head], there], grad_scores, preferred_element_type=jnp.float32
            )
            if first:
                across_buf[parts[head], :] = across
            else:
                across_buf[parts[head], :] += across
        value_total[there, :] += value_parts[0] + value_parts[1]
        key_total[there, :] += key_parts[0] + key_parts[1]

    differentiate(rows, step, True)

    @pl.loop(0, step)
    def _(index):
        differentiate(pl.ds(pl.multiple_of(index * block, block), block), index, False)

    query_total[rows, :] = across_buf[...].T

    @pl.when(step == block_count - 1)
    def _():
        lanes = cos_ref[...], above_ref[...], below_ref[...]
        for slot, field in enumerate(
            (
                turn_back(query_total[...] * scale, *lanes),
                turn_back(key_total[...] * scale, *lanes),
                value_total[...],
            )
        ):
            low = field.astype(grads_ref.dtype)
            grads_ref[slot] = low
            sums_ref[slot] = jnp.sum(low.astype(jnp.float32), axis=0, keepdims=True)


def attention(joined, grad_mixed, lanes, first, last, earlier=None):
    rows, width = grad_mixed.shape
    block = min(512, LENGTH)
    pairs, block_count = width // PAIR, LENGTH // block
    row_block = pl.BlockSpec((LENGTH, PAIR), lambda p, i: (0, first + p))
    table = pl.BlockSpec((LENGTH, PAIR), lambda p, i: (0, 0))
    kept = () if earlier is None else tuple(earlier)
    kernel = functools.partial(attention_kernel, block=block, block_count=block_count)

    def body(*refs):
        kernel(*refs[:7], *refs[7 + len(kept) :])

    return pl.pallas_call(
        body,
        grid=(last - first, block_count),
        in_specs=[
            row_block,
            pl.BlockSpec((LENGTH, PAIR), lambda p, i: (0, pairs + first + p)),
            pl.BlockSpec((LENGTH, PAIR), lambda p, i: (0, 2 * pairs + first + p)),
            row_block,
            table,
            table,
            table,
        ]
        + [pl.BlockSpec(memory_space=pl.ANY)] * len(kept),
        out_specs=[
            row_block,
            pl.BlockSpec((3, LENGTH, PAIR), lambda p, i: (0, 0, first + p)),
            pl.BlockSpec((3, 1, PAIR), lambda p, i: (0, 0, first + p)),
        ],
        out_shape=[
            jax.ShapeDtypeStruct((rows, width), jnp.bfloat16),
            jax.ShapeDtypeStruct((3, rows, width), jnp.bfloat16),
            jax.ShapeDtypeStruct((3, 1, width), jnp.float32),
        ],
        scratch_shapes=[
            pltpu.VMEM((PAIR, LENGTH), jnp.bfloat16),
            pltpu.VMEM((PAIR, LENGTH), jnp.bfloat16),
            pltpu.VMEM((LENGTH, PAIR), jnp.float32),
            pltpu.VMEM((LENGTH, PAIR), jnp.float32),
            pltpu.VMEM((LENGTH, PAIR), jnp.float32),
            pltpu.VMEM((2, LENGTH, block), jnp.float32),
            pltpu.VMEM((2, 2 + block_count, 1, block), jnp.float32),
            pltpu.VMEM((PAIR, block), jnp.float32),
            pltpu.VMEM((PAIR, block), jnp.float32),
        ],
        input_output_aliases={7 + i: i for i in range(len(kept))},
        compiler_params=pltpu.CompilerParams(vmem_limit_bytes=VMEM_BYTES),
        cost_estimate=SHORT,
    )(joined, joined, joined, grad_mixed, *lanes, *kept)


def norm_kernel(starts_ref, gain_ref, shift_ref, following_ref, *refs):
    count = (len(refs) - 6) // 3
    pieces = refs[:count]
    raw, normed, mean_ref, root_ref, following_out = refs[count : count + 5]
    buffers = refs[count + 5 : 2 * count + 5]
    results = refs[2 * count + 5 : 3 * count + 5]
    sems = refs[-1]
    following_out[...] = following_ref[...]
    for slot in range(count):
        pltpu.make_async_copy(pieces[slot], buffers[slot], sems.at[0, slot]).start()
    writes = []
    for slot in range(count):
        buffer, result = buffers[slot], results[slot]
        size = buffer.shape[0]
        where = pl.ds(pl.multiple_of(starts_ref[slot], size), size)
        pltpu.make_async_copy(pieces[slot], buffer, sems.at[0, slot]).wait()
        write = pltpu.make_async_copy(buffer, raw.at[where, :], sems.at[1, slot])
        write.start()
        writes.append(write)
        chunk = min(128, size)

        @pl.loop(0, size // chunk)
        def _(step, buffer=buffer, result=result, slot=slot):
            here = pl.ds(pl.multiple_of(step * chunk, chunk), chunk)
            rows = buffer[here, :].astype(jnp.float32)
            mean = jnp.mean(rows, axis=-1, keepdims=True)
            centred = rows - mean
            variance = jnp.mean(centred * centred, axis=-1, keepdims=True)
            root = lax.rsqrt(variance + epsilon)
            out = centred * root * gain_ref[...] + shift_ref[...]
            result[here, :] = out.astype(result.dtype)
            there = pl.ds(pl.multiple_of(starts_ref[slot] + step * chunk, chunk), chunk)
            mean_ref[there, :] = mean
            root_ref[there, :] = root

        write = pltpu.make_async_copy(result, normed.at[where, :], sems.at[2, slot])
        write.start()
        writes.append(write)
    for write in writes:
        write.wait()


def norm_rows(pieces, gain, shift, following):
    depth = gain.shape[0]
    total = sum(piece.shape[0] for _, piece in pieces)
    count = len(pieces)
    low = jnp.bfloat16
    starts = jnp.stack([jnp.asarray(start, jnp.int32) for start, _ in pieces])
    any_space = pl.BlockSpec(memory_space=pl.ANY)
    vmem = pl.BlockSpec(memory_space=pltpu.VMEM)
    stage = [pltpu.VMEM(piece.shape, low) for _, piece in pieces]
    return pl.pallas_call(
        norm_kernel,
        in_specs=[pl.BlockSpec(memory_space=pltpu.SMEM), vmem, vmem, vmem] + [any_space] * count,
        out_specs=[any_space, any_space, vmem, vmem, vmem],
        out_shape=[
            jax.ShapeDtypeStruct((total, depth), low),
            jax.ShapeDtypeStruct((total, depth), low),
            jax.ShapeDtypeStruct((total, 1), jnp.float32),
            jax.ShapeDtypeStruct((total, 1), jnp.float32),
            jax.ShapeDtypeStruct(following.shape, following.dtype),
        ],
        scratch_shapes=stage + stage + [pltpu.SemaphoreType.DMA((3, count))],
        compiler_params=pltpu.CompilerParams(vmem_limit_bytes=VMEM_BYTES),
        cost_estimate=SHORT,
    )(
        starts,
        gain.reshape(1, depth),
        shift.reshape(1, depth),
        following,
        *[piece for _, piece in pieces],
    )


def on_device(
    tokens,
    norm_gain,
    norm_shift,
    weight_qkv,
    bias_qkv,
    weight_dense,
    weight_up,
    bias_up,
    weight_down,
    bias_out,
    cotangent,
):
    f32, low = jnp.float32, jnp.bfloat16
    depth = tokens.shape[1]
    local_rows = tokens.shape[0]
    tensor_index = lax.axis_index("tensor")

    full_up = lax.all_gather(weight_up, "dp", axis=0, tiled=True)
    token_parts = gather_start(tokens)
    lanes = lane_tables(LENGTH)
    out_part = jnp.sum(cotangent, axis=0, dtype=f32)
    lanes, out_part, token_parts = after((lanes, out_part, token_parts))
    full_qkv = lax.all_gather(
        after(jnp.transpose(weight_qkv, (1, 0, 2)), token_parts), "dp", axis=1, tiled=True
    )
    token_parts = gather_pass(token_parts)
    all_tokens, gathered, mean, root, sent = norm_rows(
        gathered_pieces(token_parts), norm_gain, norm_shift, cotangent
    )
    grad_parts = gather_start(sent)

    full_dense = lax.all_gather(after(weight_dense, gathered), "dp", axis=1, tiled=True)
    active, slope = hidden_rows(gathered, full_up, bias_up)
    grad_parts, active = after((grad_parts, active))
    full_down = lax.all_gather(after(weight_down, grad_parts), "dp", axis=1, tiled=True)
    grad_parts = gather_pass(grad_parts)
    joined = joined_rows(after(gathered, active, grad_parts[:3]), full_qkv, bias_qkv, lanes)
    grad_parts, joined = after((grad_parts, joined))
    grad_rows, grad_mixed, grad_down = first_grads(
        gathered_pieces(grad_parts), active, full_dense
    )
    dense_parts = gather_start(after(full_dense, grad_mixed))
    grad_down_sum = lax.psum_scatter(grad_down, "dp", scatter_dimension=1, tiled=True)

    pairs = grad_mixed.shape[1] // PAIR
    part = attention(joined, grad_mixed, lanes, 0, pairs // 2)
    dense_parts, part = after((dense_parts, part))
    dense_parts = gather_pass(dense_parts)
    feed_cuts = feed_rows(after(active, part[0]), full_down)
    feed_cuts, dense_parts = after((feed_cuts, dense_parts))
    feed_parts = scatter_send(feed_cuts)
    grad_hidden, grad_up, bias_up_part = hidden_grads(
        after(grad_rows, feed_cuts), full_down, slope, gathered
    )
    grad_up, feed_parts = after((grad_up, feed_parts))
    grad_up_sum = lax.psum_scatter(
        after(grad_up, grad_down_sum), "dp", scatter_dimension=0, tiled=True
    )
    feed_parts = scatter_pass(scatter_fold(feed_parts))
    part = attention(after(joined, grad_up), grad_mixed, lanes, pairs // 2, pairs, part)
    mixed, grad_joined, bias_qkv_part = part
    mixed, grad_joined, feed_parts = after((mixed, grad_joined, feed_parts))

    mixed_parts = exchange_start(mixed)
    grad_qkv = qkv_grads(gathered, grad_joined)
    grad_qkv, mixed_parts = after((grad_qkv, mixed_parts))
    grad_dense = jnp.einsum(
        "tk,td->kd", after(mixed, grad_qkv), grad_rows, preferred_element_type=f32
    ).astype(low)
    own_mean = lax.dynamic_slice_in_dim(mean, tensor_index * local_rows, local_rows, 0)
    own_root = lax.dynamic_slice_in_dim(root, tensor_index * local_rows, local_rows, 0)
    own_mean, own_root, grad_dense = after((own_mean, own_root, grad_dense))
    grad_qkv_sum = lax.psum_scatter(
        after(grad_qkv, grad_up_sum, grad_dense), "dp", scatter_dimension=1, tiled=True
    )
    half = depth // 2
    sources = full_qkv, grad_hidden, full_up, all_tokens, mean, root
    *left_sums, left_cuts = normed_grads(after(grad_joined, grad_dense), *sources, 0, half)
    left_parts = scatter_send(left_cuts)
    *right_sums, right_cuts = normed_grads(after(grad_joined, left_cuts), *sources, half, depth)
    right_cuts, right_sums, left_parts = after((right_cuts, right_sums, left_parts))
    sums = jnp.concatenate(
        [left_sums[0][0], right_sums[0][0], left_sums[1][0], right_sums[1][0], out_part]
    ).reshape(-1, PAIR)
    right_parts = scatter_send(right_cuts)
    left_parts, sums = after((scatter_fold(left_parts), sums))
    over_group = exchange_sum(sums, "tensor")
    left_parts = scatter_pass(left_parts)
    block_out = finish_output(
        after(mixed_parts, right_cuts), dense_parts, tokens, bias_out, feed_parts
    )
    block_out, right_parts, left_parts, over_group = after(
        (block_out, right_parts, left_parts, over_group)
    )
    grad_dense_sum = lax.psum_scatter(
        after(grad_dense, grad_qkv_sum, block_out), "dp", scatter_dimension=1, tiled=True
    )
    right_parts = scatter_pass(scatter_fold(right_parts))
    bias_size = bias_qkv.size
    over_dp = jnp.concatenate(
        [over_group.reshape(-1), bias_qkv_part.reshape(-1), bias_up_part.reshape(-1)]
    ).reshape(-1, PAIR)
    over_dp = over_dp + swap(over_dp, "dp", 1)
    over_dp = exchange_sum(over_dp, "dp", 2).reshape(-1)
    grad_gain, grad_shift, grad_bias_out = over_dp[: 3 * depth].reshape(3, depth)
    grad_bias_qkv = over_dp[3 * depth : 3 * depth + bias_size].reshape(bias_qkv.shape)
    grad_bias_up = over_dp[3 * depth + bias_size :]
    grad_tokens = token_grads(
        left_parts, right_parts, tokens, cotangent, own_mean, own_root, norm_gain
    )
    return (
        block_out,
        grad_tokens,
        grad_gain,
        grad_shift,
        jnp.transpose(grad_qkv_sum, (1, 0, 2)).astype(f32),
        grad_bias_qkv,
        grad_dense_sum.astype(f32),
        grad_up_sum.astype(f32),
        grad_bias_up,
        grad_down_sum.astype(f32),
        grad_bias_out,
    )


def solution(mesh):
    in_specs = (
        P(("dp", "tensor"), None),
        P(),
        P(),
        P("dp", None, "tensor"),
        P(None, "tensor"),
        P("tensor", "dp"),
        P("dp", "tensor"),
        P("tensor"),
        P("tensor", "dp"),
        P(),
        P(("dp", "tensor"), None),
    )
    out_specs = (
        P(("dp", "tensor"), None),
        P(("dp", "tensor"), None),
        P(),
        P(),
        P("dp", None, "tensor"),
        P(None, "tensor"),
        P("tensor", "dp"),
        P("dp", "tensor"),
        P("tensor"),
        P("tensor", "dp"),
        P(),
    )
    return jax.shard_map(
        on_device, mesh=mesh, in_specs=in_specs, out_specs=out_specs, check_vma=False
    )
```

time: 688 us -> 611 us (0.89)
  matrix products: 121 us -> 10 us
  Pallas kernels: 303 us -> 389 us
  local copies, waits for them, and re-layouts: 54.6 us -> 21.8 us
  other arithmetic: 44.9 us -> 15.4 us
  waiting for transfers between devices: 92 us -> 103 us
    pallas_call x6 -> x14, Pallas kernels: 91.7 us -> 209 us  [the longest x2 48.8 us: normed_grads(): whole_call(kernel, [SMEM] + [ANY] * 5 + [VMEM] * 2, [VMEM, VMEM] + [ANY]...]
    dot_general x7 -> x1, matrix products: 121 us -> 10 us  [on_device(): jnp.einsum('tk,td->kd', after(mixed, grad_qkv), grad_rows, preferred_elem...]
    pallas_call x2, Pallas kernels: 143 us -> 112 us  [attention(): pl.pallas_call(body, grid=(last - first, block_count), in_specs=[row_bloc...]
    convert_element_type x6 -> x0, other arithmetic: 14.4 us -> none  [the longest x3 5.06 us: scatter_fold(): (wide(one_high) + wide(second_far)).astype(low.dtype)]
    dynamic_slice x4 -> x1, local copies, waits for them, and re-layouts: 16.3 us -> 1.88 us  [on_device(): lax.dynamic_slice_in_dim(root, tensor_index * local_rows, local_rows, 0)]
    slice x6 -> x0, local copies, waits for them, and re-layouts: 12.4 us -> none  [the longest x3 6.7 us: gather_pass(): one[:half]]
    add x5 -> x1, other arithmetic: 12.3 us -> 0.01 us  [on_device(): over_dp = over_dp + swap(over_dp, 'dp', 1)]
    all_gather x1, waiting for transfers between devices: 0.02 us -> 7.83 us  [on_device(): lax.all_gather(after(weight_dense, gathered), 'dp', axis=1, tiled=True)]
  transfers between devices with their start and end apart: 51 -> 48, of which waited for: 14 -> 19; matrix products, arithmetic and copies ran while one was open for 32% -> 8% of each run, Pallas kernels for 45% -> 65%
where the time goes in v3:
time: 611 us; the launch traced here: 602 us
  Pallas kernels  389 us (64%)
  waiting for transfers between devices  103 us (17%)
  starting transfers between devices  47.3 us (8%)
  local copies, waits for them, and re-layouts  21.8 us (4%)
  other arithmetic  15.4 us (3%)
  between operations  15 us (2%)
  matrix products  10 us (2%)
    pallas_call x2, Pallas kernels, attention(): pl.pallas_call(body, grid=(last - first, block_count), in_specs=[row_bloc...  112 us
    ppermute x40, waiting for transfers between devices, swap(): return lax.ppermute(value, axis, [(i, i ^ bit) for i in range(count)])  80.7 us
    pallas_call x2, Pallas kernels, normed_grads(): whole_call(kernel, [SMEM] + [ANY] * 5 + [VMEM] * 2, [VMEM, VMEM] + [ANY]...  48.8 us
    pallas_call x1, Pallas kernels, hidden_grads(): whole_call(hidden_grads_kernel, [ANY] * 4, [ANY, ANY, VMEM], [jax.ShapeDt...  48.3 us
    ppermute x40, starting transfers between devices, swap(): return lax.ppermute(value, axis, [(i, i ^ bit) for i in range(count)])  46.4 us
    pallas_call x1, Pallas kernels, hidden_rows(): pl.pallas_call(hidden_kernel, grid=(width // columns, rows // block), in_...  32.6 us
    pallas_call x1, Pallas kernels, first_grads(): whole_call(first_grads_kernel, [SMEM] + [ANY] * (2 + count), [ANY, VMEM,...  30.6 us
    pallas_call x1, Pallas kernels, feed_rows(): whole_call(functools.partial(feed_kernel, halves=halves), [SMEM] + [ANY]...  23.6 us
  transfers between devices with their start and end apart: 48, of which 19 were waited for; matrix products, arithmetic and copies ran while one was open for 8% of the time, Pallas kernels for 65%

profile of v3, /device:TPU:0, one launch (start us, length us, event | category | flops | bytes accessed | tf_op | source)
XLA Modules:
  0.0 602.3 jit_solution(9514386282456564483)
XLA Ops:
  8.0 3.0 collective-permute-start.1
  12.5 5.5 multiply_sine_fusion
  18.2 4.5 concatenate.17.below_ref.refs_6_
  22.6 4.4 concatenate.16.above_ref.refs_5_
  28.1 4.5 concatenate.15.cos_ref.refs_4_
  33.0 23.9 %collective-permute-done.1.two_ref.refs_2_ = bf16[512,2048]{1,0:T(8,128)(2,1)} collective-permute-done((bf16[512,2048]{1,0:T(8,128)(2,1)}, bf16[512,2048]{1,0:T(8,128)(2,1)}, u32[]{:S(2)}, u32[]{:S(2)}) %collective-permute-start.1) | collective-permute-done | bytes 2097184 | tf_op jit(solution)/shard_map/ppermute | solution.py:32
  58.5 3.7 shard_map.194
  64.7 21.4 %collective-permute-done.2.refs_3_ = bf16[256,2048]{1,0:T(8,128)(2,1)} collective-permute-done((bf16[256,2048]{1,0:T(8,128)(2,1)}, bf16[256,2048]{1,0:T(8,128)(2,1)}, u32[]{:S(2)}, u32[]{:S(2)}) %collective-permute-start.2) | collective-permute-done | bytes 1048608 | tf_op jit(solution)/shard_map/ppermute | solution.py:32
  86.5 12.5 %shard_map.195 = (bf16[2048,2048]{1,0:T(8,128)(2,1)}, bf16[2048,2048]{1,0:T(8,128)(2,1)}, f32[2048,1]{1,0:T(8,128)}, f32[2048,1]{1,0:T(8,128)}, bf16[512,2048]{1,0:T(8,128)(2,1)}) custom-call(s32[5]{0:T(128)} %stack.19.starts_ref, f32[1,2048]{1,0:T(1,128)} %bitcast.46, f32[1,2048]{1,0:T(1,128)} %bitcast.50, bf16[512,2048]{1,0:T(8,128)(2,1)} %refs_13_.1, ...), custom_call_target="tpu_custom_call" | custom-call | flops 1 | bytes 1 | tf_op jit(solution)/shard_map/pallas_call | solution.py:1122
  102.0 32.6 %shard_map.196 = (bf16[2048,2048]{1,0:T(8,128)(2,1)}, bf16[2048,2048]{1,0:T(8,128)(2,1)}) custom-call(bf16[2048,2048]{1,0:T(8,128)(2,1)} %get-tuple-element.204.x_ref.x, bf16[2048,2048]{1,0:T(8,128)(2,1)} %all-gather.5.cloned.1.call-done.w_ref.up, f32[1,2048]{1,0:T(1,128)} %bitcast.48), custom_call_target="tpu_custom_call" | custom-call | flops 1 | bytes 1 | tf_op jit(solution)/shard_map/pallas_call | solution.py:250
  134.6 10.1 %collective-permute-done.5.two_ref.refs_2_ = bf16[512,2048]{1,0:T(8,128)(2,1)} collective-permute-done((bf16[512,2048]{1,0:T(8,128)(2,1)}, bf16[512,2048]{1,0:T(8,128)(2,1)}, u32[]{:S(2)}, u32[]{:S(2)}) %collective-permute-start.5) | collective-permute-done | bytes 2097184 | tf_op jit(solution)/shard_map/ppermute | solution.py:32
  146.0 3.6 shard_map.197
  152.5 6.8 %all-gather.7.cloned.1.call-done.w_ref.qkv = bf16[3,2048,512]{2,1,0:T(8,128)(2,1)} async-done(((bf16[3,256,512]{2,1,0:T(8,128)(2,1)}), bf16[3,2048,512]{2,1,0:T(8,128)(2,1)}) %all-gather.7.cloned.1.call-update) | async-done | bytes 6291472 | tf_op jit(solution)/shard_map/all_gather | solution.py:1168
  159.3 23.3 %shard_map.198.refs_0_.refs_1_.refs_2_ = bf16[2048,1536]{1,0:T(8,128)(2,1)} custom-call(bf16[2048,2048]{1,0:T(8,128)(2,1)} %get-tuple-element.204.x_ref.x, bf16[3,2048,512]{2,1,0:T(8,128)(2,1)} %all-gather.7.cloned.1.call-done.w_ref.qkv, f32[3,1,512]{2,1,0:T(1,128)} %reshape.89.bias_ref, f32[2048,128]{1,0:T(8,128)} %concatenate.15.cos_ref.refs_4_, ...), custom_call_target="tpu_custom_call" | custom-call | flops 1 | bytes 1 | tf_op jit(solution)/shard_map/pallas_call | solution.py:217
  182.6 7.8 %all-gather.9.cloned.1.call-done.dense.refs_4_ = bf16[512,2048]{1,0:T(8,128)(2,1)} async-done(((bf16[512,256]{1,0:T(8,128)(2,1)}), bf16[512,2048]{1,0:T(8,128)(2,1)}) %all-gather.9.cloned.1.call-update) | async-done | bytes 2097168 | tf_op jit(solution)/shard_map/all_gather | solution.py:1177
  190.4 30.6 %shard_map.199 = (bf16[2048,2048]{1,0:T(8,128)(2,1)}, bf16[2048,512]{1,0:T(8,128)(2,1)}, bf16[2048,2048]{1,0:T(8,128)(2,1)}) custom-call(s32[5]{0:T(128)} %stack.19.starts_ref, bf16[2048,2048]{1,0:T(8,128)(2,1)} %get-tuple-element.223.active, bf16[512,2048]{1,0:T(8,128)(2,1)} %all-gather.9.cloned.1.call-done.dense.refs_4_, ...), custom_call_target="tpu_custom_call" | custom-call | flops 1 | bytes 1 | tf_op jit(solution)/shard_map/pallas_call | solution.py:391
  224.0 55.7 %shard_map.200 = (bf16[2048,512]{1,0:T(8,128)(2,1)}, bf16[3,2048,512]{2,1,0:T(8,128)(2,1)}, f32[3,1,512]{2,1,0:T(1,128)}) custom-call(bf16[2048,1536]{1,0:T(8,128)(2,1)} %shard_map.198.refs_0_.refs_1_.refs_2_, bf16[2048,1536]{1,0:T(8,128)(2,1)} %shard_map.198.refs_0_.refs_1_.refs_2_, bf16[2048,1536]{1,0:T(8,128)(2,1)} %shard_map.198.refs_0_.refs_1_.refs_2_, ...), custom_call_target="tpu_custom_call" | custom-call | flops 1 | bytes 1 | tf_op jit(solution)/shard_map/pallas_call | solution.py:1031
  279.7 3.9 shard_map.202
  285.7 23.6 %shard_map.201 = (bf16[256,2048]{1,0:T(8,128)(2,1)}, bf16[256,2048]{1,0:T(8,128)(2,1)}, bf16[256,2048]{1,0:T(8,128)(2,1)}, bf16[256,2048]{1,0:T(8,128)(2,1)}, bf...) custom-call(s32[4]{0:T(128)} %pad_add_fusion.starts_ref, ...), custom_call_target="tpu_custom_call" | custom-call | flops 1 | bytes 1 | tf_op jit(solution)/shard_map/pallas_call | solution.py:479
  313.4 48.3 %shard_map.203 = (bf16[2048,2048]{1,0:T(8,128)(2,1)}, bf16[2048,2048]{1,0:T(8,128)(2,1)}, f32[2,1,1024]{2,1,0:T(1,128)}) custom-call(bf16[2048,2048]{1,0:T(8,128)(2,1)} %get-tuple-element.246.grad_rows, bf16[2048,2048]{1,0:T(8,128)(2,1)} %all-gather.11.cloned.1.call-done.weight, bf16[2048,2048]{1,0:T(8,128)(2,1)} %get-tuple-element.247.slope, ...), custom_call_target="tpu_custom_call" | custom-call | flops 1 | bytes 1 | tf_op jit(solution)/shard_map/pallas_call | solution.py:592
  363.5 3.8 shard_map.205
  370.2 56.0 %shard_map.204 = (bf16[2048,512]{1,0:T(8,128)(2,1)}, bf16[3,2048,512]{2,1,0:T(8,128)(2,1)}, f32[3,1,512]{2,1,0:T(1,128)}) custom-call(bf16[2048,1536]{1,0:T(8,128)(2,1)} %shard_map.198.refs_0_.refs_1_.refs_2_, bf16[2048,1536]{1,0:T(8,128)(2,1)} %shard_map.198.refs_0_.refs_1_.refs_2_, ...), custom_call_target="tpu_custom_call", output_to_operand_aliasing={{0}: (7, {}), {1}: (8, {}), {2}: (9, {})} | custom-call | flops 1 | bytes 1 | tf_op jit(solution)/shard_map/pallas_call | solution.py:1031
  434.5 18.1 %shard_map.206 = bf16[3,2048,512]{2,1,0:T(8,128)(2,1)} custom-call(bf16[2048,2048]{1,0:T(8,128)(2,1)} %get-tuple-element.204.x_ref.x, bf16[3,2048,512]{2,1,0:T(8,128)(2,1)} %get-tuple-element.287.joined), custom_call_target="tpu_custom_call" | custom-call | flops 1 | bytes 1 | tf_op jit(solution)/shard_map/pallas_call | solution.py:650
  452.6 10.0 %convolution_convert_fusion = bf16[512,2048]{1,0:T(8,128)(2,1)} fusion(bf16[2048,512]{1,0:T(8,128)(2,1)} %get-tuple-element.274, bf16[2048,2048]{1,0:T(8,128)(2,1)} %get-tuple-element.246.grad_rows), kind=kOutput, calls=%fused_computation.1 | convolution fusion | flops 4296015872 | bytes 12582912 | tf_op jit(solution)/shard_map/tk,td->kd/dot_general | solution.py:1212
  462.7 24.8 %shard_map.207 = (f32[1,1024]{1,0:T(1,128)}, f32[1,1024]{1,0:T(1,128)}, bf16[256,1024]{1,0:T(8,128)(2,1)}, bf16[256,1024]{1,0:T(8,128)(2,1)}, bf16[256,1024]{1,0...) custom-call(s32[4]{0:T(128)} %pad_add_fusion.starts_ref, ...), custom_call_target="tpu_custom_call" | custom-call | flops 1 | bytes 1 | tf_op jit(solution)/shard_map/pallas_call | solution.py:759
  491.6 24.1 %shard_map.208 = (f32[1,1024]{1,0:T(1,128)}, f32[1,1024]{1,0:T(1,128)}, bf16[256,1024]{1,0:T(8,128)(2,1)}, bf16[256,1024]{1,0:T(8,128)(2,1)}, bf16[256,1024]{1,0...) custom-call(s32[4]{0:T(128)} %pad_add_fusion.starts_ref, ...), custom_call_target="tpu_custom_call" | custom-call | flops 1 | bytes 1 | tf_op jit(solution)/shard_map/pallas_call | solution.py:759
  525.1 5.6 collective-permute-done.32
  534.3 10.4 %shard_map.209 = bf16[512,2048]{1,0:T(8,128)(2,1)} custom-call(bf16[512,512]{1,0:T(8,128)(2,1)} %get-tuple-element.306.refs_0_, bf16[512,512]{1,0:T(8,128)(2,1)} %collective-permute-done.18.refs_1_, bf16[512,512]{1,0:T(8,128)(2,1)} %collective-permute-done.19.refs_2_, bf16[512,512]{1,0:T(8,128)(2,1)} %collective-permute-done.20.refs_3_, ...), custom_call_target="tpu_custom_call" | custom-call | flops 1 | bytes 1 | tf_op jit(solution)/shard_map/pallas_call | solution.py:809
  544.8 4.7 collective-permute-done.25.b_ref
  549.4 7.2 %collective-permute-done.27.refs_8_ = bf16[256,1024]{1,0:T(8,128)(2,1)} collective-permute-done((bf16[256,1024]{1,0:T(8,128)(2,1)}, bf16[256,1024]{1,0:T(8,128)(2,1)}, u32[]{:S(2)}, u32[]{:S(2)}) %collective-permute-start.27) | collective-permute-done | bytes 524320 | tf_op jit(solution)/shard_map/ppermute | solution.py:32
  574.2 9.2 %shard_map.212 = bf16[512,2048]{1,0:T(8,128)(2,1)} custom-call(bf16[256,1024]{1,0:T(8,128)(2,1)} %collective-permute-done.29.refs_0_, bf16[256,1024]{1,0:T(8,128)(2,1)} %collective-permute-done.30.refs_1_, bf16[256,1024]{1,0:T(8,128)(2,1)} %collective-permute-done.23.refs_2_, bf16[256,1024]{1,0:T(8,128)(2,1)} %collective-permute-done.24.refs_3_, ...), custom_call_target="tpu_custom_call" | custom-call | flops 1 | bytes 1 | tf_op jit(solution)/shard_map/pallas_call | solution.py:869
  587.7 5.6 reduce-scatter.11.cloned.1.call-done
  (143 shorter events, 78.1 us)
Async XLA Ops:
  7.2 94.8 %all-gather.5.cloned.1.call-start = ((), (), s32[]{:S(2)}) async-start(), calls=%async_computation.4 | async-start | bytes 9437184 | tf_op jit(solution)/shard_map/all_gather | solution.py:1163
  7.9 151.4 %all-gather.7.cloned.1.call-start = ((), (), s32[]{:S(2)}) async-start(), calls=%async_computation.5 | async-start | bytes 7077888 | tf_op jit(solution)/shard_map/all_gather | solution.py:1168
  8.0 49.0 %collective-permute-start.1 = (bf16[512,2048]{1,0:T(8,128)(2,1)}, bf16[512,2048]{1,0:T(8,128)(2,1)}, u32[]{:S(2)}, u32[]{:S(2)}) collective-permute-start(bf16[512,2048]{1,0:T(8,128)(2,1)} %refs_12_.1), channel_id=1, source_target_pairs={{0,2},{1,3},{2,0},{3,1},{4,6},{5,7},{6,4},{7,5},{8,10},{9,11},{10,... | collective-permute-start | bytes 6291464 | tf_op jit(solution)/shard_map/ppermute | solution.py:32
  11.0 47.4 %collective-permute-start = (bf16[512,2048]{1,0:T(8,128)(2,1)}, bf16[512,2048]{1,0:T(8,128)(2,1)}, u32[]{:S(2)}, u32[]{:S(2)}) collective-permute-start(bf16[512,2048]{1,0:T(8,128)(2,1)} %refs_12_.1), channel_id=1, source_target_pairs={{0,1},{1,0},{2,3},{3,2},{4,5},{5,4},{6,7},{7,6},{8,9},{9,8},{10,11... | collective-permute-start | bytes 6291464 | tf_op jit(solution)/shard_map/ppermute | solution.py:32
  58.4 132.0 %all-gather.9.cloned.1.call-start = ((), (), s32[]{:S(2)}) async-start(), calls=%async_computation.6 | async-start | bytes 2359296 | tf_op jit(solution)/shard_map/all_gather | solution.py:1177
  62.1 24.0 %collective-permute-start.2 = (bf16[256,2048]{1,0:T(8,128)(2,1)}, bf16[256,2048]{1,0:T(8,128)(2,1)}, u32[]{:S(2)}, u32[]{:S(2)}) collective-permute-start(bf16[256,2048]{1,0:T(8,128)(2,1)} %get-tuple-element.193), channel_id=1, source_target_pairs={{0,2},{1,3},{2,0},{3,1},{4,6},{5,7},{6,4},{7,5},{8,10},{9,11},{10,... | collective-permute-start | bytes 3145736 | tf_op jit(solution)/shard_map/ppermute | solution.py:32
  62.4 24.1 %collective-permute-start.3 = (bf16[256,2048]{1,0:T(8,128)(2,1)}, bf16[256,2048]{1,0:T(8,128)(2,1)}, u32[]{:S(2)}, u32[]{:S(2)}) collective-permute-start(bf16[256,2048]{1,0:T(8,128)(2,1)} %get-tuple-element.194), channel_id=1, source_target_pairs={{0,1},{1,0},{2,3},{3,2},{4,5},{5,4},{6,7},{7,6},{8,9},{9,8},{10,11... | collective-permute-start | bytes 3145736 | tf_op jit(solution)/shard_map/ppermute | solution.py:32
  99.0 186.6 %all-gather.11.cloned.1.call-start = ((), (), s32[]{:S(2)}) async-start(), calls=%async_computation.7 | async-start | bytes 9437184 | tf_op jit(solution)/shard_map/all_gather | solution.py:1180
  99.1 45.7 %collective-permute-start.5 = (bf16[512,2048]{1,0:T(8,128)(2,1)}, bf16[512,2048]{1,0:T(8,128)(2,1)}, u32[]{:S(2)}, u32[]{:S(2)}) collective-permute-start(bf16[512,2048]{1,0:T(8,128)(2,1)} %get-tuple-element.211.refs_0_), channel_id=1, source_target_pairs={{0,2},{1,3},{2,0},{3,1},{4,6},{5,7},{6,4},{7,5},{8,10},{9,11},{10,... | collective-permute-start | bytes 6291464 | tf_op jit(solution)/shard_map/ppermute | solution.py:32
  100.5 44.9 %collective-permute-start.4 = (bf16[512,2048]{1,0:T(8,128)(2,1)}, bf16[512,2048]{1,0:T(8,128)(2,1)}, u32[]{:S(2)}, u32[]{:S(2)}) collective-permute-start(bf16[512,2048]{1,0:T(8,128)(2,1)} %get-tuple-element.211.refs_0_), channel_id=1, source_target_pairs={{0,1},{1,0},{2,3},{3,2},{4,5},{5,4},{6,7},{7,6},{8,9},{9,8},{10,11... | collective-permute-start | bytes 6291464 | tf_op jit(solution)/shard_map/ppermute | solution.py:32
  145.4 218.0 %reduce-scatter.5.cloned.1.call-start = ((), (), s32[]{:S(2)}) async-start(), calls=%async_computation.8 | async-start | bytes 9437184 | tf_op jit(solution)/shard_map/reduce_scatter | solution.py:1188
  149.6 33.0 %collective-permute-start.6 = (bf16[256,2048]{1,0:T(8,128)(2,1)}, bf16[256,2048]{1,0:T(8,128)(2,1)}, u32[]{:S(2)}, u32[]{:S(2)}) collective-permute-start(bf16[256,2048]{1,0:T(8,128)(2,1)} %get-tuple-element.201), channel_id=1, source_target_pairs={{0,2},{1,3},{2,0},{3,1},{4,6},{5,7},{6,4},{7,5},{8,10},{9,11},{10,... | collective-permute-start | bytes 3145736 | tf_op jit(solution)/shard_map/ppermute | solution.py:32
  150.7 31.9 %collective-permute-start.7 = (bf16[256,2048]{1,0:T(8,128)(2,1)}, bf16[256,2048]{1,0:T(8,128)(2,1)}, u32[]{:S(2)}, u32[]{:S(2)}) collective-permute-start(bf16[256,2048]{1,0:T(8,128)(2,1)} %get-tuple-element.202), channel_id=1, source_target_pairs={{0,1},{1,0},{2,3},{3,2},{4,5},{5,4},{6,7},{7,6},{8,9},{9,8},{10,11... | collective-permute-start | bytes 3145736 | tf_op jit(solution)/shard_map/ppermute | solution.py:32
  221.1 241.6 %reduce-scatter.7.cloned.1.call-start = ((), (), s32[]{:S(2)}) async-start(), calls=%async_computation.9 | async-start | bytes 9437184 | tf_op jit(solution)/shard_map/reduce_scatter | solution.py:1201
  221.3 58.4 %collective-permute-start.9 = (bf16[512,2048]{1,0:T(8,128)(2,1)}, bf16[512,2048]{1,0:T(8,128)(2,1)}, u32[]{:S(2)}, u32[]{:S(2)}) collective-permute-start(bf16[512,2048]{1,0:T(8,128)(2,1)} %all-gather.9.cloned.1.call-done.dense.refs_4_), channel_id=1, source_target_pairs={{0,2},{1,3},{2,0},{3,1},{4,6},{5,7},{6,4},{7,5},{8,10},{9,11},{10,... | collective-permute-start | bytes 6291464 | tf_op jit(solution)/shard_map/ppermute | solution.py:32
  222.6 57.2 %collective-permute-start.8 = (bf16[512,2048]{1,0:T(8,128)(2,1)}, bf16[512,2048]{1,0:T(8,128)(2,1)}, u32[]{:S(2)}, u32[]{:S(2)}) collective-permute-start(bf16[512,2048]{1,0:T(8,128)(2,1)} %all-gather.9.cloned.1.call-done.dense.refs_4_), channel_id=1, source_target_pairs={{0,1},{1,0},{2,3},{3,2},{4,5},{5,4},{6,7},{7,6},{8,9},{9,8},{10,11... | collective-permute-start | bytes 6291464 | tf_op jit(solution)/shard_map/ppermute | solution.py:32
  283.6 25.6 %collective-permute-start.10 = (bf16[256,2048]{1,0:T(8,128)(2,1)}, bf16[256,2048]{1,0:T(8,128)(2,1)}, u32[]{:S(2)}, u32[]{:S(2)}) collective-permute-start(bf16[256,2048]{1,0:T(8,128)(2,1)} %get-tuple-element.236), channel_id=1, source_target_pairs={{0,2},{1,3},{2,0},{3,1},{4,6},{5,7},{6,4},{7,5},{8,10},{9,11},{10,... | collective-permute-start | bytes 3145736 | tf_op jit(solution)/shard_map/ppermute | solution.py:32
  284.7 24.6 %collective-permute-start.11 = (bf16[256,2048]{1,0:T(8,128)(2,1)}, bf16[256,2048]{1,0:T(8,128)(2,1)}, u32[]{:S(2)}, u32[]{:S(2)}) collective-permute-start(bf16[256,2048]{1,0:T(8,128)(2,1)} %get-tuple-element.237), channel_id=1, source_target_pairs={{0,1},{1,0},{2,3},{3,2},{4,5},{5,4},{6,7},{7,6},{8,9},{9,8},{10,11... | collective-permute-start | bytes 3145736 | tf_op jit(solution)/shard_map/ppermute | solution.py:32
  309.3 52.4 %collective-permute-start.12 = (bf16[256,2048]{1,0:T(8,128)(2,1)}, bf16[256,2048]{1,0:T(8,128)(2,1)}, u32[]{:S(2)}, u32[]{:S(2)}) collective-permute-start(bf16[256,2048]{1,0:T(8,128)(2,1)} %get-tuple-element.238), channel_id=1, source_target_pairs={{0,1},{1,0},{2,3},{3,2},{4,5},{5,4},{6,7},{7,6},{8,9},{9,8},{10,11... | collective-permute-start | bytes 3145736 | tf_op jit(solution)/shard_map/ppermute | solution.py:32
  311.1 50.6 %collective-permute-start.13 = (bf16[256,2048]{1,0:T(8,128)(2,1)}, bf16[256,2048]{1,0:T(8,128)(2,1)}, u32[]{:S(2)}, u32[]{:S(2)}) collective-permute-start(bf16[256,2048]{1,0:T(8,128)(2,1)} %get-tuple-element.239), channel_id=1, source_target_pairs={{0,2},{1,3},{2,0},{3,1},{4,6},{5,7},{6,4},{7,5},{8,10},{9,11},{10,... | collective-permute-start | bytes 3145736 | tf_op jit(solution)/shard_map/ppermute | solution.py:32
  312.0 49.7 %collective-permute-start.14 = (bf16[256,2048]{1,0:T(8,128)(2,1)}, bf16[256,2048]{1,0:T(8,128)(2,1)}, u32[]{:S(2)}, u32[]{:S(2)}) collective-permute-start(bf16[256,2048]{1,0:T(8,128)(2,1)} %get-tuple-element.240), channel_id=1, source_target_pairs={{0,1},{1,0},{2,3},{3,2},{4,5},{5,4},{6,7},{7,6},{8,9},{9,8},{10,11... | collective-permute-start | bytes 3145736 | tf_op jit(solution)/shard_map/ppermute | solution.py:32
  313.1 48.6 %collective-permute-start.15 = (bf16[256,2048]{1,0:T(8,128)(2,1)}, bf16[256,2048]{1,0:T(8,128)(2,1)}, u32[]{:S(2)}, u32[]{:S(2)}) collective-permute-start(bf16[256,2048]{1,0:T(8,128)(2,1)} %get-tuple-element.243), channel_id=1, source_target_pairs={{0,2},{1,3},{2,0},{3,1},{4,6},{5,7},{6,4},{7,5},{8,10},{9,11},{10,... | collective-permute-start | bytes 3145736 | tf_op jit(solution)/shard_map/ppermute | solution.py:32
  363.5 193.2 %reduce-scatter.9.cloned.1.call-start = ((), (), s32[]{:S(2)}) async-start(), calls=%async_computation.10 | async-start | bytes 7077888 | tf_op jit(solution)/shard_map/reduce_scatter | solution.py:1218
  367.3 58.9 %collective-permute-start.16 = (bf16[256,2048]{1,0:T(8,128)(2,1)}, bf16[256,2048]{1,0:T(8,128)(2,1)}, u32[]{:S(2)}, u32[]{:S(2)}) collective-permute-start(bf16[256,2048]{1,0:T(8,128)(2,1)} %get-tuple-element.259), channel_id=1, source_target_pairs={{0,2},{1,3},{2,0},{3,1},{4,6},{5,7},{6,4},{7,5},{8,10},{9,11},{10,... | collective-permute-start | bytes 3145736 | tf_op jit(solution)/shard_map/ppermute | solution.py:32
  368.8 57.4 %collective-permute-start.17 = (bf16[256,2048]{1,0:T(8,128)(2,1)}, bf16[256,2048]{1,0:T(8,128)(2,1)}, u32[]{:S(2)}, u32[]{:S(2)}) collective-permute-start(bf16[256,2048]{1,0:T(8,128)(2,1)} %get-tuple-element.260), channel_id=1, source_target_pairs={{0,1},{1,0},{2,3},{3,2},{4,5},{5,4},{6,7},{7,6},{8,9},{9,8},{10,11... | collective-permute-start | bytes 3145736 | tf_op jit(solution)/shard_map/ppermute | solution.py:32
  462.6 130.6 %reduce-scatter.11.cloned.1.call-start = ((), (), s32[]{:S(2)}) async-start(), calls=%async_computation.11 | async-start | bytes 2359296 | tf_op jit(solution)/shard_map/reduce_scatter | solution.py:1240
  487.5 28.2 %collective-permute-start.21 = (bf16[256,1024]{1,0:T(8,128)(2,1)}, bf16[256,1024]{1,0:T(8,128)(2,1)}, u32[]{:S(2)}, u32[]{:S(2)}) collective-permute-start(bf16[256,1024]{1,0:T(8,128)(2,1)} %get-tuple-element.279), channel_id=1, source_target_pairs={{0,1},{1,0},{2,3},{3,2},{4,5},{5,4},{6,7},{7,6},{8,9},{9,8},{10,11... | collective-permute-start | bytes 1572872 | tf_op jit(solution)/shard_map/ppermute | solution.py:32
  488.5 27.2 %collective-permute-start.22 = (bf16[256,1024]{1,0:T(8,128)(2,1)}, bf16[256,1024]{1,0:T(8,128)(2,1)}, u32[]{:S(2)}, u32[]{:S(2)}) collective-permute-start(bf16[256,1024]{1,0:T(8,128)(2,1)} %get-tuple-element.280), channel_id=1, source_target_pairs={{0,2},{1,3},{2,0},{3,1},{4,6},{5,7},{6,4},{7,5},{8,10},{9,11},{10,... | collective-permute-start | bytes 1572872 | tf_op jit(solution)/shard_map/ppermute | solution.py:32
  488.9 26.8 %collective-permute-start.23 = (bf16[256,1024]{1,0:T(8,128)(2,1)}, bf16[256,1024]{1,0:T(8,128)(2,1)}, u32[]{:S(2)}, u32[]{:S(2)}) collective-permute-start(bf16[256,1024]{1,0:T(8,128)(2,1)} %get-tuple-element.281), channel_id=1, source_target_pairs={{0,1},{1,0},{2,3},{3,2},{4,5},{5,4},{6,7},{7,6},{8,9},{9,8},{10,11... | collective-permute-start | bytes 1572872 | tf_op jit(solution)/shard_map/ppermute | solution.py:32
  490.6 25.2 %collective-permute-start.24 = (bf16[256,1024]{1,0:T(8,128)(2,1)}, bf16[256,1024]{1,0:T(8,128)(2,1)}, u32[]{:S(2)}, u32[]{:S(2)}) collective-permute-start(bf16[256,1024]{1,0:T(8,128)(2,1)} %get-tuple-element.284), channel_id=1, source_target_pairs={{0,2},{1,3},{2,0},{3,1},{4,6},{5,7},{6,4},{7,5},{8,10},{9,11},{10,... | collective-permute-start | bytes 1572872 | tf_op jit(solution)/shard_map/ppermute | solution.py:32
  524.6 24.9 %collective-permute-start.25 = (bf16[256,1024]{1,0:T(8,128)(2,1)}, bf16[256,1024]{1,0:T(8,128)(2,1)}, u32[]{:S(2)}, u32[]{:S(2)}) collective-permute-start(bf16[256,1024]{1,0:T(8,128)(2,1)} %get-tuple-element.298), channel_id=1, source_target_pairs={{0,1},{1,0},{2,3},{3,2},{4,5},{5,4},{6,7},{7,6},{8,9},{9,8},{10,11... | collective-permute-start | bytes 1572872 | tf_op jit(solution)/shard_map/ppermute | solution.py:32
  532.3 24.4 %collective-permute-start.27 = (bf16[256,1024]{1,0:T(8,128)(2,1)}, bf16[256,1024]{1,0:T(8,128)(2,1)}, u32[]{:S(2)}, u32[]{:S(2)}) collective-permute-start(bf16[256,1024]{1,0:T(8,128)(2,1)} %get-tuple-element.300), channel_id=1, source_target_pairs={{0,1},{1,0},{2,3},{3,2},{4,5},{5,4},{6,7},{7,6},{8,9},{9,8},{10,11... | collective-permute-start | bytes 1572872 | tf_op jit(solution)/shard_map/ppermute | solution.py:32
  (25 other events, 295.8 us)
Sparse Core Ops, SparseCore 0:
  9.6 84.7 all-gather.4
  96.0 63.2 all-gather.6
  160.9 29.5 all-gather.8
  191.9 81.5 all-gather.10
  275.6 87.8 reduce-scatter.4
  365.6 87.9 reduce-scatter.6
  462.8 68.5 reduce-scatter.8
  556.8 36.4 reduce-scatter.10

commit v4 on v3

--- a/solution.py
+++ b/solution.py
@@ -314,10 +314,10 @@
         write(step, step % 2).wait()
 
 
-def first_grads_kernel(starts_ref, active, dense, *refs):
-    count = len(refs) - 11
+def first_grads_kernel(starts_ref, active, *refs):
+    count = len(refs) - 9
     pieces = refs[:count]
-    rows_out, mixed_out, down_out, grad_buf, active_buf, dense_buf, tiles = refs[count:-4]
+    rows_out, down_out, grad_buf, active_buf, tiles = refs[count:-4]
     piece_sems, load_sems, row_sems, tile_sems = refs[-4:]
     _, rows, half = grad_buf.shape
     blocks, _, block = active_buf.shape
@@ -341,32 +341,26 @@
             grad_buf.at[side], rows_out.at[:, pl.ds(side * half, half)], row_sems.at[side]
         )
 
-    dense_copy = pltpu.make_async_copy(dense, dense_buf, load_sems.at[blocks])
-    dense_copy.start()
-    for slot in range(count):
+    active_copy(0).start()
+    for side in range(2):
+        for slot in range(count):
+            piece_copy(slot, side).start()
+    for index in range(1, blocks):
+        active_copy(index).start()
+
+    def compute(step):
+        for index in range(blocks):
+            pl.when(step == 2 * index)(active_copy(index).wait)
         for side in range(2):
-            piece_copy(slot, side).start()
-    for index in range(blocks):
-        active_copy(index).start()
-    dense_copy.wait()
-    for slot in range(count):
-        for side in range(2):
-            piece_copy(slot, side).wait()
-        size = pieces[slot].shape[0]
-        chunk = min(512, size)
-
-        @pl.loop(0, size // chunk)
-        def _(step, slot=slot, chunk=chunk):
-            here = pl.ds(pl.multiple_of(starts_ref[slot] + step * chunk, chunk), chunk)
-            mixed_out[here, :] = (
-                nt_dot(grad_buf[0, here, :], dense_buf[:, :half])
-                + nt_dot(grad_buf[1, here, :], dense_buf[:, half:])
-            ).astype(mixed_out.dtype)
-
-    for side in range(2):
-        row_copy(side).start()
-    for index in range(blocks):
-        active_copy(index).wait()
+
+            @pl.when(step == side)
+            def _(side=side):
+                for slot in range(count):
+                    piece_copy(slot, side).wait()
+                row_copy(side).start()
+
+        return tn_dot(active_buf[lax.div(step, 2)], grad_buf[lax.rem(step, 2)])
+
     tile_loop(
         2 * blocks,
         tiles,
@@ -375,39 +369,37 @@
             pl.ds(pl.multiple_of(lax.div(step, 2) * block, block), block),
             pl.ds(pl.multiple_of(lax.rem(step, 2) * half, half), half),
         ],
-        lambda step: tn_dot(active_buf[lax.div(step, 2)], grad_buf[lax.rem(step, 2)]),
+        compute,
     )
     for side in range(2):
         row_copy(side).wait()
 
 
-def first_grads(pieces, active, dense):
+def first_grads(pieces, active):
     low = jnp.bfloat16
     rows, hidden = active.shape
-    width, depth = dense.shape
+    depth = pieces[0][1].shape[1]
     half, block = depth // 2, min(512, hidden)
     count = len(pieces)
     starts = jnp.stack([jnp.asarray(start, jnp.int32) for start, _ in pieces])
     return whole_call(
         first_grads_kernel,
-        [SMEM] + [ANY] * (2 + count),
-        [ANY, VMEM, ANY],
+        [SMEM] + [ANY] * (1 + count),
+        [ANY, ANY],
         [
             jax.ShapeDtypeStruct((rows, depth), low),
-            jax.ShapeDtypeStruct((rows, width), low),
             jax.ShapeDtypeStruct((hidden, depth), low),
         ],
         [
             pltpu.VMEM((2, rows, half), low),
             pltpu.VMEM((hidden // block, rows, block), low),
-            pltpu.VMEM((width, depth), low),
             pltpu.VMEM((2, block, half), low),
             pltpu.SemaphoreType.DMA((count, 2)),
-            pltpu.SemaphoreType.DMA((hidden // block + 1,)),
+            pltpu.SemaphoreType.DMA((hidden // block,)),
             pltpu.SemaphoreType.DMA((2,)),
             pltpu.SemaphoreType.DMA((2,)),
         ],
-    )(starts, active, dense, *[piece for _, piece in pieces])
+    )(starts, active, *[piece for _, piece in pieces])
 
 
 def feed_kernel(starts_ref, active, weight, *refs, halves):
@@ -613,28 +605,42 @@
     )(grad_rows, weight, slope, x)
 
 
-def qkv_grads_kernel(x, joined, out, x_buf, joined_buf, tiles, x_sems, joined_sems, tile_sems):
-    blocks, _, block = x_buf.shape
-    x_loads = [
-        pltpu.make_async_copy(columns_of(x, i, block), x_buf.at[i], x_sems.at[i])
-        for i in range(blocks)
-    ]
-    joined_loads = [
-        pltpu.make_async_copy(joined.at[i], joined_buf.at[i], joined_sems.at[i]) for i in range(3)
-    ]
-    joined_loads[0].start()
-    for copy in x_loads + joined_loads[1:]:
-        copy.start()
+def last_grads_kernel(
+    x, joined, grad_rows, mixed, out, x_buf, joined_buf, tiles, x_sems, joined_sems, tile_sems
+):
+    blocks = x_buf.shape[0] // 2
+    block = x_buf.shape[2]
+
+    def x_load(index):
+        source = x if index < blocks else grad_rows
+        return pltpu.make_async_copy(
+            columns_of(source, index % blocks, block), x_buf.at[index], x_sems.at[index]
+        )
+
+    def joined_load(slot):
+        source = joined.at[slot] if slot < 3 else mixed
+        return pltpu.make_async_copy(source, joined_buf.at[slot], joined_sems.at[slot])
+
+    joined_load(0).start()
+    for index in range(blocks):
+        x_load(index).start()
+    for slot in range(1, 4):
+        joined_load(slot).start()
+    for index in range(blocks, 2 * blocks):
+        x_load(index).start()
 
     def compute(step):
-        for index in range(3):
-            pl.when(step == index * blocks)(joined_loads[index].wait)
+        for slot in range(4):
+            pl.when(step == slot * blocks)(joined_load(slot).wait)
         for index in range(blocks):
-            pl.when(step == index)(x_loads[index].wait)
-        return tn_dot(x_buf[lax.rem(step, blocks)], joined_buf[lax.div(step, blocks)])
+            pl.when(step == index)(x_load(index).wait)
+            pl.when(step == 3 * blocks + index)(x_load(blocks + index).wait)
+        slot = lax.div(step, blocks)
+        index = lax.rem(step, blocks) + blocks * lax.div(slot, 3)
+        return tn_dot(x_buf[index], joined_buf[slot])
 
     tile_loop(
-        3 * blocks,
+        4 * blocks,
         tiles,
         tile_sems,
         lambda step: rows_of(out.at[lax.div(step, blocks)], lax.rem(step, blocks), block),
@@ -642,25 +648,25 @@
     )
 
 
-def qkv_grads(x, joined):
+def last_grads(x, joined, grad_rows, mixed):
     low = jnp.bfloat16
     rows, depth = x.shape
     width = joined.shape[2]
     block = min(1024, depth)
     return whole_call(
-        qkv_grads_kernel,
-        [ANY] * 2,
+        last_grads_kernel,
+        [ANY] * 4,
         ANY,
-        jax.ShapeDtypeStruct((3, depth, width), low),
+        jax.ShapeDtypeStruct((4, depth, width), low),
         [
-            pltpu.VMEM((depth // block, rows, block), low),
-            pltpu.VMEM((3, rows, width), low),
+            pltpu.VMEM((2 * depth // block, rows, block), low),
+            pltpu.VMEM((4, rows, width), low),
             pltpu.VMEM((2, block, width), low),
-            pltpu.SemaphoreType.DMA((depth // block,)),
-            pltpu.SemaphoreType.DMA((3,)),
+            pltpu.SemaphoreType.DMA((2 * depth // block,)),
+            pltpu.SemaphoreType.DMA((4,)),
             pltpu.SemaphoreType.DMA((2,)),
         ],
-    )(x, joined)
+    )(x, joined, grad_rows, mixed)
 
 
 def normed_grads_kernel(
@@ -820,39 +826,30 @@
     )(*mixed_parts, *dense_parts, tokens, bias.reshape(1, depth), *feed_parts)
 
 
-def token_grads_kernel(*refs):
+def token_grads_kernel(*refs, steps):
     left, right = refs[:6], refs[6:12]
     token_ref, grad_ref, mean_ref, root_ref, gain_ref, out_ref = refs[12:]
-    half = left[4].shape[0]
     split = left[4].shape[1]
-    chunk = min(32, half)
-    for upper in range(2):
-        chosen = [(side[4 + upper], side[2 + upper], side[upper]) for side in (left, right)]
-
-        @pl.loop(0, half // chunk)
-        def _(step, chosen=chosen, upper=upper):
-            there = pl.ds(pl.multiple_of(step * chunk, chunk), chunk)
-            here = pl.ds(pl.multiple_of(upper * half + step * chunk, chunk), chunk)
-            scaled = []
-            hats = []
-            for side, parts in enumerate(chosen):
-                columns = slice(side * split, (side + 1) * split)
-                total = sum(wide(part[there, :]) for part in parts)
-                scaled.append(total * gain_ref[:, columns])
-                hats.append(
-                    (wide(token_ref[here, columns]) - mean_ref[here, :]) * root_ref[here, :]
-                )
-            count = 2 * split
-            mean = sum(jnp.sum(v, axis=-1, keepdims=True) for v in scaled) / count
-            slant = (
-                sum(jnp.sum(v * h, axis=-1, keepdims=True) for v, h in zip(scaled, hats)) / count
-            )
-            for side in range(2):
-                columns = slice(side * split, (side + 1) * split)
-                grad = root_ref[here, :] * (scaled[side] - mean - hats[side] * slant)
-                out_ref[here, columns] = (wide(grad_ref[here, columns]) + grad).astype(
-                    out_ref.dtype
-                )
+    mean_own, root_own = mean_ref[...], root_ref[...]
+
+    def rows_of_half(upper):
+        scaled, hats = [], []
+        for side, parts in enumerate((left, right)):
+            columns = slice(side * split, (side + 1) * split)
+            total = sum(wide(parts[at + upper][...]) for at in (4, 2, 0))
+            scaled.append(total * gain_ref[:, columns])
+            hats.append((wide(token_ref[:, columns]) - mean_own) * root_own)
+        count = 2 * split
+        mean = sum(jnp.sum(v, axis=-1, keepdims=True) for v in scaled) / count
+        slant = sum(jnp.sum(v * h, axis=-1, keepdims=True) for v, h in zip(scaled, hats)) / count
+        for side in range(2):
+            columns = slice(side * split, (side + 1) * split)
+            grad = root_own * (scaled[side] - mean - hats[side] * slant)
+            out_ref[:, columns] = (wide(grad_ref[:, columns]) + grad).astype(out_ref.dtype)
+
+    step = pl.program_id(0)
+    pl.when(step < steps)(lambda: rows_of_half(0))
+    pl.when(step >= steps)(lambda: rows_of_half(1))
 
 
 def token_grads(left_parts, right_parts, tokens, cotangent, mean, root, gain):
@@ -866,8 +863,20 @@
             - hat * jnp.mean(scaled * hat, axis=-1, keepdims=True)
         )
         return (wide(cotangent) + grad_input).astype(tokens.dtype)
+    half, split = left_parts[4].shape
+    rows, depth = tokens.shape
+    chunk = min(64, half)
+    steps = half // chunk
+    low_part = pl.BlockSpec((chunk, split), lambda i: (jnp.minimum(i, steps - 1), 0))
+    high_part = pl.BlockSpec((chunk, split), lambda i: (jnp.maximum(i - steps, 0), 0))
+    row_block = pl.BlockSpec((chunk, depth), lambda i: (i, 0))
+    thin = pl.BlockSpec((chunk, 1), lambda i: (i, 0))
     return pl.pallas_call(
-        token_grads_kernel,
+        functools.partial(token_grads_kernel, steps=steps),
+        grid=(rows // chunk,),
+        in_specs=[low_part, high_part] * 6
+        + [row_block, row_block, thin, thin, pl.BlockSpec((1, depth), lambda i: (0, 0))],
+        out_specs=row_block,
         out_shape=jax.ShapeDtypeStruct(tokens.shape, tokens.dtype),
         compiler_params=pltpu.CompilerParams(vmem_limit_bytes=VMEM_BYTES),
         cost_estimate=SHORT,
@@ -950,11 +959,19 @@
             top_buf[head, 1] = total
             out_buf[parts[head], :] = out
 
-    weigh(rows, step, True)
-
-    @pl.loop(0, step)
-    def _(index):
-        weigh(pl.ds(pl.multiple_of(index * block, block), block), index, False)
+    def over_blocks(act):
+        act(rows, step, True)
+
+        @pl.when(lax.rem(step, 2) == 1)
+        def _():
+            act(pl.ds(pl.multiple_of((step - 1) * block, block), block), step - 1, False)
+
+        @pl.loop(0, lax.div(step, 2))
+        def _(index):
+            start = pl.multiple_of(index * 2 * block, 2 * block)
+            act(pl.ds(start, 2 * block), 2 * index, False)
+
+    over_blocks(weigh)
 
     grads_across = grads.T.astype(jnp.float32)
     inner, share = [], []
@@ -993,12 +1010,7 @@
         value_total[there, :] += value_parts[0] + value_parts[1]
         key_total[there, :] += key_parts[0] + key_parts[1]
 
-    differentiate(rows, step, True)
-
-    @pl.loop(0, step)
-    def _(index):
-        differentiate(pl.ds(pl.multiple_of(index * block, block), block), index, False)
-
+    over_blocks(differentiate)
     query_total[rows, :] = across_buf[...].T
 
     @pl.when(step == block_count - 1)
@@ -1175,15 +1187,19 @@
     grad_parts = gather_start(sent)
 
     full_dense = lax.all_gather(after(weight_dense, gathered), "dp", axis=1, tiled=True)
+    own_mean = lax.dynamic_slice_in_dim(mean, tensor_index * local_rows, local_rows, 0)
+    own_root = lax.dynamic_slice_in_dim(root, tensor_index * local_rows, local_rows, 0)
     active, slope = hidden_rows(gathered, full_up, bias_up)
+    own_mean, own_root, active = after((own_mean, own_root, active))
     grad_parts, active = after((grad_parts, active))
     full_down = lax.all_gather(after(weight_down, grad_parts), "dp", axis=1, tiled=True)
     grad_parts = gather_pass(grad_parts)
     joined = joined_rows(after(gathered, active, grad_parts[:3]), full_qkv, bias_qkv, lanes)
     grad_parts, joined = after((grad_parts, joined))
-    grad_rows, grad_mixed, grad_down = first_grads(
-        gathered_pieces(grad_parts), active, full_dense
-    )
+    grad_rows, grad_down = first_grads(gathered_pieces(grad_parts), active)
+    grad_mixed = jnp.einsum(
+        "td,kd->tk", grad_rows, after(full_dense, grad_down), preferred_element_type=f32
+    ).astype(low)
     dense_parts = gather_start(after(full_dense, grad_mixed))
     grad_down_sum = lax.psum_scatter(grad_down, "dp", scatter_dimension=1, tiled=True)
 
@@ -1198,29 +1214,24 @@
         after(grad_rows, feed_cuts), full_down, slope, gathered
     )
     grad_up, feed_parts = after((grad_up, feed_parts))
+    feed_parts = scatter_fold(feed_parts)
     grad_up_sum = lax.psum_scatter(
-        after(grad_up, grad_down_sum), "dp", scatter_dimension=0, tiled=True
-    )
-    feed_parts = scatter_pass(scatter_fold(feed_parts))
+        after(grad_up, grad_down_sum, feed_parts[:2]), "dp", scatter_dimension=0, tiled=True
+    )
+    feed_parts = scatter_pass(feed_parts)
     part = attention(after(joined, grad_up), grad_mixed, lanes, pairs // 2, pairs, part)
     mixed, grad_joined, bias_qkv_part = part
     mixed, grad_joined, feed_parts = after((mixed, grad_joined, feed_parts))
 
     mixed_parts = exchange_start(mixed)
-    grad_qkv = qkv_grads(gathered, grad_joined)
-    grad_qkv, mixed_parts = after((grad_qkv, mixed_parts))
-    grad_dense = jnp.einsum(
-        "tk,td->kd", after(mixed, grad_qkv), grad_rows, preferred_element_type=f32
-    ).astype(low)
-    own_mean = lax.dynamic_slice_in_dim(mean, tensor_index * local_rows, local_rows, 0)
-    own_root = lax.dynamic_slice_in_dim(root, tensor_index * local_rows, local_rows, 0)
-    own_mean, own_root, grad_dense = after((own_mean, own_root, grad_dense))
-    grad_qkv_sum = lax.psum_scatter(
-        after(grad_qkv, grad_up_sum, grad_dense), "dp", scatter_dimension=1, tiled=True
+    grad_last = last_grads(gathered, grad_joined, grad_rows, mixed)
+    grad_last, mixed_parts = after((grad_last, mixed_parts))
+    grad_last_sum = lax.psum_scatter(
+        after(grad_last, grad_up_sum), "dp", scatter_dimension=1, tiled=True
     )
     half = depth // 2
     sources = full_qkv, grad_hidden, full_up, all_tokens, mean, root
-    *left_sums, left_cuts = normed_grads(after(grad_joined, grad_dense), *sources, 0, half)
+    *left_sums, left_cuts = normed_grads(after(grad_joined, grad_last), *sources, 0, half)
     left_parts = scatter_send(left_cuts)
     *right_sums, right_cuts = normed_grads(after(grad_joined, left_cuts), *sources, half, depth)
     right_cuts, right_sums, left_parts = after((right_cuts, right_sums, left_parts))
@@ -1237,9 +1248,6 @@
     block_out, right_parts, left_parts, over_group = after(
         (block_out, right_parts, left_parts, over_group)
     )
-    grad_dense_sum = lax.psum_scatter(
-        after(grad_dense, grad_qkv_sum, block_out), "dp", scatter_dimension=1, tiled=True
-    )
     right_parts = scatter_pass(scatter_fold(right_parts))
     bias_size = bias_qkv.size
     over_dp = jnp.concatenate(
@@ -1250,6 +1258,10 @@
     grad_gain, grad_shift, grad_bias_out = over_dp[: 3 * depth].reshape(3, depth)
     grad_bias_qkv = over_dp[3 * depth : 3 * depth + bias_size].reshape(bias_qkv.shape)
     grad_bias_up = over_dp[3 * depth + bias_size :]
+    last = jnp.transpose(grad_last_sum, (1, 0, 2)).astype(f32)
+    ready = grad_up_sum.astype(f32), grad_down_sum.astype(f32), last
+    ready, left_parts = after((ready, left_parts))
+    grad_up_sum, grad_down_sum, last = ready
     grad_tokens = token_grads(
         left_parts, right_parts, tokens, cotangent, own_mean, own_root, norm_gain
     )
@@ -1258,12 +1270,12 @@
         grad_tokens,
         grad_gain,
         grad_shift,
-        jnp.transpose(grad_qkv_sum, (1, 0, 2)).astype(f32),
+        last[:, :3],
         grad_bias_qkv,
-        grad_dense_sum.astype(f32),
-        grad_up_sum.astype(f32),
+        jnp.transpose(last[:, 3]),
+        grad_up_sum,
         grad_bias_up,
-        grad_down_sum.astype(f32),
+        grad_down_sum,
         grad_bias_out,
     )
 

time: 611 us -> 595 us (0.974)
  waiting for transfers between devices: 103 us -> 90.8 us
    all_gather x1, waiting for transfers between devices: 7.83 us -> 0.02 us  [on_device(): lax.all_gather(after(weight_dense, gathered), 'dp', axis=1, tiled=True)]
  transfers between devices with their start and end apart: 48 -> 47, of which waited for: 19 -> 17; matrix products, arithmetic and copies ran while one was open for 8% -> 8% of each run, Pallas kernels for 65% -> 64%
where the time goes in v4:
time: 595 us; the launch traced here: 587 us
  Pallas kernels  384 us (65%)
  waiting for transfers between devices  90.8 us (15%)
  starting transfers between devices  48.9 us (8%)
  local copies, waits for them, and re-layouts  24.2 us (4%)
  between operations  14.7 us (2%)
  other arithmetic  14.4 us (2%)
  matrix products  9.87 us (2%)
    pallas_call x2, Pallas kernels, attention(): pl.pallas_call(body, grid=(last - first, block_count), in_specs=[row_bloc...  108 us
    ppermute x40, waiting for transfers between devices, swap(): return lax.ppermute(value, axis, [(i, i ^ bit) for i in range(count)])  77.2 us
    pallas_call x1, Pallas kernels, hidden_grads(): whole_call(hidden_grads_kernel, [ANY] * 4, [ANY, ANY, VMEM], [jax.ShapeDt...  48.3 us
    ppermute x40, starting transfers between devices, swap(): return lax.ppermute(value, axis, [(i, i ^ bit) for i in range(count)])  48.2 us
    pallas_call x2, Pallas kernels, normed_grads(): whole_call(kernel, [SMEM] + [ANY] * 5 + [VMEM] * 2, [VMEM, VMEM] + [ANY]...  48.2 us
    pallas_call x1, Pallas kernels, hidden_rows(): pl.pallas_call(hidden_kernel, grid=(width // columns, rows // block), in_...  32 us
    pallas_call x1, Pallas kernels, first_grads(): whole_call(first_grads_kernel, [SMEM] + [ANY] * (1 + count), [ANY, ANY],...  25.5 us
    pallas_call x1, Pallas kernels, feed_rows(): whole_call(functools.partial(feed_kernel, halves=halves), [SMEM] + [ANY]...  23.5 us
  transfers between devices with their start and end apart: 47, of which 17 were waited for; matrix products, arithmetic and copies ran while one was open for 8% of the time, Pallas kernels for 64%

profile of v4, /device:TPU:0, one launch (start us, length us, event | category | flops | bytes accessed | tf_op | source)
XLA Modules:
  0.0 586.9 jit_solution(5802971689865799757)
XLA Ops:
  8.0 3.0 collective-permute-start.1
  12.5 5.5 multiply_sine_fusion
  18.2 4.5 concatenate.17.below_ref.refs_6_
  22.7 4.4 concatenate.16.above_ref.refs_5_
  28.1 4.5 concatenate.15.cos_ref.refs_4_
  33.0 24.0 %collective-permute-done.1.two_ref.refs_2_ = bf16[512,2048]{1,0:T(8,128)(2,1)} collective-permute-done((bf16[512,2048]{1,0:T(8,128)(2,1)}, bf16[512,2048]{1,0:T(8,128)(2,1)}, u32[]{:S(2)}, u32[]{:S(2)}) %collective-permute-start.1) | collective-permute-done | bytes 2097184 | tf_op jit(solution)/shard_map/ppermute | solution.py:32
  58.5 3.7 shard_map.194
  64.7 21.4 %collective-permute-done.2.refs_3_ = bf16[256,2048]{1,0:T(8,128)(2,1)} collective-permute-done((bf16[256,2048]{1,0:T(8,128)(2,1)}, bf16[256,2048]{1,0:T(8,128)(2,1)}, u32[]{:S(2)}, u32[]{:S(2)}) %collective-permute-start.2) | collective-permute-done | bytes 1048608 | tf_op jit(solution)/shard_map/ppermute | solution.py:32
  86.5 12.5 %shard_map.195 = (bf16[2048,2048]{1,0:T(8,128)(2,1)}, bf16[2048,2048]{1,0:T(8,128)(2,1)}, f32[2048,1]{1,0:T(8,128)}, f32[2048,1]{1,0:T(8,128)}, bf16[512,2048]{1,0:T(8,128)(2,1)}) custom-call(s32[5]{0:T(128)} %stack.19.starts_ref, f32[1,2048]{1,0:T(1,128)} %bitcast.50, f32[1,2048]{1,0:T(1,128)} %bitcast.54, bf16[512,2048]{1,0:T(8,128)(2,1)} %refs_13_.1, ...), custom_call_target="tpu_custom_call" | custom-call | flops 1 | bytes 1 | tf_op jit(solution)/shard_map/pallas_call | solution.py:1134
  104.0 32.0 %shard_map.196 = (bf16[2048,2048]{1,0:T(8,128)(2,1)}, bf16[2048,2048]{1,0:T(8,128)(2,1)}) custom-call(bf16[2048,2048]{1,0:T(8,128)(2,1)} %get-tuple-element.214.x_ref.x, bf16[2048,2048]{1,0:T(8,128)(2,1)} %all-gather.5.cloned.1.call-done.w_ref.up, f32[1,2048]{1,0:T(1,128)} %bitcast.52), custom_call_target="tpu_custom_call" | custom-call | flops 1 | bytes 1 | tf_op jit(solution)/shard_map/pallas_call | solution.py:250
  135.9 8.8 %collective-permute-done.5.two_ref.refs_2_ = bf16[512,2048]{1,0:T(8,128)(2,1)} collective-permute-done((bf16[512,2048]{1,0:T(8,128)(2,1)}, bf16[512,2048]{1,0:T(8,128)(2,1)}, u32[]{:S(2)}, u32[]{:S(2)}) %collective-permute-start.5) | collective-permute-done | bytes 2097184 | tf_op jit(solution)/shard_map/ppermute | solution.py:32
  145.9 3.7 shard_map.197
  152.6 6.7 %all-gather.7.cloned.1.call-done.w_ref.qkv = bf16[3,2048,512]{2,1,0:T(8,128)(2,1)} async-done(((bf16[3,256,512]{2,1,0:T(8,128)(2,1)}), bf16[3,2048,512]{2,1,0:T(8,128)(2,1)}) %all-gather.7.cloned.1.call-update) | async-done | bytes 6291472 | tf_op jit(solution)/shard_map/all_gather | solution.py:1180
  159.3 23.3 %shard_map.198.refs_0_.refs_1_.refs_2_ = bf16[2048,1536]{1,0:T(8,128)(2,1)} custom-call(bf16[2048,2048]{1,0:T(8,128)(2,1)} %get-tuple-element.214.x_ref.x, bf16[3,2048,512]{2,1,0:T(8,128)(2,1)} %all-gather.7.cloned.1.call-done.w_ref.qkv, f32[3,1,512]{2,1,0:T(1,128)} %reshape.89.bias_ref, f32[2048,128]{1,0:T(8,128)} %concatenate.15.cos_ref.refs_4_, ...), custom_call_target="tpu_custom_call" | custom-call | flops 1 | bytes 1 | tf_op jit(solution)/shard_map/pallas_call | solution.py:217
  182.6 25.5 %shard_map.199 = (bf16[2048,2048]{1,0:T(8,128)(2,1)}, bf16[2048,2048]{1,0:T(8,128)(2,1)}) custom-call(s32[5]{0:T(128)} %stack.19.starts_ref, bf16[2048,2048]{1,0:T(8,128)(2,1)} %get-tuple-element.234.active, bf16[512,2048]{1,0:T(8,128)(2,1)} %get-tuple-element.220.refs_0_, bf16[512,2048]{1,0:T(8,128)(2,1)} %collective-permute-done.4.one_ref.refs_1_, ...), custom_call_target="tpu_custom_call" | custom-call | flops 1 | bytes 1 | tf_op jit(solution)/shard_map/pallas_call | solution.py:385
  208.2 9.9 %convolution_convert_fusion.refs_3_ = bf16[2048,512]{1,0:T(8,128)(2,1)} fusion(bf16[2048,2048]{1,0:T(8,128)(2,1)} %get-tuple-element.257.grad_rows, bf16[512,2048]{1,0:T(8,128)(2,1)} %all-gather.9.cloned.1.call-done.refs_4_), kind=kOutput, calls=%fused_computation.1 | convolution fusion | flops 4296015872 | bytes 12582912 | tf_op jit(solution)/shard_map/td,kd->tk/dot_general | solution.py:1200
  221.2 54.0 %shard_map.200 = (bf16[2048,512]{1,0:T(8,128)(2,1)}, bf16[3,2048,512]{2,1,0:T(8,128)(2,1)}, f32[3,1,512]{2,1,0:T(1,128)}) custom-call(bf16[2048,1536]{1,0:T(8,128)(2,1)} %shard_map.198.refs_0_.refs_1_.refs_2_, bf16[2048,1536]{1,0:T(8,128)(2,1)} %shard_map.198.refs_0_.refs_1_.refs_2_, bf16[2048,1536]{1,0:T(8,128)(2,1)} %shard_map.198.refs_0_.refs_1_.refs_2_, ...), custom_call_target="tpu_custom_call" | custom-call | flops 1 | bytes 1 | tf_op jit(solution)/shard_map/pallas_call | solution.py:1043
  275.2 3.7 shard_map.202
  280.5 23.5 %shard_map.201 = (bf16[256,2048]{1,0:T(8,128)(2,1)}, bf16[256,2048]{1,0:T(8,128)(2,1)}, bf16[256,2048]{1,0:T(8,128)(2,1)}, bf16[256,2048]{1,0:T(8,128)(2,1)}, bf...) custom-call(s32[4]{0:T(128)} %pad_add_fusion.starts_ref, ...), custom_call_target="tpu_custom_call" | custom-call | flops 1 | bytes 1 | tf_op jit(solution)/shard_map/pallas_call | solution.py:471
  308.3 48.3 %shard_map.203 = (bf16[2048,2048]{1,0:T(8,128)(2,1)}, bf16[2048,2048]{1,0:T(8,128)(2,1)}, f32[2,1,1024]{2,1,0:T(1,128)}) custom-call(bf16[2048,2048]{1,0:T(8,128)(2,1)} %get-tuple-element.257.grad_rows, bf16[2048,2048]{1,0:T(8,128)(2,1)} %all-gather.11.cloned.1.call-done.weight, bf16[2048,2048]{1,0:T(8,128)(2,1)} %get-tuple-element.258.slope, ...), custom_call_target="tpu_custom_call" | custom-call | flops 1 | bytes 1 | tf_op jit(solution)/shard_map/pallas_call | solution.py:584
  356.7 3.9 shard_map.205
  366.5 54.2 %shard_map.204 = (bf16[2048,512]{1,0:T(8,128)(2,1)}, bf16[3,2048,512]{2,1,0:T(8,128)(2,1)}, f32[3,1,512]{2,1,0:T(1,128)}) custom-call(bf16[2048,1536]{1,0:T(8,128)(2,1)} %shard_map.198.refs_0_.refs_1_.refs_2_, bf16[2048,1536]{1,0:T(8,128)(2,1)} %shard_map.198.refs_0_.refs_1_.refs_2_, ...), custom_call_target="tpu_custom_call", output_to_operand_aliasing={{0}: (7, {}), {1}: (8, {}), {2}: (9, {})} | custom-call | flops 1 | bytes 1 | tf_op jit(solution)/shard_map/pallas_call | solution.py:1043
  427.1 23.0 %shard_map.206 = bf16[4,2048,512]{2,1,0:T(8,128)(2,1)} custom-call(bf16[2048,2048]{1,0:T(8,128)(2,1)} %get-tuple-element.214.x_ref.x, bf16[3,2048,512]{2,1,0:T(8,128)(2,1)} %get-tuple-element.294.joined, bf16[2048,2048]{1,0:T(8,128)(2,1)} %get-tuple-element.257.grad_rows, bf16[2048,512]{1,0:T(8,128)(2,1)} %get-tuple-element.277.mixed), custom_call_target="tpu_custom_call" | custom-call | flops 1 | bytes 1 | tf_op jit(solution)/shard_map/pallas_call | solution.py:656
  450.2 3.3 reduce-scatter.6.cloned.1.call-done
  453.4 24.1 %shard_map.207 = (f32[1,1024]{1,0:T(1,128)}, f32[1,1024]{1,0:T(1,128)}, bf16[256,1024]{1,0:T(8,128)(2,1)}, bf16[256,1024]{1,0:T(8,128)(2,1)}, bf16[256,1024]{1,0...) custom-call(s32[4]{0:T(128)} %pad_add_fusion.starts_ref, ...), custom_call_target="tpu_custom_call" | custom-call | flops 1 | bytes 1 | tf_op jit(solution)/shard_map/pallas_call | solution.py:765
  481.6 24.1 %shard_map.208 = (f32[1,1024]{1,0:T(1,128)}, f32[1,1024]{1,0:T(1,128)}, bf16[256,1024]{1,0:T(8,128)(2,1)}, bf16[256,1024]{1,0:T(8,128)(2,1)}, bf16[256,1024]{1,0...) custom-call(s32[4]{0:T(128)} %pad_add_fusion.starts_ref, ...), custom_call_target="tpu_custom_call" | custom-call | flops 1 | bytes 1 | tf_op jit(solution)/shard_map/pallas_call | solution.py:765
  516.6 4.8 collective-permute-done.32
  524.9 10.5 %shard_map.209 = bf16[512,2048]{1,0:T(8,128)(2,1)} custom-call(bf16[512,512]{1,0:T(8,128)(2,1)} %get-tuple-element.313.refs_0_, bf16[512,512]{1,0:T(8,128)(2,1)} %collective-permute-done.18.refs_1_, bf16[512,512]{1,0:T(8,128)(2,1)} %collective-permute-done.19.refs_2_, bf16[512,512]{1,0:T(8,128)(2,1)} %collective-permute-done.20.refs_3_, ...), custom_call_target="tpu_custom_call" | custom-call | flops 1 | bytes 1 | tf_op jit(solution)/shard_map/pallas_call | solution.py:815
  535.5 4.5 collective-permute-done.25.b_ref
  540.0 6.2 %collective-permute-done.27.refs_8_ = bf16[256,1024]{1,0:T(8,128)(2,1)} collective-permute-done((bf16[256,1024]{1,0:T(8,128)(2,1)}, bf16[256,1024]{1,0:T(8,128)(2,1)}, u32[]{:S(2)}, u32[]{:S(2)}) %collective-permute-start.27) | collective-permute-done | bytes 524320 | tf_op jit(solution)/shard_map/ppermute | solution.py:32
  567.7 3.1 collective-permute-done.34.refs_6_
  571.1 8.7 %shard_map.212 = bf16[512,2048]{1,0:T(8,128)(2,1)} custom-call(bf16[256,1024]{1,0:T(8,128)(2,1)} %collective-permute-done.29.refs_0_, bf16[256,1024]{1,0:T(8,128)(2,1)} %collective-permute-done.30.refs_1_, bf16[256,1024]{1,0:T(8,128)(2,1)} %collective-permute-done.23.refs_2_, bf16[256,1024]{1,0:T(8,128)(2,1)} %collective-permute-done.24.refs_3_, ...), custom_call_target="tpu_custom_call" | custom-call | flops 1 | bytes 1 | tf_op jit(solution)/shard_map/pallas_call | solution.py:874
  (140 shorter events, 78.9 us)
Async XLA Ops:
  7.2 96.8 %all-gather.5.cloned.1.call-start = ((), (), s32[]{:S(2)}) async-start(), calls=%async_computation.3 | async-start | bytes 9437184 | tf_op jit(solution)/shard_map/all_gather | solution.py:1175
  7.9 151.4 %all-gather.7.cloned.1.call-start = ((), (), s32[]{:S(2)}) async-start(), calls=%async_computation.4 | async-start | bytes 7077888 | tf_op jit(solution)/shard_map/all_gather | solution.py:1180
  8.0 49.0 %collective-permute-start.1 = (bf16[512,2048]{1,0:T(8,128)(2,1)}, bf16[512,2048]{1,0:T(8,128)(2,1)}, u32[]{:S(2)}, u32[]{:S(2)}) collective-permute-start(bf16[512,2048]{1,0:T(8,128)(2,1)} %refs_12_.1), channel_id=1, source_target_pairs={{0,2},{1,3},{2,0},{3,1},{4,6},{5,7},{6,4},{7,5},{8,10},{9,11},{10,... | collective-permute-start | bytes 6291464 | tf_op jit(solution)/shard_map/ppermute | solution.py:32
  11.0 47.4 %collective-permute-start = (bf16[512,2048]{1,0:T(8,128)(2,1)}, bf16[512,2048]{1,0:T(8,128)(2,1)}, u32[]{:S(2)}, u32[]{:S(2)}) collective-permute-start(bf16[512,2048]{1,0:T(8,128)(2,1)} %refs_12_.1), channel_id=1, source_target_pairs={{0,1},{1,0},{2,3},{3,2},{4,5},{5,4},{6,7},{7,6},{8,9},{9,8},{10,11... | collective-permute-start | bytes 6291464 | tf_op jit(solution)/shard_map/ppermute | solution.py:32
  58.4 149.8 %all-gather.9.cloned.1.call-start = ((), (), s32[]{:S(2)}) async-start(), calls=%async_computation.5 | async-start | bytes 2359296 | tf_op jit(solution)/shard_map/all_gather | solution.py:1189
  62.4 24.1 %collective-permute-start.3 = (bf16[256,2048]{1,0:T(8,128)(2,1)}, bf16[256,2048]{1,0:T(8,128)(2,1)}, u32[]{:S(2)}, u32[]{:S(2)}) collective-permute-start(bf16[256,2048]{1,0:T(8,128)(2,1)} %get-tuple-element.201), channel_id=1, source_target_pairs={{0,1},{1,0},{2,3},{3,2},{4,5},{5,4},{6,7},{7,6},{8,9},{9,8},{10,11... | collective-permute-start | bytes 3145736 | tf_op jit(solution)/shard_map/ppermute | solution.py:32
  99.0 181.5 %all-gather.11.cloned.1.call-start = ((), (), s32[]{:S(2)}) async-start(), calls=%async_computation.6 | async-start | bytes 9437184 | tf_op jit(solution)/shard_map/all_gather | solution.py:1195
  99.1 45.7 %collective-permute-start.5 = (bf16[512,2048]{1,0:T(8,128)(2,1)}, bf16[512,2048]{1,0:T(8,128)(2,1)}, u32[]{:S(2)}, u32[]{:S(2)}) collective-permute-start(bf16[512,2048]{1,0:T(8,128)(2,1)} %get-tuple-element.220.refs_0_), channel_id=1, source_target_pairs={{0,2},{1,3},{2,0},{3,1},{4,6},{5,7},{6,4},{7,5},{8,10},{9,11},{10,... | collective-permute-start | bytes 6291464 | tf_op jit(solution)/shard_map/ppermute | solution.py:32
  100.5 44.9 %collective-permute-start.4 = (bf16[512,2048]{1,0:T(8,128)(2,1)}, bf16[512,2048]{1,0:T(8,128)(2,1)}, u32[]{:S(2)}, u32[]{:S(2)}) collective-permute-start(bf16[512,2048]{1,0:T(8,128)(2,1)} %get-tuple-element.220.refs_0_), channel_id=1, source_target_pairs={{0,1},{1,0},{2,3},{3,2},{4,5},{5,4},{6,7},{7,6},{8,9},{9,8},{10,11... | collective-permute-start | bytes 6291464 | tf_op jit(solution)/shard_map/ppermute | solution.py:32
  145.4 218.0 %reduce-scatter.4.cloned.1.call-start = ((), (), s32[]{:S(2)}) async-start(), calls=%async_computation.7 | async-start | bytes 9437184 | tf_op jit(solution)/shard_map/reduce_scatter | solution.py:1204
  149.6 33.0 %collective-permute-start.6 = (bf16[256,2048]{1,0:T(8,128)(2,1)}, bf16[256,2048]{1,0:T(8,128)(2,1)}, u32[]{:S(2)}, u32[]{:S(2)}) collective-permute-start(bf16[256,2048]{1,0:T(8,128)(2,1)} %get-tuple-element.211), channel_id=1, source_target_pairs={{0,2},{1,3},{2,0},{3,1},{4,6},{5,7},{6,4},{7,5},{8,10},{9,11},{10,... | collective-permute-start | bytes 3145736 | tf_op jit(solution)/shard_map/ppermute | solution.py:32
  150.8 31.8 %collective-permute-start.7 = (bf16[256,2048]{1,0:T(8,128)(2,1)}, bf16[256,2048]{1,0:T(8,128)(2,1)}, u32[]{:S(2)}, u32[]{:S(2)}) collective-permute-start(bf16[256,2048]{1,0:T(8,128)(2,1)} %get-tuple-element.212), channel_id=1, source_target_pairs={{0,1},{1,0},{2,3},{3,2},{4,5},{5,4},{6,7},{7,6},{8,9},{9,8},{10,11... | collective-permute-start | bytes 3145736 | tf_op jit(solution)/shard_map/ppermute | solution.py:32
  208.2 245.3 %reduce-scatter.6.cloned.1.call-start = ((), (), s32[]{:S(2)}) async-start(), calls=%async_computation.8 | async-start | bytes 9437184 | tf_op jit(solution)/shard_map/reduce_scatter | solution.py:1218
  218.1 57.1 %collective-permute-start.9 = (bf16[512,2048]{1,0:T(8,128)(2,1)}, bf16[512,2048]{1,0:T(8,128)(2,1)}, u32[]{:S(2)}, u32[]{:S(2)}) collective-permute-start(bf16[512,2048]{1,0:T(8,128)(2,1)} %all-gather.9.cloned.1.call-done.refs_4_), channel_id=1, source_target_pairs={{0,2},{1,3},{2,0},{3,1},{4,6},{5,7},{6,4},{7,5},{8,10},{9,11},{10,... | collective-permute-start | bytes 6291464 | tf_op jit(solution)/shard_map/ppermute | solution.py:32
  219.7 55.5 %collective-permute-start.8 = (bf16[512,2048]{1,0:T(8,128)(2,1)}, bf16[512,2048]{1,0:T(8,128)(2,1)}, u32[]{:S(2)}, u32[]{:S(2)}) collective-permute-start(bf16[512,2048]{1,0:T(8,128)(2,1)} %all-gather.9.cloned.1.call-done.refs_4_), channel_id=1, source_target_pairs={{0,1},{1,0},{2,3},{3,2},{4,5},{5,4},{6,7},{7,6},{8,9},{9,8},{10,11... | collective-permute-start | bytes 6291464 | tf_op jit(solution)/shard_map/ppermute | solution.py:32
  278.9 25.1 %collective-permute-start.10 = (bf16[256,2048]{1,0:T(8,128)(2,1)}, bf16[256,2048]{1,0:T(8,128)(2,1)}, u32[]{:S(2)}, u32[]{:S(2)}) collective-permute-start(bf16[256,2048]{1,0:T(8,128)(2,1)} %get-tuple-element.247), channel_id=1, source_target_pairs={{0,2},{1,3},{2,0},{3,1},{4,6},{5,7},{6,4},{7,5},{8,10},{9,11},{10,... | collective-permute-start | bytes 3145736 | tf_op jit(solution)/shard_map/ppermute | solution.py:32
  279.5 24.8 %collective-permute-start.11 = (bf16[256,2048]{1,0:T(8,128)(2,1)}, bf16[256,2048]{1,0:T(8,128)(2,1)}, u32[]{:S(2)}, u32[]{:S(2)}) collective-permute-start(bf16[256,2048]{1,0:T(8,128)(2,1)} %get-tuple-element.248), channel_id=1, source_target_pairs={{0,1},{1,0},{2,3},{3,2},{4,5},{5,4},{6,7},{7,6},{8,9},{9,8},{10,11... | collective-permute-start | bytes 3145736 | tf_op jit(solution)/shard_map/ppermute | solution.py:32
  304.3 52.4 %collective-permute-start.12 = (bf16[256,2048]{1,0:T(8,128)(2,1)}, bf16[256,2048]{1,0:T(8,128)(2,1)}, u32[]{:S(2)}, u32[]{:S(2)}) collective-permute-start(bf16[256,2048]{1,0:T(8,128)(2,1)} %get-tuple-element.249), channel_id=1, source_target_pairs={{0,1},{1,0},{2,3},{3,2},{4,5},{5,4},{6,7},{7,6},{8,9},{9,8},{10,11... | collective-permute-start | bytes 3145736 | tf_op jit(solution)/shard_map/ppermute | solution.py:32
  305.7 51.0 %collective-permute-start.13 = (bf16[256,2048]{1,0:T(8,128)(2,1)}, bf16[256,2048]{1,0:T(8,128)(2,1)}, u32[]{:S(2)}, u32[]{:S(2)}) collective-permute-start(bf16[256,2048]{1,0:T(8,128)(2,1)} %get-tuple-element.250), channel_id=1, source_target_pairs={{0,2},{1,3},{2,0},{3,1},{4,6},{5,7},{6,4},{7,5},{8,10},{9,11},{10,... | collective-permute-start | bytes 3145736 | tf_op jit(solution)/shard_map/ppermute | solution.py:32
  307.2 49.5 %collective-permute-start.14 = (bf16[256,2048]{1,0:T(8,128)(2,1)}, bf16[256,2048]{1,0:T(8,128)(2,1)}, u32[]{:S(2)}, u32[]{:S(2)}) collective-permute-start(bf16[256,2048]{1,0:T(8,128)(2,1)} %get-tuple-element.251), channel_id=1, source_target_pairs={{0,1},{1,0},{2,3},{3,2},{4,5},{5,4},{6,7},{7,6},{8,9},{9,8},{10,11... | collective-permute-start | bytes 3145736 | tf_op jit(solution)/shard_map/ppermute | solution.py:32
  307.8 48.9 %collective-permute-start.15 = (bf16[256,2048]{1,0:T(8,128)(2,1)}, bf16[256,2048]{1,0:T(8,128)(2,1)}, u32[]{:S(2)}, u32[]{:S(2)}) collective-permute-start(bf16[256,2048]{1,0:T(8,128)(2,1)} %get-tuple-element.254), channel_id=1, source_target_pairs={{0,2},{1,3},{2,0},{3,1},{4,6},{5,7},{6,4},{7,5},{8,10},{9,11},{10,... | collective-permute-start | bytes 3145736 | tf_op jit(solution)/shard_map/ppermute | solution.py:32
  363.5 200.4 %reduce-scatter.8.cloned.1.call-start = ((), (), s32[]{:S(2)}) async-start(), calls=%async_computation.9 | async-start | bytes 9437184 | tf_op jit(solution)/shard_map/reduce_scatter | solution.py:1229
  363.5 57.3 %collective-permute-start.16 = (bf16[256,2048]{1,0:T(8,128)(2,1)}, bf16[256,2048]{1,0:T(8,128)(2,1)}, u32[]{:S(2)}, u32[]{:S(2)}) collective-permute-start(bf16[256,2048]{1,0:T(8,128)(2,1)} %get-tuple-element.270), channel_id=1, source_target_pairs={{0,2},{1,3},{2,0},{3,1},{4,6},{5,7},{6,4},{7,5},{8,10},{9,11},{10,... | collective-permute-start | bytes 3145736 | tf_op jit(solution)/shard_map/ppermute | solution.py:32
  365.1 55.7 %collective-permute-start.17 = (bf16[256,2048]{1,0:T(8,128)(2,1)}, bf16[256,2048]{1,0:T(8,128)(2,1)}, u32[]{:S(2)}, u32[]{:S(2)}) collective-permute-start(bf16[256,2048]{1,0:T(8,128)(2,1)} %get-tuple-element.271), channel_id=1, source_target_pairs={{0,1},{1,0},{2,3},{3,2},{4,5},{5,4},{6,7},{7,6},{8,9},{9,8},{10,11... | collective-permute-start | bytes 3145736 | tf_op jit(solution)/shard_map/ppermute | solution.py:32
  423.7 26.5 %collective-permute-start.20 = (bf16[512,512]{1,0:T(8,128)(2,1)}, bf16[512,512]{1,0:T(8,128)(2,1)}, u32[]{:S(2)}, u32[]{:S(2)}) collective-permute-start(bf16[512,512]{1,0:T(8,128)(2,1)} %get-tuple-element.405), channel_id=1, source_target_pairs={{0,3},{1,2},{2,1},{3,0},{4,7},{5,6},{6,5},{7,4},{8,11},{9,10},{10,... | collective-permute-start | bytes 1572872 | tf_op jit(solution)/shard_map/ppermute | solution.py:32
  424.3 25.9 %collective-permute-start.19 = (bf16[512,512]{1,0:T(8,128)(2,1)}, bf16[512,512]{1,0:T(8,128)(2,1)}, u32[]{:S(2)}, u32[]{:S(2)}) collective-permute-start(bf16[512,512]{1,0:T(8,128)(2,1)} %get-tuple-element.406), channel_id=1, source_target_pairs={{0,2},{1,3},{2,0},{3,1},{4,6},{5,7},{6,4},{7,5},{8,10},{9,11},{10,... | collective-permute-start | bytes 1572872 | tf_op jit(solution)/shard_map/ppermute | solution.py:32
  425.7 24.5 %collective-permute-start.18 = (bf16[512,512]{1,0:T(8,128)(2,1)}, bf16[512,512]{1,0:T(8,128)(2,1)}, u32[]{:S(2)}, u32[]{:S(2)}) collective-permute-start(bf16[512,512]{1,0:T(8,128)(2,1)} %get-tuple-element.407), channel_id=1, source_target_pairs={{0,1},{1,0},{2,3},{3,2},{4,5},{5,4},{6,7},{7,6},{8,9},{9,8},{10,11... | collective-permute-start | bytes 1572872 | tf_op jit(solution)/shard_map/ppermute | solution.py:32
  477.5 28.3 %collective-permute-start.21 = (bf16[256,1024]{1,0:T(8,128)(2,1)}, bf16[256,1024]{1,0:T(8,128)(2,1)}, u32[]{:S(2)}, u32[]{:S(2)}) collective-permute-start(bf16[256,1024]{1,0:T(8,128)(2,1)} %get-tuple-element.286), channel_id=1, source_target_pairs={{0,1},{1,0},{2,3},{3,2},{4,5},{5,4},{6,7},{7,6},{8,9},{9,8},{10,11... | collective-permute-start | bytes 1572872 | tf_op jit(solution)/shard_map/ppermute | solution.py:32
  479.1 26.8 %collective-permute-start.22 = (bf16[256,1024]{1,0:T(8,128)(2,1)}, bf16[256,1024]{1,0:T(8,128)(2,1)}, u32[]{:S(2)}, u32[]{:S(2)}) collective-permute-start(bf16[256,1024]{1,0:T(8,128)(2,1)} %get-tuple-element.287), channel_id=1, source_target_pairs={{0,2},{1,3},{2,0},{3,1},{4,6},{5,7},{6,4},{7,5},{8,10},{9,11},{10,... | collective-permute-start | bytes 1572872 | tf_op jit(solution)/shard_map/ppermute | solution.py:32
  480.5 25.3 %collective-permute-start.23 = (bf16[256,1024]{1,0:T(8,128)(2,1)}, bf16[256,1024]{1,0:T(8,128)(2,1)}, u32[]{:S(2)}, u32[]{:S(2)}) collective-permute-start(bf16[256,1024]{1,0:T(8,128)(2,1)} %get-tuple-element.288), channel_id=1, source_target_pairs={{0,1},{1,0},{2,3},{3,2},{4,5},{5,4},{6,7},{7,6},{8,9},{9,8},{10,11... | collective-permute-start | bytes 1572872 | tf_op jit(solution)/shard_map/ppermute | solution.py:32
  481.1 24.7 %collective-permute-start.24 = (bf16[256,1024]{1,0:T(8,128)(2,1)}, bf16[256,1024]{1,0:T(8,128)(2,1)}, u32[]{:S(2)}, u32[]{:S(2)}) collective-permute-start(bf16[256,1024]{1,0:T(8,128)(2,1)} %get-tuple-element.291), channel_id=1, source_target_pairs={{0,2},{1,3},{2,0},{3,1},{4,6},{5,7},{6,4},{7,5},{8,10},{9,11},{10,... | collective-permute-start | bytes 1572872 | tf_op jit(solution)/shard_map/ppermute | solution.py:32
  515.1 24.9 %collective-permute-start.25 = (bf16[256,1024]{1,0:T(8,128)(2,1)}, bf16[256,1024]{1,0:T(8,128)(2,1)}, u32[]{:S(2)}, u32[]{:S(2)}) collective-permute-start(bf16[256,1024]{1,0:T(8,128)(2,1)} %get-tuple-element.305), channel_id=1, source_target_pairs={{0,1},{1,0},{2,3},{3,2},{4,5},{5,4},{6,7},{7,6},{8,9},{9,8},{10,11... | collective-permute-start | bytes 1572872 | tf_op jit(solution)/shard_map/ppermute | solution.py:32
  (23 other events, 290.3 us)
Sparse Core Ops, SparseCore 0:
  9.6 84.7 all-gather.4
  96.0 63.2 all-gather.6
  160.9 29.5 all-gather.8
  191.9 81.5 all-gather.10
  275.6 87.7 reduce-scatter.3
  365.6 87.7 reduce-scatter.5
  455.7 87.9 reduce-scatter.7

commit v5 on v4

--- a/solution.py
+++ b/solution.py
@@ -82,44 +82,45 @@
     count = lax.axis_size("tensor")
     rows = total // count
     me = lax.axis_index("tensor")
-    order = [me ^ bit for bit in (3, 1, 2, 0)] if count == 4 else list(range(count))
+    if count == 4:
+        order = [me ^ bit for bit in (3, 1, 2, 0)]
+        half = rows // 2
+        places = (((0, 0), (1, 0)), ((0, half), (3, 0)), ((2, 0), (1, half)), ((4, 0), (5, 0)))
+        sizes = (rows, rows, half, half, half, half)
+    else:
+        order = list(range(count))
+        places = tuple(((owner, 0),) for owner in range(count))
+        sizes = (rows,) * count
     starts = jnp.stack([jnp.asarray(owner * rows, jnp.int32) for owner in order])
-    return starts, count, 2 if count == 4 else 1
+    return starts, places, sizes
 
 
 def scatter_send(cuts):
     if lax.axis_size("tensor") != 4:
         whole = wide(jnp.concatenate(cuts))
         return (lax.psum_scatter(whole, "tensor", scatter_dimension=0, tiled=True),)
-    far_low, far_high, one_low, one_high, two_low, two_high, low, high = cuts
-    return (
-        swap(far_low, "tensor", 1),
-        swap(far_high, "tensor", 2),
-        swap(one_low, "tensor", 1),
-        swap(two_high, "tensor", 2),
-        two_low,
-        one_high,
-        low,
-        high,
-    )
+    for_one, for_two, two_low, one_high, low, high = cuts
+    return swap(for_one, "tensor", 1), swap(for_two, "tensor", 2), two_low, one_high, low, high
 
 
 def fold_kernel(a_ref, b_ref, c_ref, d_ref, ab_ref, cd_ref):
-    ab_ref[...] = (wide(a_ref[...]) + wide(b_ref[...])).astype(ab_ref.dtype)
-    cd_ref[...] = (wide(c_ref[...]) + wide(d_ref[...])).astype(cd_ref.dtype)
+    half = a_ref.shape[0]
+    ab_ref[...] = (wide(a_ref[...]) + wide(b_ref[:half, :])).astype(ab_ref.dtype)
+    cd_ref[...] = (wide(c_ref[...]) + wide(d_ref[:half, :])).astype(cd_ref.dtype)
 
 
 def scatter_fold(parts):
     if len(parts) == 1:
         return parts
-    first_far, second_far, first_near, second_near, two_low, one_high, low, high = parts
+    first, second, two_low, one_high, low, high = parts
     shape = jax.ShapeDtypeStruct(low.shape, low.dtype)
     forward = pl.pallas_call(
         fold_kernel,
         out_shape=[shape, shape],
         compiler_params=pltpu.CompilerParams(vmem_limit_bytes=VMEM_BYTES),
-    )(two_low, first_far, one_high, second_far)
-    return (*forward, first_near, second_near, low, high)
+        cost_estimate=SHORT,
+    )(two_low, first, one_high, second)
+    return (*forward, first, second, low, high)
 
 
 def scatter_pass(parts):
@@ -402,10 +403,10 @@
     )(starts, active, *[piece for _, piece in pieces])
 
 
-def feed_kernel(starts_ref, active, weight, *refs, halves):
+def feed_kernel(starts_ref, active, weight, *refs, places):
     cuts = refs[:-5]
     active_buf, weight_buf, out_buf, load_sems, cut_sems = refs[-5:]
-    owners = len(cuts) // halves
+    owners, halves = len(places), len(places[0])
     rows = active_buf.shape[0]
     half = weight_buf.shape[2]
     owner_rows = rows // owners
@@ -431,7 +432,10 @@
     def cut_copy(owner, part_of, side):
         return pltpu.make_async_copy(
             out_buf.at[side, pl.ds(owner * owner_rows + part_of * piece, piece), :],
-            cuts[owner * halves + part_of].at[:, pl.ds(pl.multiple_of(side * half, half), half)],
+            cuts[places[owner][part_of][0]].at[
+                pl.ds(places[owner][part_of][1], piece),
+                pl.ds(pl.multiple_of(side * half, half), half),
+            ],
             cut_sems.at[side, owner * halves + part_of],
         )
 
@@ -465,14 +469,14 @@
     rows, hidden = active.shape
     depth = weight.shape[1]
     half = depth // 2
-    starts, owners, halves = owner_cuts(rows)
-    cut = jax.ShapeDtypeStruct((rows // owners // halves, depth), low)
+    starts, places, sizes = owner_cuts(rows)
+    owners, halves = len(places), len(places[0])
     return tuple(
         whole_call(
-            functools.partial(feed_kernel, halves=halves),
+            functools.partial(feed_kernel, places=places),
             [SMEM] + [ANY] * 2,
-            [ANY] * (owners * halves),
-            [cut] * (owners * halves),
+            [ANY] * len(sizes),
+            [jax.ShapeDtypeStruct((size, depth), low) for size in sizes],
             [
                 pltpu.VMEM((rows, hidden), low),
                 pltpu.VMEM((2, hidden, half), low),
@@ -670,21 +674,24 @@
 
 
 def normed_grads_kernel(
-    starts_ref, joined, qkv, hidden, up, x, mean_ref, root_ref, gain_ref, shift_ref, *refs, halves
+    starts_ref, joined, qkv, hidden, up, x, mean_ref, root_ref, gain_ref, shift_ref, *refs, places
 ):
     cuts = refs[:-8]
     joined_buf, qkv_buf, hidden_buf, up_buf, x_buf, out_buf, load_sems, cut_sems = refs[-8:]
-    owners = len(cuts) // halves
+    owners, halves = len(places), len(places[0])
     rows = hidden_buf.shape[0]
     owner_rows = rows // owners
     piece = owner_rows // halves
+    columns = up_buf.shape[0]
+    chunk = min(512, columns)
+    chunks = columns // chunk
 
     def load(source, target, index):
         return pltpu.make_async_copy(source, target, load_sems.at[index])
 
     def row_loads(owner):
         here = pl.ds(pl.multiple_of(starts_ref[owner], owner_rows), owner_rows)
-        at = 4 + owner * 3
+        at = 2 + owner * 3
         return (
             load(hidden.at[here, :], hidden_buf.at[here, :], at),
             load(joined.at[:, here, :], joined_buf.at[:, here, :], at + 1),
@@ -705,22 +712,21 @@
         copy.wait()
 
     def cut_copy(owner, part_of):
+        array, row = places[owner][part_of]
         return pltpu.make_async_copy(
             out_buf.at[pl.ds(owner * owner_rows + part_of * piece, piece), :],
-            cuts[owner * halves + part_of],
+            cuts[array].at[pl.ds(row, piece), :],
             cut_sems.at[owner * halves + part_of],
         )
 
     @pl.loop(0, owners)
     def _(owner):
+        here = pl.ds(pl.multiple_of(starts_ref[owner], owner_rows), owner_rows)
+        there = pl.ds(pl.multiple_of(owner * owner_rows, owner_rows), owner_rows)
         for copy in row_loads(owner):
             copy.wait()
-        here = pl.ds(pl.multiple_of(starts_ref[owner], owner_rows), owner_rows)
-        there = pl.ds(pl.multiple_of(owner * owner_rows, owner_rows), owner_rows)
-        columns = up_buf.shape[0]
-        chunk = min(512, columns)
-        for start in range(0, columns, chunk):
-            mine = slice(start, start + chunk)
+        for index in range(chunks):
+            mine = slice(index * chunk, (index + 1) * chunk)
             total = nt_dot(hidden_buf[here, :], up_buf[mine, :])
             for slot in range(3):
                 total += nt_dot(joined_buf[slot, here, :], qkv_buf[slot, mine, :])
@@ -745,8 +751,8 @@
     rows, units = hidden.shape
     width = joined.shape[2]
     columns = last - first
-    starts, owners, halves = owner_cuts(rows)
-    cut = jax.ShapeDtypeStruct((rows // owners // halves, columns), low)
+    starts, places, sizes = owner_cuts(rows)
+    owners, halves = len(places), len(places[0])
     line = jax.ShapeDtypeStruct((1, columns), jnp.float32)
 
     def kernel(starts_ref, joined, qkv, hidden, up, x, *refs):
@@ -759,14 +765,14 @@
             up.at[mine, :],
             x.at[:, mine],
             *refs,
-            halves=halves,
+            places=places,
         )
 
     result = whole_call(
         kernel,
         [SMEM] + [ANY] * 5 + [VMEM] * 2,
-        [VMEM, VMEM] + [ANY] * (owners * halves),
-        [line, line] + [cut] * (owners * halves),
+        [VMEM, VMEM] + [ANY] * len(sizes),
+        [line, line] + [jax.ShapeDtypeStruct((size, columns), low) for size in sizes],
         [
             pltpu.VMEM((3, rows, width), low),
             pltpu.VMEM((3, columns, width), low),
@@ -774,7 +780,7 @@
             pltpu.VMEM((columns, units), low),
             pltpu.VMEM((rows, columns), low),
             pltpu.VMEM((rows, columns), low),
-            pltpu.SemaphoreType.DMA((4 + 3 * owners,)),
+            pltpu.SemaphoreType.DMA((2 + 3 * owners,)),
             pltpu.SemaphoreType.DMA((owners * halves,)),
         ],
     )(starts, joined, qkv, hidden, up, x, mean, root)
@@ -818,7 +824,9 @@
         in_specs=[pl.BlockSpec(piece.shape, lambda j: (0, 0)) for piece in mixed_parts]
         + [column_block(piece) for piece in dense_parts]
         + [column_block(tokens), pl.BlockSpec((1, columns), lambda j: (0, j))]
-        + [column_block(piece) for piece in feed_parts],
+        + [column_block(piece) for piece in feed_parts[:2]]
+        + [pl.BlockSpec((rows // 2, columns), lambda j: (1, j))] * 2
+        + [column_block(piece) for piece in feed_parts[4:]],
         out_specs=column_block(tokens),
         out_shape=jax.ShapeDtypeStruct(tokens.shape, tokens.dtype),
         compiler_params=pltpu.CompilerParams(vmem_limit_bytes=VMEM_BYTES),
@@ -869,12 +877,14 @@
     steps = half // chunk
     low_part = pl.BlockSpec((chunk, split), lambda i: (jnp.minimum(i, steps - 1), 0))
     high_part = pl.BlockSpec((chunk, split), lambda i: (jnp.maximum(i - steps, 0), 0))
+    low_near = pl.BlockSpec((chunk, split), lambda i: (steps + jnp.minimum(i, steps - 1), 0))
+    high_near = pl.BlockSpec((chunk, split), lambda i: (jnp.maximum(i, steps), 0))
     row_block = pl.BlockSpec((chunk, depth), lambda i: (i, 0))
     thin = pl.BlockSpec((chunk, 1), lambda i: (i, 0))
     return pl.pallas_call(
         functools.partial(token_grads_kernel, steps=steps),
         grid=(rows // chunk,),
-        in_specs=[low_part, high_part] * 6
+        in_specs=[low_part, high_part, low_near, high_near, low_part, high_part] * 2
         + [row_block, row_block, thin, thin, pl.BlockSpec((1, depth), lambda i: (0, 0))],
         out_specs=row_block,
         out_shape=jax.ShapeDtypeStruct(tokens.shape, tokens.dtype),
@@ -1239,25 +1249,29 @@
         [left_sums[0][0], right_sums[0][0], left_sums[1][0], right_sums[1][0], out_part]
     ).reshape(-1, PAIR)
     right_parts = scatter_send(right_cuts)
-    left_parts, sums = after((scatter_fold(left_parts), sums))
-    over_group = exchange_sum(sums, "tensor")
-    left_parts = scatter_pass(left_parts)
+    left_parts = scatter_pass(scatter_fold(left_parts))
     block_out = finish_output(
         after(mixed_parts, right_cuts), dense_parts, tokens, bias_out, feed_parts
     )
-    block_out, right_parts, left_parts, over_group = after(
-        (block_out, right_parts, left_parts, over_group)
-    )
-    right_parts = scatter_pass(scatter_fold(right_parts))
+    small = jnp.concatenate(
+        [sums.reshape(-1), bias_qkv_part.reshape(-1), bias_up_part.reshape(-1)]
+    ).reshape(-1, PAIR)
+    block_out, small = after((block_out, small))
+    small = jnp.sum(lax.all_gather(small, "dp", axis=0), axis=0)
+    block_out, right_parts, left_parts, small = after(
+        (block_out, right_parts, left_parts, small)
+    )
+    right_parts = scatter_fold(right_parts)
+    right_parts, small, grad_up_sum, grad_down_sum = after(
+        (right_parts, small, grad_up_sum, grad_down_sum)
+    )
+    right_parts = scatter_pass(right_parts)
+    small = small.reshape(-1)
+    over_all = exchange_sum(small[: 3 * depth].reshape(-1, PAIR), "tensor")
+    grad_gain, grad_shift, grad_bias_out = over_all.reshape(3, depth)
     bias_size = bias_qkv.size
-    over_dp = jnp.concatenate(
-        [over_group.reshape(-1), bias_qkv_part.reshape(-1), bias_up_part.reshape(-1)]
-    ).reshape(-1, PAIR)
-    over_dp = over_dp + swap(over_dp, "dp", 1)
-    over_dp = exchange_sum(over_dp, "dp", 2).reshape(-1)
-    grad_gain, grad_shift, grad_bias_out = over_dp[: 3 * depth].reshape(3, depth)
-    grad_bias_qkv = over_dp[3 * depth : 3 * depth + bias_size].reshape(bias_qkv.shape)
-    grad_bias_up = over_dp[3 * depth + bias_size :]
+    grad_bias_qkv = small[3 * depth : 3 * depth + bias_size].reshape(bias_qkv.shape)
+    grad_bias_up = small[3 * depth + bias_size :]
     last = jnp.transpose(grad_last_sum, (1, 0, 2)).astype(f32)
     ready = grad_up_sum.astype(f32), grad_down_sum.astype(f32), last
     ready, left_parts = after((ready, left_parts))

time: 595 us -> 585 us (0.983)
  blocking collectives: 0 us -> 16.1 us
  waiting for transfers between devices: 90.8 us -> 75 us
  starting transfers between devices: 48.9 us -> 38.1 us
    ppermute x40 -> x30, waiting for transfers between devices: 77.2 us -> 60.1 us  [swap(): return lax.ppermute(value, axis, [(i, i ^ bit) for i in range(count)])]
    all_gather x0 -> x1, blocking collectives: none -> 16.1 us  [on_device(): small = jnp.sum(lax.all_gather(small, 'dp', axis=0), axis=0)]
    ppermute x40 -> x30, starting transfers between devices: 48.2 us -> 37.6 us  [swap(): return lax.ppermute(value, axis, [(i, i ^ bit) for i in range(count)])]
  transfers between devices with their start and end apart: 47 -> 37, of which waited for: 17 -> 13; matrix products, arithmetic and copies ran while one was open for 8% -> 8% of each run, Pallas kernels for 64% -> 65%
where the time goes in v5:
time: 585 us; the launch traced here: 576 us
  Pallas kernels  385 us (66%)
  waiting for transfers between devices  75 us (13%)
  starting transfers between devices  38.1 us (7%)
  local copies, waits for them, and re-layouts  25 us (4%)
  blocking collectives  16.1 us (3%)
  between operations  14.7 us (3%)
  other arithmetic  12.4 us (2%)
  matrix products  9.87 us (2%)
    pallas_call x2, Pallas kernels, attention(): pl.pallas_call(body, grid=(last - first, block_count), in_specs=[row_bloc...  108 us
    ppermute x30, waiting for transfers between devices, swap(): return lax.ppermute(value, axis, [(i, i ^ bit) for i in range(count)])  60.1 us
    pallas_call x1, Pallas kernels, hidden_grads(): whole_call(hidden_grads_kernel, [ANY] * 4, [ANY, ANY, VMEM], [jax.ShapeDt...  48.3 us
    pallas_call x2, Pallas kernels, normed_grads(): whole_call(kernel, [SMEM] + [ANY] * 5 + [VMEM] * 2, [VMEM, VMEM] + [ANY]...  48.2 us
    ppermute x30, starting transfers between devices, swap(): return lax.ppermute(value, axis, [(i, i ^ bit) for i in range(count)])  37.6 us
    pallas_call x1, Pallas kernels, hidden_rows(): pl.pallas_call(hidden_kernel, grid=(width // columns, rows // block), in_...  32 us
    pallas_call x1, Pallas kernels, first_grads(): whole_call(first_grads_kernel, [SMEM] + [ANY] * (1 + count), [ANY, ANY],...  25.6 us
    pallas_call x1, Pallas kernels, feed_rows(): whole_call(functools.partial(feed_kernel, places=places), [SMEM] + [ANY]...  23.6 us
  transfers between devices with their start and end apart: 37, of which 13 were waited for; matrix products, arithmetic and copies ran while one was open for 8% of the time, Pallas kernels for 65%

profile of v5, /device:TPU:0, one launch (start us, length us, event | category | flops | bytes accessed | tf_op | source)
XLA Modules:
  0.0 576.4 jit_solution(16546547446083189463)
XLA Ops:
  8.0 3.0 collective-permute-start.1
  12.5 5.5 multiply_sine_fusion
  18.2 4.6 concatenate.14.below_ref.refs_6_
  22.8 4.4 concatenate.13.above_ref.refs_5_
  28.2 4.6 concatenate.12.cos_ref.refs_4_
  33.2 23.7 %collective-permute-done.1.two_ref.refs_2_ = bf16[512,2048]{1,0:T(8,128)(2,1)} collective-permute-done((bf16[512,2048]{1,0:T(8,128)(2,1)}, bf16[512,2048]{1,0:T(8,128)(2,1)}, u32[]{:S(2)}, u32[]{:S(2)}) %collective-permute-start.1) | collective-permute-done | bytes 2097184 | tf_op jit(solution)/shard_map/ppermute | solution.py:32
  58.5 3.7 shard_map.194
  64.7 21.4 %collective-permute-done.2.refs_3_ = bf16[256,2048]{1,0:T(8,128)(2,1)} collective-permute-done((bf16[256,2048]{1,0:T(8,128)(2,1)}, bf16[256,2048]{1,0:T(8,128)(2,1)}, u32[]{:S(2)}, u32[]{:S(2)}) %collective-permute-start.2) | collective-permute-done | bytes 1048608 | tf_op jit(solution)/shard_map/ppermute | solution.py:32
  86.5 12.5 %shard_map.195 = (bf16[2048,2048]{1,0:T(8,128)(2,1)}, bf16[2048,2048]{1,0:T(8,128)(2,1)}, f32[2048,1]{1,0:T(8,128)}, f32[2048,1]{1,0:T(8,128)}, bf16[512,2048]{1,0:T(8,128)(2,1)}) custom-call(s32[5]{0:T(128)} %stack.19.starts_ref, f32[1,2048]{1,0:T(1,128)} %bitcast.35, f32[1,2048]{1,0:T(1,128)} %bitcast.40, bf16[512,2048]{1,0:T(8,128)(2,1)} %refs_13_.1, ...), custom_call_target="tpu_custom_call" | custom-call | flops 1 | bytes 1 | tf_op jit(solution)/shard_map/pallas_call | solution.py:1144
  103.9 32.0 %shard_map.196 = (bf16[2048,2048]{1,0:T(8,128)(2,1)}, bf16[2048,2048]{1,0:T(8,128)(2,1)}) custom-call(bf16[2048,2048]{1,0:T(8,128)(2,1)} %get-tuple-element.202.x_ref.x, bf16[2048,2048]{1,0:T(8,128)(2,1)} %all-gather.7.cloned.1.call-done.w_ref.up, f32[1,2048]{1,0:T(1,128)} %bitcast.37), custom_call_target="tpu_custom_call" | custom-call | flops 1 | bytes 1 | tf_op jit(solution)/shard_map/pallas_call | solution.py:251
  135.9 8.8 %collective-permute-done.5.two_ref.refs_2_ = bf16[512,2048]{1,0:T(8,128)(2,1)} collective-permute-done((bf16[512,2048]{1,0:T(8,128)(2,1)}, bf16[512,2048]{1,0:T(8,128)(2,1)}, u32[]{:S(2)}, u32[]{:S(2)}) %collective-permute-start.5) | collective-permute-done | bytes 2097184 | tf_op jit(solution)/shard_map/ppermute | solution.py:32
  145.7 3.7 shard_map.197
  152.1 7.1 %all-gather.9.cloned.1.call-done.w_ref.qkv = bf16[3,2048,512]{2,1,0:T(8,128)(2,1)} async-done(((bf16[3,256,512]{2,1,0:T(8,128)(2,1)}), bf16[3,2048,512]{2,1,0:T(8,128)(2,1)}) %all-gather.9.cloned.1.call-update) | async-done | bytes 6291472 | tf_op jit(solution)/shard_map/all_gather | solution.py:1190
  159.3 23.2 %shard_map.198.refs_0_.refs_1_.refs_2_ = bf16[2048,1536]{1,0:T(8,128)(2,1)} custom-call(bf16[2048,2048]{1,0:T(8,128)(2,1)} %get-tuple-element.202.x_ref.x, bf16[3,2048,512]{2,1,0:T(8,128)(2,1)} %all-gather.9.cloned.1.call-done.w_ref.qkv, f32[3,1,512]{2,1,0:T(1,128)} %reshape.84.bias_ref, f32[2048,128]{1,0:T(8,128)} %concatenate.12.cos_ref.refs_4_, ...), custom_call_target="tpu_custom_call" | custom-call | flops 1 | bytes 1 | tf_op jit(solution)/shard_map/pallas_call | solution.py:218
  182.5 25.6 %shard_map.199 = (bf16[2048,2048]{1,0:T(8,128)(2,1)}, bf16[2048,2048]{1,0:T(8,128)(2,1)}) custom-call(s32[5]{0:T(128)} %stack.19.starts_ref, bf16[2048,2048]{1,0:T(8,128)(2,1)} %get-tuple-element.222.active, bf16[512,2048]{1,0:T(8,128)(2,1)} %get-tuple-element.208.refs_0_, bf16[512,2048]{1,0:T(8,128)(2,1)} %collective-permute-done.4.one_ref.refs_1_, ...), custom_call_target="tpu_custom_call" | custom-call | flops 1 | bytes 1 | tf_op jit(solution)/shard_map/pallas_call | solution.py:386
  208.2 9.9 %convolution_convert_fusion.refs_3_ = bf16[2048,512]{1,0:T(8,128)(2,1)} fusion(bf16[2048,2048]{1,0:T(8,128)(2,1)} %get-tuple-element.241.grad_rows, bf16[512,2048]{1,0:T(8,128)(2,1)} %all-gather.11.cloned.1.call-done.refs_4_), kind=kOutput, calls=%fused_computation.1 | convolution fusion | flops 4296015872 | bytes 12582912 | tf_op jit(solution)/shard_map/td,kd->tk/dot_general | solution.py:1210
  221.2 54.2 %shard_map.200 = (bf16[2048,512]{1,0:T(8,128)(2,1)}, bf16[3,2048,512]{2,1,0:T(8,128)(2,1)}, f32[3,1,512]{2,1,0:T(1,128)}) custom-call(bf16[2048,1536]{1,0:T(8,128)(2,1)} %shard_map.198.refs_0_.refs_1_.refs_2_, bf16[2048,1536]{1,0:T(8,128)(2,1)} %shard_map.198.refs_0_.refs_1_.refs_2_, bf16[2048,1536]{1,0:T(8,128)(2,1)} %shard_map.198.refs_0_.refs_1_.refs_2_, ...), custom_call_target="tpu_custom_call" | custom-call | flops 1 | bytes 1 | tf_op jit(solution)/shard_map/pallas_call | solution.py:1053
  275.4 3.6 shard_map.202
  280.6 23.6 %shard_map.201 = (bf16[512,2048]{1,0:T(8,128)(2,1)}, bf16[512,2048]{1,0:T(8,128)(2,1)}, bf16[256,2048]{1,0:T(8,128)(2,1)}, bf16[256,2048]{1,0:T(8,128)(2,1)}, bf...) custom-call(s32[4]{0:T(128)} %pad_add_fusion.starts_ref, bf16[2048,2048]{1,0:T(8,128)(2,1)} %get-tuple-element.222.active, ...), custom_call_target="tpu_custom_call" | custom-call | flops 1 | bytes 1 | tf_op jit(solution)/shard_map/pallas_call | solution.py:475
  307.4 48.3 %shard_map.203 = (bf16[2048,2048]{1,0:T(8,128)(2,1)}, bf16[2048,2048]{1,0:T(8,128)(2,1)}, f32[2,1,1024]{2,1,0:T(1,128)}) custom-call(bf16[2048,2048]{1,0:T(8,128)(2,1)} %get-tuple-element.241.grad_rows, bf16[2048,2048]{1,0:T(8,128)(2,1)} %all-gather.13.cloned.1.call-done.weight, bf16[2048,2048]{1,0:T(8,128)(2,1)} %get-tuple-element.242.slope, ...), custom_call_target="tpu_custom_call" | custom-call | flops 1 | bytes 1 | tf_op jit(solution)/shard_map/pallas_call | solution.py:588
  355.7 4.5 shard_map.205
  360.2 3.3 reduce-scatter.4.cloned.1.call-done
  366.5 54.0 %shard_map.204 = (bf16[2048,512]{1,0:T(8,128)(2,1)}, bf16[3,2048,512]{2,1,0:T(8,128)(2,1)}, f32[3,1,512]{2,1,0:T(1,128)}) custom-call(bf16[2048,1536]{1,0:T(8,128)(2,1)} %shard_map.198.refs_0_.refs_1_.refs_2_, bf16[2048,1536]{1,0:T(8,128)(2,1)} %shard_map.198.refs_0_.refs_1_.refs_2_, ...), custom_call_target="tpu_custom_call", output_to_operand_aliasing={{0}: (7, {}), {1}: (8, {}), {2}: (9, {})} | custom-call | flops 1 | bytes 1 | tf_op jit(solution)/shard_map/pallas_call | solution.py:1053
  426.9 23.0 %shard_map.206 = bf16[4,2048,512]{2,1,0:T(8,128)(2,1)} custom-call(bf16[2048,2048]{1,0:T(8,128)(2,1)} %get-tuple-element.202.x_ref.x, bf16[3,2048,512]{2,1,0:T(8,128)(2,1)} %get-tuple-element.274.joined, bf16[2048,2048]{1,0:T(8,128)(2,1)} %get-tuple-element.241.grad_rows, bf16[2048,512]{1,0:T(8,128)(2,1)} %get-tuple-element.259.mixed), custom_call_target="tpu_custom_call" | custom-call | flops 1 | bytes 1 | tf_op jit(solution)/shard_map/pallas_call | solution.py:660
  449.9 3.7 reduce-scatter.6.cloned.1.call-done
  453.6 24.1 %shard_map.207 = (f32[1,1024]{1,0:T(1,128)}, f32[1,1024]{1,0:T(1,128)}, bf16[512,1024]{1,0:T(8,128)(2,1)}, bf16[512,1024]{1,0:T(8,128)(2,1)}, bf16[256,1024]{1,0...) custom-call(s32[4]{0:T(128)} %pad_add_fusion.starts_ref, ...), custom_call_target="tpu_custom_call" | custom-call | flops 1 | bytes 1 | tf_op jit(solution)/shard_map/pallas_call | solution.py:771
  480.7 24.1 %shard_map.208 = (f32[1,1024]{1,0:T(1,128)}, f32[1,1024]{1,0:T(1,128)}, bf16[512,1024]{1,0:T(8,128)(2,1)}, bf16[512,1024]{1,0:T(8,128)(2,1)}, bf16[256,1024]{1,0...) custom-call(s32[4]{0:T(128)} %pad_add_fusion.starts_ref, ...), custom_call_target="tpu_custom_call" | custom-call | flops 1 | bytes 1 | tf_op jit(solution)/shard_map/pallas_call | solution.py:771
  506.1 3.0 shard_map.210
  512.1 10.6 %shard_map.209 = bf16[512,2048]{1,0:T(8,128)(2,1)} custom-call(bf16[512,512]{1,0:T(8,128)(2,1)} %get-tuple-element.289.refs_0_, bf16[512,512]{1,0:T(8,128)(2,1)} %collective-permute-done.16.refs_1_, bf16[512,512]{1,0:T(8,128)(2,1)} %collective-permute-done.17.refs_2_, bf16[512,512]{1,0:T(8,128)(2,1)} %collective-permute-done.18.refs_3_, ...), custom_call_target="tpu_custom_call" | custom-call | flops 1 | bytes 1 | tf_op jit(solution)/shard_map/pallas_call | solution.py:821
  522.7 16.1 %all-gather.1 = f32[8,76,128]{2,1,0:T(8,128)S(1)} all-gather(f32[1,76,128]{2,1,0:T(8,128)S(1)} %bitcast.34), channel_id=2, replica_groups=mesh['dp'=8,'tensor'=4] {'dp'}, dimensions={0}, use_global_device_ids=true | all-gather | bytes 350208 | tf_op jit(solution)/shard_map/all_gather | solution.py:1260
  539.0 3.0 shard_map.211
  560.6 8.7 %shard_map.212 = bf16[512,2048]{1,0:T(8,128)(2,1)} custom-call(bf16[256,1024]{1,0:T(8,128)(2,1)} %collective-permute-done.23.refs_0_, bf16[256,1024]{1,0:T(8,128)(2,1)} %collective-permute-done.24.refs_1_, bf16[512,1024]{1,0:T(8,128)(2,1)} %collective-permute-done.19.b_ref.refs_2_, bf16[512,1024]{1,0:T(8,128)(2,1)} %collective-permute-done.20.d_ref.refs_3_, ...), custom_call_target="tpu_custom_call" | custom-call | flops 1 | bytes 1 | tf_op jit(solution)/shard_map/pallas_call | solution.py:884
  (125 shorter events, 60.1 us)
Async XLA Ops:
  7.2 96.7 %all-gather.7.cloned.1.call-start = ((), (), s32[]{:S(2)}) async-start(), calls=%async_computation.3 | async-start | bytes 9437184 | tf_op jit(solution)/shard_map/all_gather | solution.py:1185
  7.9 151.4 %all-gather.9.cloned.1.call-start = ((), (), s32[]{:S(2)}) async-start(), calls=%async_computation.4 | async-start | bytes 7077888 | tf_op jit(solution)/shard_map/all_gather | solution.py:1190
  8.0 49.0 %collective-permute-start.1 = (bf16[512,2048]{1,0:T(8,128)(2,1)}, bf16[512,2048]{1,0:T(8,128)(2,1)}, u32[]{:S(2)}, u32[]{:S(2)}) collective-permute-start(bf16[512,2048]{1,0:T(8,128)(2,1)} %refs_12_.1), channel_id=1, source_target_pairs={{0,2},{1,3},{2,0},{3,1},{4,6},{5,7},{6,4},{7,5},{8,10},{9,11},{10,... | collective-permute-start | bytes 6291464 | tf_op jit(solution)/shard_map/ppermute | solution.py:32
  11.0 47.4 %collective-permute-start = (bf16[512,2048]{1,0:T(8,128)(2,1)}, bf16[512,2048]{1,0:T(8,128)(2,1)}, u32[]{:S(2)}, u32[]{:S(2)}) collective-permute-start(bf16[512,2048]{1,0:T(8,128)(2,1)} %refs_12_.1), channel_id=1, source_target_pairs={{0,1},{1,0},{2,3},{3,2},{4,5},{5,4},{6,7},{7,6},{8,9},{9,8},{10,11... | collective-permute-start | bytes 6291464 | tf_op jit(solution)/shard_map/ppermute | solution.py:32
  58.4 149.8 %all-gather.11.cloned.1.call-start = ((), (), s32[]{:S(2)}) async-start(), calls=%async_computation.5 | async-start | bytes 2359296 | tf_op jit(solution)/shard_map/all_gather | solution.py:1199
  62.1 24.0 %collective-permute-start.2 = (bf16[256,2048]{1,0:T(8,128)(2,1)}, bf16[256,2048]{1,0:T(8,128)(2,1)}, u32[]{:S(2)}, u32[]{:S(2)}) collective-permute-start(bf16[256,2048]{1,0:T(8,128)(2,1)} %get-tuple-element.188), channel_id=1, source_target_pairs={{0,2},{1,3},{2,0},{3,1},{4,6},{5,7},{6,4},{7,5},{8,10},{9,11},{10,... | collective-permute-start | bytes 3145736 | tf_op jit(solution)/shard_map/ppermute | solution.py:32
  62.4 24.1 %collective-permute-start.3 = (bf16[256,2048]{1,0:T(8,128)(2,1)}, bf16[256,2048]{1,0:T(8,128)(2,1)}, u32[]{:S(2)}, u32[]{:S(2)}) collective-permute-start(bf16[256,2048]{1,0:T(8,128)(2,1)} %get-tuple-element.189), channel_id=1, source_target_pairs={{0,1},{1,0},{2,3},{3,2},{4,5},{5,4},{6,7},{7,6},{8,9},{9,8},{10,11... | collective-permute-start | bytes 3145736 | tf_op jit(solution)/shard_map/ppermute | solution.py:32
  99.0 181.6 %all-gather.13.cloned.1.call-start = ((), (), s32[]{:S(2)}) async-start(), calls=%async_computation.6 | async-start | bytes 9437184 | tf_op jit(solution)/shard_map/all_gather | solution.py:1205
  99.1 45.7 %collective-permute-start.5 = (bf16[512,2048]{1,0:T(8,128)(2,1)}, bf16[512,2048]{1,0:T(8,128)(2,1)}, u32[]{:S(2)}, u32[]{:S(2)}) collective-permute-start(bf16[512,2048]{1,0:T(8,128)(2,1)} %get-tuple-element.208.refs_0_), channel_id=1, source_target_pairs={{0,2},{1,3},{2,0},{3,1},{4,6},{5,7},{6,4},{7,5},{8,10},{9,11},{10,... | collective-permute-start | bytes 6291464 | tf_op jit(solution)/shard_map/ppermute | solution.py:32
  100.5 44.9 %collective-permute-start.4 = (bf16[512,2048]{1,0:T(8,128)(2,1)}, bf16[512,2048]{1,0:T(8,128)(2,1)}, u32[]{:S(2)}, u32[]{:S(2)}) collective-permute-start(bf16[512,2048]{1,0:T(8,128)(2,1)} %get-tuple-element.208.refs_0_), channel_id=1, source_target_pairs={{0,1},{1,0},{2,3},{3,2},{4,5},{5,4},{6,7},{7,6},{8,9},{9,8},{10,11... | collective-permute-start | bytes 6291464 | tf_op jit(solution)/shard_map/ppermute | solution.py:32
  145.5 218.0 %reduce-scatter.4.cloned.1.call-start = ((), (), s32[]{:S(2)}) async-start(), calls=%async_computation.7 | async-start | bytes 9437184 | tf_op jit(solution)/shard_map/reduce_scatter | solution.py:1214
  149.3 33.2 %collective-permute-start.6 = (bf16[256,2048]{1,0:T(8,128)(2,1)}, bf16[256,2048]{1,0:T(8,128)(2,1)}, u32[]{:S(2)}, u32[]{:S(2)}) collective-permute-start(bf16[256,2048]{1,0:T(8,128)(2,1)} %get-tuple-element.199), channel_id=1, source_target_pairs={{0,2},{1,3},{2,0},{3,1},{4,6},{5,7},{6,4},{7,5},{8,10},{9,11},{10,... | collective-permute-start | bytes 3145736 | tf_op jit(solution)/shard_map/ppermute | solution.py:32
  150.4 32.1 %collective-permute-start.7 = (bf16[256,2048]{1,0:T(8,128)(2,1)}, bf16[256,2048]{1,0:T(8,128)(2,1)}, u32[]{:S(2)}, u32[]{:S(2)}) collective-permute-start(bf16[256,2048]{1,0:T(8,128)(2,1)} %get-tuple-element.200), channel_id=1, source_target_pairs={{0,1},{1,0},{2,3},{3,2},{4,5},{5,4},{6,7},{7,6},{8,9},{9,8},{10,11... | collective-permute-start | bytes 3145736 | tf_op jit(solution)/shard_map/ppermute | solution.py:32
  208.2 245.5 %reduce-scatter.6.cloned.1.call-start = ((), (), s32[]{:S(2)}) async-start(), calls=%async_computation.8 | async-start | bytes 9437184 | tf_op jit(solution)/shard_map/reduce_scatter | solution.py:1228
  218.1 57.3 %collective-permute-start.9 = (bf16[512,2048]{1,0:T(8,128)(2,1)}, bf16[512,2048]{1,0:T(8,128)(2,1)}, u32[]{:S(2)}, u32[]{:S(2)}) collective-permute-start(bf16[512,2048]{1,0:T(8,128)(2,1)} %all-gather.11.cloned.1.call-done.refs_4_), channel_id=1, source_target_pairs={{0,2},{1,3},{2,0},{3,1},{4,6},{5,7},{6,4},{7,5},{8,10},{9,11},{10,... | collective-permute-start | bytes 6291464 | tf_op jit(solution)/shard_map/ppermute | solution.py:32
  219.7 55.7 %collective-permute-start.8 = (bf16[512,2048]{1,0:T(8,128)(2,1)}, bf16[512,2048]{1,0:T(8,128)(2,1)}, u32[]{:S(2)}, u32[]{:S(2)}) collective-permute-start(bf16[512,2048]{1,0:T(8,128)(2,1)} %all-gather.11.cloned.1.call-done.refs_4_), channel_id=1, source_target_pairs={{0,1},{1,0},{2,3},{3,2},{4,5},{5,4},{6,7},{7,6},{8,9},{9,8},{10,11... | collective-permute-start | bytes 6291464 | tf_op jit(solution)/shard_map/ppermute | solution.py:32
  279.0 25.2 %collective-permute-start.10 = (bf16[256,2048]{1,0:T(8,128)(2,1)}, bf16[256,2048]{1,0:T(8,128)(2,1)}, u32[]{:S(2)}, u32[]{:S(2)}) collective-permute-start(bf16[256,2048]{1,0:T(8,128)(2,1)} %get-tuple-element.233), channel_id=1, source_target_pairs={{0,2},{1,3},{2,0},{3,1},{4,6},{5,7},{6,4},{7,5},{8,10},{9,11},{10,... | collective-permute-start | bytes 3145736 | tf_op jit(solution)/shard_map/ppermute | solution.py:32
  279.6 24.8 %collective-permute-start.11 = (bf16[256,2048]{1,0:T(8,128)(2,1)}, bf16[256,2048]{1,0:T(8,128)(2,1)}, u32[]{:S(2)}, u32[]{:S(2)}) collective-permute-start(bf16[256,2048]{1,0:T(8,128)(2,1)} %get-tuple-element.234), channel_id=1, source_target_pairs={{0,1},{1,0},{2,3},{3,2},{4,5},{5,4},{6,7},{7,6},{8,9},{9,8},{10,11... | collective-permute-start | bytes 3145736 | tf_op jit(solution)/shard_map/ppermute | solution.py:32
  304.4 51.3 %collective-permute-start.12 = (bf16[512,2048]{1,0:T(8,128)(2,1)}, bf16[512,2048]{1,0:T(8,128)(2,1)}, u32[]{:S(2)}, u32[]{:S(2)}) collective-permute-start(bf16[512,2048]{1,0:T(8,128)(2,1)} %get-tuple-element.235), channel_id=1, source_target_pairs={{0,1},{1,0},{2,3},{3,2},{4,5},{5,4},{6,7},{7,6},{8,9},{9,8},{10,11... | collective-permute-start | bytes 6291464 | tf_op jit(solution)/shard_map/ppermute | solution.py:32
  305.9 49.8 %collective-permute-start.13 = (bf16[512,2048]{1,0:T(8,128)(2,1)}, bf16[512,2048]{1,0:T(8,128)(2,1)}, u32[]{:S(2)}, u32[]{:S(2)}) collective-permute-start(bf16[512,2048]{1,0:T(8,128)(2,1)} %get-tuple-element.236), channel_id=1, source_target_pairs={{0,2},{1,3},{2,0},{3,1},{4,6},{5,7},{6,4},{7,5},{8,10},{9,11},{10,... | collective-permute-start | bytes 6291464 | tf_op jit(solution)/shard_map/ppermute | solution.py:32
  363.5 190.1 %reduce-scatter.8.cloned.1.call-start = ((), (), s32[]{:S(2)}) async-start(), calls=%async_computation.9 | async-start | bytes 9437184 | tf_op jit(solution)/shard_map/reduce_scatter | solution.py:1239
  363.5 57.0 %collective-permute-start.14 = (bf16[256,2048]{1,0:T(8,128)(2,1)}, bf16[256,2048]{1,0:T(8,128)(2,1)}, u32[]{:S(2)}, u32[]{:S(2)}) collective-permute-start(bf16[256,2048]{1,0:T(8,128)(2,1)} %get-tuple-element.254), channel_id=1, source_target_pairs={{0,2},{1,3},{2,0},{3,1},{4,6},{5,7},{6,4},{7,5},{8,10},{9,11},{10,... | collective-permute-start | bytes 3145736 | tf_op jit(solution)/shard_map/ppermute | solution.py:32
  365.1 55.5 %collective-permute-start.15 = (bf16[256,2048]{1,0:T(8,128)(2,1)}, bf16[256,2048]{1,0:T(8,128)(2,1)}, u32[]{:S(2)}, u32[]{:S(2)}) collective-permute-start(bf16[256,2048]{1,0:T(8,128)(2,1)} %get-tuple-element.255), channel_id=1, source_target_pairs={{0,1},{1,0},{2,3},{3,2},{4,5},{5,4},{6,7},{7,6},{8,9},{9,8},{10,11... | collective-permute-start | bytes 3145736 | tf_op jit(solution)/shard_map/ppermute | solution.py:32
  423.4 26.5 %collective-permute-start.18 = (bf16[512,512]{1,0:T(8,128)(2,1)}, bf16[512,512]{1,0:T(8,128)(2,1)}, u32[]{:S(2)}, u32[]{:S(2)}) collective-permute-start(bf16[512,512]{1,0:T(8,128)(2,1)} %get-tuple-element.392), channel_id=1, source_target_pairs={{0,3},{1,2},{2,1},{3,0},{4,7},{5,6},{6,5},{7,4},{8,11},{9,10},{10,... | collective-permute-start | bytes 1572872 | tf_op jit(solution)/shard_map/ppermute | solution.py:32
  424.1 25.8 %collective-permute-start.17 = (bf16[512,512]{1,0:T(8,128)(2,1)}, bf16[512,512]{1,0:T(8,128)(2,1)}, u32[]{:S(2)}, u32[]{:S(2)}) collective-permute-start(bf16[512,512]{1,0:T(8,128)(2,1)} %get-tuple-element.393), channel_id=1, source_target_pairs={{0,2},{1,3},{2,0},{3,1},{4,6},{5,7},{6,4},{7,5},{8,10},{9,11},{10,... | collective-permute-start | bytes 1572872 | tf_op jit(solution)/shard_map/ppermute | solution.py:32
  425.5 24.4 %collective-permute-start.16 = (bf16[512,512]{1,0:T(8,128)(2,1)}, bf16[512,512]{1,0:T(8,128)(2,1)}, u32[]{:S(2)}, u32[]{:S(2)}) collective-permute-start(bf16[512,512]{1,0:T(8,128)(2,1)} %get-tuple-element.394), channel_id=1, source_target_pairs={{0,1},{1,0},{2,3},{3,2},{4,5},{5,4},{6,7},{7,6},{8,9},{9,8},{10,11... | collective-permute-start | bytes 1572872 | tf_op jit(solution)/shard_map/ppermute | solution.py:32
  477.7 27.1 %collective-permute-start.19 = (bf16[512,1024]{1,0:T(8,128)(2,1)}, bf16[512,1024]{1,0:T(8,128)(2,1)}, u32[]{:S(2)}, u32[]{:S(2)}) collective-permute-start(bf16[512,1024]{1,0:T(8,128)(2,1)} %get-tuple-element.268), channel_id=1, source_target_pairs={{0,1},{1,0},{2,3},{3,2},{4,5},{5,4},{6,7},{7,6},{8,9},{9,8},{10,11... | collective-permute-start | bytes 3145736 | tf_op jit(solution)/shard_map/ppermute | solution.py:32
  479.3 25.6 %collective-permute-start.20 = (bf16[512,1024]{1,0:T(8,128)(2,1)}, bf16[512,1024]{1,0:T(8,128)(2,1)}, u32[]{:S(2)}, u32[]{:S(2)}) collective-permute-start(bf16[512,1024]{1,0:T(8,128)(2,1)} %get-tuple-element.269), channel_id=1, source_target_pairs={{0,2},{1,3},{2,0},{3,1},{4,6},{5,7},{6,4},{7,5},{8,10},{9,11},{10,... | collective-permute-start | bytes 3145736 | tf_op jit(solution)/shard_map/ppermute | solution.py:32
  504.9 34.2 %collective-permute-start.21 = (bf16[512,1024]{1,0:T(8,128)(2,1)}, bf16[512,1024]{1,0:T(8,128)(2,1)}, u32[]{:S(2)}, u32[]{:S(2)}) collective-permute-start(bf16[512,1024]{1,0:T(8,128)(2,1)} %get-tuple-element.283), channel_id=1, source_target_pairs={{0,1},{1,0},{2,3},{3,2},{4,5},{5,4},{6,7},{7,6},{8,9},{9,8},{10,11... | collective-permute-start | bytes 3145736 | tf_op jit(solution)/shard_map/ppermute | solution.py:32
  505.5 33.5 %collective-permute-start.22 = (bf16[512,1024]{1,0:T(8,128)(2,1)}, bf16[512,1024]{1,0:T(8,128)(2,1)}, u32[]{:S(2)}, u32[]{:S(2)}) collective-permute-start(bf16[512,1024]{1,0:T(8,128)(2,1)} %get-tuple-element.284), channel_id=1, source_target_pairs={{0,2},{1,3},{2,0},{3,1},{4,6},{5,7},{6,4},{7,5},{8,10},{9,11},{10,... | collective-permute-start | bytes 3145736 | tf_op jit(solution)/shard_map/ppermute | solution.py:32
  509.2 29.9 %collective-permute-start.23 = (bf16[256,1024]{1,0:T(8,128)(2,1)}, bf16[256,1024]{1,0:T(8,128)(2,1)}, u32[]{:S(2)}, u32[]{:S(2)}) collective-permute-start(bf16[256,1024]{1,0:T(8,128)(2,1)} %get-tuple-element.316), channel_id=1, source_target_pairs={{0,2},{1,3},{2,0},{3,1},{4,6},{5,7},{6,4},{7,5},{8,10},{9,11},{10,... | collective-permute-start | bytes 1572872 | tf_op jit(solution)/shard_map/ppermute | solution.py:32
  510.6 28.4 %collective-permute-start.24 = (bf16[256,1024]{1,0:T(8,128)(2,1)}, bf16[256,1024]{1,0:T(8,128)(2,1)}, u32[]{:S(2)}, u32[]{:S(2)}) collective-permute-start(bf16[256,1024]{1,0:T(8,128)(2,1)} %get-tuple-element.317), channel_id=1, source_target_pairs={{0,1},{1,0},{2,3},{3,2},{4,5},{5,4},{6,7},{7,6},{8,9},{9,8},{10,11... | collective-permute-start | bytes 1572872 | tf_op jit(solution)/shard_map/ppermute | solution.py:32
  (14 other events, 159.8 us)
Sparse Core Ops, SparseCore 0:
  9.6 84.7 all-gather.6
  96.0 63.2 all-gather.8
  160.9 29.5 all-gather.10
  191.9 81.5 all-gather.12
  275.6 87.8 reduce-scatter.3
  365.6 87.9 reduce-scatter.5
  455.9 90.5 reduce-scatter.7

commit v6 on v5

--- a/solution.py
+++ b/solution.py
@@ -873,7 +873,7 @@
         return (wide(cotangent) + grad_input).astype(tokens.dtype)
     half, split = left_parts[4].shape
     rows, depth = tokens.shape
-    chunk = min(64, half)
+    chunk = min(128, half)
     steps = half // chunk
     low_part = pl.BlockSpec((chunk, split), lambda i: (jnp.minimum(i, steps - 1), 0))
     high_part = pl.BlockSpec((chunk, split), lambda i: (jnp.maximum(i - steps, 0), 0))
@@ -1226,7 +1226,7 @@
     grad_up, feed_parts = after((grad_up, feed_parts))
     feed_parts = scatter_fold(feed_parts)
     grad_up_sum = lax.psum_scatter(
-        after(grad_up, grad_down_sum, feed_parts[:2]), "dp", scatter_dimension=0, tiled=True
+        after(grad_up, feed_parts[:2]), "dp", scatter_dimension=0, tiled=True
     )
     feed_parts = scatter_pass(feed_parts)
     part = attention(after(joined, grad_up), grad_mixed, lanes, pairs // 2, pairs, part)
@@ -1237,7 +1237,7 @@
     grad_last = last_grads(gathered, grad_joined, grad_rows, mixed)
     grad_last, mixed_parts = after((grad_last, mixed_parts))
     grad_last_sum = lax.psum_scatter(
-        after(grad_last, grad_up_sum), "dp", scatter_dimension=1, tiled=True
+        grad_last, "dp", scatter_dimension=1, tiled=True
     )
     half = depth // 2
     sources = full_qkv, grad_hidden, full_up, all_tokens, mean, root

time: 585 us -> 575 us (0.983)
  waiting for transfers between devices: 75 us -> 68.2 us
  transfers between devices with their start and end apart: 37 -> 37, of which waited for: 13 -> 12; matrix products, arithmetic and copies ran while one was open for 8% -> 8% of each run, Pallas kernels for 65% -> 67%
where the time goes in v6:
time: 575 us; the launch traced here: 566 us
  Pallas kernels  384 us (67%)
  waiting for transfers between devices  68.2 us (12%)
  starting transfers between devices  36.3 us (6%)
  local copies, waits for them, and re-layouts  25 us (4%)
  blocking collectives  16.1 us (3%)
  between operations  14.7 us (3%)
  other arithmetic  12.4 us (2%)
  matrix products  9.88 us (2%)
    pallas_call x2, Pallas kernels, attention(): pl.pallas_call(body, grid=(last - first, block_count), in_specs=[row_bloc...  108 us
    ppermute x30, waiting for transfers between devices, swap(): return lax.ppermute(value, axis, [(i, i ^ bit) for i in range(count)])  59.2 us
    pallas_call x2, Pallas kernels, normed_grads(): whole_call(kernel, [SMEM] + [ANY] * 5 + [VMEM] * 2, [VMEM, VMEM] + [ANY]...  48.3 us
    pallas_call x1, Pallas kernels, hidden_grads(): whole_call(hidden_grads_kernel, [ANY] * 4, [ANY, ANY, VMEM], [jax.ShapeDt...  48.2 us
    ppermute x30, starting transfers between devices, swap(): return lax.ppermute(value, axis, [(i, i ^ bit) for i in range(count)])  35.8 us
    pallas_call x1, Pallas kernels, hidden_rows(): pl.pallas_call(hidden_kernel, grid=(width // columns, rows // block), in_...  32 us
    pallas_call x1, Pallas kernels, first_grads(): whole_call(first_grads_kernel, [SMEM] + [ANY] * (1 + count), [ANY, ANY],...  25.6 us
    pallas_call x1, Pallas kernels, feed_rows(): whole_call(functools.partial(feed_kernel, places=places), [SMEM] + [ANY]...  23.6 us
  transfers between devices with their start and end apart: 37, of which 12 were waited for; matrix products, arithmetic and copies ran while one was open for 8% of the time, Pallas kernels for 67%

profile of v6, /device:TPU:0, one launch (start us, length us, event | category | flops | bytes accessed | tf_op | source)
XLA Modules:
  0.0 566.3 jit_solution(9452511194907160562)
XLA Ops:
  8.0 3.0 collective-permute-start.1
  12.5 5.5 multiply_sine_fusion
  18.2 4.6 concatenate.14.below_ref.refs_6_
  22.8 4.4 concatenate.13.above_ref.refs_5_
  28.2 4.6 concatenate.12.cos_ref.refs_4_
  33.2 23.7 %collective-permute-done.1.two_ref.refs_2_ = bf16[512,2048]{1,0:T(8,128)(2,1)} collective-permute-done((bf16[512,2048]{1,0:T(8,128)(2,1)}, bf16[512,2048]{1,0:T(8,128)(2,1)}, u32[]{:S(2)}, u32[]{:S(2)}) %collective-permute-start.1) | collective-permute-done | bytes 2097184 | tf_op jit(solution)/shard_map/ppermute | solution.py:32
  58.5 3.7 shard_map.194
  64.7 21.4 %collective-permute-done.2.refs_3_ = bf16[256,2048]{1,0:T(8,128)(2,1)} collective-permute-done((bf16[256,2048]{1,0:T(8,128)(2,1)}, bf16[256,2048]{1,0:T(8,128)(2,1)}, u32[]{:S(2)}, u32[]{:S(2)}) %collective-permute-start.2) | collective-permute-done | bytes 1048608 | tf_op jit(solution)/shard_map/ppermute | solution.py:32
  86.5 12.5 %shard_map.195 = (bf16[2048,2048]{1,0:T(8,128)(2,1)}, bf16[2048,2048]{1,0:T(8,128)(2,1)}, f32[2048,1]{1,0:T(8,128)}, f32[2048,1]{1,0:T(8,128)}, bf16[512,2048]{1,0:T(8,128)(2,1)}) custom-call(s32[5]{0:T(128)} %stack.19.starts_ref, f32[1,2048]{1,0:T(1,128)} %bitcast.35, f32[1,2048]{1,0:T(1,128)} %bitcast.40, bf16[512,2048]{1,0:T(8,128)(2,1)} %refs_13_.1, ...), custom_call_target="tpu_custom_call" | custom-call | flops 1 | bytes 1 | tf_op jit(solution)/shard_map/pallas_call | solution.py:1144
  104.0 32.0 %shard_map.196 = (bf16[2048,2048]{1,0:T(8,128)(2,1)}, bf16[2048,2048]{1,0:T(8,128)(2,1)}) custom-call(bf16[2048,2048]{1,0:T(8,128)(2,1)} %get-tuple-element.201.x_ref.x, bf16[2048,2048]{1,0:T(8,128)(2,1)} %all-gather.7.cloned.1.call-done.w_ref.up, f32[1,2048]{1,0:T(1,128)} %bitcast.37), custom_call_target="tpu_custom_call" | custom-call | flops 1 | bytes 1 | tf_op jit(solution)/shard_map/pallas_call | solution.py:251
  136.0 8.8 %collective-permute-done.5.two_ref.refs_2_ = bf16[512,2048]{1,0:T(8,128)(2,1)} collective-permute-done((bf16[512,2048]{1,0:T(8,128)(2,1)}, bf16[512,2048]{1,0:T(8,128)(2,1)}, u32[]{:S(2)}, u32[]{:S(2)}) %collective-permute-start.5) | collective-permute-done | bytes 2097184 | tf_op jit(solution)/shard_map/ppermute | solution.py:32
  145.9 3.6 shard_map.197
  152.2 7.1 %all-gather.9.cloned.1.call-done.w_ref.qkv = bf16[3,2048,512]{2,1,0:T(8,128)(2,1)} async-done(((bf16[3,256,512]{2,1,0:T(8,128)(2,1)}), bf16[3,2048,512]{2,1,0:T(8,128)(2,1)}) %all-gather.9.cloned.1.call-update) | async-done | bytes 6291472 | tf_op jit(solution)/shard_map/all_gather | solution.py:1190
  159.3 23.2 %shard_map.198.refs_0_.refs_1_.refs_2_ = bf16[2048,1536]{1,0:T(8,128)(2,1)} custom-call(bf16[2048,2048]{1,0:T(8,128)(2,1)} %get-tuple-element.201.x_ref.x, bf16[3,2048,512]{2,1,0:T(8,128)(2,1)} %all-gather.9.cloned.1.call-done.w_ref.qkv, f32[3,1,512]{2,1,0:T(1,128)} %reshape.84.bias_ref, f32[2048,128]{1,0:T(8,128)} %concatenate.12.cos_ref.refs_4_, ...), custom_call_target="tpu_custom_call" | custom-call | flops 1 | bytes 1 | tf_op jit(solution)/shard_map/pallas_call | solution.py:218
  182.5 25.6 %shard_map.199 = (bf16[2048,2048]{1,0:T(8,128)(2,1)}, bf16[2048,2048]{1,0:T(8,128)(2,1)}) custom-call(s32[5]{0:T(128)} %stack.19.starts_ref, bf16[2048,2048]{1,0:T(8,128)(2,1)} %get-tuple-element.221.active, bf16[512,2048]{1,0:T(8,128)(2,1)} %get-tuple-element.207.refs_0_, bf16[512,2048]{1,0:T(8,128)(2,1)} %collective-permute-done.4.one_ref.refs_1_, ...), custom_call_target="tpu_custom_call" | custom-call | flops 1 | bytes 1 | tf_op jit(solution)/shard_map/pallas_call | solution.py:386
  208.2 9.9 %convolution_convert_fusion.refs_3_ = bf16[2048,512]{1,0:T(8,128)(2,1)} fusion(bf16[2048,2048]{1,0:T(8,128)(2,1)} %get-tuple-element.240.grad_rows, bf16[512,2048]{1,0:T(8,128)(2,1)} %all-gather.11.cloned.1.call-done.refs_4_), kind=kOutput, calls=%fused_computation.1 | convolution fusion | flops 4296015872 | bytes 12582912 | tf_op jit(solution)/shard_map/td,kd->tk/dot_general | solution.py:1210
  221.2 54.2 %shard_map.200 = (bf16[2048,512]{1,0:T(8,128)(2,1)}, bf16[3,2048,512]{2,1,0:T(8,128)(2,1)}, f32[3,1,512]{2,1,0:T(1,128)}) custom-call(bf16[2048,1536]{1,0:T(8,128)(2,1)} %shard_map.198.refs_0_.refs_1_.refs_2_, bf16[2048,1536]{1,0:T(8,128)(2,1)} %shard_map.198.refs_0_.refs_1_.refs_2_, bf16[2048,1536]{1,0:T(8,128)(2,1)} %shard_map.198.refs_0_.refs_1_.refs_2_, ...), custom_call_target="tpu_custom_call" | custom-call | flops 1 | bytes 1 | tf_op jit(solution)/shard_map/pallas_call | solution.py:1053
  275.4 3.6 shard_map.202
  280.6 23.6 %shard_map.201 = (bf16[512,2048]{1,0:T(8,128)(2,1)}, bf16[512,2048]{1,0:T(8,128)(2,1)}, bf16[256,2048]{1,0:T(8,128)(2,1)}, bf16[256,2048]{1,0:T(8,128)(2,1)}, bf...) custom-call(s32[4]{0:T(128)} %pad_add_fusion.starts_ref, bf16[2048,2048]{1,0:T(8,128)(2,1)} %get-tuple-element.221.active, ...), custom_call_target="tpu_custom_call" | custom-call | flops 1 | bytes 1 | tf_op jit(solution)/shard_map/pallas_call | solution.py:475
  307.4 48.2 %shard_map.203 = (bf16[2048,2048]{1,0:T(8,128)(2,1)}, bf16[2048,2048]{1,0:T(8,128)(2,1)}, f32[2,1,1024]{2,1,0:T(1,128)}) custom-call(bf16[2048,2048]{1,0:T(8,128)(2,1)} %get-tuple-element.240.grad_rows, bf16[2048,2048]{1,0:T(8,128)(2,1)} %all-gather.13.cloned.1.call-done.weight, bf16[2048,2048]{1,0:T(8,128)(2,1)} %get-tuple-element.241.slope, ...), custom_call_target="tpu_custom_call" | custom-call | flops 1 | bytes 1 | tf_op jit(solution)/shard_map/pallas_call | solution.py:588
  355.6 4.5 shard_map.205
  361.4 54.1 %shard_map.204 = (bf16[2048,512]{1,0:T(8,128)(2,1)}, bf16[3,2048,512]{2,1,0:T(8,128)(2,1)}, f32[3,1,512]{2,1,0:T(1,128)}) custom-call(bf16[2048,1536]{1,0:T(8,128)(2,1)} %shard_map.198.refs_0_.refs_1_.refs_2_, bf16[2048,1536]{1,0:T(8,128)(2,1)} %shard_map.198.refs_0_.refs_1_.refs_2_, ...), custom_call_target="tpu_custom_call", output_to_operand_aliasing={{0}: (7, {}), {1}: (8, {}), {2}: (9, {})} | custom-call | flops 1 | bytes 1 | tf_op jit(solution)/shard_map/pallas_call | solution.py:1053
  415.5 2.9 constant_dynamic-slice_fusion
  421.9 23.0 %shard_map.206 = bf16[4,2048,512]{2,1,0:T(8,128)(2,1)} custom-call(bf16[2048,2048]{1,0:T(8,128)(2,1)} %get-tuple-element.201.x_ref.x, bf16[3,2048,512]{2,1,0:T(8,128)(2,1)} %get-tuple-element.273.joined, bf16[2048,2048]{1,0:T(8,128)(2,1)} %get-tuple-element.240.grad_rows, bf16[2048,512]{1,0:T(8,128)(2,1)} %get-tuple-element.258.mixed), custom_call_target="tpu_custom_call" | custom-call | flops 1 | bytes 1 | tf_op jit(solution)/shard_map/pallas_call | solution.py:660
  444.9 24.3 %shard_map.207 = (f32[1,1024]{1,0:T(1,128)}, f32[1,1024]{1,0:T(1,128)}, bf16[512,1024]{1,0:T(8,128)(2,1)}, bf16[512,1024]{1,0:T(8,128)(2,1)}, bf16[256,1024]{1,0...) custom-call(s32[4]{0:T(128)} %pad_add_fusion.starts_ref, ...), custom_call_target="tpu_custom_call" | custom-call | flops 1 | bytes 1 | tf_op jit(solution)/shard_map/pallas_call | solution.py:771
  472.1 24.0 %shard_map.208 = (f32[1,1024]{1,0:T(1,128)}, f32[1,1024]{1,0:T(1,128)}, bf16[512,1024]{1,0:T(8,128)(2,1)}, bf16[512,1024]{1,0:T(8,128)(2,1)}, bf16[256,1024]{1,0...) custom-call(s32[4]{0:T(128)} %pad_add_fusion.starts_ref, ...), custom_call_target="tpu_custom_call" | custom-call | flops 1 | bytes 1 | tf_op jit(solution)/shard_map/pallas_call | solution.py:771
  497.6 3.0 shard_map.210
  503.4 10.6 %shard_map.209 = bf16[512,2048]{1,0:T(8,128)(2,1)} custom-call(bf16[512,512]{1,0:T(8,128)(2,1)} %get-tuple-element.288.refs_0_, bf16[512,512]{1,0:T(8,128)(2,1)} %collective-permute-done.16.refs_1_, bf16[512,512]{1,0:T(8,128)(2,1)} %collective-permute-done.17.refs_2_, bf16[512,512]{1,0:T(8,128)(2,1)} %collective-permute-done.18.refs_3_, ...), custom_call_target="tpu_custom_call" | custom-call | flops 1 | bytes 1 | tf_op jit(solution)/shard_map/pallas_call | solution.py:821
  514.1 16.1 %all-gather.1 = f32[8,76,128]{2,1,0:T(8,128)S(1)} all-gather(f32[1,76,128]{2,1,0:T(8,128)S(1)} %bitcast.34), channel_id=2, replica_groups=mesh['dp'=8,'tensor'=4] {'dp'}, dimensions={0}, use_global_device_ids=true | all-gather | bytes 350208 | tf_op jit(solution)/shard_map/all_gather | solution.py:1260
  530.7 3.0 shard_map.211
  540.5 2.8 convert_element_type.42
  552.1 7.2 %shard_map.212 = bf16[512,2048]{1,0:T(8,128)(2,1)} custom-call(bf16[256,1024]{1,0:T(8,128)(2,1)} %collective-permute-done.23.refs_0_, bf16[256,1024]{1,0:T(8,128)(2,1)} %collective-permute-done.24.refs_1_, bf16[512,1024]{1,0:T(8,128)(2,1)} %collective-permute-done.19.b_ref.refs_2_, bf16[512,1024]{1,0:T(8,128)(2,1)} %collective-permute-done.20.d_ref.refs_3_, ...), custom_call_target="tpu_custom_call" | custom-call | flops 1 | bytes 1 | tf_op jit(solution)/shard_map/pallas_call | solution.py:884
  (125 shorter events, 52.9 us)
Async XLA Ops:
  7.2 96.8 %all-gather.7.cloned.1.call-start = ((), (), s32[]{:S(2)}) async-start(), calls=%async_computation.3 | async-start | bytes 9437184 | tf_op jit(solution)/shard_map/all_gather | solution.py:1185
  7.9 151.4 %all-gather.9.cloned.1.call-start = ((), (), s32[]{:S(2)}) async-start(), calls=%async_computation.4 | async-start | bytes 7077888 | tf_op jit(solution)/shard_map/all_gather | solution.py:1190
  8.0 49.0 %collective-permute-start.1 = (bf16[512,2048]{1,0:T(8,128)(2,1)}, bf16[512,2048]{1,0:T(8,128)(2,1)}, u32[]{:S(2)}, u32[]{:S(2)}) collective-permute-start(bf16[512,2048]{1,0:T(8,128)(2,1)} %refs_12_.1), channel_id=1, source_target_pairs={{0,2},{1,3},{2,0},{3,1},{4,6},{5,7},{6,4},{7,5},{8,10},{9,11},{10,... | collective-permute-start | bytes 6291464 | tf_op jit(solution)/shard_map/ppermute | solution.py:32
  11.0 47.4 %collective-permute-start = (bf16[512,2048]{1,0:T(8,128)(2,1)}, bf16[512,2048]{1,0:T(8,128)(2,1)}, u32[]{:S(2)}, u32[]{:S(2)}) collective-permute-start(bf16[512,2048]{1,0:T(8,128)(2,1)} %refs_12_.1), channel_id=1, source_target_pairs={{0,1},{1,0},{2,3},{3,2},{4,5},{5,4},{6,7},{7,6},{8,9},{9,8},{10,11... | collective-permute-start | bytes 6291464 | tf_op jit(solution)/shard_map/ppermute | solution.py:32
  58.4 149.8 %all-gather.11.cloned.1.call-start = ((), (), s32[]{:S(2)}) async-start(), calls=%async_computation.5 | async-start | bytes 2359296 | tf_op jit(solution)/shard_map/all_gather | solution.py:1199
  62.1 24.0 %collective-permute-start.2 = (bf16[256,2048]{1,0:T(8,128)(2,1)}, bf16[256,2048]{1,0:T(8,128)(2,1)}, u32[]{:S(2)}, u32[]{:S(2)}) collective-permute-start(bf16[256,2048]{1,0:T(8,128)(2,1)} %get-tuple-element.187), channel_id=1, source_target_pairs={{0,2},{1,3},{2,0},{3,1},{4,6},{5,7},{6,4},{7,5},{8,10},{9,11},{10,... | collective-permute-start | bytes 3145736 | tf_op jit(solution)/shard_map/ppermute | solution.py:32
  62.4 24.1 %collective-permute-start.3 = (bf16[256,2048]{1,0:T(8,128)(2,1)}, bf16[256,2048]{1,0:T(8,128)(2,1)}, u32[]{:S(2)}, u32[]{:S(2)}) collective-permute-start(bf16[256,2048]{1,0:T(8,128)(2,1)} %get-tuple-element.188), channel_id=1, source_target_pairs={{0,1},{1,0},{2,3},{3,2},{4,5},{5,4},{6,7},{7,6},{8,9},{9,8},{10,11... | collective-permute-start | bytes 3145736 | tf_op jit(solution)/shard_map/ppermute | solution.py:32
  99.0 181.6 %all-gather.13.cloned.1.call-start = ((), (), s32[]{:S(2)}) async-start(), calls=%async_computation.6 | async-start | bytes 9437184 | tf_op jit(solution)/shard_map/all_gather | solution.py:1205
  99.1 45.7 %collective-permute-start.5 = (bf16[512,2048]{1,0:T(8,128)(2,1)}, bf16[512,2048]{1,0:T(8,128)(2,1)}, u32[]{:S(2)}, u32[]{:S(2)}) collective-permute-start(bf16[512,2048]{1,0:T(8,128)(2,1)} %get-tuple-element.207.refs_0_), channel_id=1, source_target_pairs={{0,2},{1,3},{2,0},{3,1},{4,6},{5,7},{6,4},{7,5},{8,10},{9,11},{10,... | collective-permute-start | bytes 6291464 | tf_op jit(solution)/shard_map/ppermute | solution.py:32
  100.7 44.9 %collective-permute-start.4 = (bf16[512,2048]{1,0:T(8,128)(2,1)}, bf16[512,2048]{1,0:T(8,128)(2,1)}, u32[]{:S(2)}, u32[]{:S(2)}) collective-permute-start(bf16[512,2048]{1,0:T(8,128)(2,1)} %get-tuple-element.207.refs_0_), channel_id=1, source_target_pairs={{0,1},{1,0},{2,3},{3,2},{4,5},{5,4},{6,7},{7,6},{8,9},{9,8},{10,11... | collective-permute-start | bytes 6291464 | tf_op jit(solution)/shard_map/ppermute | solution.py:32
  145.7 388.0 %reduce-scatter.6.cloned.1.call-start = ((), (), s32[]{:S(2)}) async-start(), calls=%async_computation.8 | async-start | bytes 9437184 | tf_op jit(solution)/shard_map/reduce_scatter | solution.py:1214
  149.6 32.9 %collective-permute-start.6 = (bf16[256,2048]{1,0:T(8,128)(2,1)}, bf16[256,2048]{1,0:T(8,128)(2,1)}, u32[]{:S(2)}, u32[]{:S(2)}) collective-permute-start(bf16[256,2048]{1,0:T(8,128)(2,1)} %get-tuple-element.198), channel_id=1, source_target_pairs={{0,2},{1,3},{2,0},{3,1},{4,6},{5,7},{6,4},{7,5},{8,10},{9,11},{10,... | collective-permute-start | bytes 3145736 | tf_op jit(solution)/shard_map/ppermute | solution.py:32
  150.4 32.1 %collective-permute-start.7 = (bf16[256,2048]{1,0:T(8,128)(2,1)}, bf16[256,2048]{1,0:T(8,128)(2,1)}, u32[]{:S(2)}, u32[]{:S(2)}) collective-permute-start(bf16[256,2048]{1,0:T(8,128)(2,1)} %get-tuple-element.199), channel_id=1, source_target_pairs={{0,1},{1,0},{2,3},{3,2},{4,5},{5,4},{6,7},{7,6},{8,9},{9,8},{10,11... | collective-permute-start | bytes 3145736 | tf_op jit(solution)/shard_map/ppermute | solution.py:32
  208.2 325.5 %reduce-scatter.4.cloned.1.call-start = ((), (), s32[]{:S(2)}) async-start(), calls=%async_computation.7 | async-start | bytes 9437184 | tf_op jit(solution)/shard_map/reduce_scatter | solution.py:1228
  218.1 57.3 %collective-permute-start.9 = (bf16[512,2048]{1,0:T(8,128)(2,1)}, bf16[512,2048]{1,0:T(8,128)(2,1)}, u32[]{:S(2)}, u32[]{:S(2)}) collective-permute-start(bf16[512,2048]{1,0:T(8,128)(2,1)} %all-gather.11.cloned.1.call-done.refs_4_), channel_id=1, source_target_pairs={{0,2},{1,3},{2,0},{3,1},{4,6},{5,7},{6,4},{7,5},{8,10},{9,11},{10,... | collective-permute-start | bytes 6291464 | tf_op jit(solution)/shard_map/ppermute | solution.py:32
  219.7 55.7 %collective-permute-start.8 = (bf16[512,2048]{1,0:T(8,128)(2,1)}, bf16[512,2048]{1,0:T(8,128)(2,1)}, u32[]{:S(2)}, u32[]{:S(2)}) collective-permute-start(bf16[512,2048]{1,0:T(8,128)(2,1)} %all-gather.11.cloned.1.call-done.refs_4_), channel_id=1, source_target_pairs={{0,1},{1,0},{2,3},{3,2},{4,5},{5,4},{6,7},{7,6},{8,9},{9,8},{10,11... | collective-permute-start | bytes 6291464 | tf_op jit(solution)/shard_map/ppermute | solution.py:32
  279.0 25.2 %collective-permute-start.10 = (bf16[256,2048]{1,0:T(8,128)(2,1)}, bf16[256,2048]{1,0:T(8,128)(2,1)}, u32[]{:S(2)}, u32[]{:S(2)}) collective-permute-start(bf16[256,2048]{1,0:T(8,128)(2,1)} %get-tuple-element.232), channel_id=1, source_target_pairs={{0,2},{1,3},{2,0},{3,1},{4,6},{5,7},{6,4},{7,5},{8,10},{9,11},{10,... | collective-permute-start | bytes 3145736 | tf_op jit(solution)/shard_map/ppermute | solution.py:32
  279.6 24.8 %collective-permute-start.11 = (bf16[256,2048]{1,0:T(8,128)(2,1)}, bf16[256,2048]{1,0:T(8,128)(2,1)}, u32[]{:S(2)}, u32[]{:S(2)}) collective-permute-start(bf16[256,2048]{1,0:T(8,128)(2,1)} %get-tuple-element.233), channel_id=1, source_target_pairs={{0,1},{1,0},{2,3},{3,2},{4,5},{5,4},{6,7},{7,6},{8,9},{9,8},{10,11... | collective-permute-start | bytes 3145736 | tf_op jit(solution)/shard_map/ppermute | solution.py:32
  304.4 51.2 %collective-permute-start.12 = (bf16[512,2048]{1,0:T(8,128)(2,1)}, bf16[512,2048]{1,0:T(8,128)(2,1)}, u32[]{:S(2)}, u32[]{:S(2)}) collective-permute-start(bf16[512,2048]{1,0:T(8,128)(2,1)} %get-tuple-element.234), channel_id=1, source_target_pairs={{0,1},{1,0},{2,3},{3,2},{4,5},{5,4},{6,7},{7,6},{8,9},{9,8},{10,11... | collective-permute-start | bytes 6291464 | tf_op jit(solution)/shard_map/ppermute | solution.py:32
  305.9 49.7 %collective-permute-start.13 = (bf16[512,2048]{1,0:T(8,128)(2,1)}, bf16[512,2048]{1,0:T(8,128)(2,1)}, u32[]{:S(2)}, u32[]{:S(2)}) collective-permute-start(bf16[512,2048]{1,0:T(8,128)(2,1)} %get-tuple-element.235), channel_id=1, source_target_pairs={{0,2},{1,3},{2,0},{3,1},{4,6},{5,7},{6,4},{7,5},{8,10},{9,11},{10,... | collective-permute-start | bytes 6291464 | tf_op jit(solution)/shard_map/ppermute | solution.py:32
  360.1 186.4 %reduce-scatter.8.cloned.1.call-start = ((), (), s32[]{:S(2)}) async-start(), calls=%async_computation.9 | async-start | bytes 9437184 | tf_op jit(solution)/shard_map/reduce_scatter | solution.py:1239
  360.2 55.4 %collective-permute-start.14 = (bf16[256,2048]{1,0:T(8,128)(2,1)}, bf16[256,2048]{1,0:T(8,128)(2,1)}, u32[]{:S(2)}, u32[]{:S(2)}) collective-permute-start(bf16[256,2048]{1,0:T(8,128)(2,1)} %get-tuple-element.253), channel_id=1, source_target_pairs={{0,2},{1,3},{2,0},{3,1},{4,6},{5,7},{6,4},{7,5},{8,10},{9,11},{10,... | collective-permute-start | bytes 3145736 | tf_op jit(solution)/shard_map/ppermute | solution.py:32
  360.8 54.7 %collective-permute-start.15 = (bf16[256,2048]{1,0:T(8,128)(2,1)}, bf16[256,2048]{1,0:T(8,128)(2,1)}, u32[]{:S(2)}, u32[]{:S(2)}) collective-permute-start(bf16[256,2048]{1,0:T(8,128)(2,1)} %get-tuple-element.254), channel_id=1, source_target_pairs={{0,1},{1,0},{2,3},{3,2},{4,5},{5,4},{6,7},{7,6},{8,9},{9,8},{10,11... | collective-permute-start | bytes 3145736 | tf_op jit(solution)/shard_map/ppermute | solution.py:32
  418.4 26.5 %collective-permute-start.18 = (bf16[512,512]{1,0:T(8,128)(2,1)}, bf16[512,512]{1,0:T(8,128)(2,1)}, u32[]{:S(2)}, u32[]{:S(2)}) collective-permute-start(bf16[512,512]{1,0:T(8,128)(2,1)} %get-tuple-element.390), channel_id=1, source_target_pairs={{0,3},{1,2},{2,1},{3,0},{4,7},{5,6},{6,5},{7,4},{8,11},{9,10},{10,... | collective-permute-start | bytes 1572872 | tf_op jit(solution)/shard_map/ppermute | solution.py:32
  420.7 24.2 %collective-permute-start.17 = (bf16[512,512]{1,0:T(8,128)(2,1)}, bf16[512,512]{1,0:T(8,128)(2,1)}, u32[]{:S(2)}, u32[]{:S(2)}) collective-permute-start(bf16[512,512]{1,0:T(8,128)(2,1)} %get-tuple-element.391), channel_id=1, source_target_pairs={{0,2},{1,3},{2,0},{3,1},{4,6},{5,7},{6,4},{7,5},{8,10},{9,11},{10,... | collective-permute-start | bytes 1572872 | tf_op jit(solution)/shard_map/ppermute | solution.py:32
  421.3 23.6 %collective-permute-start.16 = (bf16[512,512]{1,0:T(8,128)(2,1)}, bf16[512,512]{1,0:T(8,128)(2,1)}, u32[]{:S(2)}, u32[]{:S(2)}) collective-permute-start(bf16[512,512]{1,0:T(8,128)(2,1)} %get-tuple-element.392), channel_id=1, source_target_pairs={{0,1},{1,0},{2,3},{3,2},{4,5},{5,4},{6,7},{7,6},{8,9},{9,8},{10,11... | collective-permute-start | bytes 1572872 | tf_op jit(solution)/shard_map/ppermute | solution.py:32
  469.2 27.0 %collective-permute-start.19 = (bf16[512,1024]{1,0:T(8,128)(2,1)}, bf16[512,1024]{1,0:T(8,128)(2,1)}, u32[]{:S(2)}, u32[]{:S(2)}) collective-permute-start(bf16[512,1024]{1,0:T(8,128)(2,1)} %get-tuple-element.267), channel_id=1, source_target_pairs={{0,1},{1,0},{2,3},{3,2},{4,5},{5,4},{6,7},{7,6},{8,9},{9,8},{10,11... | collective-permute-start | bytes 3145736 | tf_op jit(solution)/shard_map/ppermute | solution.py:32
  470.7 25.6 %collective-permute-start.20 = (bf16[512,1024]{1,0:T(8,128)(2,1)}, bf16[512,1024]{1,0:T(8,128)(2,1)}, u32[]{:S(2)}, u32[]{:S(2)}) collective-permute-start(bf16[512,1024]{1,0:T(8,128)(2,1)} %get-tuple-element.268), channel_id=1, source_target_pairs={{0,2},{1,3},{2,0},{3,1},{4,6},{5,7},{6,4},{7,5},{8,10},{9,11},{10,... | collective-permute-start | bytes 3145736 | tf_op jit(solution)/shard_map/ppermute | solution.py:32
  496.2 34.5 %collective-permute-start.21 = (bf16[512,1024]{1,0:T(8,128)(2,1)}, bf16[512,1024]{1,0:T(8,128)(2,1)}, u32[]{:S(2)}, u32[]{:S(2)}) collective-permute-start(bf16[512,1024]{1,0:T(8,128)(2,1)} %get-tuple-element.282), channel_id=1, source_target_pairs={{0,1},{1,0},{2,3},{3,2},{4,5},{5,4},{6,7},{7,6},{8,9},{9,8},{10,11... | collective-permute-start | bytes 3145736 | tf_op jit(solution)/shard_map/ppermute | solution.py:32
  496.9 33.8 %collective-permute-start.22 = (bf16[512,1024]{1,0:T(8,128)(2,1)}, bf16[512,1024]{1,0:T(8,128)(2,1)}, u32[]{:S(2)}, u32[]{:S(2)}) collective-permute-start(bf16[512,1024]{1,0:T(8,128)(2,1)} %get-tuple-element.283), channel_id=1, source_target_pairs={{0,2},{1,3},{2,0},{3,1},{4,6},{5,7},{6,4},{7,5},{8,10},{9,11},{10,... | collective-permute-start | bytes 3145736 | tf_op jit(solution)/shard_map/ppermute | solution.py:32
  500.6 30.1 %collective-permute-start.23 = (bf16[256,1024]{1,0:T(8,128)(2,1)}, bf16[256,1024]{1,0:T(8,128)(2,1)}, u32[]{:S(2)}, u32[]{:S(2)}) collective-permute-start(bf16[256,1024]{1,0:T(8,128)(2,1)} %get-tuple-element.315), channel_id=1, source_target_pairs={{0,2},{1,3},{2,0},{3,1},{4,6},{5,7},{6,4},{7,5},{8,10},{9,11},{10,... | collective-permute-start | bytes 1572872 | tf_op jit(solution)/shard_map/ppermute | solution.py:32
  502.0 28.7 %collective-permute-start.24 = (bf16[256,1024]{1,0:T(8,128)(2,1)}, bf16[256,1024]{1,0:T(8,128)(2,1)}, u32[]{:S(2)}, u32[]{:S(2)}) collective-permute-start(bf16[256,1024]{1,0:T(8,128)(2,1)} %get-tuple-element.316), channel_id=1, source_target_pairs={{0,1},{1,0},{2,3},{3,2},{4,5},{5,4},{6,7},{7,6},{8,9},{9,8},{10,11... | collective-permute-start | bytes 1572872 | tf_op jit(solution)/shard_map/ppermute | solution.py:32
  (14 other events, 160.2 us)
Sparse Core Ops, SparseCore 0:
  9.6 84.7 all-gather.6
  96.0 63.2 all-gather.8
  160.9 29.5 all-gather.10
  191.9 81.5 all-gather.12
  275.6 87.7 reduce-scatter.5
  365.6 87.9 reduce-scatter.3
  455.9 90.5 reduce-scatter.7

commit v7 on v6

--- a/solution.py
+++ b/solution.py
@@ -700,9 +700,9 @@
 
     weights = [load(up, up_buf, 0), load(qkv, qkv_buf, 1)]
     weights[0].start()
-    for copy in row_loads(0):
+    first_loads = row_loads(0)
+    for copy in (*first_loads[:2], weights[1], first_loads[2]):
         copy.start()
-    weights[1].start()
     for owner in range(1, owners):
         for copy in row_loads(owner):
             copy.start()
@@ -873,7 +873,7 @@
         return (wide(cotangent) + grad_input).astype(tokens.dtype)
     half, split = left_parts[4].shape
     rows, depth = tokens.shape
-    chunk = min(128, half)
+    chunk = min(256, half)
     steps = half // chunk
     low_part = pl.BlockSpec((chunk, split), lambda i: (jnp.minimum(i, steps - 1), 0))
     high_part = pl.BlockSpec((chunk, split), lambda i: (jnp.maximum(i - steps, 0), 0))

time: 575 us -> 574 us (level)
  transfers between devices with their start and end apart: 37 -> 37, of which waited for: 12 -> 12; matrix products, arithmetic and copies ran while one was open for 8% -> 8% of each run, Pallas kernels for 67% -> 66%
where the time goes in v7:
time: 574 us; the launch traced here: 566 us
  Pallas kernels  384 us (67%)
  waiting for transfers between devices  68 us (12%)
  starting transfers between devices  36.4 us (6%)
  local copies, waits for them, and re-layouts  25 us (4%)
  blocking collectives  16.1 us (3%)
  between operations  14.8 us (3%)
  other arithmetic  12.4 us (2%)
  matrix products  9.88 us (2%)
    pallas_call x2, Pallas kernels, attention(): pl.pallas_call(body, grid=(last - first, block_count), in_specs=[row_bloc...  108 us
    ppermute x30, waiting for transfers between devices, swap(): return lax.ppermute(value, axis, [(i, i ^ bit) for i in range(count)])  58.6 us
    pallas_call x1, Pallas kernels, hidden_grads(): whole_call(hidden_grads_kernel, [ANY] * 4, [ANY, ANY, VMEM], [jax.ShapeDt...  48.2 us
    pallas_call x2, Pallas kernels, normed_grads(): whole_call(kernel, [SMEM] + [ANY] * 5 + [VMEM] * 2, [VMEM, VMEM] + [ANY]...  48 us
    ppermute x30, starting transfers between devices, swap(): return lax.ppermute(value, axis, [(i, i ^ bit) for i in range(count)])  35.9 us
    pallas_call x1, Pallas kernels, hidden_rows(): pl.pallas_call(hidden_kernel, grid=(width // columns, rows // block), in_...  32 us
    pallas_call x1, Pallas kernels, first_grads(): whole_call(first_grads_kernel, [SMEM] + [ANY] * (1 + count), [ANY, ANY],...  25.6 us
    pallas_call x1, Pallas kernels, feed_rows(): whole_call(functools.partial(feed_kernel, places=places), [SMEM] + [ANY]...  23.6 us
  transfers between devices with their start and end apart: 37, of which 12 were waited for; matrix products, arithmetic and copies ran while one was open for 8% of the time, Pallas kernels for 66%

profile of v7, /device:TPU:0, one launch (start us, length us, event | category | flops | bytes accessed | tf_op | source)
XLA Modules:
  0.0 566.2 jit_solution(12288072243124964052)
XLA Ops:
  8.0 3.0 collective-permute-start.1
  12.5 5.5 multiply_sine_fusion
  18.2 4.6 concatenate.14.below_ref.refs_6_
  22.8 4.4 concatenate.13.above_ref.refs_5_
  28.2 4.6 concatenate.12.cos_ref.refs_4_
  33.2 23.7 %collective-permute-done.1.two_ref.refs_2_ = bf16[512,2048]{1,0:T(8,128)(2,1)} collective-permute-done((bf16[512,2048]{1,0:T(8,128)(2,1)}, bf16[512,2048]{1,0:T(8,128)(2,1)}, u32[]{:S(2)}, u32[]{:S(2)}) %collective-permute-start.1) | collective-permute-done | bytes 2097184 | tf_op jit(solution)/shard_map/ppermute | solution.py:32
  58.5 3.7 shard_map.194
  64.7 21.4 %collective-permute-done.2.refs_3_ = bf16[256,2048]{1,0:T(8,128)(2,1)} collective-permute-done((bf16[256,2048]{1,0:T(8,128)(2,1)}, bf16[256,2048]{1,0:T(8,128)(2,1)}, u32[]{:S(2)}, u32[]{:S(2)}) %collective-permute-start.2) | collective-permute-done | bytes 1048608 | tf_op jit(solution)/shard_map/ppermute | solution.py:32
  86.5 12.5 %shard_map.195 = (bf16[2048,2048]{1,0:T(8,128)(2,1)}, bf16[2048,2048]{1,0:T(8,128)(2,1)}, f32[2048,1]{1,0:T(8,128)}, f32[2048,1]{1,0:T(8,128)}, bf16[512,2048]{1,0:T(8,128)(2,1)}) custom-call(s32[5]{0:T(128)} %stack.19.starts_ref, f32[1,2048]{1,0:T(1,128)} %bitcast.35, f32[1,2048]{1,0:T(1,128)} %bitcast.40, bf16[512,2048]{1,0:T(8,128)(2,1)} %refs_13_.1, ...), custom_call_target="tpu_custom_call" | custom-call | flops 1 | bytes 1 | tf_op jit(solution)/shard_map/pallas_call | solution.py:1144
  104.0 32.0 %shard_map.196 = (bf16[2048,2048]{1,0:T(8,128)(2,1)}, bf16[2048,2048]{1,0:T(8,128)(2,1)}) custom-call(bf16[2048,2048]{1,0:T(8,128)(2,1)} %get-tuple-element.201.x_ref.x, bf16[2048,2048]{1,0:T(8,128)(2,1)} %all-gather.7.cloned.1.call-done.w_ref.up, f32[1,2048]{1,0:T(1,128)} %bitcast.37), custom_call_target="tpu_custom_call" | custom-call | flops 1 | bytes 1 | tf_op jit(solution)/shard_map/pallas_call | solution.py:251
  136.0 8.8 %collective-permute-done.5.two_ref.refs_2_ = bf16[512,2048]{1,0:T(8,128)(2,1)} collective-permute-done((bf16[512,2048]{1,0:T(8,128)(2,1)}, bf16[512,2048]{1,0:T(8,128)(2,1)}, u32[]{:S(2)}, u32[]{:S(2)}) %collective-permute-start.5) | collective-permute-done | bytes 2097184 | tf_op jit(solution)/shard_map/ppermute | solution.py:32
  145.9 3.6 shard_map.197
  152.2 7.1 %all-gather.9.cloned.1.call-done.w_ref.qkv = bf16[3,2048,512]{2,1,0:T(8,128)(2,1)} async-done(((bf16[3,256,512]{2,1,0:T(8,128)(2,1)}), bf16[3,2048,512]{2,1,0:T(8,128)(2,1)}) %all-gather.9.cloned.1.call-update) | async-done | bytes 6291472 | tf_op jit(solution)/shard_map/all_gather | solution.py:1190
  159.3 23.2 %shard_map.198.refs_0_.refs_1_.refs_2_ = bf16[2048,1536]{1,0:T(8,128)(2,1)} custom-call(bf16[2048,2048]{1,0:T(8,128)(2,1)} %get-tuple-element.201.x_ref.x, bf16[3,2048,512]{2,1,0:T(8,128)(2,1)} %all-gather.9.cloned.1.call-done.w_ref.qkv, f32[3,1,512]{2,1,0:T(1,128)} %reshape.84.bias_ref, f32[2048,128]{1,0:T(8,128)} %concatenate.12.cos_ref.refs_4_, ...), custom_call_target="tpu_custom_call" | custom-call | flops 1 | bytes 1 | tf_op jit(solution)/shard_map/pallas_call | solution.py:218
  182.5 25.6 %shard_map.199 = (bf16[2048,2048]{1,0:T(8,128)(2,1)}, bf16[2048,2048]{1,0:T(8,128)(2,1)}) custom-call(s32[5]{0:T(128)} %stack.19.starts_ref, bf16[2048,2048]{1,0:T(8,128)(2,1)} %get-tuple-element.221.active, bf16[512,2048]{1,0:T(8,128)(2,1)} %get-tuple-element.207.refs_0_, bf16[512,2048]{1,0:T(8,128)(2,1)} %collective-permute-done.4.one_ref.refs_1_, ...), custom_call_target="tpu_custom_call" | custom-call | flops 1 | bytes 1 | tf_op jit(solution)/shard_map/pallas_call | solution.py:386
  208.2 9.9 %convolution_convert_fusion.refs_3_ = bf16[2048,512]{1,0:T(8,128)(2,1)} fusion(bf16[2048,2048]{1,0:T(8,128)(2,1)} %get-tuple-element.240.grad_rows, bf16[512,2048]{1,0:T(8,128)(2,1)} %all-gather.11.cloned.1.call-done.refs_4_), kind=kOutput, calls=%fused_computation.1 | convolution fusion | flops 4296015872 | bytes 12582912 | tf_op jit(solution)/shard_map/td,kd->tk/dot_general | solution.py:1210
  221.2 54.2 %shard_map.200 = (bf16[2048,512]{1,0:T(8,128)(2,1)}, bf16[3,2048,512]{2,1,0:T(8,128)(2,1)}, f32[3,1,512]{2,1,0:T(1,128)}) custom-call(bf16[2048,1536]{1,0:T(8,128)(2,1)} %shard_map.198.refs_0_.refs_1_.refs_2_, bf16[2048,1536]{1,0:T(8,128)(2,1)} %shard_map.198.refs_0_.refs_1_.refs_2_, bf16[2048,1536]{1,0:T(8,128)(2,1)} %shard_map.198.refs_0_.refs_1_.refs_2_, ...), custom_call_target="tpu_custom_call" | custom-call | flops 1 | bytes 1 | tf_op jit(solution)/shard_map/pallas_call | solution.py:1053
  275.4 3.6 shard_map.202
  280.6 23.6 %shard_map.201 = (bf16[512,2048]{1,0:T(8,128)(2,1)}, bf16[512,2048]{1,0:T(8,128)(2,1)}, bf16[256,2048]{1,0:T(8,128)(2,1)}, bf16[256,2048]{1,0:T(8,128)(2,1)}, bf...) custom-call(s32[4]{0:T(128)} %pad_add_fusion.starts_ref, bf16[2048,2048]{1,0:T(8,128)(2,1)} %get-tuple-element.221.active, ...), custom_call_target="tpu_custom_call" | custom-call | flops 1 | bytes 1 | tf_op jit(solution)/shard_map/pallas_call | solution.py:475
  307.4 48.2 %shard_map.203 = (bf16[2048,2048]{1,0:T(8,128)(2,1)}, bf16[2048,2048]{1,0:T(8,128)(2,1)}, f32[2,1,1024]{2,1,0:T(1,128)}) custom-call(bf16[2048,2048]{1,0:T(8,128)(2,1)} %get-tuple-element.240.grad_rows, bf16[2048,2048]{1,0:T(8,128)(2,1)} %all-gather.13.cloned.1.call-done.weight, bf16[2048,2048]{1,0:T(8,128)(2,1)} %get-tuple-element.241.slope, ...), custom_call_target="tpu_custom_call" | custom-call | flops 1 | bytes 1 | tf_op jit(solution)/shard_map/pallas_call | solution.py:588
  355.6 4.5 shard_map.205
  361.4 54.1 %shard_map.204 = (bf16[2048,512]{1,0:T(8,128)(2,1)}, bf16[3,2048,512]{2,1,0:T(8,128)(2,1)}, f32[3,1,512]{2,1,0:T(1,128)}) custom-call(bf16[2048,1536]{1,0:T(8,128)(2,1)} %shard_map.198.refs_0_.refs_1_.refs_2_, bf16[2048,1536]{1,0:T(8,128)(2,1)} %shard_map.198.refs_0_.refs_1_.refs_2_, ...), custom_call_target="tpu_custom_call", output_to_operand_aliasing={{0}: (7, {}), {1}: (8, {}), {2}: (9, {})} | custom-call | flops 1 | bytes 1 | tf_op jit(solution)/shard_map/pallas_call | solution.py:1053
  415.5 2.9 constant_dynamic-slice_fusion
  421.9 23.0 %shard_map.206 = bf16[4,2048,512]{2,1,0:T(8,128)(2,1)} custom-call(bf16[2048,2048]{1,0:T(8,128)(2,1)} %get-tuple-element.201.x_ref.x, bf16[3,2048,512]{2,1,0:T(8,128)(2,1)} %get-tuple-element.273.joined, bf16[2048,2048]{1,0:T(8,128)(2,1)} %get-tuple-element.240.grad_rows, bf16[2048,512]{1,0:T(8,128)(2,1)} %get-tuple-element.258.mixed), custom_call_target="tpu_custom_call" | custom-call | flops 1 | bytes 1 | tf_op jit(solution)/shard_map/pallas_call | solution.py:660
  444.9 24.0 %shard_map.207 = (f32[1,1024]{1,0:T(1,128)}, f32[1,1024]{1,0:T(1,128)}, bf16[512,1024]{1,0:T(8,128)(2,1)}, bf16[512,1024]{1,0:T(8,128)(2,1)}, bf16[256,1024]{1,0...) custom-call(s32[4]{0:T(128)} %pad_add_fusion.starts_ref, ...), custom_call_target="tpu_custom_call" | custom-call | flops 1 | bytes 1 | tf_op jit(solution)/shard_map/pallas_call | solution.py:771
  471.9 24.0 %shard_map.208 = (f32[1,1024]{1,0:T(1,128)}, f32[1,1024]{1,0:T(1,128)}, bf16[512,1024]{1,0:T(8,128)(2,1)}, bf16[512,1024]{1,0:T(8,128)(2,1)}, bf16[256,1024]{1,0...) custom-call(s32[4]{0:T(128)} %pad_add_fusion.starts_ref, ...), custom_call_target="tpu_custom_call" | custom-call | flops 1 | bytes 1 | tf_op jit(solution)/shard_map/pallas_call | solution.py:771
  497.2 3.0 shard_map.210
  503.1 10.6 %shard_map.209 = bf16[512,2048]{1,0:T(8,128)(2,1)} custom-call(bf16[512,512]{1,0:T(8,128)(2,1)} %get-tuple-element.288.refs_0_, bf16[512,512]{1,0:T(8,128)(2,1)} %collective-permute-done.16.refs_1_, bf16[512,512]{1,0:T(8,128)(2,1)} %collective-permute-done.17.refs_2_, bf16[512,512]{1,0:T(8,128)(2,1)} %collective-permute-done.18.refs_3_, ...), custom_call_target="tpu_custom_call" | custom-call | flops 1 | bytes 1 | tf_op jit(solution)/shard_map/pallas_call | solution.py:821
  513.7 16.1 %all-gather.1 = f32[8,76,128]{2,1,0:T(8,128)S(1)} all-gather(f32[1,76,128]{2,1,0:T(8,128)S(1)} %bitcast.34), channel_id=2, replica_groups=mesh['dp'=8,'tensor'=4] {'dp'}, dimensions={0}, use_global_device_ids=true | all-gather | bytes 350208 | tf_op jit(solution)/shard_map/all_gather | solution.py:1260
  530.4 3.0 shard_map.211
  540.2 2.8 convert_element_type.42
  551.6 7.5 %shard_map.212 = bf16[512,2048]{1,0:T(8,128)(2,1)} custom-call(bf16[256,1024]{1,0:T(8,128)(2,1)} %collective-permute-done.23.refs_0_, bf16[256,1024]{1,0:T(8,128)(2,1)} %collective-permute-done.24.refs_1_, bf16[512,1024]{1,0:T(8,128)(2,1)} %collective-permute-done.19.b_ref.refs_2_, bf16[512,1024]{1,0:T(8,128)(2,1)} %collective-permute-done.20.d_ref.refs_3_, ...), custom_call_target="tpu_custom_call" | custom-call | flops 1 | bytes 1 | tf_op jit(solution)/shard_map/pallas_call | solution.py:884
  (125 shorter events, 52.8 us)
Async XLA Ops:
  7.2 96.8 %all-gather.7.cloned.1.call-start = ((), (), s32[]{:S(2)}) async-start(), calls=%async_computation.3 | async-start | bytes 9437184 | tf_op jit(solution)/shard_map/all_gather | solution.py:1185
  7.9 151.4 %all-gather.9.cloned.1.call-start = ((), (), s32[]{:S(2)}) async-start(), calls=%async_computation.4 | async-start | bytes 7077888 | tf_op jit(solution)/shard_map/all_gather | solution.py:1190
  8.0 49.0 %collective-permute-start.1 = (bf16[512,2048]{1,0:T(8,128)(2,1)}, bf16[512,2048]{1,0:T(8,128)(2,1)}, u32[]{:S(2)}, u32[]{:S(2)}) collective-permute-start(bf16[512,2048]{1,0:T(8,128)(2,1)} %refs_12_.1), channel_id=1, source_target_pairs={{0,2},{1,3},{2,0},{3,1},{4,6},{5,7},{6,4},{7,5},{8,10},{9,11},{10,... | collective-permute-start | bytes 6291464 | tf_op jit(solution)/shard_map/ppermute | solution.py:32
  11.0 47.4 %collective-permute-start = (bf16[512,2048]{1,0:T(8,128)(2,1)}, bf16[512,2048]{1,0:T(8,128)(2,1)}, u32[]{:S(2)}, u32[]{:S(2)}) collective-permute-start(bf16[512,2048]{1,0:T(8,128)(2,1)} %refs_12_.1), channel_id=1, source_target_pairs={{0,1},{1,0},{2,3},{3,2},{4,5},{5,4},{6,7},{7,6},{8,9},{9,8},{10,11... | collective-permute-start | bytes 6291464 | tf_op jit(solution)/shard_map/ppermute | solution.py:32
  58.4 149.8 %all-gather.11.cloned.1.call-start = ((), (), s32[]{:S(2)}) async-start(), calls=%async_computation.5 | async-start | bytes 2359296 | tf_op jit(solution)/shard_map/all_gather | solution.py:1199
  62.1 24.0 %collective-permute-start.2 = (bf16[256,2048]{1,0:T(8,128)(2,1)}, bf16[256,2048]{1,0:T(8,128)(2,1)}, u32[]{:S(2)}, u32[]{:S(2)}) collective-permute-start(bf16[256,2048]{1,0:T(8,128)(2,1)} %get-tuple-element.187), channel_id=1, source_target_pairs={{0,2},{1,3},{2,0},{3,1},{4,6},{5,7},{6,4},{7,5},{8,10},{9,11},{10,... | collective-permute-start | bytes 3145736 | tf_op jit(solution)/shard_map/ppermute | solution.py:32
  62.4 24.1 %collective-permute-start.3 = (bf16[256,2048]{1,0:T(8,128)(2,1)}, bf16[256,2048]{1,0:T(8,128)(2,1)}, u32[]{:S(2)}, u32[]{:S(2)}) collective-permute-start(bf16[256,2048]{1,0:T(8,128)(2,1)} %get-tuple-element.188), channel_id=1, source_target_pairs={{0,1},{1,0},{2,3},{3,2},{4,5},{5,4},{6,7},{7,6},{8,9},{9,8},{10,11... | collective-permute-start | bytes 3145736 | tf_op jit(solution)/shard_map/ppermute | solution.py:32
  99.0 181.6 %all-gather.13.cloned.1.call-start = ((), (), s32[]{:S(2)}) async-start(), calls=%async_computation.6 | async-start | bytes 9437184 | tf_op jit(solution)/shard_map/all_gather | solution.py:1205
  99.1 45.7 %collective-permute-start.5 = (bf16[512,2048]{1,0:T(8,128)(2,1)}, bf16[512,2048]{1,0:T(8,128)(2,1)}, u32[]{:S(2)}, u32[]{:S(2)}) collective-permute-start(bf16[512,2048]{1,0:T(8,128)(2,1)} %get-tuple-element.207.refs_0_), channel_id=1, source_target_pairs={{0,2},{1,3},{2,0},{3,1},{4,6},{5,7},{6,4},{7,5},{8,10},{9,11},{10,... | collective-permute-start | bytes 6291464 | tf_op jit(solution)/shard_map/ppermute | solution.py:32
  100.7 44.9 %collective-permute-start.4 = (bf16[512,2048]{1,0:T(8,128)(2,1)}, bf16[512,2048]{1,0:T(8,128)(2,1)}, u32[]{:S(2)}, u32[]{:S(2)}) collective-permute-start(bf16[512,2048]{1,0:T(8,128)(2,1)} %get-tuple-element.207.refs_0_), channel_id=1, source_target_pairs={{0,1},{1,0},{2,3},{3,2},{4,5},{5,4},{6,7},{7,6},{8,9},{9,8},{10,11... | collective-permute-start | bytes 6291464 | tf_op jit(solution)/shard_map/ppermute | solution.py:32
  145.7 387.6 %reduce-scatter.6.cloned.1.call-start = ((), (), s32[]{:S(2)}) async-start(), calls=%async_computation.8 | async-start | bytes 9437184 | tf_op jit(solution)/shard_map/reduce_scatter | solution.py:1214
  149.6 32.9 %collective-permute-start.6 = (bf16[256,2048]{1,0:T(8,128)(2,1)}, bf16[256,2048]{1,0:T(8,128)(2,1)}, u32[]{:S(2)}, u32[]{:S(2)}) collective-permute-start(bf16[256,2048]{1,0:T(8,128)(2,1)} %get-tuple-element.198), channel_id=1, source_target_pairs={{0,2},{1,3},{2,0},{3,1},{4,6},{5,7},{6,4},{7,5},{8,10},{9,11},{10,... | collective-permute-start | bytes 3145736 | tf_op jit(solution)/shard_map/ppermute | solution.py:32
  150.4 32.1 %collective-permute-start.7 = (bf16[256,2048]{1,0:T(8,128)(2,1)}, bf16[256,2048]{1,0:T(8,128)(2,1)}, u32[]{:S(2)}, u32[]{:S(2)}) collective-permute-start(bf16[256,2048]{1,0:T(8,128)(2,1)} %get-tuple-element.199), channel_id=1, source_target_pairs={{0,1},{1,0},{2,3},{3,2},{4,5},{5,4},{6,7},{7,6},{8,9},{9,8},{10,11... | collective-permute-start | bytes 3145736 | tf_op jit(solution)/shard_map/ppermute | solution.py:32
  208.2 325.2 %reduce-scatter.4.cloned.1.call-start = ((), (), s32[]{:S(2)}) async-start(), calls=%async_computation.7 | async-start | bytes 9437184 | tf_op jit(solution)/shard_map/reduce_scatter | solution.py:1228
  218.1 57.3 %collective-permute-start.9 = (bf16[512,2048]{1,0:T(8,128)(2,1)}, bf16[512,2048]{1,0:T(8,128)(2,1)}, u32[]{:S(2)}, u32[]{:S(2)}) collective-permute-start(bf16[512,2048]{1,0:T(8,128)(2,1)} %all-gather.11.cloned.1.call-done.refs_4_), channel_id=1, source_target_pairs={{0,2},{1,3},{2,0},{3,1},{4,6},{5,7},{6,4},{7,5},{8,10},{9,11},{10,... | collective-permute-start | bytes 6291464 | tf_op jit(solution)/shard_map/ppermute | solution.py:32
  219.7 55.7 %collective-permute-start.8 = (bf16[512,2048]{1,0:T(8,128)(2,1)}, bf16[512,2048]{1,0:T(8,128)(2,1)}, u32[]{:S(2)}, u32[]{:S(2)}) collective-permute-start(bf16[512,2048]{1,0:T(8,128)(2,1)} %all-gather.11.cloned.1.call-done.refs_4_), channel_id=1, source_target_pairs={{0,1},{1,0},{2,3},{3,2},{4,5},{5,4},{6,7},{7,6},{8,9},{9,8},{10,11... | collective-permute-start | bytes 6291464 | tf_op jit(solution)/shard_map/ppermute | solution.py:32
  279.0 25.2 %collective-permute-start.10 = (bf16[256,2048]{1,0:T(8,128)(2,1)}, bf16[256,2048]{1,0:T(8,128)(2,1)}, u32[]{:S(2)}, u32[]{:S(2)}) collective-permute-start(bf16[256,2048]{1,0:T(8,128)(2,1)} %get-tuple-element.232), channel_id=1, source_target_pairs={{0,2},{1,3},{2,0},{3,1},{4,6},{5,7},{6,4},{7,5},{8,10},{9,11},{10,... | collective-permute-start | bytes 3145736 | tf_op jit(solution)/shard_map/ppermute | solution.py:32
  279.6 24.8 %collective-permute-start.11 = (bf16[256,2048]{1,0:T(8,128)(2,1)}, bf16[256,2048]{1,0:T(8,128)(2,1)}, u32[]{:S(2)}, u32[]{:S(2)}) collective-permute-start(bf16[256,2048]{1,0:T(8,128)(2,1)} %get-tuple-element.233), channel_id=1, source_target_pairs={{0,1},{1,0},{2,3},{3,2},{4,5},{5,4},{6,7},{7,6},{8,9},{9,8},{10,11... | collective-permute-start | bytes 3145736 | tf_op jit(solution)/shard_map/ppermute | solution.py:32
  304.4 51.2 %collective-permute-start.12 = (bf16[512,2048]{1,0:T(8,128)(2,1)}, bf16[512,2048]{1,0:T(8,128)(2,1)}, u32[]{:S(2)}, u32[]{:S(2)}) collective-permute-start(bf16[512,2048]{1,0:T(8,128)(2,1)} %get-tuple-element.234), channel_id=1, source_target_pairs={{0,1},{1,0},{2,3},{3,2},{4,5},{5,4},{6,7},{7,6},{8,9},{9,8},{10,11... | collective-permute-start | bytes 6291464 | tf_op jit(solution)/shard_map/ppermute | solution.py:32
  305.9 49.7 %collective-permute-start.13 = (bf16[512,2048]{1,0:T(8,128)(2,1)}, bf16[512,2048]{1,0:T(8,128)(2,1)}, u32[]{:S(2)}, u32[]{:S(2)}) collective-permute-start(bf16[512,2048]{1,0:T(8,128)(2,1)} %get-tuple-element.235), channel_id=1, source_target_pairs={{0,2},{1,3},{2,0},{3,1},{4,6},{5,7},{6,4},{7,5},{8,10},{9,11},{10,... | collective-permute-start | bytes 6291464 | tf_op jit(solution)/shard_map/ppermute | solution.py:32
  360.1 186.4 %reduce-scatter.8.cloned.1.call-start = ((), (), s32[]{:S(2)}) async-start(), calls=%async_computation.9 | async-start | bytes 9437184 | tf_op jit(solution)/shard_map/reduce_scatter | solution.py:1239
  360.2 55.3 %collective-permute-start.14 = (bf16[256,2048]{1,0:T(8,128)(2,1)}, bf16[256,2048]{1,0:T(8,128)(2,1)}, u32[]{:S(2)}, u32[]{:S(2)}) collective-permute-start(bf16[256,2048]{1,0:T(8,128)(2,1)} %get-tuple-element.253), channel_id=1, source_target_pairs={{0,2},{1,3},{2,0},{3,1},{4,6},{5,7},{6,4},{7,5},{8,10},{9,11},{10,... | collective-permute-start | bytes 3145736 | tf_op jit(solution)/shard_map/ppermute | solution.py:32
  360.8 54.7 %collective-permute-start.15 = (bf16[256,2048]{1,0:T(8,128)(2,1)}, bf16[256,2048]{1,0:T(8,128)(2,1)}, u32[]{:S(2)}, u32[]{:S(2)}) collective-permute-start(bf16[256,2048]{1,0:T(8,128)(2,1)} %get-tuple-element.254), channel_id=1, source_target_pairs={{0,1},{1,0},{2,3},{3,2},{4,5},{5,4},{6,7},{7,6},{8,9},{9,8},{10,11... | collective-permute-start | bytes 3145736 | tf_op jit(solution)/shard_map/ppermute | solution.py:32
  418.4 26.5 %collective-permute-start.18 = (bf16[512,512]{1,0:T(8,128)(2,1)}, bf16[512,512]{1,0:T(8,128)(2,1)}, u32[]{:S(2)}, u32[]{:S(2)}) collective-permute-start(bf16[512,512]{1,0:T(8,128)(2,1)} %get-tuple-element.390), channel_id=1, source_target_pairs={{0,3},{1,2},{2,1},{3,0},{4,7},{5,6},{6,5},{7,4},{8,11},{9,10},{10,... | collective-permute-start | bytes 1572872 | tf_op jit(solution)/shard_map/ppermute | solution.py:32
  420.7 24.1 %collective-permute-start.17 = (bf16[512,512]{1,0:T(8,128)(2,1)}, bf16[512,512]{1,0:T(8,128)(2,1)}, u32[]{:S(2)}, u32[]{:S(2)}) collective-permute-start(bf16[512,512]{1,0:T(8,128)(2,1)} %get-tuple-element.391), channel_id=1, source_target_pairs={{0,2},{1,3},{2,0},{3,1},{4,6},{5,7},{6,4},{7,5},{8,10},{9,11},{10,... | collective-permute-start | bytes 1572872 | tf_op jit(solution)/shard_map/ppermute | solution.py:32
  421.3 23.6 %collective-permute-start.16 = (bf16[512,512]{1,0:T(8,128)(2,1)}, bf16[512,512]{1,0:T(8,128)(2,1)}, u32[]{:S(2)}, u32[]{:S(2)}) collective-permute-start(bf16[512,512]{1,0:T(8,128)(2,1)} %get-tuple-element.392), channel_id=1, source_target_pairs={{0,1},{1,0},{2,3},{3,2},{4,5},{5,4},{6,7},{7,6},{8,9},{9,8},{10,11... | collective-permute-start | bytes 1572872 | tf_op jit(solution)/shard_map/ppermute | solution.py:32
  468.9 27.0 %collective-permute-start.19 = (bf16[512,1024]{1,0:T(8,128)(2,1)}, bf16[512,1024]{1,0:T(8,128)(2,1)}, u32[]{:S(2)}, u32[]{:S(2)}) collective-permute-start(bf16[512,1024]{1,0:T(8,128)(2,1)} %get-tuple-element.267), channel_id=1, source_target_pairs={{0,1},{1,0},{2,3},{3,2},{4,5},{5,4},{6,7},{7,6},{8,9},{9,8},{10,11... | collective-permute-start | bytes 3145736 | tf_op jit(solution)/shard_map/ppermute | solution.py:32
  470.4 25.5 %collective-permute-start.20 = (bf16[512,1024]{1,0:T(8,128)(2,1)}, bf16[512,1024]{1,0:T(8,128)(2,1)}, u32[]{:S(2)}, u32[]{:S(2)}) collective-permute-start(bf16[512,1024]{1,0:T(8,128)(2,1)} %get-tuple-element.268), channel_id=1, source_target_pairs={{0,2},{1,3},{2,0},{3,1},{4,6},{5,7},{6,4},{7,5},{8,10},{9,11},{10,... | collective-permute-start | bytes 3145736 | tf_op jit(solution)/shard_map/ppermute | solution.py:32
  495.9 34.5 %collective-permute-start.21 = (bf16[512,1024]{1,0:T(8,128)(2,1)}, bf16[512,1024]{1,0:T(8,128)(2,1)}, u32[]{:S(2)}, u32[]{:S(2)}) collective-permute-start(bf16[512,1024]{1,0:T(8,128)(2,1)} %get-tuple-element.282), channel_id=1, source_target_pairs={{0,1},{1,0},{2,3},{3,2},{4,5},{5,4},{6,7},{7,6},{8,9},{9,8},{10,11... | collective-permute-start | bytes 3145736 | tf_op jit(solution)/shard_map/ppermute | solution.py:32
  496.6 33.8 %collective-permute-start.22 = (bf16[512,1024]{1,0:T(8,128)(2,1)}, bf16[512,1024]{1,0:T(8,128)(2,1)}, u32[]{:S(2)}, u32[]{:S(2)}) collective-permute-start(bf16[512,1024]{1,0:T(8,128)(2,1)} %get-tuple-element.283), channel_id=1, source_target_pairs={{0,2},{1,3},{2,0},{3,1},{4,6},{5,7},{6,4},{7,5},{8,10},{9,11},{10,... | collective-permute-start | bytes 3145736 | tf_op jit(solution)/shard_map/ppermute | solution.py:32
  500.2 30.2 %collective-permute-start.23 = (bf16[256,1024]{1,0:T(8,128)(2,1)}, bf16[256,1024]{1,0:T(8,128)(2,1)}, u32[]{:S(2)}, u32[]{:S(2)}) collective-permute-start(bf16[256,1024]{1,0:T(8,128)(2,1)} %get-tuple-element.315), channel_id=1, source_target_pairs={{0,2},{1,3},{2,0},{3,1},{4,6},{5,7},{6,4},{7,5},{8,10},{9,11},{10,... | collective-permute-start | bytes 1572872 | tf_op jit(solution)/shard_map/ppermute | solution.py:32
  501.6 28.7 %collective-permute-start.24 = (bf16[256,1024]{1,0:T(8,128)(2,1)}, bf16[256,1024]{1,0:T(8,128)(2,1)}, u32[]{:S(2)}, u32[]{:S(2)}) collective-permute-start(bf16[256,1024]{1,0:T(8,128)(2,1)} %get-tuple-element.316), channel_id=1, source_target_pairs={{0,1},{1,0},{2,3},{3,2},{4,5},{5,4},{6,7},{7,6},{8,9},{9,8},{10,11... | collective-permute-start | bytes 1572872 | tf_op jit(solution)/shard_map/ppermute | solution.py:32
  (14 other events, 160.0 us)
Sparse Core Ops, SparseCore 0:
  9.6 84.7 all-gather.6
  96.0 63.2 all-gather.8
  160.9 29.5 all-gather.10
  191.9 81.5 all-gather.12
  275.6 87.7 reduce-scatter.5
  365.6 87.9 reduce-scatter.3
  455.9 90.5 reduce-scatter.7
